TPU v7x, 32 devices: a whole 2x2x4 slice. The times are simulated.
32 devices in a mesh: group: 1, expert: 8 (over z, y), tensor: 2 (over x), dp: 2 (over core).
Axes of the slice: x: 2, y: 2, z: 4, core: 2. Of those that a mesh axis runs over, the one named last changes fastest.
Arguments:
- tokens: bfloat16 [1536, 4096], P(('group', 'expert', 'dp'), 'tensor'), may hold values from -6 to 6
- expert_ids: int32 [1536, 8], P(('group', 'expert', 'dp')), may hold values from 0 to 15, all different within a row; in each aligned block of 96 rows (0 to 95, 96 to 191, ...) at most 72 rows name the same one
- route_weights: float32 [1536, 8], P(('group', 'expert', 'dp')), may hold values from 0.05 to 0.3
- w_gate: bfloat16 [16, 4096, 768], P(('expert', 'dp'), 'tensor'), may hold values from -0.09375 to 0.09375
- w_up: bfloat16 [16, 4096, 768], P(('expert', 'dp'), 'tensor'), may hold values from -0.09375 to 0.09375
- w_down: bfloat16 [16, 768, 4096], P(('expert', 'dp'), None, 'tensor'), may hold values from -0.21875 to 0.21875
Outputs:
- moe_output: bfloat16 [1536, 4096], P(('group', 'expert', 'dp'), 'tensor')
Inputs may be any that keep to these rules, and one draw needn't show every extreme that they name: `expert_ids`: each row names 8 different experts; in each aligned block of 96 rows (the rows of one index pair of expert and dp) no expert is named by more than 72 rows.
All inputs are finite; a program needn't handle non-finite values.
Results may differ from a plain program's by a relative error of at most 0.017.
Values may be sent and summed in bfloat16 or wider, within the bound.
No kernel may reach another device: no remote copies, remote signals or barrier semaphores. Data moves between devices by JAX's collectives and lax.ppermute only.
A program may use at most 64 MiB of HBM per device.

v0:
```python
import jax
import jax.numpy as jnp
from jax import lax
from jax.sharding import PartitionSpec as P


def on_device(tokens, expert_ids, route_weights, w_gate, w_up, w_down):
    rows, width = tokens.shape
    top = expert_ids.shape[1]
    experts = lax.axis_size("expert") * lax.axis_size("dp")
    capacity = min(rows, max(2, 3 * rows * top // (2 * experts)))
    flat_ids = expert_ids.reshape(-1)
    onehot = (flat_ids[:, None] == jnp.arange(experts, dtype=jnp.int32)[None, :]).astype(jnp.int32)
    ranks = jnp.cumsum(onehot, axis=0) - onehot
    slot = jnp.sum(ranks * onehot, axis=1)
    target = flat_ids * capacity + slot
    source = tokens[jnp.arange(rows * top, dtype=jnp.int32) // top]
    outgoing = jnp.zeros((experts * capacity, width), jnp.bfloat16).at[target].set(source)
    outgoing = outgoing.reshape(experts, capacity, width)
    gate_local = w_gate[0]
    up_local = w_up[0]
    down_local = w_down[0]
    slots = lax.all_to_all(outgoing, ("expert", "dp"), split_axis=0, concat_axis=0, tiled=True)
    senders, count, _ = slots.shape
    flat = slots.reshape(senders * count, width)
    gate_part = jnp.dot(flat, gate_local, preferred_element_type=jnp.float32)
    up_part = jnp.dot(flat, up_local, preferred_element_type=jnp.float32)
    gate = lax.psum(gate_part.astype(jnp.bfloat16), "tensor").astype(jnp.float32)
    up = lax.psum(up_part.astype(jnp.bfloat16), "tensor").astype(jnp.float32)
    hidden = (jax.nn.silu(gate) * up).astype(jnp.bfloat16)
    result = jnp.dot(hidden, down_local, preferred_element_type=jnp.float32)
    processed = result.astype(jnp.bfloat16).reshape(senders, count, width)
    returned = lax.all_to_all(processed, ("expert", "dp"), split_axis=0, concat_axis=0, tiled=True)
    picked = returned.reshape(experts * capacity, width)[target].reshape(rows, top, width)
    mixed = jnp.sum(route_weights[:, :, None] * picked, axis=1)
    return mixed.astype(jnp.bfloat16)


def solution(mesh):
    placed = (
        P(("group", "expert", "dp"), "tensor"),
        P(("group", "expert", "dp"), None),
        P(("group", "expert", "dp"), None),
        P(("expert", "dp"), "tensor", None),
        P(("expert", "dp"), "tensor", None),
        P(("expert", "dp"), None, "tensor"),
    )
    return jax.shard_map(
        on_device,
        mesh=mesh,
        in_specs=placed,
        out_specs=P(("group", "expert", "dp"), "tensor"),
        check_vma=False,
    )
```

profile of v0, /device:TPU:13, one launch (start us, length us, event | category | flops | bytes accessed | tf_op | source)
XLA Modules:
  0.0 397.6 jit_solution(2972464461649134389)
XLA Ops:
  6.5 0.0 copy-start
  6.5 0.0 all-reduce.3.cloned.1.call-start
  6.5 0.9 copy.10
  7.5 0.1 eq.29
  7.6 0.1 eq.25
  7.6 0.7 broadcast_multiply_fusion
  8.4 1.7 reduce-window.6
  10.1 0.3 slice_reduce_fusion
  10.4 0.1 copy.9
  10.5 0.1 mul.37
  10.6 0.1 fusion.16
  10.7 31.3 %scatter_custom_fusion = bf16[1152,2048]{1,0:T(8,128)(2,1)} fusion(s32[768]{0:T(1024)S(1)} %fusion.18, bf16[96,2048]{1,0:T(8,128)(2,1)} %param.6, s32[1024]{0:T(1024)S(1)} %pad_clamp_fusion.1, bf16[]{:T(256)} %constant.26.clone.1), kind=kCustom, calls=%fused_computation.18 | custom fusion | bytes 4719104 | tf_op jit(solution)/shard_map/scatter | solution.py:18
  42.0 0.0 copy-start.2
  42.0 110.3 %all_to_all.10 = bf16[16,72,2048]{2,1,0:T(8,128)(2,1)S(1)} all-to-all(bf16[16,72,2048]{2,1,0:T(8,128)(2,1)} %bitcast.38), channel_id=1, replica_groups=mesh['group'=1,'expert'=8,'tensor'=2,'dp'=2] {'expert','dp'}, dimensions={0} | all-to-all | bytes 9437184 | tf_op jit(solution)/shard_map/all_to_all | solution.py:23
  152.3 0.0 copy-done.2
  152.3 0.0 copy-start.3
  152.3 5.0 %convolution_convert_fusion.1 = bf16[1152,768]{1,0:T(8,128)(2,1)} fusion(bf16[1152,2048]{1,0:T(8,128)(2,1)S(1)} %bitcast.40, bf16[1,2048,768]{2,1,0:T(8,128)(2,1)S(1)} %copy-done.2), kind=kOutput, calls=%fused_computation.13 | convolution fusion | flops 3624763392 | bytes 9633792 | tf_op jit(solution)/shard_map/dot_general | solution.py:27
  157.3 0.0 copy-done.3
  157.3 5.0 %convolution_convert_fusion.2 = bf16[1152,768]{1,0:T(8,128)(2,1)} fusion(bf16[1152,2048]{1,0:T(8,128)(2,1)S(1)} %bitcast.41, bf16[1,2048,768]{2,1,0:T(8,128)(2,1)S(1)} %copy-done.3), kind=kOutput, calls=%fused_computation.14 | convolution fusion | flops 3624763392 | bytes 9633792 | tf_op jit(solution)/shard_map/dot_general | solution.py:26
  162.2 0.0 all-reduce.3.cloned.1.call-update
  162.3 94.6 %all-reduce.3.cloned.1.call-done = (bf16[1152,768]{1,0:T(8,128)(2,1)}, bf16[1152,768]{1,0:T(8,128)(2,1)}) async-done(((bf16[1152,768]{1,0:T(8,128)(2,1)}, bf16[1152,768]{1,0:T(8,128)(2,1)}), (bf16[1152,768]{1,0:T(8,128)(2,1)}, bf16[1152,768]{1,0:T(8,128)(2,1)})) %all-reduce.3.cloned.1.call-update) | async-done | bytes 3538960 | tf_op jit(solution)/shard_map/psum | solution.py:29
  256.9 0.0 copy-done
  256.9 8.0 %convolution_convert_fusion = bf16[1152,2048]{1,0:T(8,128)(2,1)} fusion(bf16[1,768,2048]{2,1,0:T(8,128)(2,1)S(1)} %copy-done, bf16[1152,768]{1,0:T(8,128)(2,1)} %get-tuple-element.5, bf16[1152,768]{1,0:T(8,128)(2,1)} %get-tuple-element.6), kind=kOutput, calls=%fused_computation.3 | convolution fusion | flops 3633315840 | bytes 11403264 | tf_op jit(solution)/shard_map/dot_general | solution.py:31
  264.9 0.0 copy-start.1
  264.9 6.5 %all-to-all-start.1 = ((bf16[16,72,2048]{2,1,0:T(8,128)(2,1)}), bf16[16,72,2048]{2,1,0:T(8,128)(2,1)}, u32[]{:S(2)}, u32[]{:S(2)}) async-start(bf16[16,72,2048]{2,1,0:T(8,128)(2,1)} %bitcast.39), calls=%async_computation.1 | async-start | bytes 9437184 | tf_op jit(solution)/shard_map/all_to_all | solution.py:33
  271.4 0.0 copy-done.1
  271.4 0.1 copy.8
  271.5 103.6 %all-to-all-done.1 = bf16[16,72,2048]{2,1,0:T(8,128)(2,1)} async-done(((bf16[16,72,2048]{2,1,0:T(8,128)(2,1)}), bf16[16,72,2048]{2,1,0:T(8,128)(2,1)}, u32[]{:S(2)}, u32[]{:S(2)}) %all-to-all-start.1) | async-done | bytes 4718624 | tf_op jit(solution)/shard_map/all_to_all | solution.py:33
  375.1 10.1 %gather_fusion = bf16[768,2048]{1,0:T(8,128)(2,1)} fusion(bf16[1152,2048]{1,0:T(8,128)(2,1)} %bitcast.7, s32[1024]{0:T(1024)S(1)} %pad_clamp_fusion), kind=kCustom, calls=%fused_computation.1 | custom fusion | bytes 6294528 | tf_op jit(solution)/shard_map/gather | solution.py:34
  385.1 5.6 %fusion = bf16[96,2048]{1,0:T(8,128)(2,1)} fusion(bf16[768,2048]{1,0:T(8,128)(2,1)} %gather_fusion, f32[96,8]{1,0:T(8,128)S(1)} %copy.8), kind=kLoop, calls=%fused_computation.5 | loop fusion | flops 4521984 | bytes 3542016 | tf_op jit(solution)/shard_map/reduce_sum | solution.py:35
  (6 shorter events, 0.1 us)
Async XLA Ops:
  6.5 250.3 %copy-start = (bf16[1,768,2048]{2,1,0:T(8,128)(2,1)S(1)}, bf16[1,768,2048]{2,1,0:T(8,128)(2,1)}, u32[]{:S(2)}) copy-start(bf16[1,768,2048]{2,1,0:T(8,128)(2,1)} %param.11) | copy-start | bytes 9437188
  6.5 250.3 %all-reduce.3.cloned.1.call-start = ((), (), s32[]{:S(2)}) async-start(), calls=%async_computation.2 | async-start | bytes 7077888 | tf_op jit(solution)/shard_map/psum | solution.py:29
  42.0 110.3 %copy-start.2 = (bf16[1,2048,768]{2,1,0:T(8,128)(2,1)S(1)}, bf16[1,2048,768]{2,1,0:T(8,128)(2,1)}, u32[]{:S(2)}) copy-start(bf16[1,2048,768]{2,1,0:T(8,128)(2,1)} %param.10) | copy-start | bytes 9437188
  152.3 5.0 %copy-start.3 = (bf16[1,2048,768]{2,1,0:T(8,128)(2,1)S(1)}, bf16[1,2048,768]{2,1,0:T(8,128)(2,1)}, u32[]{:S(2)}) copy-start(bf16[1,2048,768]{2,1,0:T(8,128)(2,1)} %param.9) | copy-start | bytes 9437188
  264.9 6.5 %copy-start.1 = (f32[96,8]{0,1:T(8,128)S(1)}, f32[96,8]{0,1:T(8,128)}, u32[]{:S(2)}) copy-start(f32[96,8]{0,1:T(8,128)} %param.8) | copy-start | bytes 9220
  264.9 110.2 %all-to-all-start.1 = ((bf16[16,72,2048]{2,1,0:T(8,128)(2,1)}), bf16[16,72,2048]{2,1,0:T(8,128)(2,1)}, u32[]{:S(2)}, u32[]{:S(2)}) async-start(bf16[16,72,2048]{2,1,0:T(8,128)(2,1)} %bitcast.39), calls=%async_computation.1 | async-start | bytes 9437184 | tf_op jit(solution)/shard_map/all_to_all | solution.py:33
Sparse Core Ops, SparseCore 0:
  162.4 94.4 all-reduce.2
where the time goes:
time: 398 us
  waiting for transfers between devices  198 us (50%)
  blocking collectives  110 us (28%)
  local copies, waits for them, and re-layouts  43 us (11%)
  matrix products  18 us (5%)
  between operations  13.4 us (3%)
  other arithmetic  8.22 us (2%)
  starting transfers between devices  6.5 us (2%)
    all_to_all x1, blocking collectives, on_device(): lax.all_to_all(outgoing, ('expert', 'dp'), split_axis=0, concat_axis=0, t...  110 us
    all_to_all x1, waiting for transfers between devices, on_device(): lax.all_to_all(processed, ('expert', 'dp'), split_axis=0, concat_axis=0,...  104 us
    psum x1, waiting for transfers between devices, on_device(): up = lax.psum(up_part.astype(jnp.bfloat16), 'tensor').astype(jnp.float32)  94.6 us
    scatter x1, local copies, waits for them, and re-layouts, on_device(): jnp.zeros((experts * capacity, width), jnp.bfloat16).at[target].set(source)  31.3 us
    gather x1, local copies, waits for them, and re-layouts, on_device(): returned.reshape(experts * capacity, width)[target]  10.1 us
    dot_general x1, matrix products, on_device(): result = jnp.dot(hidden, down_local, preferred_element_type=jnp.float32)  8.03 us
  transfers between devices with their start and end apart: 2, of which 2 were waited for; matrix products, arithmetic and copies ran while one was open for 0% of the time, Pallas kernels for 0%

commit v1 on v0

v1 whole, which is shorter than its diff:
```python
import jax
import jax.numpy as jnp
from jax import lax
from jax.sharding import PartitionSpec as P

F32 = jnp.float32
BF16 = jnp.bfloat16


def on_device(tokens, expert_ids, route_weights, w_gate, w_up, w_down):
    rows, width = tokens.shape
    top = expert_ids.shape[1]
    experts = lax.axis_size("expert") * lax.axis_size("dp")
    capacity = min(rows, max(2, 3 * rows * top // (2 * experts)))
    parts = lax.axis_size("tensor")
    me = lax.axis_index("expert") * lax.axis_size("dp") + lax.axis_index("dp")
    rank = lax.axis_index("tensor")
    ids = jnp.arange(experts, dtype=jnp.int32)
    hit = expert_ids[:, :, None] == ids[None, None, :]
    dense = jnp.sum(jnp.where(hit, route_weights[:, :, None], 0.0), axis=1)
    weights = lax.all_to_all(dense.T, ("expert", "dp"), split_axis=0, concat_axis=0, tiled=True)
    everyone = lax.all_gather(tokens, ("expert", "dp"), axis=0, tiled=True)
    live = weights > 0.0
    slot = jnp.cumsum(live.astype(jnp.int32), axis=1) - 1
    slot = jnp.where(live, slot, -1)
    pick = (slot[:, None, :] == jnp.arange(capacity, dtype=jnp.int32)[None, :, None]).astype(BF16)
    chosen = jnp.einsum("scn,snd->scd", pick, everyone.reshape(experts, rows, width), preferred_element_type=F32)
    chosen = chosen.astype(BF16).reshape(parts, experts * capacity // parts, width)
    gate_part = jnp.dot(chosen, w_gate[0], preferred_element_type=F32).astype(BF16)
    up_part = jnp.dot(chosen, w_up[0], preferred_element_type=F32).astype(BF16)
    both = jnp.concatenate([gate_part, up_part], axis=2)
    total = lax.dynamic_index_in_dim(both, rank, 0, keepdims=False).astype(F32)
    for step in range(1, parts):
        sent = lax.dynamic_index_in_dim(both, (rank + step) % parts, 0, keepdims=False)
        got = lax.ppermute(sent, "tensor", [(i, (i + step) % parts) for i in range(parts)])
        total = total + got.astype(F32)
    units = w_gate.shape[2]
    hidden = (jax.nn.silu(total[:, :units]) * total[:, units:]).astype(BF16)
    pieces = [hidden]
    for step in range(1, parts):
        pieces.append(lax.ppermute(hidden, "tensor", [(i, (i + step) % parts) for i in range(parts)]))
    order = (rank - jnp.arange(parts)) % parts
    hidden_all = jnp.stack(pieces)[order].reshape(experts, capacity, units)
    spread = jnp.einsum("scn,scf->snf", pick, hidden_all, preferred_element_type=F32).astype(BF16)
    result = jnp.dot(spread.reshape(experts * rows, units), w_down[0], preferred_element_type=F32)
    term = (result * weights.reshape(experts * rows)[:, None]).astype(BF16)
    return lax.psum_scatter(term, ("expert", "dp"), scatter_dimension=0, tiled=True)


def solution(mesh):
    placed = (
        P(("group", "expert", "dp"), "tensor"),
        P(("group", "expert", "dp"), None),
        P(("group", "expert", "dp"), None),
        P(("expert", "dp"), "tensor", None),
        P(("expert", "dp"), "tensor", None),
        P(("expert", "dp"), None, "tensor"),
    )
    return jax.shard_map(
        on_device,
        mesh=mesh,
        in_specs=placed,
        out_specs=P(("group", "expert", "dp"), "tensor"),
        check_vma=False,
    )
```

time: 398 us -> 263 us (0.66)
  the two profiles are of different devices: /device:TPU:13 before, /device:TPU:0 now
where the time goes in v1:
time: 263 us; the launch traced here: 262 us
  waiting for transfers between devices  198 us (75%)
  matrix products  21.4 us (8%)
  between operations  13.5 us (5%)
  other arithmetic  13 us (5%)
  starting transfers between devices  10.4 us (4%)
  local copies, waits for them, and re-layouts  6.01 us (2%)
    reduce_scatter x1, waiting for transfers between devices, on_device(): lax.psum_scatter(term, ('expert', 'dp'), scatter_dimension=0, tiled=True)  84 us
    all_gather x1, waiting for transfers between devices, on_device(): everyone = lax.all_gather(tokens, ('expert', 'dp'), axis=0, tiled=True)  51.4 us
    ppermute x1, waiting for transfers between devices, on_device(): lax.ppermute(sent, 'tensor', [(i, (i + step) % parts) for i in range(part...  39.6 us
    ppermute x1, waiting for transfers between devices, on_device(): lax.ppermute(hidden, 'tensor', [(i, (i + step) % parts) for i in range(pa...  16.1 us
    all_to_all x1, starting transfers between devices, on_device(): lax.all_to_all(dense.T, ('expert', 'dp'), split_axis=0, concat_axis=0, ti...  7.39 us
    dot_general x1, matrix products, on_device(): jnp.dot(spread.reshape(experts * rows, units), w_down[0], preferred_eleme...  7.1 us
    all_to_all x1, waiting for transfers between devices, on_device(): lax.all_to_all(dense.T, ('expert', 'dp'), split_axis=0, concat_axis=0, ti...  6.27 us
  transfers between devices with their start and end apart: 5, of which 5 were waited for; matrix products, arithmetic and copies ran while one was open for 2% of the time, Pallas kernels for 0%

profile of v1, /device:TPU:0, one launch (start us, length us, event | category | flops | bytes accessed | tf_op | source)
XLA Modules:
  0.0 262.4 jit_solution(9908485151622136694)
XLA Ops:
  6.5 0.0 copy-start
  6.5 0.0 all-gather.2.cloned.1.call-start
  6.5 0.7 all-gather.2.cloned.1.call-update
  7.3 1.5 select_reduce_fusion
  8.8 7.4 %all-to-all-start = ((f32[16,1,96]{2,1,0:T(1,128)}), f32[16,1,96]{2,1,0:T(1,128)S(1)}, u32[]{:S(2)}, u32[]{:S(2)}) async-start(f32[16,1,96]{2,1,0:T(1,128)} %bitcast.2), calls=%async_computation | async-start | bytes 16384 | tf_op jit(solution)/shard_map/all_to_all | solution.py:21
  16.2 0.0 reduce-scatter.2.cloned.1.call-start
  16.3 6.3 %all-to-all-done = f32[16,1,96]{2,1,0:T(1,128)S(1)} async-done(((f32[16,1,96]{2,1,0:T(1,128)}), f32[16,1,96]{2,1,0:T(1,128)S(1)}, u32[]{:S(2)}, u32[]{:S(2)}) %all-to-all-start) | async-done | bytes 6176 | tf_op jit(solution)/shard_map/all_to_all | solution.py:21
  22.5 0.3 reduce_window_sum.11
  22.8 51.4 %all-gather.2.cloned.1.call-done = bf16[1536,2048]{1,0:T(8,128)(2,1)} async-done(((bf16[96,2048]{1,0:T(8,128)(2,1)}), bf16[1536,2048]{1,0:T(8,128)(2,1)}) %all-gather.2.cloned.1.call-update) | async-done | bytes 6291472 | tf_op jit(solution)/shard_map/all_gather | solution.py:22
  74.2 0.0 copy-start.4
  74.2 4.3 %convolution_convert_fusion = bf16[16,72,2048]{2,1,0:T(8,128)(2,1)S(1)} fusion(bf16[16,96,2048]{2,1,0:T(8,128)(2,1)} %bitcast.45, s32[16,96]{1,0:T(8,128)S(1)} %select_bitcast_fusion), kind=kOutput, calls=%fused_computation.6 | convolution fusion | flops 455454720 | bytes 11016192 | tf_op jit(solution)/shard_map/scn,snd->scd/dot_general | solution.py:27
  78.5 0.0 copy-done.4
  78.5 0.0 copy-start.5
  78.6 3.9 %fusion.10 = bf16[2,576,768]{2,1,0:T(8,128)(2,1)S(1)} fusion(bf16[2,576,2048]{2,1,0:T(8,128)(2,1)S(1)} %bitcast.46, bf16[1,2048,768]{2,1,0:T(8,128)(2,1)S(1)} %copy-done.4), kind=kOutput, calls=%fused_computation.21 | convolution fusion | flops 3624763392 | bytes 9633792 | tf_op jit(solution)/shard_map/dot_general | solution.py:29
  82.4 0.0 copy-done.5
  82.4 0.0 copy-start.2
  82.4 3.9 %fusion.13 = bf16[2,576,768]{2,1,0:T(8,128)(2,1)S(1)} fusion(bf16[2,576,2048]{2,1,0:T(8,128)(2,1)S(1)} %bitcast.47, bf16[1,2048,768]{2,1,0:T(8,128)(2,1)S(1)} %copy-done.5), kind=kOutput, calls=%fused_computation.22 | convolution fusion | flops 3624763392 | bytes 9633792 | tf_op jit(solution)/shard_map/dot_general | solution.py:30
  86.3 0.0 copy-done.2
  86.3 0.0 copy-start.3
  86.3 1.5 fusion.6
  87.8 0.3 copy-done.3
  88.2 1.5 collective-permute-start
  89.6 39.6 %collective-permute-done = bf16[576,1536]{1,0:T(8,128)(2,1)} collective-permute-done((bf16[576,1536]{1,0:T(8,128)(2,1)}, bf16[576,1536]{1,0:T(8,128)(2,1)}, u32[]{:S(2)}, u32[]{:S(2)}) %collective-permute-start) | collective-permute-done | bytes 1769504 | tf_op jit(solution)/shard_map/ppermute | solution.py:35
  129.3 2.5 convert_add_fusion
  131.7 0.0 copy-start.1
  131.8 1.7 copy-done.1
  133.5 1.4 fusion.9
  134.9 1.5 collective-permute-start.1
  136.4 0.5 broadcast.92
  136.9 0.7 reduce.3
  137.6 0.1 mul.19
  137.7 2.5 fusion.26
  140.2 16.1 %collective-permute-done.1 = bf16[576,768]{1,0:T(8,128)(2,1)} collective-permute-done((bf16[576,768]{1,0:T(8,128)(2,1)}, bf16[576,768]{1,0:T(8,128)(2,1)}, u32[]{:S(2)}, u32[]{:S(2)}) %collective-permute-start.1) | collective-permute-done | bytes 884768 | tf_op jit(solution)/shard_map/ppermute | solution.py:41
  156.2 2.6 pad_maximum_fusion
  158.8 3.3 %gather_fusion = bf16[2,576,768]{2,1,0:T(8,128)(2,1)} fusion(bf16[2,576,768]{2,1,0:T(8,128)(2,1)} %pad_maximum_fusion, s32[1024]{0:T(1024)S(1)} %pad_clamp_fusion), kind=kCustom, calls=%fused_computation | custom fusion | bytes 3538952 | tf_op jit(solution)/shard_map/gather | solution.py:43
  162.1 2.3 convolution_convert_fusion.1
  164.4 0.0 copy-done
  164.4 7.1 %multiply_convert_fusion = bf16[1536,2048]{1,0:T(8,128)(2,1)} fusion(bf16[1536,768]{1,0:T(8,128)(2,1)S(1)} %bitcast.48, f32[1536]{0:T(1024)S(1)} %mul.19, bf16[1,768,2048]{2,1,0:T(8,128)(2,1)S(1)} %copy-done), kind=kOutput, calls=%fused_computation.1 | convolution fusion | flops 4838129664 | bytes 11802624 | tf_op jit(solution)/shard_map/dot_general | solution.py:45
  171.6 0.0 reduce-scatter.2.cloned.1.call-update
  171.6 84.0 %reduce-scatter.2.cloned.1.call-done = bf16[96,2048]{1,0:T(8,128)(2,1)} async-done(((bf16[1536,2048]{1,0:T(8,128)(2,1)}), bf16[96,2048]{1,0:T(8,128)(2,1)}) %reduce-scatter.2.cloned.1.call-update) | async-done | bytes 393232 | tf_op jit(solution)/shard_map/reduce_scatter | solution.py:47
  (4 shorter events, 0.0 us)
Async XLA Ops:
  6.5 157.9 %copy-start = (bf16[1,768,2048]{2,1,0:T(8,128)(2,1)S(1)}, bf16[1,768,2048]{2,1,0:T(8,128)(2,1)}, u32[]{:S(2)}) copy-start(bf16[1,768,2048]{2,1,0:T(8,128)(2,1)} %param.11) | copy-start | bytes 9437188
  6.5 67.7 %all-gather.2.cloned.1.call-start = ((), (), s32[]{:S(2)}) async-start(), calls=%async_computation.2 | async-start | bytes 6684672 | tf_op jit(solution)/shard_map/all_gather | solution.py:22
  8.8 13.7 %all-to-all-start = ((f32[16,1,96]{2,1,0:T(1,128)}), f32[16,1,96]{2,1,0:T(1,128)S(1)}, u32[]{:S(2)}, u32[]{:S(2)}) async-start(f32[16,1,96]{2,1,0:T(1,128)} %bitcast.2), calls=%async_computation | async-start | bytes 16384 | tf_op jit(solution)/shard_map/all_to_all | solution.py:21
  16.2 239.4 %reduce-scatter.2.cloned.1.call-start = ((), (), s32[]{:S(2)}) async-start(), calls=%async_computation.3 | async-start | bytes 6684672 | tf_op jit(solution)/shard_map/reduce_scatter | solution.py:47
  74.2 4.3 %copy-start.4 = (bf16[1,2048,768]{2,1,0:T(8,128)(2,1)S(1)}, bf16[1,2048,768]{2,1,0:T(8,128)(2,1)}, u32[]{:S(2)}) copy-start(bf16[1,2048,768]{2,1,0:T(8,128)(2,1)} %param.9) | copy-start | bytes 9437188
  78.5 3.9 %copy-start.5 = (bf16[1,2048,768]{2,1,0:T(8,128)(2,1)S(1)}, bf16[1,2048,768]{2,1,0:T(8,128)(2,1)}, u32[]{:S(2)}) copy-start(bf16[1,2048,768]{2,1,0:T(8,128)(2,1)} %param.10) | copy-start | bytes 9437188
  82.4 3.9 %copy-start.2 = (bf16[2,576,768]{2,1,0:T(8,128)(2,1)}, bf16[2,576,768]{2,1,0:T(8,128)(2,1)S(1)}, u32[]{:S(2)}) copy-start(bf16[2,576,768]{2,1,0:T(8,128)(2,1)S(1)} %fusion.10) | copy-start | bytes 5308420
  86.3 1.8 copy-start.3
  88.2 41.1 %collective-permute-start = (bf16[576,1536]{1,0:T(8,128)(2,1)}, bf16[576,1536]{1,0:T(8,128)(2,1)}, u32[]{:S(2)}, u32[]{:S(2)}) collective-permute-start(bf16[576,1536]{1,0:T(8,128)(2,1)} %fusion.6), channel_id=1, source_target_pairs={{0,2},{2,0},{1,3},{3,1},{4,6},{6,4},{5,7},{7,5},{8,10},{10,8},{9,1... | collective-permute-start | bytes 5308424 | tf_op jit(solution)/shard_map/ppermute | solution.py:35
  131.7 1.7 copy-start.1
  134.9 21.3 %collective-permute-start.1 = (bf16[576,768]{1,0:T(8,128)(2,1)}, bf16[576,768]{1,0:T(8,128)(2,1)}, u32[]{:S(2)}, u32[]{:S(2)}) collective-permute-start(bf16[576,768]{1,0:T(8,128)(2,1)} %fusion.9), channel_id=1, source_target_pairs={{0,2},{2,0},{1,3},{3,1},{4,6},{6,4},{5,7},{7,5},{8,10},{10,8},{9,1... | collective-permute-start | bytes 2654216 | tf_op jit(solution)/shard_map/ppermute | solution.py:41
Sparse Core Ops, SparseCore 0:
  9.6 64.5 all-gather.1
  171.7 83.8 reduce-scatter.1

commit v2 on v1

v2 whole, which is shorter than its diff:
```python
import functools

import jax
import jax.numpy as jnp
from jax import lax
from jax.experimental import pallas as pl
from jax.experimental.pallas import tpu as pltpu
from jax.sharding import PartitionSpec as P

F32 = jnp.float32
BF16 = jnp.bfloat16
LANES = 128
VMEM = 48 * 1024 * 1024


def tile(extent, choices):
    for size in choices:
        if extent % size == 0:
            return size
    return extent


def slot_row(tails, me, experts, rows, capacity):
    total = tails.shape[0]
    column = lax.broadcasted_iota(jnp.int32, (8, tails.shape[1]), 1)
    mark = jnp.where((column == me) | (column == experts + me), 1.0, 0.0).astype(BF16)
    weight = lax.dot_general(mark, tails, (((1,), (1,)), ((), ())), preferred_element_type=F32)
    live = weight > 0.0
    above = lax.broadcasted_iota(jnp.int32, (total, total), 0)
    own = lax.broadcasted_iota(jnp.int32, (total, total), 1)
    ahead = jnp.where((above < own) & (above // rows == own // rows), 1.0, 0.0).astype(BF16)
    before = jnp.dot(jnp.where(live, 1.0, 0.0).astype(BF16), ahead, preferred_element_type=F32)
    base = lax.broadcasted_iota(jnp.int32, (8, total), 1) // rows * capacity
    return jnp.where(live, before.astype(jnp.int32) + base, -1)[0:1]


def slot_column(tails, me, experts, rows, capacity):
    total = tails.shape[0]
    column = lax.broadcasted_iota(jnp.int32, tails.shape, 1)
    mine = (column == me) | (column == experts + me)
    weight = jnp.sum(jnp.where(mine, tails.astype(F32), 0.0), axis=1, keepdims=True)
    live = weight > 0.0
    own = lax.broadcasted_iota(jnp.int32, (total, total), 0)
    above = lax.broadcasted_iota(jnp.int32, (total, total), 1)
    ahead = jnp.where((above < own) & (above // rows == own // rows), 1.0, 0.0).astype(BF16)
    flags = jnp.broadcast_to(jnp.where(live, 1.0, 0.0), (total, LANES)).astype(BF16)
    before = jnp.dot(ahead, flags, preferred_element_type=F32)[:, 0:1]
    base = lax.broadcasted_iota(jnp.int32, (total, 1), 0) // rows * capacity
    return jnp.where(live, before.astype(jnp.int32) + base, -1), weight


def pick_kernel(width, experts, capacity, me_ref, a_ref, b_ref, c_ref, d_ref, w_ref, chosen_ref, part_ref):
    rows = a_ref.shape[0]
    count = 4 * capacity

    @pl.when(pl.program_id(0) == 0)
    def _():
        blocks = (a_ref, b_ref, c_ref, d_ref)
        tails = jnp.concatenate([r[:, width:] for r in blocks], axis=0)
        slot = slot_row(tails, me_ref[0], experts, rows, capacity)
        place = lax.broadcasted_iota(jnp.int32, (count, 4 * rows), 0)
        pick = jnp.where(place == slot, 1.0, 0.0).astype(BF16)
        x = jnp.concatenate([r[:, :width] for r in blocks], axis=0)
        chosen_ref[...] = jnp.dot(pick, x, preferred_element_type=F32).astype(BF16)

    part_ref[...] = jnp.dot(chosen_ref[...], w_ref[...], preferred_element_type=F32).astype(BF16)


def pick_rows(me, blocks, weights, width, experts, capacity):
    rows, padded = blocks[0].shape
    columns = weights.shape[1]
    step = tile(columns, (256, 384))
    whole = pl.BlockSpec((rows, padded), lambda i: (0, 0))
    count = 4 * capacity
    return pl.pallas_call(
        functools.partial(pick_kernel, width, experts, capacity),
        grid=(columns // step,),
        out_shape=(
            jax.ShapeDtypeStruct((count, width), BF16),
            jax.ShapeDtypeStruct((count, columns), BF16),
        ),
        in_specs=[pl.BlockSpec(memory_space=pltpu.SMEM)] + [whole] * 4 + [pl.BlockSpec((width, step), lambda i: (0, i))],
        out_specs=(
            pl.BlockSpec((count, width), lambda i: (0, 0)),
            pl.BlockSpec((count, step), lambda i: (0, i)),
        ),
        compiler_params=pltpu.CompilerParams(vmem_limit_bytes=VMEM),
        cost_estimate=pl.CostEstimate(
            flops=2 * count * width * columns + 8 * count * rows * width,
            bytes_accessed=2 * (4 * rows * padded + width * columns + count * (width + columns)),
            transcendentals=0,
        ),
    )(me, *blocks, weights)


def down_kernel(experts, capacity, rows, pieces, me_ref, *refs):
    hidden_refs = refs[:pieces]
    tail_refs = refs[pieces:pieces + 4]
    w_ref, out_ref, spread_ref, weight_ref = refs[pieces + 4:]
    total = 4 * rows

    @pl.when(pl.program_id(0) == 0)
    def _():
        tails = jnp.concatenate([r[...] for r in tail_refs], axis=0)
        slot, weight = slot_column(tails, me_ref[0], experts, rows, capacity)
        place = lax.broadcasted_iota(jnp.int32, (total, 4 * capacity), 1)
        spread = jnp.where(place == slot, 1.0, 0.0).astype(BF16)
        units = hidden_refs[0].shape[1]
        for i, ref in enumerate(hidden_refs):
            value = jnp.dot(spread, ref[...], preferred_element_type=F32)
            spread_ref[:, i * units:(i + 1) * units] = value.astype(BF16)
        weight_ref[...] = weight

    result = jnp.dot(spread_ref[...], w_ref[...], preferred_element_type=F32)
    out_ref[...] = (result * weight_ref[...]).astype(BF16)


def down_rows(me, hiddens, blocks, weights, width, experts, capacity):
    rows, padded = blocks[0].shape
    units = weights.shape[0]
    step = tile(width, (512, 256))
    tail = pl.BlockSpec((rows, padded - width), lambda i: (0, width // (padded - width)))
    pieces = len(hiddens)
    return pl.pallas_call(
        functools.partial(down_kernel, experts, capacity, rows, pieces),
        grid=(width // step,),
        out_shape=jax.ShapeDtypeStruct((4 * rows, width), BF16),
        in_specs=[pl.BlockSpec(memory_space=pltpu.SMEM)]
        + [pl.BlockSpec(hiddens[0].shape, lambda i: (0, 0))] * pieces
        + [tail] * 4
        + [pl.BlockSpec((units, step), lambda i: (0, i))],
        out_specs=pl.BlockSpec((4 * rows, step), lambda i: (0, i)),
        scratch_shapes=[pltpu.VMEM((4 * rows, units), BF16), pltpu.VMEM((4 * rows, 1), F32)],
        compiler_params=pltpu.CompilerParams(vmem_limit_bytes=VMEM),
        cost_estimate=pl.CostEstimate(
            flops=8 * rows * units * (width + 4 * capacity),
            bytes_accessed=2 * (4 * rows * width + units * width + 4 * capacity * units),
            transcendentals=0,
        ),
    )(me, *hiddens, *blocks, weights)


def on_device(tokens, expert_ids, route_weights, w_gate, w_up, w_down):
    rows, width = tokens.shape
    top = expert_ids.shape[1]
    ring = lax.axis_size("expert")
    experts = ring * lax.axis_size("dp")
    capacity = min(rows, max(2, 3 * rows * top // (2 * experts)))
    parts = lax.axis_size("tensor")
    units = w_gate.shape[2] // parts
    me = lax.axis_index("expert") * lax.axis_size("dp") + lax.axis_index("dp")
    me = me.astype(jnp.int32).reshape(1)
    rank = lax.axis_index("tensor")
    hops = ring // 2

    def over_y(x):
        return lax.ppermute(x, "expert", [(i, i ^ 1) for i in range(ring)])

    def over_z(x):
        return lax.ppermute(x, "expert", [(i, (i + 2) % ring) for i in range(ring)])

    def over_core(x):
        return lax.ppermute(x, "dp", [(0, 1), (1, 0)])

    def over_x(x, step):
        return lax.ppermute(x, "tensor", [(i, (i + step) % parts) for i in range(parts)])

    ids = jnp.arange(experts, dtype=jnp.int32)
    hit = expert_ids[:, :, None] == ids[None, None, :]
    dense = jnp.sum(jnp.where(hit, route_weights[:, :, None], 0.0), axis=1)
    high = lax.reduce_precision(dense, 8, 7)
    low = dense - high
    spare = -(2 * experts) % LANES
    block = jnp.concatenate(
        [tokens, high.astype(BF16), low.astype(BF16), jnp.zeros((rows, spare), BF16)], axis=1
    )

    def unit_slice(w, offset, axis):
        return lax.dynamic_slice_in_dim(w, (rank + offset) % parts * units, units, axis)

    away = []
    for step in range(1, parts):
        away += [unit_slice(w_gate[0], step, 1), unit_slice(w_up[0], step, 1)]
    w_away = jnp.concatenate(away, axis=1)
    w_home = jnp.concatenate([unit_slice(w_gate[0], 0, 1), unit_slice(w_up[0], 0, 1)], axis=1)
    w_out = jnp.concatenate([unit_slice(w_down[0], parts - step, 0) for step in range(parts)], axis=0)

    carried = None
    own = None
    for hop in range(hops):
        if hop > 0:
            block = over_z(block)
        beside = over_y(block)
        blocks = (block, beside, over_core(block), over_core(beside))
        chosen, away_part = pick_rows(me, blocks, w_away, width, experts, capacity)
        got = [over_x(away_part[:, 2 * units * (s - 1):2 * units * s], s) for s in range(1, parts)]
        total = jnp.dot(chosen, w_home, preferred_element_type=F32)
        for piece in got:
            total = total + piece.astype(F32)
        hidden = (jax.nn.silu(total[:, :units]) * total[:, units:]).astype(BF16)
        hiddens = [hidden] + [over_x(hidden, s) for s in range(1, parts)]
        term = down_rows(me, hiddens, blocks, w_out, width, experts, capacity)
        pair = term[:2 * rows].astype(F32) + over_core(term[2 * rows:]).astype(F32)
        here = pair[:rows] + over_y(pair[rows:].astype(BF16)).astype(F32)
        if hop == 0:
            own = here
        else:
            if carried is not None:
                here = here + carried.astype(F32)
            carried = over_z(here.astype(BF16))
    if carried is not None:
        own = own + carried.astype(F32)
    return own.astype(BF16)


def solution(mesh):
    placed = (
        P(("group", "expert", "dp"), "tensor"),
        P(("group", "expert", "dp"), None),
        P(("group", "expert", "dp"), None),
        P(("expert", "dp"), "tensor", None),
        P(("expert", "dp"), "tensor", None),
        P(("expert", "dp"), None, "tensor"),
    )
    return jax.shard_map(
        on_device,
        mesh=mesh,
        in_specs=placed,
        out_specs=P(("group", "expert", "dp"), "tensor"),
        check_vma=False,
    )
```

time: 263 us -> 155 us (0.59)
  waiting for transfers between devices: 198 us -> 62.9 us
  Pallas kernels: 0 us -> 37 us
  starting transfers between devices: 10.4 us -> 28.4 us
  matrix products: 21.4 us -> 6.5 us
  between operations: 13.5 us -> 0.42 us
  other arithmetic: 13 us -> 8.4 us
  local copies, waits for them, and re-layouts: 6.01 us -> 10.3 us
    reduce_scatter x1 -> x0, waiting for transfers between devices: 84 us -> none  [on_device(): lax.psum_scatter(term, ('expert', 'dp'), scatter_dimension=0, tiled=True)]
    all_gather x1 -> x0, waiting for transfers between devices: 51.4 us -> none  [on_device(): everyone = lax.all_gather(tokens, ('expert', 'dp'), axis=0, tiled=True)]
    pallas_call x0 -> x8, Pallas kernels: none -> 37 us  [the longest x4 19.2 us: down_rows(): pl.pallas_call(functools.partial(down_kernel, experts, capacity, rows, pi...]
    ppermute x2 -> x34, starting transfers between devices: 2.94 us -> 28.4 us  [the longest x8 9.91 us: over_y(): return lax.ppermute(x, 'expert', [(i, i ^ 1) for i in range(ring)])]
    dot_general x5 -> x4, matrix products: 21.4 us -> 6.5 us  [on_device(): total = jnp.dot(chosen, w_home, preferred_element_type=F32)]
    all_to_all x1 -> x0, starting transfers between devices: 7.39 us -> none  [on_device(): lax.all_to_all(dense.T, ('expert', 'dp'), split_axis=0, concat_axis=0, ti...]
    dynamic_slice x0 -> x2, local copies, waits for them, and re-layouts: none -> 7.21 us  [unit_slice(): lax.dynamic_slice_in_dim(w, (rank + offset) % parts * units, units, axis)]
    ppermute x2 -> x34, waiting for transfers between devices: 55.7 us -> 62.9 us  [the longest x6 25.6 us: over_z(): return lax.ppermute(x, 'expert', [(i, (i + 2) % ring) for i in range(ring)])]
  transfers between devices with their start and end apart: 5 -> 34, of which waited for: 5 -> 14; matrix products, arithmetic and copies ran while one was open for 2% -> 14% of each run, Pallas kernels for 0% -> 24%
where the time goes in v2:
time: 155 us; the launch traced here: 154 us
  waiting for transfers between devices  62.9 us (41%)
  Pallas kernels  37 us (24%)
  starting transfers between devices  28.4 us (18%)
  local copies, waits for them, and re-layouts  10.3 us (7%)
  other arithmetic  8.4 us (5%)
  matrix products  6.5 us (4%)
    ppermute x6, waiting for transfers between devices, over_z(): return lax.ppermute(x, 'expert', [(i, (i + 2) % ring) for i in range(ring)])  25.6 us
    ppermute x8, waiting for transfers between devices, over_x(): lax.ppermute(x, 'tensor', [(i, (i + step) % parts) for i in range(parts)])  20.3 us
    pallas_call x4, Pallas kernels, down_rows(): pl.pallas_call(functools.partial(down_kernel, experts, capacity, rows, pi...  19.2 us
    pallas_call x4, Pallas kernels, pick_rows(): pl.pallas_call(functools.partial(pick_kernel, width, experts, capacity),...  17.8 us
    ppermute x8, waiting for transfers between devices, over_y(): return lax.ppermute(x, 'expert', [(i, i ^ 1) for i in range(ring)])  16.9 us
    ppermute x8, starting transfers between devices, over_y(): return lax.ppermute(x, 'expert', [(i, i ^ 1) for i in range(ring)])  9.91 us
    ppermute x8, starting transfers between devices, over_x(): lax.ppermute(x, 'tensor', [(i, (i + step) % parts) for i in range(parts)])  9.01 us
    ppermute x6, starting transfers between devices, over_z(): return lax.ppermute(x, 'expert', [(i, (i + 2) % ring) for i in range(ring)])  7.65 us
  transfers between devices with their start and end apart: 34, of which 14 were waited for; matrix products, arithmetic and copies ran while one was open for 14% of the time, Pallas kernels for 24%

profile of v2, /device:TPU:0, one launch (start us, length us, event | category | flops | bytes accessed | tf_op | source)
XLA Modules:
  0.0 153.8 jit_solution(17926995404911062620)
XLA Ops:
  0.0 0.7 select_reduce_fusion
  1.1 1.1 concatenate.12.a_ref.refs_2_
  2.2 3.1 %collective-permute-start.7 = (bf16[96,2176]{1,0:T(8,128)(2,1)S(1)}, bf16[96,2176]{1,0:T(8,128)(2,1)S(1)}, u32[]{:S(2)}, u32[]{:S(2)}) collective-permute-start(bf16[96,2176]{1,0:T(8,128)(2,1)S(1)} %concatenate.12.a_ref.refs_2_), channel_id=1, source_target_pairs={{0,8},{4,12},{8,16},{12,20},{16,24},{20,28},{24,0},{28,4},{1,9},{5... | collective-permute-start | bytes 1253384 | tf_op jit(solution)/shard_map/ppermute | solution.py:160
  5.2 11.7 %collective-permute-done.7.a_ref.refs_2_ = bf16[96,2176]{1,0:T(8,128)(2,1)S(1)} collective-permute-done((bf16[96,2176]{1,0:T(8,128)(2,1)S(1)}, bf16[96,2176]{1,0:T(8,128)(2,1)S(1)}, u32[]{:S(2)}, u32[]{:S(2)}) %collective-permute-start.7) | collective-permute-done | bytes 417824 | tf_op jit(solution)/shard_map/ppermute | solution.py:160
  16.9 1.5 collective-permute-start.24
  18.4 0.5 collective-permute-start
  18.9 5.1 %dynamic-slice_bitcast_fusion.2 = (bf16[2048,384]{1,0:T(8,128)(2,1)}, bf16[2048,384]{1,0:T(8,128)(2,1)S(1)}, bf16[2048,384]{1,0:T(8,128)(2,1)S(1)}, bf16[2048,384]{1,0:T(8,128)(2,1)}) fusion(bf16[1,2048,768]{2,1,0:T(8,128)(2,1)} %param.10, s32[]{:T(128)S(6)} %select_n.41, s32[]{:T(128)S(6)} %select_n.39, bf16[1,2048,768]{2,1,0:T(8,128)(2,1)} %param.9), kind=kLoop, calls=%fused_computation.9 | loop fusion | bytes 12582920 | tf_op jit(solution)/shard_map/dynamic_slice | solution.py:179
  24.0 0.5 collective-permute-start.25
  24.6 4.9 %collective-permute-done.24.b_ref.refs_3_ = bf16[96,2176]{1,0:T(8,128)(2,1)S(1)} collective-permute-done((bf16[96,2176]{1,0:T(8,128)(2,1)S(1)}, bf16[96,2176]{1,0:T(8,128)(2,1)S(1)}, u32[]{:S(2)}, u32[]{:S(2)}) %collective-permute-start.24) | collective-permute-done | bytes 417824 | tf_op jit(solution)/shard_map/ppermute | solution.py:157
  29.5 1.9 %pad_maximum_fusion.w_ref = bf16[2048,768]{1,0:T(8,128)(2,1)} fusion(bf16[2048,384]{1,0:T(8,128)(2,1)S(1)} %get-tuple-element.26, bf16[2048,384]{1,0:T(8,128)(2,1)S(1)} %get-tuple-element.29), kind=kLoop, calls=%fused_computation | loop fusion | flops 6291456 | bytes 6291456 | tf_op jit(solution)/shard_map/concatenate | solution.py:184
  31.4 1.4 collective-permute-done.8.a_ref.refs_2_
  32.8 1.5 collective-permute-start.17
  34.3 2.1 %dynamic-slice_bitcast_fusion.1 = (bf16[384,2048]{1,0:T(8,128)(2,1)S(1)}, bf16[384,2048]{1,0:T(8,128)(2,1)S(1)}) fusion(bf16[1,768,2048]{2,1,0:T(8,128)(2,1)} %param.11, s32[]{:T(128)S(6)} %select_n.43, s32[]{:T(128)S(6)} %select_n.39), kind=kLoop, calls=%fused_computation.8 | loop fusion | bytes 6291464 | tf_op jit(solution)/shard_map/dynamic_slice | solution.py:179
  36.4 1.8 %collective-permute-done.b_ref.refs_3_ = bf16[96,2176]{1,0:T(8,128)(2,1)S(1)} collective-permute-done((bf16[96,2176]{1,0:T(8,128)(2,1)S(1)}, bf16[96,2176]{1,0:T(8,128)(2,1)S(1)}, u32[]{:S(2)}, u32[]{:S(2)}) %collective-permute-start) | collective-permute-done | bytes 417824 | tf_op jit(solution)/shard_map/ppermute | solution.py:157
  38.2 0.5 collective-permute-start.18
  38.7 4.5 %shard_map.70 = (bf16[288,2048]{1,0:T(8,128)(2,1)S(1)}, bf16[288,768]{1,0:T(8,128)(2,1)S(1)}) custom-call(s32[1]{0:T(128)} %bitcast.me_ref, bf16[96,2176]{1,0:T(8,128)(2,1)S(1)} %collective-permute-done.7.a_ref.refs_2_, bf16[96,2176]{1,0:T(8,128)(2,1)S(1)} %collective-permute-done.24.b_ref.refs_3_, ...), custom_call_target="tpu_custom_call" | custom-call | flops 1358954496 | bytes 6438912 | tf_op jit(solution)/shard_map/pallas_call | solution.py:75
  43.2 1.2 collective-permute-start.27
  44.4 1.2 collective-permute-done.17.b_ref.refs_3_
  45.6 1.9 %pad_maximum_fusion.2.refs_6_ = bf16[768,2048]{1,0:T(8,128)(2,1)} fusion(bf16[384,2048]{1,0:T(8,128)(2,1)S(1)} %get-tuple-element.22, bf16[384,2048]{1,0:T(8,128)(2,1)S(1)} %get-tuple-element.21), kind=kLoop, calls=%fused_computation.2 | loop fusion | flops 6291456 | bytes 6291456 | tf_op jit(solution)/shard_map/concatenate | solution.py:186
  47.5 4.4 %shard_map.64 = (bf16[288,2048]{1,0:T(8,128)(2,1)S(1)}, bf16[288,768]{1,0:T(8,128)(2,1)S(1)}) custom-call(s32[1]{0:T(128)} %bitcast.me_ref, bf16[96,2176]{1,0:T(8,128)(2,1)S(1)} %concatenate.12.a_ref.refs_2_, bf16[96,2176]{1,0:T(8,128)(2,1)S(1)} %collective-permute-done.b_ref.refs_3_, bf16[96,2176]{1,0:T(8,128)(2,1)S(1)} %collective-permute-done.1.c_ref.refs_4_, ...), custom_call_target="tpu_custom_call" | custom-call | flops 1358954496 | bytes 6438912 | tf_op jit(solution)/shard_map/pallas_call | solution.py:75
  52.0 1.3 collective-permute-start.3
  53.3 1.5 collective-permute-start.10
  54.8 4.5 %shard_map.68 = (bf16[288,2048]{1,0:T(8,128)(2,1)S(1)}, bf16[288,768]{1,0:T(8,128)(2,1)S(1)}) custom-call(s32[1]{0:T(128)} %bitcast.me_ref, bf16[96,2176]{1,0:T(8,128)(2,1)S(1)} %collective-permute-done.8.a_ref.refs_2_, bf16[96,2176]{1,0:T(8,128)(2,1)S(1)} %collective-permute-done.17.b_ref.refs_3_, ...), custom_call_target="tpu_custom_call" | custom-call | flops 1358954496 | bytes 6438912 | tf_op jit(solution)/shard_map/pallas_call | solution.py:75
  59.3 0.6 collective-permute-start.20
  59.9 1.1 convolution_add_fusion
  61.1 0.1 fusion.7.refs_0_
  61.2 1.6 %collective-permute-start.28 = (bf16[288,384]{1,0:T(8,128)(2,1)S(1)}, bf16[288,384]{1,0:T(8,128)(2,1)S(1)}, u32[]{:S(2)}, u32[]{:S(2)}) collective-permute-start(bf16[288,384]{1,0:T(8,128)(2,1)S(1)} %fusion.7.refs_0_), channel_id=1, source_target_pairs={{0,2},{2,0},{1,3},{3,1},{4,6},{6,4},{5,7},{7,5},{8,10},{10,8},{9,1... | collective-permute-start | bytes 663560 | tf_op jit(solution)/shard_map/ppermute | solution.py:166
  62.7 2.8 %collective-permute-done.3 = bf16[288,768]{1,0:T(8,128)(2,1)} collective-permute-done((bf16[288,768]{1,0:T(8,128)(2,1)S(1)}, bf16[288,768]{1,0:T(8,128)(2,1)}, u32[]{:S(2)}, u32[]{:S(2)}) %collective-permute-start.3) | collective-permute-done | bytes 442400 | tf_op jit(solution)/shard_map/ppermute | solution.py:166
  65.5 2.1 %convolution_add_fusion.3 = f32[288,768]{1,0:T(8,128)S(1)} fusion(bf16[288,2048]{1,0:T(8,128)(2,1)S(1)} %get-tuple-element.13, bf16[288,768]{1,0:T(8,128)(2,1)} %collective-permute-done.3, bf16[2048,384]{1,0:T(8,128)(2,1)S(1)} %copy-done, bf16[2048,384]{1,0:T(8,128)(2,1)S(1)} %copy-done.2), kind=kOutput, calls=%fused_computation.16 | convolution fusion | flops 912703488 | bytes 5652480 | tf_op jit(solution)/shard_map/dot_general | solution.py:197
  67.8 11.5 %collective-permute-done.28.refs_1_ = bf16[288,384]{1,0:T(8,128)(2,1)S(1)} collective-permute-done((bf16[288,384]{1,0:T(8,128)(2,1)S(1)}, bf16[288,384]{1,0:T(8,128)(2,1)S(1)}, u32[]{:S(2)}, u32[]{:S(2)}) %collective-permute-start.28) | collective-permute-done | bytes 221216 | tf_op jit(solution)/shard_map/ppermute | solution.py:166
  79.3 4.8 %shard_map.71 = bf16[384,2048]{1,0:T(8,128)(2,1)S(1)} custom-call(s32[1]{0:T(128)} %bitcast.me_ref, bf16[288,384]{1,0:T(8,128)(2,1)S(1)} %fusion.7.refs_0_, bf16[288,384]{1,0:T(8,128)(2,1)S(1)} %collective-permute-done.28.refs_1_, bf16[96,2176]{1,0:T(8,128)(2,1)S(1)} %collective-permute-done.7.a_ref.refs_2_, ...), custom_call_target="tpu_custom_call" | custom-call | flops 1377828864 | bytes 5160960 | tf_op jit(solution)/shard_map/pallas_call | solution.py:124
  84.3 1.2 copy-done.3
  85.5 2.1 %convolution_add_fusion.1 = f32[288,768]{1,0:T(8,128)S(1)} fusion(bf16[288,2048]{1,0:T(8,128)(2,1)S(1)} %get-tuple-element.17, bf16[288,768]{1,0:T(8,128)(2,1)} %collective-permute-done.20, bf16[2048,384]{1,0:T(8,128)(2,1)S(1)} %copy-done, bf16[2048,384]{1,0:T(8,128)(2,1)S(1)} %copy-done.3), kind=kOutput, calls=%fused_computation.14 | convolution fusion | flops 912703488 | bytes 5652480 | tf_op jit(solution)/shard_map/dot_general | solution.py:197
  87.8 1.1 collective-permute-start.21
  89.0 1.1 collective-permute-start.4
  90.1 4.5 %shard_map.66 = (bf16[288,2048]{1,0:T(8,128)(2,1)S(1)}, bf16[288,768]{1,0:T(8,128)(2,1)S(1)}) custom-call(s32[1]{0:T(128)} %bitcast.me_ref, bf16[96,2176]{1,0:T(8,128)(2,1)S(1)} %collective-permute-done.9.a_ref.refs_2_, bf16[96,2176]{1,0:T(8,128)(2,1)S(1)} %collective-permute-done.10.b_ref.refs_3_, ...), custom_call_target="tpu_custom_call" | custom-call | flops 1358954496 | bytes 6438912 | tf_op jit(solution)/shard_map/pallas_call | solution.py:75
  94.5 1.1 collective-permute-start.13
  95.6 0.6 collective-permute-done.21.refs_1_
  96.2 4.8 %shard_map.69 = bf16[384,2048]{1,0:T(8,128)(2,1)S(1)} custom-call(s32[1]{0:T(128)} %bitcast.me_ref, bf16[288,384]{1,0:T(8,128)(2,1)S(1)} %fusion.8.refs_0_, bf16[288,384]{1,0:T(8,128)(2,1)S(1)} %collective-permute-done.21.refs_1_, bf16[96,2176]{1,0:T(8,128)(2,1)S(1)} %collective-permute-done.8.a_ref.refs_2_, ...), custom_call_target="tpu_custom_call" | custom-call | flops 1377828864 | bytes 5160960 | tf_op jit(solution)/shard_map/pallas_call | solution.py:124
  101.1 1.4 convert_add_fusion
  102.6 1.1 collective-permute-start.30
  103.7 5.4 %collective-permute-done.13 = bf16[288,768]{1,0:T(8,128)(2,1)S(1)} collective-permute-done((bf16[288,768]{1,0:T(8,128)(2,1)S(1)}, bf16[288,768]{1,0:T(8,128)(2,1)S(1)}, u32[]{:S(2)}, u32[]{:S(2)}) %collective-permute-start.13) | collective-permute-done | bytes 442400 | tf_op jit(solution)/shard_map/ppermute | solution.py:166
  109.1 1.1 convolution_add_fusion.2
  110.4 1.1 collective-permute-start.14
  111.5 2.6 %collective-permute-done.30 = bf16[96,2048]{1,0:T(8,128)(2,1)S(1)} collective-permute-done((bf16[96,2048]{1,0:T(8,128)(2,1)S(1)}, bf16[96,2048]{1,0:T(8,128)(2,1)S(1)}, u32[]{:S(2)}, u32[]{:S(2)}) %collective-permute-start.30) | collective-permute-done | bytes 393248 | tf_op jit(solution)/shard_map/ppermute | solution.py:157
  114.2 1.2 collective-permute-start.31
  115.4 0.2 convert_add_fusion.1
  115.7 1.6 %collective-permute-start.23 = (bf16[96,2048]{1,0:T(8,128)(2,1)S(1)}, bf16[96,2048]{1,0:T(8,128)(2,1)S(1)}, u32[]{:S(2)}, u32[]{:S(2)}) collective-permute-start(bf16[96,2048]{1,0:T(8,128)(2,1)S(1)} %slice.167), channel_id=1, source_target_pairs={{0,4},{4,0},{8,12},{12,8},{16,20},{20,16},{24,28},{28,24},{1,5},{5... | collective-permute-start | bytes 1179656 | tf_op jit(solution)/shard_map/ppermute | solution.py:157
  117.3 4.8 %shard_map.67 = bf16[384,2048]{1,0:T(8,128)(2,1)S(1)} custom-call(s32[1]{0:T(128)} %bitcast.me_ref, bf16[288,384]{1,0:T(8,128)(2,1)S(1)} %fusion.9.refs_0_, bf16[288,384]{1,0:T(8,128)(2,1)S(1)} %collective-permute-done.14.refs_1_, bf16[96,2176]{1,0:T(8,128)(2,1)S(1)} %collective-permute-done.9.a_ref.refs_2_, ...), custom_call_target="tpu_custom_call" | custom-call | flops 1377828864 | bytes 5160960 | tf_op jit(solution)/shard_map/pallas_call | solution.py:124
  122.2 4.8 %shard_map.65 = bf16[384,2048]{1,0:T(8,128)(2,1)S(1)} custom-call(s32[1]{0:T(128)} %bitcast.me_ref, bf16[288,384]{1,0:T(8,128)(2,1)S(1)} %fusion.10.refs_0_, bf16[288,384]{1,0:T(8,128)(2,1)S(1)} %collective-permute-done.4.refs_1_, bf16[96,2176]{1,0:T(8,128)(2,1)S(1)} %concatenate.12.a_ref.refs_2_, bf16[96,2176]{1,0:T(8,128)(2,1)S(1)} %collective-permute-done.b_ref.refs_3_, ...), custom_call_target="tpu_custom_call" | custom-call | flops 1377828864 | bytes 5160960 | tf_op jit(solution)/shard_map/pallas_call | solution.py:124
  127.1 0.5 collective-permute-start.5
  127.6 0.1 fusion.2
  127.8 1.6 %collective-permute-start.32 = (bf16[96,2048]{1,0:T(8,128)(2,1)S(1)}, bf16[96,2048]{1,0:T(8,128)(2,1)S(1)}, u32[]{:S(2)}, u32[]{:S(2)}) collective-permute-start(bf16[96,2048]{1,0:T(8,128)(2,1)S(1)} %fusion.2), channel_id=1, source_target_pairs={{0,8},{4,12},{8,16},{12,20},{16,24},{20,28},{24,0},{28,4},{1,9},{5... | collective-permute-start | bytes 1179656 | tf_op jit(solution)/shard_map/ppermute | solution.py:160
  129.4 0.2 convert_add_fusion.2
  129.7 0.6 collective-permute-start.16
  130.3 0.2 convert_add_fusion.3
  130.5 1.6 %collective-permute-start.6 = (bf16[96,2048]{1,0:T(8,128)(2,1)S(1)}, bf16[96,2048]{1,0:T(8,128)(2,1)S(1)}, u32[]{:S(2)}, u32[]{:S(2)}) collective-permute-start(bf16[96,2048]{1,0:T(8,128)(2,1)S(1)} %slice.169), channel_id=1, source_target_pairs={{0,4},{4,0},{8,12},{12,8},{16,20},{20,16},{24,28},{28,24},{1,5},{5... | collective-permute-start | bytes 1179656 | tf_op jit(solution)/shard_map/ppermute | solution.py:157
  132.1 8.6 %collective-permute-done.32 = bf16[96,2048]{1,0:T(8,128)(2,1)S(1)} collective-permute-done((bf16[96,2048]{1,0:T(8,128)(2,1)S(1)}, bf16[96,2048]{1,0:T(8,128)(2,1)S(1)}, u32[]{:S(2)}, u32[]{:S(2)}) %collective-permute-start.32) | collective-permute-done | bytes 393248 | tf_op jit(solution)/shard_map/ppermute | solution.py:160
  140.7 1.1 collective-permute-done.16
  141.8 0.2 fusion.4
  141.9 1.7 %collective-permute-start.33 = (bf16[96,2048]{1,0:T(8,128)(2,1)S(1)}, bf16[96,2048]{1,0:T(8,128)(2,1)S(1)}, u32[]{:S(2)}, u32[]{:S(2)}) collective-permute-start(bf16[96,2048]{1,0:T(8,128)(2,1)S(1)} %fusion.4), channel_id=1, source_target_pairs={{0,8},{4,12},{8,16},{12,20},{16,24},{20,28},{24,0},{28,4},{1,9},{5... | collective-permute-start | bytes 1179656 | tf_op jit(solution)/shard_map/ppermute | solution.py:160
  143.6 5.3 %collective-permute-done.6 = bf16[96,2048]{1,0:T(8,128)(2,1)S(1)} collective-permute-done((bf16[96,2048]{1,0:T(8,128)(2,1)S(1)}, bf16[96,2048]{1,0:T(8,128)(2,1)S(1)}, u32[]{:S(2)}, u32[]{:S(2)}) %collective-permute-start.6) | collective-permute-done | bytes 393248 | tf_op jit(solution)/shard_map/ppermute | solution.py:157
  149.0 4.0 %collective-permute-done.33 = bf16[96,2048]{1,0:T(8,128)(2,1)S(1)} collective-permute-done((bf16[96,2048]{1,0:T(8,128)(2,1)S(1)}, bf16[96,2048]{1,0:T(8,128)(2,1)S(1)}, u32[]{:S(2)}, u32[]{:S(2)}) %collective-permute-start.33) | collective-permute-done | bytes 393248 | tf_op jit(solution)/shard_map/ppermute | solution.py:160
  152.9 0.9 fusion.6
  (58 shorter events, 1.6 us)
Async XLA Ops:
  2.2 14.7 %collective-permute-start.7 = (bf16[96,2176]{1,0:T(8,128)(2,1)S(1)}, bf16[96,2176]{1,0:T(8,128)(2,1)S(1)}, u32[]{:S(2)}, u32[]{:S(2)}) collective-permute-start(bf16[96,2176]{1,0:T(8,128)(2,1)S(1)} %concatenate.12.a_ref.refs_2_), channel_id=1, source_target_pairs={{0,8},{4,12},{8,16},{12,20},{16,24},{20,28},{24,0},{28,4},{1,9},{5... | collective-permute-start | bytes 1253384 | tf_op jit(solution)/shard_map/ppermute | solution.py:160
  16.9 12.6 %collective-permute-start.24 = (bf16[96,2176]{1,0:T(8,128)(2,1)S(1)}, bf16[96,2176]{1,0:T(8,128)(2,1)S(1)}, u32[]{:S(2)}, u32[]{:S(2)}) collective-permute-start(bf16[96,2176]{1,0:T(8,128)(2,1)S(1)} %collective-permute-done.7.a_ref.refs_2_), channel_id=1, source_target_pairs={{0,4},{4,0},{8,12},{12,8},{16,20},{20,16},{24,28},{28,24},{1,5},{5... | collective-permute-start | bytes 1253384 | tf_op jit(solution)/shard_map/ppermute | solution.py:157
  18.4 19.8 %collective-permute-start = (bf16[96,2176]{1,0:T(8,128)(2,1)S(1)}, bf16[96,2176]{1,0:T(8,128)(2,1)S(1)}, u32[]{:S(2)}, u32[]{:S(2)}) collective-permute-start(bf16[96,2176]{1,0:T(8,128)(2,1)S(1)} %concatenate.12.a_ref.refs_2_), channel_id=1, source_target_pairs={{0,4},{4,0},{8,12},{12,8},{16,20},{20,16},{24,28},{28,24},{1,5},{5... | collective-permute-start | bytes 1253384 | tf_op jit(solution)/shard_map/ppermute | solution.py:157
  18.9 24.2 %collective-permute-start.1 = (bf16[96,2176]{1,0:T(8,128)(2,1)S(1)}, bf16[96,2176]{1,0:T(8,128)(2,1)S(1)}, u32[]{:S(2)}, u32[]{:S(2)}) collective-permute-start(bf16[96,2176]{1,0:T(8,128)(2,1)S(1)} %concatenate.12.a_ref.refs_2_), channel_id=1, source_target_pairs={{0,1},{1,0},{2,3},{3,2},{4,5},{5,4},{6,7},{7,6},{8,9},{9,8},{10,11... | collective-permute-start | bytes 1253384 | tf_op jit(solution)/shard_map/ppermute | solution.py:163
  18.9 13.9 %collective-permute-start.8 = (bf16[96,2176]{1,0:T(8,128)(2,1)S(1)}, bf16[96,2176]{1,0:T(8,128)(2,1)S(1)}, u32[]{:S(2)}, u32[]{:S(2)}) collective-permute-start(bf16[96,2176]{1,0:T(8,128)(2,1)S(1)} %collective-permute-done.7.a_ref.refs_2_), channel_id=1, source_target_pairs={{0,8},{4,12},{8,16},{12,20},{16,24},{20,28},{24,0},{28,4},{1,9},{5... | collective-permute-start | bytes 1253384 | tf_op jit(solution)/shard_map/ppermute | solution.py:160
  24.0 14.2 %collective-permute-start.25 = (bf16[96,2176]{1,0:T(8,128)(2,1)S(1)}, bf16[96,2176]{1,0:T(8,128)(2,1)S(1)}, u32[]{:S(2)}, u32[]{:S(2)}) collective-permute-start(bf16[96,2176]{1,0:T(8,128)(2,1)S(1)} %collective-permute-done.7.a_ref.refs_2_), channel_id=1, source_target_pairs={{0,1},{1,0},{2,3},{3,2},{4,5},{5,4},{6,7},{7,6},{8,9},{9,8},{10,11... | collective-permute-start | bytes 1253384 | tf_op jit(solution)/shard_map/ppermute | solution.py:163
  29.5 9.2 %collective-permute-start.26 = (bf16[96,2176]{1,0:T(8,128)(2,1)S(1)}, bf16[96,2176]{1,0:T(8,128)(2,1)S(1)}, u32[]{:S(2)}, u32[]{:S(2)}) collective-permute-start(bf16[96,2176]{1,0:T(8,128)(2,1)S(1)} %collective-permute-done.24.b_ref.refs_3_), channel_id=1, source_target_pairs={{0,1},{1,0},{2,3},{3,2},{4,5},{5,4},{6,7},{7,6},{8,9},{9,8},{10,11... | collective-permute-start | bytes 1253384 | tf_op jit(solution)/shard_map/ppermute | solution.py:163
  32.8 12.9 %collective-permute-start.17 = (bf16[96,2176]{1,0:T(8,128)(2,1)S(1)}, bf16[96,2176]{1,0:T(8,128)(2,1)S(1)}, u32[]{:S(2)}, u32[]{:S(2)}) collective-permute-start(bf16[96,2176]{1,0:T(8,128)(2,1)S(1)} %collective-permute-done.8.a_ref.refs_2_), channel_id=1, source_target_pairs={{0,4},{4,0},{8,12},{12,8},{16,20},{20,16},{24,28},{28,24},{1,5},{5... | collective-permute-start | bytes 1253384 | tf_op jit(solution)/shard_map/ppermute | solution.py:157
  38.2 9.3 %collective-permute-start.2 = (bf16[96,2176]{1,0:T(8,128)(2,1)S(1)}, bf16[96,2176]{1,0:T(8,128)(2,1)S(1)}, u32[]{:S(2)}, u32[]{:S(2)}) collective-permute-start(bf16[96,2176]{1,0:T(8,128)(2,1)S(1)} %collective-permute-done.b_ref.refs_3_), channel_id=1, source_target_pairs={{0,1},{1,0},{2,3},{3,2},{4,5},{5,4},{6,7},{7,6},{8,9},{9,8},{10,11... | collective-permute-start | bytes 1253384 | tf_op jit(solution)/shard_map/ppermute | solution.py:163
  38.2 16.6 %collective-permute-start.18 = (bf16[96,2176]{1,0:T(8,128)(2,1)S(1)}, bf16[96,2176]{1,0:T(8,128)(2,1)S(1)}, u32[]{:S(2)}, u32[]{:S(2)}) collective-permute-start(bf16[96,2176]{1,0:T(8,128)(2,1)S(1)} %collective-permute-done.8.a_ref.refs_2_), channel_id=1, source_target_pairs={{0,1},{1,0},{2,3},{3,2},{4,5},{5,4},{6,7},{7,6},{8,9},{9,8},{10,11... | collective-permute-start | bytes 1253384 | tf_op jit(solution)/shard_map/ppermute | solution.py:163
  38.7 14.6 %collective-permute-start.9 = (bf16[96,2176]{1,0:T(8,128)(2,1)S(1)}, bf16[96,2176]{1,0:T(8,128)(2,1)S(1)}, u32[]{:S(2)}, u32[]{:S(2)}) collective-permute-start(bf16[96,2176]{1,0:T(8,128)(2,1)S(1)} %collective-permute-done.8.a_ref.refs_2_), channel_id=1, source_target_pairs={{0,8},{4,12},{8,16},{12,20},{16,24},{20,28},{24,0},{28,4},{1,9},{5... | collective-permute-start | bytes 1253384 | tf_op jit(solution)/shard_map/ppermute | solution.py:160
  43.2 16.7 %collective-permute-start.27 = (bf16[288,768]{1,0:T(8,128)(2,1)S(1)}, bf16[288,768]{1,0:T(8,128)(2,1)S(1)}, u32[]{:S(2)}, u32[]{:S(2)}) collective-permute-start(bf16[288,768]{1,0:T(8,128)(2,1)S(1)} %get-tuple-element.20), channel_id=1, source_target_pairs={{0,2},{2,0},{1,3},{3,1},{4,6},{6,4},{5,7},{7,5},{8,10},{10,8},{9,1... | collective-permute-start | bytes 1327112 | tf_op jit(solution)/shard_map/ppermute | solution.py:166
  45.6 9.2 %collective-permute-start.19 = (bf16[96,2176]{1,0:T(8,128)(2,1)S(1)}, bf16[96,2176]{1,0:T(8,128)(2,1)S(1)}, u32[]{:S(2)}, u32[]{:S(2)}) collective-permute-start(bf16[96,2176]{1,0:T(8,128)(2,1)S(1)} %collective-permute-done.17.b_ref.refs_3_), channel_id=1, source_target_pairs={{0,1},{1,0},{2,3},{3,2},{4,5},{5,4},{6,7},{7,6},{8,9},{9,8},{10,11... | collective-permute-start | bytes 1253384 | tf_op jit(solution)/shard_map/ppermute | solution.py:163
  52.0 7.9 %copy-start = (bf16[2048,384]{1,0:T(8,128)(2,1)S(1)}, bf16[2048,384]{1,0:T(8,128)(2,1)}, u32[]{:S(2)}) copy-start(bf16[2048,384]{1,0:T(8,128)(2,1)} %get-tuple-element.25) | copy-start | bytes 4718596
  52.0 7.9 %copy-start.1 = (bf16[2048,384]{1,0:T(8,128)(2,1)S(1)}, bf16[2048,384]{1,0:T(8,128)(2,1)}, u32[]{:S(2)}) copy-start(bf16[2048,384]{1,0:T(8,128)(2,1)} %get-tuple-element.30) | copy-start | bytes 4718596
  52.0 13.5 %collective-permute-start.3 = (bf16[288,768]{1,0:T(8,128)(2,1)S(1)}, bf16[288,768]{1,0:T(8,128)(2,1)}, u32[]{:S(2)}, u32[]{:S(2)}) collective-permute-start(bf16[288,768]{1,0:T(8,128)(2,1)S(1)} %get-tuple-element.14), channel_id=1, source_target_pairs={{0,2},{2,0},{1,3},{3,1},{4,6},{6,4},{5,7},{7,5},{8,10},{10,8},{9,1... | collective-permute-start | bytes 1327112 | tf_op jit(solution)/shard_map/ppermute | solution.py:166
  53.3 14.4 %collective-permute-start.10 = (bf16[96,2176]{1,0:T(8,128)(2,1)S(1)}, bf16[96,2176]{1,0:T(8,128)(2,1)S(1)}, u32[]{:S(2)}, u32[]{:S(2)}) collective-permute-start(bf16[96,2176]{1,0:T(8,128)(2,1)S(1)} %collective-permute-done.9.a_ref.refs_2_), channel_id=1, source_target_pairs={{0,4},{4,0},{8,12},{12,8},{16,20},{20,16},{24,28},{28,24},{1,5},{5... | collective-permute-start | bytes 1253384 | tf_op jit(solution)/shard_map/ppermute | solution.py:157
  54.8 35.2 %collective-permute-start.11 = (bf16[96,2176]{1,0:T(8,128)(2,1)S(1)}, bf16[96,2176]{1,0:T(8,128)(2,1)S(1)}, u32[]{:S(2)}, u32[]{:S(2)}) collective-permute-start(bf16[96,2176]{1,0:T(8,128)(2,1)S(1)} %collective-permute-done.9.a_ref.refs_2_), channel_id=1, source_target_pairs={{0,1},{1,0},{2,3},{3,2},{4,5},{5,4},{6,7},{7,6},{8,9},{9,8},{10,11... | collective-permute-start | bytes 1253384 | tf_op jit(solution)/shard_map/ppermute | solution.py:163
  59.3 24.9 %collective-permute-start.20 = (bf16[288,768]{1,0:T(8,128)(2,1)S(1)}, bf16[288,768]{1,0:T(8,128)(2,1)}, u32[]{:S(2)}, u32[]{:S(2)}) collective-permute-start(bf16[288,768]{1,0:T(8,128)(2,1)S(1)} %get-tuple-element.18), channel_id=1, source_target_pairs={{0,2},{2,0},{1,3},{3,1},{4,6},{6,4},{5,7},{7,5},{8,10},{10,8},{9,1... | collective-permute-start | bytes 1327112 | tf_op jit(solution)/shard_map/ppermute | solution.py:166
  59.9 5.6 %copy-start.2 = (bf16[2048,384]{1,0:T(8,128)(2,1)S(1)}, bf16[2048,384]{1,0:T(8,128)(2,1)}, u32[]{:S(2)}) copy-start(bf16[2048,384]{1,0:T(8,128)(2,1)} %get-tuple-element.30) | copy-start | bytes 4718596
  61.2 18.1 %collective-permute-start.28 = (bf16[288,384]{1,0:T(8,128)(2,1)S(1)}, bf16[288,384]{1,0:T(8,128)(2,1)S(1)}, u32[]{:S(2)}, u32[]{:S(2)}) collective-permute-start(bf16[288,384]{1,0:T(8,128)(2,1)S(1)} %fusion.7.refs_0_), channel_id=1, source_target_pairs={{0,2},{2,0},{1,3},{3,1},{4,6},{6,4},{5,7},{7,5},{8,10},{10,8},{9,1... | collective-permute-start | bytes 663560 | tf_op jit(solution)/shard_map/ppermute | solution.py:166
  67.7 22.4 %collective-permute-start.12 = (bf16[96,2176]{1,0:T(8,128)(2,1)S(1)}, bf16[96,2176]{1,0:T(8,128)(2,1)S(1)}, u32[]{:S(2)}, u32[]{:S(2)}) collective-permute-start(bf16[96,2176]{1,0:T(8,128)(2,1)S(1)} %collective-permute-done.10.b_ref.refs_3_), channel_id=1, source_target_pairs={{0,1},{1,0},{2,3},{3,2},{4,5},{5,4},{6,7},{7,6},{8,9},{9,8},{10,11... | collective-permute-start | bytes 1253384 | tf_op jit(solution)/shard_map/ppermute | solution.py:163
  84.1 1.4 copy-start.3
  84.2 16.9 %collective-permute-start.29 = (bf16[192,2048]{1,0:T(8,128)(2,1)S(1)}, bf16[192,2048]{1,0:T(8,128)(2,1)}, u32[]{:S(2)}, u32[]{:S(2)}) collective-permute-start(bf16[192,2048]{1,0:T(8,128)(2,1)S(1)} %slice.121), channel_id=1, source_target_pairs={{0,1},{1,0},{2,3},{3,2},{4,5},{5,4},{6,7},{7,6},{8,9},{9,8},{10,11... | collective-permute-start | bytes 2359304 | tf_op jit(solution)/shard_map/ppermute | solution.py:163
  87.8 8.4 %collective-permute-start.21 = (bf16[288,384]{1,0:T(8,128)(2,1)S(1)}, bf16[288,384]{1,0:T(8,128)(2,1)S(1)}, u32[]{:S(2)}, u32[]{:S(2)}) collective-permute-start(bf16[288,384]{1,0:T(8,128)(2,1)S(1)} %fusion.8.refs_0_), channel_id=1, source_target_pairs={{0,2},{2,0},{1,3},{3,1},{4,6},{6,4},{5,7},{7,5},{8,10},{10,8},{9,1... | collective-permute-start | bytes 663560 | tf_op jit(solution)/shard_map/ppermute | solution.py:166
  89.0 33.2 %collective-permute-start.4 = (bf16[288,384]{1,0:T(8,128)(2,1)S(1)}, bf16[288,384]{1,0:T(8,128)(2,1)S(1)}, u32[]{:S(2)}, u32[]{:S(2)}) collective-permute-start(bf16[288,384]{1,0:T(8,128)(2,1)S(1)} %fusion.10.refs_0_), channel_id=1, source_target_pairs={{0,2},{2,0},{1,3},{3,1},{4,6},{6,4},{5,7},{7,5},{8,10},{10,8},{9,1... | collective-permute-start | bytes 663560 | tf_op jit(solution)/shard_map/ppermute | solution.py:166
  94.5 14.6 %collective-permute-start.13 = (bf16[288,768]{1,0:T(8,128)(2,1)S(1)}, bf16[288,768]{1,0:T(8,128)(2,1)S(1)}, u32[]{:S(2)}, u32[]{:S(2)}) collective-permute-start(bf16[288,768]{1,0:T(8,128)(2,1)S(1)} %get-tuple-element.16), channel_id=1, source_target_pairs={{0,2},{2,0},{1,3},{3,1},{4,6},{6,4},{5,7},{7,5},{8,10},{10,8},{9,1... | collective-permute-start | bytes 1327112 | tf_op jit(solution)/shard_map/ppermute | solution.py:166
  101.0 8.1 %copy-start.4 = (bf16[2048,384]{1,0:T(8,128)(2,1)S(1)}, bf16[2048,384]{1,0:T(8,128)(2,1)}, u32[]{:S(2)}) copy-start(bf16[2048,384]{1,0:T(8,128)(2,1)} %get-tuple-element.30) | copy-start | bytes 4718596
  101.0 14.4 %collective-permute-start.22 = (bf16[192,2048]{1,0:T(8,128)(2,1)S(1)}, bf16[192,2048]{1,0:T(8,128)(2,1)S(1)}, u32[]{:S(2)}, u32[]{:S(2)}) collective-permute-start(bf16[192,2048]{1,0:T(8,128)(2,1)S(1)} %slice.115), channel_id=1, source_target_pairs={{0,1},{1,0},{2,3},{3,2},{4,5},{5,4},{6,7},{7,6},{8,9},{9,8},{10,11... | collective-permute-start | bytes 2359304 | tf_op jit(solution)/shard_map/ppermute | solution.py:163
  102.6 11.5 %collective-permute-start.30 = (bf16[96,2048]{1,0:T(8,128)(2,1)S(1)}, bf16[96,2048]{1,0:T(8,128)(2,1)S(1)}, u32[]{:S(2)}, u32[]{:S(2)}) collective-permute-start(bf16[96,2048]{1,0:T(8,128)(2,1)S(1)} %slice.166), channel_id=1, source_target_pairs={{0,4},{4,0},{8,12},{12,8},{16,20},{20,16},{24,28},{28,24},{1,5},{5... | collective-permute-start | bytes 1179656 | tf_op jit(solution)/shard_map/ppermute | solution.py:157
  110.4 6.9 %collective-permute-start.14 = (bf16[288,384]{1,0:T(8,128)(2,1)S(1)}, bf16[288,384]{1,0:T(8,128)(2,1)S(1)}, u32[]{:S(2)}, u32[]{:S(2)}) collective-permute-start(bf16[288,384]{1,0:T(8,128)(2,1)S(1)} %fusion.9.refs_0_), channel_id=1, source_target_pairs={{0,2},{2,0},{1,3},{3,1},{4,6},{6,4},{5,7},{7,5},{8,10},{10,8},{9,1... | collective-permute-start | bytes 663560 | tf_op jit(solution)/shard_map/ppermute | solution.py:166
  114.2 13.4 %collective-permute-start.31 = (bf16[96,2048]{1,0:T(8,128)(2,1)S(1)}, bf16[96,2048]{1,0:T(8,128)(2,1)S(1)}, u32[]{:S(2)}, u32[]{:S(2)}) collective-permute-start(bf16[96,2048]{1,0:T(8,128)(2,1)S(1)} %fusion), channel_id=1, source_target_pairs={{0,8},{4,12},{8,16},{12,20},{16,24},{20,28},{24,0},{28,4},{1,9},{5... | collective-permute-start | bytes 1179656 | tf_op jit(solution)/shard_map/ppermute | solution.py:160
  115.7 12.0 %collective-permute-start.23 = (bf16[96,2048]{1,0:T(8,128)(2,1)S(1)}, bf16[96,2048]{1,0:T(8,128)(2,1)S(1)}, u32[]{:S(2)}, u32[]{:S(2)}) collective-permute-start(bf16[96,2048]{1,0:T(8,128)(2,1)S(1)} %slice.167), channel_id=1, source_target_pairs={{0,4},{4,0},{8,12},{12,8},{16,20},{20,16},{24,28},{28,24},{1,5},{5... | collective-permute-start | bytes 1179656 | tf_op jit(solution)/shard_map/ppermute | solution.py:157
  122.1 7.3 %collective-permute-start.15 = (bf16[192,2048]{1,0:T(8,128)(2,1)S(1)}, bf16[192,2048]{1,0:T(8,128)(2,1)S(1)}, u32[]{:S(2)}, u32[]{:S(2)}) collective-permute-start(bf16[192,2048]{1,0:T(8,128)(2,1)S(1)} %slice.109), channel_id=1, source_target_pairs={{0,1},{1,0},{2,3},{3,2},{4,5},{5,4},{6,7},{7,6},{8,9},{9,8},{10,11... | collective-permute-start | bytes 2359304 | tf_op jit(solution)/shard_map/ppermute | solution.py:163
  127.1 3.2 %collective-permute-start.5 = (bf16[192,2048]{1,0:T(8,128)(2,1)S(1)}, bf16[192,2048]{1,0:T(8,128)(2,1)S(1)}, u32[]{:S(2)}, u32[]{:S(2)}) collective-permute-start(bf16[192,2048]{1,0:T(8,128)(2,1)S(1)} %slice.103), channel_id=1, source_target_pairs={{0,1},{1,0},{2,3},{3,2},{4,5},{5,4},{6,7},{7,6},{8,9},{9,8},{10,11... | collective-permute-start | bytes 2359304 | tf_op jit(solution)/shard_map/ppermute | solution.py:163
  127.8 12.9 %collective-permute-start.32 = (bf16[96,2048]{1,0:T(8,128)(2,1)S(1)}, bf16[96,2048]{1,0:T(8,128)(2,1)S(1)}, u32[]{:S(2)}, u32[]{:S(2)}) collective-permute-start(bf16[96,2048]{1,0:T(8,128)(2,1)S(1)} %fusion.2), channel_id=1, source_target_pairs={{0,8},{4,12},{8,16},{12,20},{16,24},{20,28},{24,0},{28,4},{1,9},{5... | collective-permute-start | bytes 1179656 | tf_op jit(solution)/shard_map/ppermute | solution.py:160
  129.7 12.1 %collective-permute-start.16 = (bf16[96,2048]{1,0:T(8,128)(2,1)S(1)}, bf16[96,2048]{1,0:T(8,128)(2,1)S(1)}, u32[]{:S(2)}, u32[]{:S(2)}) collective-permute-start(bf16[96,2048]{1,0:T(8,128)(2,1)S(1)} %slice.168), channel_id=1, source_target_pairs={{0,4},{4,0},{8,12},{12,8},{16,20},{20,16},{24,28},{28,24},{1,5},{5... | collective-permute-start | bytes 1179656 | tf_op jit(solution)/shard_map/ppermute | solution.py:157
  130.5 18.4 %collective-permute-start.6 = (bf16[96,2048]{1,0:T(8,128)(2,1)S(1)}, bf16[96,2048]{1,0:T(8,128)(2,1)S(1)}, u32[]{:S(2)}, u32[]{:S(2)}) collective-permute-start(bf16[96,2048]{1,0:T(8,128)(2,1)S(1)} %slice.169), channel_id=1, source_target_pairs={{0,4},{4,0},{8,12},{12,8},{16,20},{20,16},{24,28},{28,24},{1,5},{5... | collective-permute-start | bytes 1179656 | tf_op jit(solution)/shard_map/ppermute | solution.py:157
  141.9 11.0 %collective-permute-start.33 = (bf16[96,2048]{1,0:T(8,128)(2,1)S(1)}, bf16[96,2048]{1,0:T(8,128)(2,1)S(1)}, u32[]{:S(2)}, u32[]{:S(2)}) collective-permute-start(bf16[96,2048]{1,0:T(8,128)(2,1)S(1)} %fusion.4), channel_id=1, source_target_pairs={{0,8},{4,12},{8,16},{12,20},{16,24},{20,28},{24,0},{28,4},{1,9},{5... | collective-permute-start | bytes 1179656 | tf_op jit(solution)/shard_map/ppermute | solution.py:160

commit v3 on v0

v3 whole, which is shorter than its diff:
```python
import functools

import jax
import jax.numpy as jnp
from jax import lax
from jax.experimental import pallas as pl
from jax.experimental.pallas import tpu as pltpu
from jax.sharding import PartitionSpec as P

F32 = jnp.float32
BF16 = jnp.bfloat16
LANES = 128
VMEM = 24 * 1024 * 1024
SMEM = pl.BlockSpec(memory_space=pltpu.SMEM)
ANY = pl.BlockSpec(memory_space=pl.ANY)


def tile(extent, choices):
    for size in choices:
        if extent % size == 0:
            return size
    return extent


def whole(x):
    return pl.BlockSpec(x.shape, lambda i: (0,) * len(x.shape))


def params():
    return pltpu.CompilerParams(vmem_limit_bytes=VMEM)


def cost():
    return pl.CostEstimate(flops=1, bytes_accessed=1, transcendentals=0)


def block_kernel(experts, tokens_ref, ids_ref, route_ref, out_ref):
    rows, width = tokens_ref.shape
    out_ref[:, :width] = tokens_ref[...]
    ids = ids_ref[...].T
    route = route_ref[...].T
    column = lax.broadcasted_iota(jnp.int32, (rows, out_ref.shape[1] - width), 1)
    expert = jnp.where(column < experts, column, column - experts)
    value = jnp.zeros(column.shape, F32)
    for k in range(ids.shape[1]):
        value = value + jnp.where(expert == ids[:, k:k + 1], route[:, k:k + 1], 0.0)
    high = value.astype(BF16).astype(F32)
    out_ref[:, width:] = jnp.where(column < experts, high, value - high).astype(BF16)


def make_block(tokens, expert_ids, route_weights, experts):
    rows, width = tokens.shape
    padded = width + 2 * experts + (-(2 * experts)) % LANES
    args = (tokens, expert_ids.T, route_weights.T)
    return pl.pallas_call(
        functools.partial(block_kernel, experts),
        grid=(1,),
        out_shape=jax.ShapeDtypeStruct((rows, padded), BF16),
        in_specs=[whole(a) for a in args],
        out_specs=pl.BlockSpec((rows, padded), lambda i: (0, 0)),
        compiler_params=params(),
        cost_estimate=cost(),
    )(*args)


def slot_row(tails, me, experts, rows, capacity):
    total = tails.shape[0]
    column = lax.broadcasted_iota(jnp.int32, (8, tails.shape[1]), 1)
    mark = jnp.where((column == me) | (column == experts + me), 1.0, 0.0).astype(BF16)
    weight = lax.dot_general(mark, tails, (((1,), (1,)), ((), ())), preferred_element_type=F32)
    live = weight > 0.0
    number = lax.broadcasted_iota(jnp.int32, (8, total), 1) // rows
    above = lax.broadcasted_iota(jnp.int32, (total, total), 0)
    own = lax.broadcasted_iota(jnp.int32, (total, total), 1)
    ahead = jnp.where((above < own) & (above >= (number * rows)[0:1]), 1.0, 0.0).astype(BF16)
    before = jnp.dot(jnp.where(live, 1.0, 0.0).astype(BF16), ahead, preferred_element_type=F32)
    return jnp.where(live, before.astype(jnp.int32) + number * capacity, -1)[0:1]


def slot_column(tails, me, experts, rows, capacity):
    total = tails.shape[0]
    column = lax.broadcasted_iota(jnp.int32, tails.shape, 1)
    mine = (column == me) | (column == experts + me)
    weight = jnp.sum(jnp.where(mine, tails.astype(F32), 0.0), axis=1, keepdims=True)
    live = weight > 0.0
    number = lax.broadcasted_iota(jnp.int32, (total, 1), 0) // rows
    own = lax.broadcasted_iota(jnp.int32, (total, total), 0)
    above = lax.broadcasted_iota(jnp.int32, (total, total), 1)
    ahead = jnp.where((above < own) & (above >= number * rows), 1.0, 0.0).astype(BF16)
    flags = jnp.broadcast_to(jnp.where(live, 1.0, 0.0), (total, LANES)).astype(BF16)
    before = jnp.dot(ahead, flags, preferred_element_type=F32)[:, 0:1]
    return jnp.where(live, before.astype(jnp.int32) + number * capacity, -1), weight


def layout(groups, capacity):
    offsets, total = [], 0
    for _, members in groups:
        offsets.append(total)
        total += -(-len(members) * capacity // 16) * 16
    return offsets + [total]


def multiply(x_ref, rows, weights, start, units, out_ref):
    def store(x, w, column, count):
        out_ref[rows, column:column + count] = jnp.dot(x, w, preferred_element_type=F32).astype(out_ref.dtype)

    x = x_ref[rows, :]
    if start is None:
        w_ref = weights[0]
        step = tile(w_ref.shape[1], (256, 384))
        for column in range(0, w_ref.shape[1], step):
            store(x, w_ref[:, column:column + step], column, step)
        return
    full = units // 256 * 256
    for i, ref in enumerate(weights):
        for column in range(0, full, 256):
            store(x, ref[:, pl.ds(pl.multiple_of(start + column, LANES), 256)], i * units + column, 256)
    if full < units:
        rest = pl.ds(pl.multiple_of(start + full, LANES), units - full)
        w = jnp.concatenate([ref[:, rest] for ref in weights], axis=1)
        y = jnp.dot(x, w, preferred_element_type=F32).astype(out_ref.dtype)
        out_ref[rows, full:units] = y[:, :units - full]
        out_ref[rows, units + full:] = y[:, units - full:]


def pick_kernel(width, experts, capacity, units, groups, count, kinds, split, copied, scalars, *refs):
    blocks, weights = refs[:count], refs[count:]
    if copied:
        *_, source_ref, chosen_ref, part_ref, target_ref, sem = refs
        copy = pltpu.make_async_copy(source_ref, target_ref, sem)
        copy.start()
    else:
        chosen_ref, part_ref = refs[-2:]
    rows = blocks[0].shape[0]
    offsets = layout(groups, capacity)
    step = tile(width, (512, 256))
    for g, (expert, members) in enumerate(groups):
        tails = jnp.concatenate([blocks[m][:, width:] for m in members], axis=0)
        slot = slot_row(tails, scalars[expert], experts, rows, capacity)
        here = offsets[g + 1] - offsets[g]
        place = lax.broadcasted_iota(jnp.int32, (here, len(members) * rows), 0)
        pick = jnp.where(place == slot, 1.0, 0.0).astype(BF16)
        for column in range(0, width, step):
            x = jnp.concatenate([blocks[m][:, column:column + step] for m in members], axis=0)
            value = jnp.dot(pick, x, preferred_element_type=F32).astype(BF16)
            chosen_ref[offsets[g]:offsets[g + 1], column:column + step] = value
    for g in range(len(groups)):
        mine = weights[kinds * g:kinds * (g + 1)]
        multiply(chosen_ref, slice(offsets[g], offsets[g + 1]), mine, scalars[2] if split else None, units, part_ref)
    if copied:
        copy.wait()


def pick_rows(scalars, groups, blocks, weights, split, copying, after, width, experts, capacity, units):
    columns = 2 * units if split else weights[0][0].shape[1]
    taken = layout(groups, capacity)[-1]
    flat = [w for expert, _ in groups for w in weights[expert]]
    kinds = len(weights[0])
    copied = len(copying)
    kernel = functools.partial(pick_kernel, width, experts, capacity, units, groups, len(blocks), kinds, split, copied)
    return pl.pallas_call(
        kernel,
        grid=(1,),
        out_shape=(
            jax.ShapeDtypeStruct((taken, width), BF16),
            jax.ShapeDtypeStruct((taken, columns), BF16),
            *[jax.ShapeDtypeStruct(a.shape, a.dtype) for a in copying],
        ),
        in_specs=[SMEM] + [whole(x) for x in (*blocks, *flat)] + [ANY] * (len(after) + copied),
        out_specs=(
            pl.BlockSpec((taken, width), lambda i: (0, 0)),
            pl.BlockSpec((taken, columns), lambda i: (0, 0)),
            *[ANY] * copied,
        ),
        scratch_shapes=[pltpu.SemaphoreType.DMA] * copied,
        compiler_params=params(),
        cost_estimate=cost(),
    )(scalars, *blocks, *flat, *after, *copying)


def home_kernel(capacity, units, groups, kinds, split, passed, scalars, x_ref, *refs):
    out_ref = refs[-1 - passed]
    offsets = layout(groups, capacity)
    for g in range(len(groups)):
        mine = refs[kinds * g:kinds * (g + 1)]
        multiply(x_ref, slice(offsets[g], offsets[g + 1]), mine, scalars[3] if split else None, units, out_ref)


def home_rows(scalars, groups, chosen, weights, split, passing, after, capacity, units):
    flat = [w for expert, _ in groups for w in weights[expert]]
    out = jax.ShapeDtypeStruct((chosen.shape[0], 2 * units), F32)
    args = (scalars, chosen, *flat, *after, *passing)
    result = pl.pallas_call(
        functools.partial(home_kernel, capacity, units, groups, len(weights[0]), split, len(passing)),
        grid=(1,),
        out_shape=(out, *[jax.ShapeDtypeStruct(p.shape, p.dtype) for p in passing]),
        in_specs=[SMEM, whole(chosen)] + [whole(w) for w in flat] + [ANY] * (len(after) + len(passing)),
        out_specs=(whole(out), *[ANY] * len(passing)),
        input_output_aliases={len(args) - len(passing) + i: 1 + i for i in range(len(passing))},
        compiler_params=params(),
        cost_estimate=cost(),
    )(*args)
    return result[0], result[1:]


def down_kernel(experts, capacity, groups, count, pieces, wide, passed, scalars, *refs):
    hiddens, refs = refs[:pieces], refs[pieces:]
    tail_refs, weights = refs[:count], refs[count:]
    scratch = refs[-2 * len(groups):]
    out_ref = refs[-2 * len(groups) - 1 - passed]
    rows = tail_refs[0].shape[0]
    units = hiddens[0].shape[1]
    offsets = layout(groups, capacity)
    starts = [scalars[4 + s] for s in range(pieces)]
    for g, (expert, members) in enumerate(groups):
        spread_ref, weight_ref = scratch[2 * g:2 * g + 2]
        tails = jnp.concatenate([tail_refs[m][...] for m in members], axis=0)
        slot, weight = slot_column(tails, scalars[expert], experts, rows, capacity)
        weight_ref[...] = weight
        place = lax.broadcasted_iota(jnp.int32, (len(members) * rows, offsets[g + 1] - offsets[g]), 1)
        spread = jnp.where(place == slot, 1.0, 0.0).astype(BF16)
        for s, ref in enumerate(hiddens):
            value = jnp.dot(spread, ref[offsets[g]:offsets[g + 1], :], preferred_element_type=F32).astype(BF16)
            if wide:
                spread_ref[:, pl.ds(pl.multiple_of(starts[s], LANES), units)] = value
            else:
                spread_ref[s] = value
    width = out_ref.shape[1]
    step = tile(width, (256,))

    @pl.loop(0, width // step)
    def _(i):
        span = pl.ds(pl.multiple_of(i * step, LANES), step)
        sums = [None] * count
        for g, (expert, members) in enumerate(groups):
            spread_ref, weight_ref = scratch[2 * g:2 * g + 2]
            w_ref = weights[g]
            if wide:
                result = jnp.dot(spread_ref[...], w_ref[:, span], preferred_element_type=F32)
            else:
                result = jnp.zeros((len(members) * rows, step), F32)
                for s in range(pieces):
                    w = w_ref[pl.ds(pl.multiple_of(starts[s], 16), units), span]
                    result = result + jnp.dot(spread_ref[s], w, preferred_element_type=F32)
            result = result * weight_ref[...]
            for k, m in enumerate(members):
                part = result[k * rows:(k + 1) * rows]
                sums[m] = part if sums[m] is None else sums[m] + part
        for m, value in enumerate(sums):
            out_ref[m * rows:(m + 1) * rows, span] = value.astype(BF16)


def down_rows(scalars, groups, hiddens, blocks, weights, passing, after, width, experts, capacity):
    rows, padded = blocks[0].shape
    units = hiddens[0].shape[1]
    pieces = len(hiddens)
    wide = units % LANES == 0
    tail = pl.BlockSpec((rows, padded - width), lambda i: (0, width // (padded - width)))
    scratch = []
    for _, members in groups:
        spread = (len(members) * rows, pieces * units) if wide else (pieces, len(members) * rows, units)
        scratch += [pltpu.VMEM(spread, BF16), pltpu.VMEM((len(members) * rows, 1), F32)]
    out = jax.ShapeDtypeStruct((len(blocks) * rows, width), BF16)
    args = (scalars, *hiddens, *blocks, *[weights[e] for e, _ in groups], *after, *passing)
    result = pl.pallas_call(
        functools.partial(down_kernel, experts, capacity, groups, len(blocks), pieces, wide, len(passing)),
        grid=(1,),
        out_shape=(out, *[jax.ShapeDtypeStruct(p.shape, p.dtype) for p in passing]),
        in_specs=[SMEM] + [whole(h) for h in hiddens] + [tail] * len(blocks)
        + [whole(weights[0])] * len(groups) + [ANY] * (len(after) + len(passing)),
        out_specs=(whole(out), *[ANY] * len(passing)),
        input_output_aliases={len(args) - len(passing) + i: 1 + i for i in range(len(passing))},
        scratch_shapes=scratch,
        compiler_params=params(),
        cost_estimate=cost(),
    )(*args)
    return result[0], result[1:]


def on_device(tokens, expert_ids, route_weights, w_gate, w_up, w_down):
    rows, width = tokens.shape
    top = expert_ids.shape[1]
    ring = lax.axis_size("expert")
    experts = ring * lax.axis_size("dp")
    capacity = min(rows, max(2, 3 * rows * top // (2 * experts)))
    parts = lax.axis_size("tensor")
    units = w_gate.shape[2] // parts
    core = lax.axis_index("dp")
    rank = lax.axis_index("tensor")
    hops = ring // 2

    def over_y(x):
        return lax.ppermute(x, "expert", [(i, i ^ 1) for i in range(ring)])

    def over_z(x):
        return lax.ppermute(x, "expert", [(i, (i + 2) % ring) for i in range(ring)])

    def over_core(x):
        return lax.ppermute(x, "dp", [(0, 1), (1, 0)])

    def over_x(x, step):
        return lax.ppermute(x, "tensor", [(i, (i + step) % parts) for i in range(parts)])

    first = lax.axis_index("expert") * 2
    scalars = [first + core, first + 1 - core, (rank + 1) % parts * units, rank * units]
    scalars += [(rank + parts - s) % parts * units for s in range(parts)]
    scalars = jnp.stack([jnp.asarray(s, jnp.int32) for s in scalars])
    gates = (w_gate[0], over_core(w_gate)[0])
    ups = (w_up[0], over_core(w_up)[0])
    split = parts == 2 and units % LANES == 0
    if split:
        away = home = tuple(zip(gates, ups))
    else:
        def unit_slice(w, offset):
            return lax.dynamic_slice_in_dim(w, (rank + offset) % parts * units, units, 1)

        away, home = [], []
        for gate, up in zip(gates, ups):
            pairs = [(unit_slice(gate, s), unit_slice(up, s)) for s in range(parts)]
            away.append((jnp.concatenate([w for pair in pairs[1:] for w in pair], axis=1),))
            home.append((jnp.concatenate(pairs[0], axis=1),))

    blocks, arrived = {(0, "s"): make_block(tokens, expert_ids, route_weights, experts)}, {}

    def send_on(hop):
        block = blocks[hop, "s"]
        if hop + 1 < hops:
            arrived[hop + 1] = over_z(block)
        blocks[hop, "b"] = over_y(block)

    both = ((0, (0, 1)), (1, (0, 1)))
    one = ((0, (0,)), (1, (0,)))
    plan = [([(0, "s")], ((0, (0,)),)), ([(0, "s"), (0, "b")], ((1, (0, 1)), (0, (1,)))), ([(1, "s")], one)]
    plan += [([(hop, "b"), (hop + 1, "s")], both) for hop in range(1, hops - 2)]
    plan += [([(hops - 2, "b"), (hops - 1, "b")], both), ([(hops - 1, "s")], one)]
    count = len(plan)
    chosen, parts_in, totals, hidden, returned = {}, {}, {}, {}, {}
    downs = [w_down[0]]
    order = [scalars]

    def pick(i):
        keys, groups = plan[i]
        mine = [blocks[k] for k in keys]
        copying = [w_down] if i == 1 else []
        chosen[i], part, *copies = pick_rows(
            scalars, groups, mine, away, split, copying, order, width, experts, capacity, units
        )
        downs.extend(over_core(c)[0] for c in copies)
        parts_in[i] = [over_x(part[:, 2 * units * (s - 1):2 * units * s], s) for s in range(1, parts)]
        order[:] = [part]

    def home_product(i, hop):
        passing = [arrived[hop]] if hop in arrived else []
        totals[i], passed = home_rows(scalars, plan[i][1], chosen[i], home, split, passing, order, capacity, units)
        order[:] = [totals[i]]
        if passing:
            blocks[hop, "s"] = passed[0]
            send_on(hop)

    def activate(i):
        total = totals[i]
        for piece in parts_in[i]:
            total = total + piece.astype(F32)
        value = (jax.nn.silu(total[:, :units]) * total[:, units:]).astype(BF16)
        hidden[i] = [value] + [over_x(value, s) for s in range(1, parts)]
        order.append(value)

    def down_product(i, hop):
        keys, groups = plan[i]
        mine = [blocks[k] for k in keys]
        passing = [arrived[hop]] if hop in arrived else []
        term, passed = down_rows(
            scalars, groups, hidden[i], mine, downs, passing, order, width, experts, capacity
        )
        order[:] = [term]
        if passing:
            blocks[hop, "s"] = passed[0]
            send_on(hop)
        for k, (at, kind) in enumerate(keys):
            piece = term[k * rows:(k + 1) * rows]
            if kind == "b":
                piece = over_y(piece)
            returned.setdefault(at, []).append(piece)

    arriving = []

    def add_hop(hop):
        total = sum(x.astype(F32) for x in returned[hop])
        if hop > 0:
            total = total.astype(BF16)
            arriving.append(lax.ppermute(total, "expert", [(i, (i - 2 * hop) % ring) for i in range(ring)]))
        else:
            arriving.append(total)
        order.append(total)

    send_on(0)
    added = 0
    for i in range(count + 2):
        if i == 1:
            activate(0)
        if i < count:
            pick(i)
        if 1 <= i - 1 < count:
            activate(i - 1)
        if i < count:
            home_product(i, {0: 1, 2: 2}.get(i))
        if (5 <= i < count or i > count) and added < hops - 2:
            add_hop(added)
            added += 1
        if 0 <= i - 2 < count:
            down_product(i - 2, i if i >= 3 else None)
    for hop in range(added, hops):
        add_hop(hop)
    return sum(x.astype(F32) for x in arriving).astype(BF16)


def solution(mesh):
    placed = (
        P(("group", "expert", "dp"), "tensor"),
        P(("group", "expert", "dp"), None),
        P(("group", "expert", "dp"), None),
        P(("expert", "dp"), "tensor", None),
        P(("expert", "dp"), "tensor", None),
        P(("expert", "dp"), None, "tensor"),
    )
    return jax.shard_map(
        on_device,
        mesh=mesh,
        in_specs=placed,
        out_specs=P(("group", "expert", "dp"), "tensor"),
        check_vma=False,
    )
```

time: 398 us -> 156 us (0.39)
  the two profiles are of different devices: /device:TPU:13 before, /device:TPU:0 now
where the time goes in v3:
time: 156 us; the launch traced here: 155 us
  Pallas kernels  62.6 us (40%)
  waiting for transfers between devices  52 us (33%)
  starting transfers between devices  31.2 us (20%)
  local copies, waits for them, and re-layouts  6.35 us (4%)
  other arithmetic  2.33 us (1%)
    ppermute x8, waiting for transfers between devices, over_y(): return lax.ppermute(x, 'expert', [(i, i ^ 1) for i in range(ring)])  25.8 us
    pallas_call x6, Pallas kernels, down_rows(): pl.pallas_call(functools.partial(down_kernel, experts, capacity, groups,...  22.7 us
    pallas_call x6, Pallas kernels, pick_rows(): pl.pallas_call(kernel, grid=(1,), out_shape=(jax.ShapeDtypeStruct((taken,...  22 us
    ppermute x3, waiting for transfers between devices, add_hop(): lax.ppermute(total, 'expert', [(i, (i - 2 * hop) % ring) for i in range(r...  20 us
    pallas_call x6, Pallas kernels, home_rows(): pl.pallas_call(functools.partial(home_kernel, capacity, units, groups, le...  16.6 us
    ppermute x12, starting transfers between devices, over_x(): lax.ppermute(x, 'tensor', [(i, (i + step) % parts) for i in range(parts)])  12.9 us
    ppermute x8, starting transfers between devices, over_y(): return lax.ppermute(x, 'expert', [(i, i ^ 1) for i in range(ring)])  8.41 us
    unnamed x16, local copies, waits for them, and re-layouts  6.16 us
  transfers between devices with their start and end apart: 29, of which 11 were waited for; matrix products, arithmetic and copies ran while one was open for 1% of the time, Pallas kernels for 38%

profile of v3, /device:TPU:0, one launch (start us, length us, event | category | flops | bytes accessed | tf_op | source)
XLA Modules:
  0.0 154.8 jit_solution(7661621035330962240)
XLA Ops:
  0.0 0.5 collective-permute-start.3
  0.5 1.0 copy-done.5
  1.5 0.7 copy-done.6
  2.2 0.7 copy-done.7
  2.9 1.2 shard_map.64.refs_0_.refs_2_
  4.1 3.0 %collective-permute-start = (bf16[96,2176]{1,0:T(8,128)(2,1)}, bf16[96,2176]{1,0:T(8,128)(2,1)}, u32[]{:S(2)}, u32[]{:S(2)}) collective-permute-start(bf16[96,2176]{1,0:T(8,128)(2,1)} %shard_map.64.refs_0_.refs_2_), channel_id=1, source_target_pairs={{0,8},{4,12},{8,16},{12,20},{16,24},{20,28},{24,0},{28,4},{1,9},{5... | collective-permute-start | bytes 1253384 | tf_op jit(solution)/shard_map/ppermute | solution.py:296
  7.2 1.9 %copy-done = bf16[1,2048,768]{2,1,0:T(8,128)(2,1)S(1)} copy-done((bf16[1,2048,768]{2,1,0:T(8,128)(2,1)S(1)}, bf16[1,2048,768]{2,1,0:T(8,128)(2,1)}, u32[]{:S(2)}) %copy-start) | copy-done | bytes 3145752
  9.1 1.9 %copy-done.2 = bf16[1,2048,768]{2,1,0:T(8,128)(2,1)S(1)} copy-done((bf16[1,2048,768]{2,1,0:T(8,128)(2,1)S(1)}, bf16[1,2048,768]{2,1,0:T(8,128)(2,1)}, u32[]{:S(2)}) %copy-start.2) | copy-done | bytes 3145752
  10.9 2.2 %shard_map.65 = (bf16[80,2048]{1,0:T(8,128)(2,1)S(1)}, bf16[80,768]{1,0:T(8,128)(2,1)S(1)}) custom-call(s32[6]{0:T(128)S(1)} %stack.24.scalars.refs_3_, bf16[96,2176]{1,0:T(8,128)(2,1)} %shard_map.64.refs_0_.refs_2_, bf16[2048,768]{1,0:T(8,128)(2,1)S(1)} %bitcast.13, bf16[2048,768]{1,0:T(8,128)(2,1)S(1)} %bitcast.25, s32[6]{0:T(128)S(1)} %stack.24.scalars.refs_3_), custom_call_target="tpu_custom_call" | custom-call | flops 1 | bytes 1 | tf_op jit(solution)/shard_map/pallas_call | solution.py:161
  13.2 1.6 %collective-permute-start.1 = (bf16[80,768]{1,0:T(8,128)(2,1)S(1)}, bf16[80,768]{1,0:T(8,128)(2,1)S(1)}, u32[]{:S(2)}, u32[]{:S(2)}) collective-permute-start(bf16[80,768]{1,0:T(8,128)(2,1)S(1)} %get-tuple-element.25.refs_2_), channel_id=1, source_target_pairs={{0,2},{2,0},{1,3},{3,1},{4,6},{6,4},{5,7},{7,5},{8,10},{10,8},{9,1... | collective-permute-start | bytes 368648 | tf_op jit(solution)/shard_map/ppermute | solution.py:302
  14.8 1.5 collective-permute-start.5
  16.3 2.9 %collective-permute-done.refs_3_ = bf16[96,2176]{1,0:T(8,128)(2,1)} collective-permute-done((bf16[96,2176]{1,0:T(8,128)(2,1)}, bf16[96,2176]{1,0:T(8,128)(2,1)}, u32[]{:S(2)}, u32[]{:S(2)}) %collective-permute-start) | collective-permute-done | bytes 417824 | tf_op jit(solution)/shard_map/ppermute | solution.py:296
  19.2 1.2 shard_map.66
  20.5 5.4 %collective-permute-done.5.refs_1_.refs_3_ = bf16[96,2176]{1,0:T(8,128)(2,1)S(1)} collective-permute-done((bf16[96,2176]{1,0:T(8,128)(2,1)}, bf16[96,2176]{1,0:T(8,128)(2,1)S(1)}, u32[]{:S(2)}, u32[]{:S(2)}) %collective-permute-start.5) | collective-permute-done | bytes 417824 | tf_op jit(solution)/shard_map/ppermute | solution.py:293
  26.0 4.2 %shard_map.67 = (bf16[224,2048]{1,0:T(8,128)(2,1)S(1)}, bf16[224,768]{1,0:T(8,128)(2,1)S(1)}, bf16[1,768,2048]{2,1,0:T(8,128)(2,1)S(1)}) custom-call(s32[6]{0:T(128)S(1)} %stack.24.scalars.refs_3_, bf16[96,2176]{1,0:T(8,128)(2,1)} %shard_map.64.refs_0_.refs_2_, bf16[96,2176]{1,0:T(8,128)(2,1)S(1)} %collective-permute-done.5.refs_1_.refs_3_, ...), custom_call_target="tpu_custom_call" | custom-call | flops 1 | bytes 1 | tf_op jit(solution)/shard_map/pallas_call | solution.py:161
  30.3 0.6 collective-permute-start.6
  30.9 1.5 collective-permute-start.10
  32.4 1.6 %collective-permute-start.7 = (bf16[96,2176]{1,0:T(8,128)(2,1)}, bf16[96,2176]{1,0:T(8,128)(2,1)S(1)}, u32[]{:S(2)}, u32[]{:S(2)}) collective-permute-start(bf16[96,2176]{1,0:T(8,128)(2,1)} %get-tuple-element.27.refs_0_.refs_2_), channel_id=1, source_target_pairs={{0,8},{4,12},{8,16},{12,20},{16,24},{20,28},{24,0},{28,4},{1,9},{5... | collective-permute-start | bytes 1253384 | tf_op jit(solution)/shard_map/ppermute | solution.py:296
  34.0 3.1 %shard_map.68.refs_5_ = f32[224,768]{1,0:T(8,128)S(1)} custom-call(s32[6]{0:T(128)S(1)} %stack.24.scalars.refs_3_, bf16[224,2048]{1,0:T(8,128)(2,1)S(1)} %get-tuple-element.28.x_ref, bf16[2048,768]{1,0:T(8,128)(2,1)S(1)} %bitcast.38, bf16[2048,768]{1,0:T(8,128)(2,1)} %bitcast.11.refs_3_.refs_1_.refs_4_.refs_5_, bf16[2048,768]{1,0:T(8,128)(2,1)S(1)} %bitcast.16, ...), custom_call_target="tpu_custom_call" | custom-call | flops 1 | bytes 1 | tf_op jit(solution)/shard_map/pallas_call | solution.py:193
  37.0 1.6 %collective-permute-start.2 = (bf16[80,384]{1,0:T(8,128)(2,1)S(1)}, bf16[80,384]{1,0:T(8,128)(2,1)S(1)}, u32[]{:S(2)}, u32[]{:S(2)}) collective-permute-start(bf16[80,384]{1,0:T(8,128)(2,1)S(1)} %fusion.5.refs_7_.refs_0_), channel_id=1, source_target_pairs={{0,2},{2,0},{1,3},{3,1},{4,6},{6,4},{5,7},{7,5},{8,10},{10,8},{9,1... | collective-permute-start | bytes 184328 | tf_op jit(solution)/shard_map/ppermute | solution.py:302
  38.6 4.0 %shard_map.69 = (bf16[160,2048]{1,0:T(8,128)(2,1)S(1)}, bf16[160,768]{1,0:T(8,128)(2,1)S(1)}) custom-call(s32[6]{0:T(128)S(1)} %stack.24.scalars.refs_3_, bf16[96,2176]{1,0:T(8,128)(2,1)} %get-tuple-element.27.refs_0_.refs_2_, bf16[2048,768]{1,0:T(8,128)(2,1)S(1)} %bitcast.17, bf16[2048,768]{1,0:T(8,128)(2,1)S(1)} %bitcast.29, ...), custom_call_target="tpu_custom_call" | custom-call | flops 1 | bytes 1 | tf_op jit(solution)/shard_map/pallas_call | solution.py:161
  42.6 0.6 collective-permute-start.11
  43.4 2.4 %collective-permute-done.7.refs_6_ = bf16[96,2176]{1,0:T(8,128)(2,1)S(1)} collective-permute-done((bf16[96,2176]{1,0:T(8,128)(2,1)}, bf16[96,2176]{1,0:T(8,128)(2,1)S(1)}, u32[]{:S(2)}, u32[]{:S(2)}) %collective-permute-start.7) | collective-permute-done | bytes 417824 | tf_op jit(solution)/shard_map/ppermute | solution.py:296
  45.8 1.5 collective-permute-start.8
  47.3 3.1 %shard_map.70 = (f32[160,768]{1,0:T(8,128)S(1)}, bf16[96,2176]{1,0:T(8,128)(2,1)S(1)}) custom-call(s32[6]{0:T(128)S(1)} %stack.24.scalars.refs_3_, bf16[160,2048]{1,0:T(8,128)(2,1)S(1)} %get-tuple-element.30.x_ref, bf16[2048,768]{1,0:T(8,128)(2,1)S(1)} %bitcast.18, bf16[2048,768]{1,0:T(8,128)(2,1)S(1)} %bitcast.30, ...), custom_call_target="tpu_custom_call", output_to_operand_aliasing={{1}: (8, {})} | custom-call | flops 1 | bytes 1 | tf_op jit(solution)/shard_map/pallas_call | solution.py:193
  50.5 0.2 collective-permute-start.12
  50.7 3.0 %shard_map.71.refs_6_ = bf16[96,2048]{1,0:T(8,128)(2,1)S(1)} custom-call(s32[6]{0:T(128)S(1)} %stack.24.scalars.refs_3_, bf16[80,384]{1,0:T(8,128)(2,1)S(1)} %fusion.5.refs_7_.refs_0_, bf16[80,384]{1,0:T(8,128)(2,1)S(1)} %collective-permute-done.2.refs_1_, bf16[96,2176]{1,0:T(8,128)(2,1)} %shard_map.64.refs_0_.refs_2_, bf16[768,2048]{1,0:T(8,128)(2,1)S(1)} %bitcast.47, ...), custom_call_target="tpu_custom_call" | custom-call | flops 1 | bytes 1 | tf_op jit(solution)/shard_map/pallas_call | solution.py:265
  53.7 3.9 %shard_map.72 = (bf16[288,2048]{1,0:T(8,128)(2,1)S(1)}, bf16[288,768]{1,0:T(8,128)(2,1)S(1)}) custom-call(s32[6]{0:T(128)S(1)} %stack.24.scalars.refs_3_, bf16[96,2176]{1,0:T(8,128)(2,1)S(1)} %collective-permute-done.10.refs_0_.refs_2_, bf16[96,2176]{1,0:T(8,128)(2,1)S(1)} %get-tuple-element.34.refs_1_.refs_3_, bf16[2048,768]{1,0:T(8,128)(2,1)S(1)} %bitcast.19, ...), custom_call_target="tpu_custom_call" | custom-call | flops 1 | bytes 1 | tf_op jit(solution)/shard_map/pallas_call | solution.py:161
  57.6 0.6 collective-permute-start.17
  58.3 1.6 %collective-permute-start.14 = (bf16[160,384]{1,0:T(8,128)(2,1)S(1)}, bf16[160,384]{1,0:T(8,128)(2,1)S(1)}, u32[]{:S(2)}, u32[]{:S(2)}) collective-permute-start(bf16[160,384]{1,0:T(8,128)(2,1)S(1)} %fusion.4.refs_5_.refs_0_), channel_id=1, source_target_pairs={{0,2},{2,0},{1,3},{3,1},{4,6},{6,4},{5,7},{7,5},{8,10},{10,8},{9,1... | collective-permute-start | bytes 368648 | tf_op jit(solution)/shard_map/ppermute | solution.py:302
  59.9 3.0 %shard_map.73.refs_6_ = f32[288,768]{1,0:T(8,128)S(1)} custom-call(s32[6]{0:T(128)S(1)} %stack.24.scalars.refs_3_, bf16[288,2048]{1,0:T(8,128)(2,1)S(1)} %get-tuple-element.35.x_ref, bf16[2048,768]{1,0:T(8,128)(2,1)S(1)} %bitcast.20, bf16[2048,768]{1,0:T(8,128)(2,1)S(1)} %bitcast.32, bf16[2048,768]{1,0:T(8,128)(2,1)S(1)} %bitcast.42, ...), custom_call_target="tpu_custom_call" | custom-call | flops 1 | bytes 1 | tf_op jit(solution)/shard_map/pallas_call | solution.py:193
  62.9 0.6 collective-permute-start.15
  63.5 4.1 %shard_map.74 = (bf16[192,2048]{1,0:T(8,128)(2,1)S(1)}, bf16[96,2176]{1,0:T(8,128)(2,1)S(1)}) custom-call(s32[6]{0:T(128)S(1)} %stack.24.scalars.refs_3_, bf16[224,384]{1,0:T(8,128)(2,1)S(1)} %fusion.2.refs_5_.refs_0_, bf16[224,384]{1,0:T(8,128)(2,1)S(1)} %collective-permute-done.8.refs_1_, ...), custom_call_target="tpu_custom_call", output_to_operand_aliasing={{1}: (8, {})} | custom-call | flops 1 | bytes 1 | tf_op jit(solution)/shard_map/pallas_call | solution.py:265
  67.6 1.6 %collective-permute-start.16 = (bf16[96,2176]{1,0:T(8,128)(2,1)S(1)}, bf16[96,2176]{1,0:T(8,128)(2,1)S(1)}, u32[]{:S(2)}, u32[]{:S(2)}) collective-permute-start(bf16[96,2176]{1,0:T(8,128)(2,1)S(1)} %get-tuple-element.38.refs_0_.refs_2_), channel_id=1, source_target_pairs={{0,4},{4,0},{8,12},{12,8},{16,20},{20,16},{24,28},{28,24},{1,5},{5... | collective-permute-start | bytes 1253384 | tf_op jit(solution)/shard_map/ppermute | solution.py:293
  69.2 0.6 collective-permute-start.13
  69.9 0.1 fusion.1.refs_5_.refs_0_
  70.0 0.6 collective-permute-start.18
  70.6 5.0 %collective-permute-done.15.refs_0_.refs_2_ = bf16[96,2176]{1,0:T(8,128)(2,1)S(1)} collective-permute-done((bf16[96,2176]{1,0:T(8,128)(2,1)S(1)}, bf16[96,2176]{1,0:T(8,128)(2,1)S(1)}, u32[]{:S(2)}, u32[]{:S(2)}) %collective-permute-start.15) | collective-permute-done | bytes 417824 | tf_op jit(solution)/shard_map/ppermute | solution.py:293
  75.6 9.0 %collective-permute-done.16.refs_1_.refs_3_ = bf16[96,2176]{1,0:T(8,128)(2,1)S(1)} collective-permute-done((bf16[96,2176]{1,0:T(8,128)(2,1)S(1)}, bf16[96,2176]{1,0:T(8,128)(2,1)S(1)}, u32[]{:S(2)}, u32[]{:S(2)}) %collective-permute-start.16) | collective-permute-done | bytes 417824 | tf_op jit(solution)/shard_map/ppermute | solution.py:293
  84.5 3.9 %shard_map.75 = (bf16[288,2048]{1,0:T(8,128)(2,1)S(1)}, bf16[288,768]{1,0:T(8,128)(2,1)S(1)}) custom-call(s32[6]{0:T(128)S(1)} %stack.24.scalars.refs_3_, bf16[96,2176]{1,0:T(8,128)(2,1)S(1)} %collective-permute-done.15.refs_0_.refs_2_, bf16[96,2176]{1,0:T(8,128)(2,1)S(1)} %collective-permute-done.16.refs_1_.refs_3_, bf16[2048,768]{1,0:T(8,128)(2,1)S(1)} %bitcast.21, ...), custom_call_target="tpu_custom_call" | custom-call | flops 1 | bytes 1 | tf_op jit(solution)/shard_map/pallas_call | solution.py:161
  88.4 0.6 collective-permute-start.19
  89.0 3.0 %shard_map.76.refs_5_ = f32[288,768]{1,0:T(8,128)S(1)} custom-call(s32[6]{0:T(128)S(1)} %stack.24.scalars.refs_3_, bf16[288,2048]{1,0:T(8,128)(2,1)S(1)} %get-tuple-element.39.x_ref, bf16[2048,768]{1,0:T(8,128)(2,1)S(1)} %bitcast.22, bf16[2048,768]{1,0:T(8,128)(2,1)S(1)} %bitcast.34, bf16[2048,768]{1,0:T(8,128)(2,1)S(1)} %bitcast.44, ...), custom_call_target="tpu_custom_call" | custom-call | flops 1 | bytes 1 | tf_op jit(solution)/shard_map/pallas_call | solution.py:193
  92.0 3.8 %shard_map.77.refs_5_ = bf16[96,2048]{1,0:T(8,128)(2,1)S(1)} custom-call(s32[6]{0:T(128)S(1)} %stack.24.scalars.refs_3_, bf16[160,384]{1,0:T(8,128)(2,1)S(1)} %fusion.4.refs_5_.refs_0_, bf16[160,384]{1,0:T(8,128)(2,1)S(1)} %collective-permute-done.14.refs_1_, bf16[96,2176]{1,0:T(8,128)(2,1)} %get-tuple-element.27.refs_0_.refs_2_, ...), custom_call_target="tpu_custom_call" | custom-call | flops 1 | bytes 1 | tf_op jit(solution)/shard_map/pallas_call | solution.py:265
  95.9 0.1 convert_add_fusion.2.refs_7_
  96.0 3.8 %shard_map.78 = (bf16[160,2048]{1,0:T(8,128)(2,1)S(1)}, bf16[160,768]{1,0:T(8,128)(2,1)S(1)}) custom-call(s32[6]{0:T(128)S(1)} %stack.24.scalars.refs_3_, bf16[96,2176]{1,0:T(8,128)(2,1)S(1)} %get-tuple-element.38.refs_0_.refs_2_, bf16[2048,768]{1,0:T(8,128)(2,1)S(1)} %bitcast.23, bf16[2048,768]{1,0:T(8,128)(2,1)S(1)} %bitcast.35, ...), custom_call_target="tpu_custom_call" | custom-call | flops 1 | bytes 1 | tf_op jit(solution)/shard_map/pallas_call | solution.py:161
  99.9 1.6 %collective-permute-start.23 = (bf16[160,768]{1,0:T(8,128)(2,1)S(1)}, bf16[160,768]{1,0:T(8,128)(2,1)S(1)}, u32[]{:S(2)}, u32[]{:S(2)}) collective-permute-start(bf16[160,768]{1,0:T(8,128)(2,1)S(1)} %get-tuple-element.42.refs_4_), channel_id=1, source_target_pairs={{0,2},{2,0},{1,3},{3,1},{4,6},{6,4},{5,7},{7,5},{8,10},{10,8},{9,1... | collective-permute-start | bytes 737288 | tf_op jit(solution)/shard_map/ppermute | solution.py:302
  101.7 0.5 collective-permute-start.22
  102.2 3.1 %shard_map.79.refs_6_ = f32[160,768]{1,0:T(8,128)S(1)} custom-call(s32[6]{0:T(128)S(1)} %stack.24.scalars.refs_3_, bf16[160,2048]{1,0:T(8,128)(2,1)S(1)} %get-tuple-element.41.x_ref, bf16[2048,768]{1,0:T(8,128)(2,1)S(1)} %bitcast.24, bf16[2048,768]{1,0:T(8,128)(2,1)S(1)} %bitcast.36, bf16[2048,768]{1,0:T(8,128)(2,1)S(1)} %bitcast.46, ...), custom_call_target="tpu_custom_call" | custom-call | flops 1 | bytes 1 | tf_op jit(solution)/shard_map/pallas_call | solution.py:193
  105.4 0.8 collective-permute-done.23
  106.3 1.6 %collective-permute-start.27 = (bf16[160,384]{1,0:T(8,128)(2,1)S(1)}, bf16[160,384]{1,0:T(8,128)(2,1)S(1)}, u32[]{:S(2)}, u32[]{:S(2)}) collective-permute-start(bf16[160,384]{1,0:T(8,128)(2,1)S(1)} %fusion.3.refs_7_.refs_0_), channel_id=1, source_target_pairs={{0,2},{2,0},{1,3},{3,1},{4,6},{6,4},{5,7},{7,5},{8,10},{10,8},{9,1... | collective-permute-start | bytes 368648 | tf_op jit(solution)/shard_map/ppermute | solution.py:302
  107.9 4.1 %shard_map.80.refs_6_ = bf16[192,2048]{1,0:T(8,128)(2,1)S(1)} custom-call(s32[6]{0:T(128)S(1)} %stack.24.scalars.refs_3_, bf16[288,384]{1,0:T(8,128)(2,1)S(1)} %fusion.1.refs_5_.refs_0_, bf16[288,384]{1,0:T(8,128)(2,1)S(1)} %collective-permute-done.18.refs_1_, bf16[96,2176]{1,0:T(8,128)(2,1)S(1)} %collective-permute-done.10.refs_0_.refs_2_, ...), custom_call_target="tpu_custom_call" | custom-call | flops 1 | bytes 1 | tf_op jit(solution)/shard_map/pallas_call | solution.py:265
  112.1 0.6 collective-permute-start.20
  112.6 4.1 %shard_map.81.refs_5_ = bf16[192,2048]{1,0:T(8,128)(2,1)S(1)} custom-call(s32[6]{0:T(128)S(1)} %stack.24.scalars.refs_3_, bf16[288,384]{1,0:T(8,128)(2,1)S(1)} %fusion.refs_5_.refs_0_, bf16[288,384]{1,0:T(8,128)(2,1)S(1)} %collective-permute-done.22.refs_1_, bf16[96,2176]{1,0:T(8,128)(2,1)S(1)} %collective-permute-done.15.refs_0_.refs_2_, ...), custom_call_target="tpu_custom_call" | custom-call | flops 1 | bytes 1 | tf_op jit(solution)/shard_map/pallas_call | solution.py:265
  116.8 1.6 %collective-permute-start.26 = (bf16[96,2048]{1,0:T(8,128)(2,1)S(1)}, bf16[96,2048]{1,0:T(8,128)(2,1)S(1)}, u32[]{:S(2)}, u32[]{:S(2)}) collective-permute-start(bf16[96,2048]{1,0:T(8,128)(2,1)S(1)} %get-tuple-element.44), channel_id=1, source_target_pairs={{0,4},{4,0},{8,12},{12,8},{16,20},{20,16},{24,28},{28,24},{1,5},{5... | collective-permute-start | bytes 1179656 | tf_op jit(solution)/shard_map/ppermute | solution.py:293
  118.4 0.5 collective-permute-start.24
  118.9 5.3 %collective-permute-done.20 = bf16[96,2048]{1,0:T(8,128)(2,1)S(1)} collective-permute-done((bf16[96,2048]{1,0:T(8,128)(2,1)S(1)}, bf16[96,2048]{1,0:T(8,128)(2,1)S(1)}, u32[]{:S(2)}, u32[]{:S(2)}) %collective-permute-start.20) | collective-permute-done | bytes 393248 | tf_op jit(solution)/shard_map/ppermute | solution.py:293
  124.3 3.7 %collective-permute-start.21 = (bf16[96,2048]{1,0:T(8,128)(2,1)S(1)}, bf16[96,2048]{1,0:T(8,128)(2,1)S(1)}, u32[]{:S(2)}, u32[]{:S(2)}) collective-permute-start(bf16[96,2048]{1,0:T(8,128)(2,1)S(1)} %add_convert_fusion.3.refs_6_), channel_id=1, source_target_pairs={{0,24},{4,28},{8,0},{12,4},{16,8},{20,12},{24,16},{28,20},{1,25},{... | collective-permute-start | bytes 1179656 | tf_op jit(solution)/shard_map/ppermute | solution.py:391
  128.0 3.6 %shard_map.82 = bf16[96,2048]{1,0:T(8,128)(2,1)S(1)} custom-call(s32[6]{0:T(128)S(1)} %stack.24.scalars.refs_3_, bf16[160,384]{1,0:T(8,128)(2,1)S(1)} %fusion.3.refs_7_.refs_0_, bf16[160,384]{1,0:T(8,128)(2,1)S(1)} %collective-permute-done.27.refs_1_, bf16[96,2176]{1,0:T(8,128)(2,1)S(1)} %get-tuple-element.38.refs_0_.refs_2_, ...), custom_call_target="tpu_custom_call" | custom-call | flops 1 | bytes 1 | tf_op jit(solution)/shard_map/pallas_call | solution.py:265
  131.8 1.2 collective-permute-done.24
  133.1 0.7 collective-permute-start.25
  133.8 0.4 collective-permute-done.21
  134.2 7.5 %collective-permute-done.28 = bf16[96,2048]{1,0:T(8,128)(2,1)S(1)} collective-permute-done((bf16[96,2048]{1,0:T(8,128)(2,1)S(1)}, bf16[96,2048]{1,0:T(8,128)(2,1)S(1)}, u32[]{:S(2)}, u32[]{:S(2)}) %collective-permute-start.28) | collective-permute-done | bytes 393248 | tf_op jit(solution)/shard_map/ppermute | solution.py:391
  141.6 12.2 %collective-permute-done.25 = bf16[96,2048]{1,0:T(8,128)(2,1)S(1)} collective-permute-done((bf16[96,2048]{1,0:T(8,128)(2,1)S(1)}, bf16[96,2048]{1,0:T(8,128)(2,1)S(1)}, u32[]{:S(2)}, u32[]{:S(2)}) %collective-permute-start.25) | collective-permute-done | bytes 393248 | tf_op jit(solution)/shard_map/ppermute | solution.py:391
  153.8 1.0 add_convert_fusion
  (50 shorter events, 1.5 us)
Async XLA Ops:
  0.0 26.0 %collective-permute-start.3 = (bf16[1,2048,768]{2,1,0:T(8,128)(2,1)}, bf16[1,2048,768]{2,1,0:T(8,128)(2,1)S(1)}, u32[]{:S(2)}, u32[]{:S(2)}) collective-permute-start(bf16[1,2048,768]{2,1,0:T(8,128)(2,1)} %param.9), channel_id=1, source_target_pairs={{0,1},{1,0},{2,3},{3,2},{4,5},{5,4},{6,7},{7,6},{8,9},{9,8},{10,11... | collective-permute-start | bytes 9437192 | tf_op jit(solution)/shard_map/ppermute | solution.py:299
  0.5 25.5 %collective-permute-start.4 = (bf16[1,2048,768]{2,1,0:T(8,128)(2,1)}, bf16[1,2048,768]{2,1,0:T(8,128)(2,1)}, u32[]{:S(2)}, u32[]{:S(2)}) collective-permute-start(bf16[1,2048,768]{2,1,0:T(8,128)(2,1)} %param.10), channel_id=1, source_target_pairs={{0,1},{1,0},{2,3},{3,2},{4,5},{5,4},{6,7},{7,6},{8,9},{9,8},{10,11... | collective-permute-start | bytes 9437192 | tf_op jit(solution)/shard_map/ppermute | solution.py:299
  0.5 1.0 copy-start.5
  1.5 0.7 copy-start.6
  2.2 0.7 copy-start.7
  4.1 15.2 %collective-permute-start = (bf16[96,2176]{1,0:T(8,128)(2,1)}, bf16[96,2176]{1,0:T(8,128)(2,1)}, u32[]{:S(2)}, u32[]{:S(2)}) collective-permute-start(bf16[96,2176]{1,0:T(8,128)(2,1)} %shard_map.64.refs_0_.refs_2_), channel_id=1, source_target_pairs={{0,8},{4,12},{8,16},{12,20},{16,24},{20,28},{24,0},{28,4},{1,9},{5... | collective-permute-start | bytes 1253384 | tf_op jit(solution)/shard_map/ppermute | solution.py:296
  7.2 1.9 %copy-start = (bf16[1,2048,768]{2,1,0:T(8,128)(2,1)S(1)}, bf16[1,2048,768]{2,1,0:T(8,128)(2,1)}, u32[]{:S(2)}) copy-start(bf16[1,2048,768]{2,1,0:T(8,128)(2,1)} %param.9) | copy-start | bytes 9437188
  9.1 1.9 %copy-start.2 = (bf16[1,2048,768]{2,1,0:T(8,128)(2,1)S(1)}, bf16[1,2048,768]{2,1,0:T(8,128)(2,1)}, u32[]{:S(2)}) copy-start(bf16[1,2048,768]{2,1,0:T(8,128)(2,1)} %param.10) | copy-start | bytes 9437188
  10.9 8.3 %copy-start.1 = (bf16[1,2048,768]{2,1,0:T(8,128)(2,1)S(1)}, bf16[1,2048,768]{2,1,0:T(8,128)(2,1)}, u32[]{:S(2)}) copy-start(bf16[1,2048,768]{2,1,0:T(8,128)(2,1)} %param.9) | copy-start | bytes 9437188
  10.9 8.3 %copy-start.3 = (bf16[1,2048,768]{2,1,0:T(8,128)(2,1)S(1)}, bf16[1,2048,768]{2,1,0:T(8,128)(2,1)}, u32[]{:S(2)}) copy-start(bf16[1,2048,768]{2,1,0:T(8,128)(2,1)} %param.10) | copy-start | bytes 9437188
  13.2 7.3 %collective-permute-start.1 = (bf16[80,768]{1,0:T(8,128)(2,1)S(1)}, bf16[80,768]{1,0:T(8,128)(2,1)S(1)}, u32[]{:S(2)}, u32[]{:S(2)}) collective-permute-start(bf16[80,768]{1,0:T(8,128)(2,1)S(1)} %get-tuple-element.25.refs_2_), channel_id=1, source_target_pairs={{0,2},{2,0},{1,3},{3,1},{4,6},{6,4},{5,7},{7,5},{8,10},{10,8},{9,1... | collective-permute-start | bytes 368648 | tf_op jit(solution)/shard_map/ppermute | solution.py:302
  14.8 11.2 %collective-permute-start.5 = (bf16[96,2176]{1,0:T(8,128)(2,1)}, bf16[96,2176]{1,0:T(8,128)(2,1)S(1)}, u32[]{:S(2)}, u32[]{:S(2)}) collective-permute-start(bf16[96,2176]{1,0:T(8,128)(2,1)} %shard_map.64.refs_0_.refs_2_), channel_id=1, source_target_pairs={{0,4},{4,0},{8,12},{12,8},{16,20},{20,16},{24,28},{28,24},{1,5},{5... | collective-permute-start | bytes 1253384 | tf_op jit(solution)/shard_map/ppermute | solution.py:293
  19.2 6.7 %copy-start.4 = (bf16[1,768,2048]{2,1,0:T(8,128)(2,1)S(1)}, bf16[1,768,2048]{2,1,0:T(8,128)(2,1)}, u32[]{:S(2)}) copy-start(bf16[1,768,2048]{2,1,0:T(8,128)(2,1)} %refs_8_.1) | copy-start | bytes 9437188
  30.2 33.3 %collective-permute-start.9 = (bf16[1,768,2048]{2,1,0:T(8,128)(2,1)S(1)}, bf16[1,768,2048]{2,1,0:T(8,128)(2,1)S(1)}, u32[]{:S(2)}, u32[]{:S(2)}) collective-permute-start(bf16[1,768,2048]{2,1,0:T(8,128)(2,1)S(1)} %get-tuple-element.33), channel_id=1, source_target_pairs={{0,1},{1,0},{2,3},{3,2},{4,5},{5,4},{6,7},{7,6},{8,9},{9,8},{10,11... | collective-permute-start | bytes 9437192 | tf_op jit(solution)/shard_map/ppermute | solution.py:299
  30.3 12.3 %collective-permute-start.6 = (bf16[224,768]{1,0:T(8,128)(2,1)S(1)}, bf16[224,768]{1,0:T(8,128)(2,1)S(1)}, u32[]{:S(2)}, u32[]{:S(2)}) collective-permute-start(bf16[224,768]{1,0:T(8,128)(2,1)S(1)} %get-tuple-element.29.refs_4_), channel_id=1, source_target_pairs={{0,2},{2,0},{1,3},{3,1},{4,6},{6,4},{5,7},{7,5},{8,10},{10,8},{9,1... | collective-permute-start | bytes 1032200 | tf_op jit(solution)/shard_map/ppermute | solution.py:302
  30.9 22.8 %collective-permute-start.10 = (bf16[96,2176]{1,0:T(8,128)(2,1)}, bf16[96,2176]{1,0:T(8,128)(2,1)S(1)}, u32[]{:S(2)}, u32[]{:S(2)}) collective-permute-start(bf16[96,2176]{1,0:T(8,128)(2,1)} %get-tuple-element.27.refs_0_.refs_2_), channel_id=1, source_target_pairs={{0,4},{4,0},{8,12},{12,8},{16,20},{20,16},{24,28},{28,24},{1,5},{5... | collective-permute-start | bytes 1253384 | tf_op jit(solution)/shard_map/ppermute | solution.py:293
  32.4 13.4 %collective-permute-start.7 = (bf16[96,2176]{1,0:T(8,128)(2,1)}, bf16[96,2176]{1,0:T(8,128)(2,1)S(1)}, u32[]{:S(2)}, u32[]{:S(2)}) collective-permute-start(bf16[96,2176]{1,0:T(8,128)(2,1)} %get-tuple-element.27.refs_0_.refs_2_), channel_id=1, source_target_pairs={{0,8},{4,12},{8,16},{12,20},{16,24},{20,28},{24,0},{28,4},{1,9},{5... | collective-permute-start | bytes 1253384 | tf_op jit(solution)/shard_map/ppermute | solution.py:296
  37.0 13.4 %collective-permute-start.2 = (bf16[80,384]{1,0:T(8,128)(2,1)S(1)}, bf16[80,384]{1,0:T(8,128)(2,1)S(1)}, u32[]{:S(2)}, u32[]{:S(2)}) collective-permute-start(bf16[80,384]{1,0:T(8,128)(2,1)S(1)} %fusion.5.refs_7_.refs_0_), channel_id=1, source_target_pairs={{0,2},{2,0},{1,3},{3,1},{4,6},{6,4},{5,7},{7,5},{8,10},{10,8},{9,1... | collective-permute-start | bytes 184328 | tf_op jit(solution)/shard_map/ppermute | solution.py:302
  42.6 15.6 %collective-permute-start.11 = (bf16[160,768]{1,0:T(8,128)(2,1)S(1)}, bf16[160,768]{1,0:T(8,128)(2,1)S(1)}, u32[]{:S(2)}, u32[]{:S(2)}) collective-permute-start(bf16[160,768]{1,0:T(8,128)(2,1)S(1)} %get-tuple-element.31.refs_4_), channel_id=1, source_target_pairs={{0,2},{2,0},{1,3},{3,1},{4,6},{6,4},{5,7},{7,5},{8,10},{10,8},{9,1... | collective-permute-start | bytes 737288 | tf_op jit(solution)/shard_map/ppermute | solution.py:302
  45.8 17.1 %collective-permute-start.8 = (bf16[224,384]{1,0:T(8,128)(2,1)S(1)}, bf16[224,384]{1,0:T(8,128)(2,1)S(1)}, u32[]{:S(2)}, u32[]{:S(2)}) collective-permute-start(bf16[224,384]{1,0:T(8,128)(2,1)S(1)} %fusion.2.refs_5_.refs_0_), channel_id=1, source_target_pairs={{0,2},{2,0},{1,3},{3,1},{4,6},{6,4},{5,7},{7,5},{8,10},{10,8},{9,1... | collective-permute-start | bytes 516104 | tf_op jit(solution)/shard_map/ppermute | solution.py:302
  50.5 13.0 %collective-permute-start.12 = (bf16[96,2176]{1,0:T(8,128)(2,1)S(1)}, bf16[96,2176]{1,0:T(8,128)(2,1)S(1)}, u32[]{:S(2)}, u32[]{:S(2)}) collective-permute-start(bf16[96,2176]{1,0:T(8,128)(2,1)S(1)} %get-tuple-element.34.refs_1_.refs_3_), channel_id=1, source_target_pairs={{0,8},{4,12},{8,16},{12,20},{16,24},{20,28},{24,0},{28,4},{1,9},{5... | collective-permute-start | bytes 1253384 | tf_op jit(solution)/shard_map/ppermute | solution.py:296
  57.6 12.2 %collective-permute-start.17 = (bf16[288,768]{1,0:T(8,128)(2,1)S(1)}, bf16[288,768]{1,0:T(8,128)(2,1)S(1)}, u32[]{:S(2)}, u32[]{:S(2)}) collective-permute-start(bf16[288,768]{1,0:T(8,128)(2,1)S(1)} %get-tuple-element.36.refs_4_), channel_id=1, source_target_pairs={{0,2},{2,0},{1,3},{3,1},{4,6},{6,4},{5,7},{7,5},{8,10},{10,8},{9,1... | collective-permute-start | bytes 1327112 | tf_op jit(solution)/shard_map/ppermute | solution.py:302
  58.3 33.7 %collective-permute-start.14 = (bf16[160,384]{1,0:T(8,128)(2,1)S(1)}, bf16[160,384]{1,0:T(8,128)(2,1)S(1)}, u32[]{:S(2)}, u32[]{:S(2)}) collective-permute-start(bf16[160,384]{1,0:T(8,128)(2,1)S(1)} %fusion.4.refs_5_.refs_0_), channel_id=1, source_target_pairs={{0,2},{2,0},{1,3},{3,1},{4,6},{6,4},{5,7},{7,5},{8,10},{10,8},{9,1... | collective-permute-start | bytes 368648 | tf_op jit(solution)/shard_map/ppermute | solution.py:302
  62.9 12.6 %collective-permute-start.15 = (bf16[96,2176]{1,0:T(8,128)(2,1)S(1)}, bf16[96,2176]{1,0:T(8,128)(2,1)S(1)}, u32[]{:S(2)}, u32[]{:S(2)}) collective-permute-start(bf16[96,2176]{1,0:T(8,128)(2,1)S(1)} %get-tuple-element.34.refs_1_.refs_3_), channel_id=1, source_target_pairs={{0,4},{4,0},{8,12},{12,8},{16,20},{20,16},{24,28},{28,24},{1,5},{5... | collective-permute-start | bytes 1253384 | tf_op jit(solution)/shard_map/ppermute | solution.py:293
  67.6 16.9 %collective-permute-start.16 = (bf16[96,2176]{1,0:T(8,128)(2,1)S(1)}, bf16[96,2176]{1,0:T(8,128)(2,1)S(1)}, u32[]{:S(2)}, u32[]{:S(2)}) collective-permute-start(bf16[96,2176]{1,0:T(8,128)(2,1)S(1)} %get-tuple-element.38.refs_0_.refs_2_), channel_id=1, source_target_pairs={{0,4},{4,0},{8,12},{12,8},{16,20},{20,16},{24,28},{28,24},{1,5},{5... | collective-permute-start | bytes 1253384 | tf_op jit(solution)/shard_map/ppermute | solution.py:293
  69.2 26.7 %collective-permute-start.13 = (bf16[96,2048]{1,0:T(8,128)(2,1)S(1)}, bf16[96,2048]{1,0:T(8,128)(2,1)S(1)}, u32[]{:S(2)}, u32[]{:S(2)}) collective-permute-start(bf16[96,2048]{1,0:T(8,128)(2,1)S(1)} %slice.61), channel_id=1, source_target_pairs={{0,4},{4,0},{8,12},{12,8},{16,20},{20,16},{24,28},{28,24},{1,5},{5... | collective-permute-start | bytes 1179656 | tf_op jit(solution)/shard_map/ppermute | solution.py:293
  70.0 37.9 %collective-permute-start.18 = (bf16[288,384]{1,0:T(8,128)(2,1)S(1)}, bf16[288,384]{1,0:T(8,128)(2,1)S(1)}, u32[]{:S(2)}, u32[]{:S(2)}) collective-permute-start(bf16[288,384]{1,0:T(8,128)(2,1)S(1)} %fusion.1.refs_5_.refs_0_), channel_id=1, source_target_pairs={{0,2},{2,0},{1,3},{3,1},{4,6},{6,4},{5,7},{7,5},{8,10},{10,8},{9,1... | collective-permute-start | bytes 663560 | tf_op jit(solution)/shard_map/ppermute | solution.py:302
  88.4 13.1 %collective-permute-start.19 = (bf16[288,768]{1,0:T(8,128)(2,1)S(1)}, bf16[288,768]{1,0:T(8,128)(2,1)S(1)}, u32[]{:S(2)}, u32[]{:S(2)}) collective-permute-start(bf16[288,768]{1,0:T(8,128)(2,1)S(1)} %get-tuple-element.40.refs_4_), channel_id=1, source_target_pairs={{0,2},{2,0},{1,3},{3,1},{4,6},{6,4},{5,7},{7,5},{8,10},{10,8},{9,1... | collective-permute-start | bytes 1327112 | tf_op jit(solution)/shard_map/ppermute | solution.py:302
  99.9 6.3 %collective-permute-start.23 = (bf16[160,768]{1,0:T(8,128)(2,1)S(1)}, bf16[160,768]{1,0:T(8,128)(2,1)S(1)}, u32[]{:S(2)}, u32[]{:S(2)}) collective-permute-start(bf16[160,768]{1,0:T(8,128)(2,1)S(1)} %get-tuple-element.42.refs_4_), channel_id=1, source_target_pairs={{0,2},{2,0},{1,3},{3,1},{4,6},{6,4},{5,7},{7,5},{8,10},{10,8},{9,1... | collective-permute-start | bytes 737288 | tf_op jit(solution)/shard_map/ppermute | solution.py:302
  101.7 10.9 %collective-permute-start.22 = (bf16[288,384]{1,0:T(8,128)(2,1)S(1)}, bf16[288,384]{1,0:T(8,128)(2,1)S(1)}, u32[]{:S(2)}, u32[]{:S(2)}) collective-permute-start(bf16[288,384]{1,0:T(8,128)(2,1)S(1)} %fusion.refs_5_.refs_0_), channel_id=1, source_target_pairs={{0,2},{2,0},{1,3},{3,1},{4,6},{6,4},{5,7},{7,5},{8,10},{10,8},{9,1... | collective-permute-start | bytes 663560 | tf_op jit(solution)/shard_map/ppermute | solution.py:302
  106.3 21.7 %collective-permute-start.27 = (bf16[160,384]{1,0:T(8,128)(2,1)S(1)}, bf16[160,384]{1,0:T(8,128)(2,1)S(1)}, u32[]{:S(2)}, u32[]{:S(2)}) collective-permute-start(bf16[160,384]{1,0:T(8,128)(2,1)S(1)} %fusion.3.refs_7_.refs_0_), channel_id=1, source_target_pairs={{0,2},{2,0},{1,3},{3,1},{4,6},{6,4},{5,7},{7,5},{8,10},{10,8},{9,1... | collective-permute-start | bytes 368648 | tf_op jit(solution)/shard_map/ppermute | solution.py:302
  112.1 12.1 %collective-permute-start.20 = (bf16[96,2048]{1,0:T(8,128)(2,1)S(1)}, bf16[96,2048]{1,0:T(8,128)(2,1)S(1)}, u32[]{:S(2)}, u32[]{:S(2)}) collective-permute-start(bf16[96,2048]{1,0:T(8,128)(2,1)S(1)} %slice.82), channel_id=1, source_target_pairs={{0,4},{4,0},{8,12},{12,8},{16,20},{20,16},{24,28},{28,24},{1,5},{5... | collective-permute-start | bytes 1179656 | tf_op jit(solution)/shard_map/ppermute | solution.py:293
  116.8 14.8 %collective-permute-start.26 = (bf16[96,2048]{1,0:T(8,128)(2,1)S(1)}, bf16[96,2048]{1,0:T(8,128)(2,1)S(1)}, u32[]{:S(2)}, u32[]{:S(2)}) collective-permute-start(bf16[96,2048]{1,0:T(8,128)(2,1)S(1)} %get-tuple-element.44), channel_id=1, source_target_pairs={{0,4},{4,0},{8,12},{12,8},{16,20},{20,16},{24,28},{28,24},{1,5},{5... | collective-permute-start | bytes 1179656 | tf_op jit(solution)/shard_map/ppermute | solution.py:293
  118.4 14.5 %collective-permute-start.24 = (bf16[96,2048]{1,0:T(8,128)(2,1)S(1)}, bf16[96,2048]{1,0:T(8,128)(2,1)S(1)}, u32[]{:S(2)}, u32[]{:S(2)}) collective-permute-start(bf16[96,2048]{1,0:T(8,128)(2,1)S(1)} %get-tuple-element.43), channel_id=1, source_target_pairs={{0,4},{4,0},{8,12},{12,8},{16,20},{20,16},{24,28},{28,24},{1,5},{5... | collective-permute-start | bytes 1179656 | tf_op jit(solution)/shard_map/ppermute | solution.py:293
  124.3 9.9 %collective-permute-start.21 = (bf16[96,2048]{1,0:T(8,128)(2,1)S(1)}, bf16[96,2048]{1,0:T(8,128)(2,1)S(1)}, u32[]{:S(2)}, u32[]{:S(2)}) collective-permute-start(bf16[96,2048]{1,0:T(8,128)(2,1)S(1)} %add_convert_fusion.3.refs_6_), channel_id=1, source_target_pairs={{0,24},{4,28},{8,0},{12,4},{16,8},{20,12},{24,16},{28,20},{1,25},{... | collective-permute-start | bytes 1179656 | tf_op jit(solution)/shard_map/ppermute | solution.py:391
  131.7 9.9 %collective-permute-start.28 = (bf16[96,2048]{1,0:T(8,128)(2,1)S(1)}, bf16[96,2048]{1,0:T(8,128)(2,1)S(1)}, u32[]{:S(2)}, u32[]{:S(2)}) collective-permute-start(bf16[96,2048]{1,0:T(8,128)(2,1)S(1)} %add_convert_fusion.1), channel_id=1, source_target_pairs={{0,8},{4,12},{8,16},{12,20},{16,24},{20,28},{24,0},{28,4},{1,9},{5... | collective-permute-start | bytes 1179656 | tf_op jit(solution)/shard_map/ppermute | solution.py:391
  133.1 20.7 %collective-permute-start.25 = (bf16[96,2048]{1,0:T(8,128)(2,1)S(1)}, bf16[96,2048]{1,0:T(8,128)(2,1)S(1)}, u32[]{:S(2)}, u32[]{:S(2)}) collective-permute-start(bf16[96,2048]{1,0:T(8,128)(2,1)S(1)} %add_convert_fusion.2), channel_id=1, source_target_pairs={{0,16},{4,20},{8,24},{12,28},{16,0},{20,4},{24,8},{28,12},{1,17},{... | collective-permute-start | bytes 1179656 | tf_op jit(solution)/shard_map/ppermute | solution.py:391

commit v4 on v0

v4 whole, which is shorter than its diff:
```python
import functools

import jax
import jax.numpy as jnp
from jax import lax
from jax.experimental import pallas as pl
from jax.experimental.pallas import tpu as pltpu
from jax.sharding import PartitionSpec as P

F32 = jnp.float32
BF16 = jnp.bfloat16
LANES = 128
VMEM = 24 * 1024 * 1024
SMEM = pl.BlockSpec(memory_space=pltpu.SMEM)
ANY = pl.BlockSpec(memory_space=pl.ANY)
HBM = pl.BlockSpec(memory_space=pltpu.HBM)


def whole(x):
    return pl.BlockSpec(x.shape, lambda i: (0,) * len(x.shape))


def params():
    return pltpu.CompilerParams(vmem_limit_bytes=VMEM)


def cost():
    return pl.CostEstimate(flops=1, bytes_accessed=1, transcendentals=0)


def block_kernel(experts, tokens_ref, ids_ref, route_ref, out_ref, ids_buffer, route_buffer, sems):
    rows, width = tokens_ref.shape
    copies = [
        pltpu.make_async_copy(ids_ref, ids_buffer, sems.at[0]),
        pltpu.make_async_copy(route_ref, route_buffer, sems.at[1]),
        pltpu.make_async_copy(tokens_ref, out_ref.at[:, :width], sems.at[2]),
    ]
    for copy in copies:
        copy.start()
    copies[0].wait()
    copies[1].wait()
    ids = ids_buffer[...].T
    route = route_buffer[...].T
    column = lax.broadcasted_iota(jnp.int32, (rows, out_ref.shape[1] - width), 1)
    expert = jnp.where(column < experts, column, column - experts)
    value = jnp.zeros(column.shape, F32)
    for k in range(ids.shape[1]):
        value = value + jnp.where(expert == ids[:, k:k + 1], route[:, k:k + 1], 0.0)
    high = value.astype(BF16).astype(F32)
    out_ref[:, width:] = jnp.where(column < experts, high, value - high).astype(BF16)
    copies[2].wait()


def make_block(tokens, expert_ids, route_weights, experts):
    rows, width = tokens.shape
    padded = width + 2 * experts + (-(2 * experts)) % LANES
    args = (tokens, expert_ids.T, route_weights.T)
    return pl.pallas_call(
        functools.partial(block_kernel, experts),
        grid=(1,),
        out_shape=jax.ShapeDtypeStruct((rows, padded), BF16),
        in_specs=[HBM] * 3,
        out_specs=pl.BlockSpec((rows, padded), lambda i: (0, 0)),
        scratch_shapes=[
            pltpu.VMEM(args[1].shape, jnp.int32),
            pltpu.VMEM(args[2].shape, F32),
            pltpu.SemaphoreType.DMA((3,)),
        ],
        compiler_params=params(),
        cost_estimate=cost(),
    )(*args)


def layout(groups, capacity):
    offsets = [0]
    for _, members in groups:
        offsets.append(offsets[-1] + -(-len(members) * capacity // 16) * 16)
    return offsets


def slot_rows(tails, expert, experts, rows, capacity):
    total = tails.shape[0]
    column = lax.broadcasted_iota(jnp.int32, (8, tails.shape[1]), 1)
    mark = jnp.where((column == expert) | (column == experts + expert), 1.0, 0.0).astype(BF16)
    weight = lax.dot_general(mark, tails, (((1,), (1,)), ((), ())), preferred_element_type=F32)
    live = weight > 0.0
    number = lax.broadcasted_iota(jnp.int32, (8, total), 1) // rows
    above = lax.broadcasted_iota(jnp.int32, (total, total), 0)
    own = lax.broadcasted_iota(jnp.int32, (total, total), 1)
    ahead = jnp.where((above < own) & (above >= (number * rows)[0:1]), 1.0, 0.0).astype(BF16)
    before = jnp.dot(jnp.where(live, 1.0, 0.0).astype(BF16), ahead, preferred_element_type=F32)
    return jnp.where(live, before.astype(jnp.int32) + number * capacity, -1)[0:1]


def slot_columns(tails, expert, experts, rows, capacity):
    total = tails.shape[0]
    column = lax.broadcasted_iota(jnp.int32, tails.shape, 1)
    mine = (column == expert) | (column == experts + expert)
    weight = jnp.sum(jnp.where(mine, tails.astype(F32), 0.0), axis=1, keepdims=True)
    live = weight > 0.0
    number = lax.broadcasted_iota(jnp.int32, (total, 1), 0) // rows
    own = lax.broadcasted_iota(jnp.int32, (total, total), 0)
    above = lax.broadcasted_iota(jnp.int32, (total, total), 1)
    ahead = jnp.where((above < own) & (above >= number * rows), 1.0, 0.0).astype(BF16)
    flags = jnp.broadcast_to(jnp.where(live, 1.0, 0.0), (total, LANES)).astype(BF16)
    before = jnp.dot(ahead, flags, preferred_element_type=F32)[:, 0:1]
    return jnp.where(live, before.astype(jnp.int32) + number * capacity, -1), weight


def ordered_call(kernel, outs, specs, args, passing, after, copying=()):
    operands = (*args, *after, *copying, *passing)
    base = len(operands) - len(passing)
    kept, handed, copied = len(outs), len(passing), len(copying)
    token = jax.ShapeDtypeStruct((8, LANES), F32)

    def with_token(*refs):
        results = refs[len(operands):]
        sources = refs[base - copied:base]
        targets = results[kept + handed:kept + handed + copied]
        copies = [pltpu.make_async_copy(a, b, results[-1].at[i]) for i, (a, b) in enumerate(zip(sources, targets))]
        for copy in copies:
            copy.start()
        results[kept + handed + copied][...] = jnp.zeros(token.shape, token.dtype)
        kernel(*refs[:len(args)], *results[:kept])
        for copy in copies:
            copy.wait()

    results = pl.pallas_call(
        with_token,
        grid=(1,),
        out_shape=(*outs, *[jax.ShapeDtypeStruct(p.shape, p.dtype) for p in (*passing, *copying)], token),
        in_specs=specs + [ANY] * (len(after) + copied + handed),
        out_specs=(*[whole(o) for o in outs], *[ANY] * (handed + copied), whole(token)),
        input_output_aliases={base + i: kept + i for i in range(handed)},
        scratch_shapes=[pltpu.SemaphoreType.DMA((copied,))] if copied else [],
        compiler_params=params(),
        cost_estimate=cost(),
    )(*operands)
    return results[:kept], results[kept:kept + handed], results[kept + handed:-1], results[-1]


def select_kernel(width, experts, capacity, groups, count, scalars, *refs):
    blocks, outs = refs[:count], refs[count:]
    rows = blocks[0].shape[0]
    step = 512
    for (expert, members), out_ref in zip(groups, outs):
        tails = jnp.concatenate([blocks[m][:, width:] for m in members], axis=0)
        slot = slot_rows(tails, scalars[expert], experts, rows, capacity)
        place = lax.broadcasted_iota(jnp.int32, (out_ref.shape[0], len(members) * rows), 0)
        pick = jnp.where(place == slot, 1.0, 0.0).astype(BF16)
        for column in range(0, width, step):
            x = jnp.concatenate([blocks[m][:, column:column + step] for m in members], axis=0)
            out_ref[:, column:column + step] = jnp.dot(pick, x, preferred_element_type=F32).astype(BF16)


def select_rows(scalars, groups, blocks, copying, after, width, experts, capacity):
    kernel = functools.partial(select_kernel, width, experts, capacity, groups, len(blocks))
    offsets = layout(groups, capacity)
    outs = [jax.ShapeDtypeStruct((b - a, width), BF16) for a, b in zip(offsets, offsets[1:])]
    specs = [SMEM] + [whole(b) for b in blocks]
    return ordered_call(kernel, outs, specs, (scalars, *blocks), [], after, copying)


def round_kernel(count, scalars, *refs):
    out_ref = refs[-1]
    units = out_ref.shape[1] // 2
    columns = pl.ds(pl.multiple_of(scalars[2], LANES), units)
    start = 0
    for g in range(count):
        rows = slice(start, start + refs[2 * g].shape[0])
        start = rows.stop
        for half in range(2):
            out_ref[rows, half * units:(half + 1) * units] = refs[2 * g + half][:, columns].astype(BF16)


def away_part(scalars, products, units, after):
    total = sum(p.shape[0] for p in products[::2])
    out = jax.ShapeDtypeStruct((total, 2 * units), BF16)
    kernel = functools.partial(round_kernel, len(products) // 2)
    return ordered_call(kernel, [out], [SMEM] + [whole(p) for p in products], (scalars, *products), [], after)


def act_kernel(count, scalars, in_ref, *refs):
    out_ref = refs[-1]
    units = out_ref.shape[1]
    columns = pl.ds(pl.multiple_of(scalars[3], LANES), units)
    start = 0
    for g in range(count):
        rows = slice(start, start + refs[2 * g].shape[0])
        start = rows.stop
        gate = refs[2 * g][:, columns] + in_ref[rows, :units].astype(F32)
        up = refs[2 * g + 1][:, columns] + in_ref[rows, units:].astype(F32)
        out_ref[rows, :] = (gate / (1.0 + jnp.exp(-gate)) * up).astype(BF16)


def activated(scalars, products, part, passing, after):
    rows, columns = part.shape
    out = jax.ShapeDtypeStruct((rows, columns // 2), BF16)
    specs = [SMEM, whole(part)] + [whole(p) for p in products]
    kernel = functools.partial(act_kernel, len(products) // 2)
    return ordered_call(kernel, [out], specs, (scalars, part, *products), passing, after)


def join_kernel(scalars, own_ref, other_ref, *outs):
    units = own_ref.shape[1]
    start = 0
    for out_ref in outs:
        rows = slice(start, start + out_ref.shape[0])
        start = rows.stop
        for place, ref in ((scalars[3], own_ref), (scalars[2], other_ref)):
            out_ref[:, pl.ds(pl.multiple_of(place, LANES), units)] = ref[rows, :]


def joined(scalars, own, other, sizes, passing, after):
    outs = [jax.ShapeDtypeStruct((n, 2 * own.shape[1]), BF16) for n in sizes]
    specs = [SMEM, whole(own), whole(other)]
    return ordered_call(join_kernel, outs, specs, (scalars, own, other), passing, after)


def expand_kernel(experts, capacity, groups, count, scalars, *refs):
    results, tail_refs = refs[:len(groups)], refs[len(groups):len(groups) + count]
    out_ref = refs[-1]
    rows = tail_refs[0].shape[0]
    spreads, weights = [], []
    for (expert, members), ref in zip(groups, results):
        tails = jnp.concatenate([tail_refs[m][...] for m in members], axis=0)
        slot, weight = slot_columns(tails, scalars[expert], experts, rows, capacity)
        place = lax.broadcasted_iota(jnp.int32, (len(members) * rows, ref.shape[0]), 1)
        spreads.append(jnp.where(place == slot, 1.0, 0.0).astype(BF16))
        weights.append(weight)
    step = 512
    for column in range(0, out_ref.shape[1], step):
        sums = [None] * count
        for (_, members), ref, spread, weight in zip(groups, results, spreads, weights):
            value = ref[:, column:column + step].astype(BF16)
            value = jnp.dot(spread, value, preferred_element_type=F32) * weight
            for k, m in enumerate(members):
                piece = value[k * rows:(k + 1) * rows]
                sums[m] = piece if sums[m] is None else sums[m] + piece
        for m, value in enumerate(sums):
            out_ref[m * rows:(m + 1) * rows, column:column + step] = value.astype(BF16)


def expand_rows(scalars, groups, results, blocks, passing, after, experts, capacity):
    rows, padded = blocks[0].shape
    width = results[0].shape[1]
    tail = pl.BlockSpec((rows, padded - width), lambda i: (0, width // (padded - width)))
    kernel = functools.partial(expand_kernel, experts, capacity, groups, len(blocks))
    out = jax.ShapeDtypeStruct((len(blocks) * rows, width), BF16)
    specs = [SMEM] + [whole(r) for r in results] + [tail] * len(blocks)
    return ordered_call(kernel, [out], specs, (scalars, *results, *blocks), passing, after)


def add_kernel(*refs):
    out_ref = refs[-1]
    total = refs[0][...].astype(F32)
    for ref in refs[1:-1]:
        total = total + ref[...].astype(F32)
    out_ref[...] = total.astype(out_ref.dtype)


def added(terms, kind, after):
    out = jax.ShapeDtypeStruct(terms[0].shape, kind)
    return ordered_call(add_kernel, [out], [whole(t) for t in terms], tuple(terms), [], after)


def on_device(tokens, expert_ids, route_weights, w_gate, w_up, w_down):
    rows, width = tokens.shape
    top = expert_ids.shape[1]
    ring = lax.axis_size("expert")
    experts = ring * lax.axis_size("dp")
    capacity = min(rows, max(2, 3 * rows * top // (2 * experts)))
    parts = lax.axis_size("tensor")
    units = w_gate.shape[2] // parts
    core = lax.axis_index("dp")
    rank = lax.axis_index("tensor")
    hops = ring // 2
    aligned = parts == 2 and units % LANES == 0

    def over_y(x):
        return lax.ppermute(x, "expert", [(i, i ^ 1) for i in range(ring)])

    def over_z(x):
        return lax.ppermute(x, "expert", [(i, (i + 2) % ring) for i in range(ring)])

    def home_over_z(x, hop):
        return lax.ppermute(x, "expert", [(i, (i - 2 * hop) % ring) for i in range(ring)])

    def home_over_both(x, hop):
        return lax.ppermute(x, "expert", [(i, ((i - 2 * hop) % ring) ^ 1) for i in range(ring)])

    def over_core(x):
        return lax.ppermute(x, "dp", [(0, 1), (1, 0)])

    def over_x(x, step):
        return lax.ppermute(x, "tensor", [(i, (i + step) % parts) for i in range(parts)])

    first = lax.axis_index("expert") * 2
    scalars = jnp.stack([first + core, first + 1 - core, (rank + 1) % parts * units, rank * units]).astype(jnp.int32)
    gates = [w_gate[0], over_core(w_gate)[0]]
    ups = [w_up[0], over_core(w_up)[0]]
    downs = [w_down[0]]

    blocks, arrived = {(0, "s"): make_block(tokens, expert_ids, route_weights, experts)}, {}

    def send_on(hop):
        block = blocks[hop, "s"]
        if hop + 1 < hops:
            arrived[hop + 1] = over_z(block)
        blocks[hop, "b"] = over_y(block)

    def passing(hop):
        return [arrived[hop]] if hop in arrived else []

    def take_on(hop, passed):
        if passed:
            blocks[hop, "s"] = passed[0]
            send_on(hop)

    both = ((0, (0, 1)), (1, (0, 1)))
    plan = [([(0, "s")], ((0, (0,)),)), ([(0, "s"), (0, "b"), (1, "s")], ((1, (0, 1, 2)), (0, (1, 2))))]
    plan += [([(hop - 1, "b"), (hop, "s")], both) for hop in range(2, hops - 1)]
    plan += [([(hops - 2, "b"), (hops - 1, "b")], both), ([(hops - 1, "s")], ((0, (0,)), (1, (0,))))]
    count = len(plan)
    order = []
    rows_in, products, parts_in, hidden, results, own_part = {}, {}, {}, {}, {}, {}
    arriving, gathered = [], []

    def select(i):
        keys, groups = plan[i]
        copying = [w_down] if i == 1 else []
        rows_in[i], _, copies, token = select_rows(
            scalars, groups, [blocks[k] for k in keys], copying, order, width, experts, capacity
        )
        downs.extend(over_core(c)[0] for c in copies)
        order[:] = [token]

    def multiply(i):
        products[i] = []
        for (expert, _), x in zip(plan[i][1], rows_in[i]):
            for w in (gates[expert], ups[expert]):
                products[i].append(jnp.dot(x, w, preferred_element_type=F32))
        if aligned:
            (part,), _, _, token = away_part(scalars, products[i], units, order)
            parts_in[i] = [over_x(part, 1)]
            order[:] = [token]
            return
        gate, up = jnp.concatenate(products[i][::2], axis=0), jnp.concatenate(products[i][1::2], axis=0)
        parts_in[i] = []
        for step in range(parts):
            start = (rank + step) % parts * units
            part = jnp.concatenate([lax.dynamic_slice_in_dim(w, start, units, 1) for w in (gate, up)], axis=1)
            if step > 0:
                part = over_x(part.astype(BF16), step)
            parts_in[i].append(part)

    def activate(i, hop):
        if aligned:
            (value,), passed, _, token = activated(scalars, products[i], parts_in[i][0], passing(hop), order)
            order[:] = [token]
            take_on(hop, passed)
        else:
            total = sum(p.astype(F32) for p in parts_in[i])
            value = (jax.nn.silu(total[:, :units]) * total[:, units:]).astype(BF16)
            take_on(hop, passing(hop))
        hidden[i] = [value] + [over_x(value, s) for s in range(1, parts)]

    def down_product(i, hop):
        offsets = layout(plan[i][1], capacity)
        if aligned:
            sizes = [b - a for a, b in zip(offsets, offsets[1:])]
            values, passed, _, token = joined(scalars, *hidden[i], sizes, passing(hop), order)
            order[:] = [token]
            take_on(hop, passed)
        else:
            behind = (rank - jnp.arange(parts)) % parts
            value = jnp.moveaxis(jnp.stack(hidden[i])[behind], 0, 1).reshape(offsets[-1], -1)
            values = [value[a:b] for a, b in zip(offsets, offsets[1:])]
            take_on(hop, passing(hop))
        results[i] = []
        for (expert, _), value in zip(plan[i][1], values):
            results[i].append(jnp.dot(value, downs[expert], preferred_element_type=F32))

    def expand(i, hop):
        keys, groups = plan[i]
        (term,), passed, _, token = expand_rows(
            scalars, groups, results[i], [blocks[k] for k in keys], passing(hop), order, experts, capacity
        )
        order[:] = [token]
        take_on(hop, passed)
        for k, (at, kind) in enumerate(keys):
            piece = term[k * rows:(k + 1) * rows]
            direct = at >= hops - 2
            if kind == "s" and at == 0:
                gathered.append(piece)
            elif kind == "s" and direct:
                arriving.append((i, home_over_z(piece, at)))
            elif kind == "s":
                own_part[at] = piece
            elif direct:
                arriving.append((i, home_over_both(piece, at)))
            else:
                own_part[at, "b"] = over_y(piece)

    def add_hop(hop):
        if hop == 0:
            gathered.append(own_part[hop, "b"])
        elif hop < hops - 2:
            (total,), _, _, token = added([own_part[hop], own_part[hop, "b"]], BF16, order)
            order[:] = [token]
            arriving.append((hop + 2, home_over_z(total, hop)))

    def gather(unit):
        here = [x for i, x in arriving if i <= unit]
        arriving[:] = [(i, x) for i, x in arriving if i > unit]
        if len(gathered) + len(here) > 1:
            (total,), _, _, token = added(gathered + here, F32, order)
            gathered[:] = [total]
            order[:] = [token]

    send_on(0)
    select(0)
    multiply(0)
    activate(0, 1)
    for i in range(1, count + 1):
        if i > 2:
            activate(i - 1, None)
        if i < count:
            select(i)
            multiply(i)
        if i == 2:
            activate(1, None)
        if i >= 3:
            add_hop(i - 3)
            gather(i - 3)
        down_product(i - 1, i + 1 if i > 1 else None)
        expand(i - 1, 2 if i == 1 else None)
    for hop in range(count - 2, hops):
        add_hop(hop)
    return sum(x.astype(F32) for x in gathered + [x for _, x in arriving]).astype(BF16)


def solution(mesh):
    placed = (
        P(("group", "expert", "dp"), "tensor"),
        P(("group", "expert", "dp"), None),
        P(("group", "expert", "dp"), None),
        P(("expert", "dp"), "tensor", None),
        P(("expert", "dp"), "tensor", None),
        P(("expert", "dp"), None, "tensor"),
    )
    return jax.shard_map(
        on_device,
        mesh=mesh,
        in_specs=placed,
        out_specs=P(("group", "expert", "dp"), "tensor"),
        check_vma=False,
    )
```

time: 398 us -> 145 us (0.36)
  the two profiles are of different devices: /device:TPU:13 before, /device:TPU:0 now
where the time goes in v4:
time: 145 us
  waiting for transfers between devices  47.1 us (32%)
  matrix products  35.3 us (24%)
  starting transfers between devices  33.9 us (23%)
  Pallas kernels  24.4 us (17%)
  local copies, waits for them, and re-layouts  2.6 us (2%)
    dot_general x18, matrix products, multiply(): products[i].append(jnp.dot(x, w, preferred_element_type=F32))  29 us
    ppermute x2, waiting for transfers between devices, home_over_both(): lax.ppermute(x, 'expert', [(i, (i - 2 * hop) % ring ^ 1) for i in range(r...  26.7 us
    pallas_call x28, Pallas kernels, ordered_call(): pl.pallas_call(with_token, grid=(1,), out_shape=(*outs, *[jax.ShapeDtypeS...  23.9 us
    ppermute x10, waiting for transfers between devices, over_x(): lax.ppermute(x, 'tensor', [(i, (i + step) % parts) for i in range(parts)])  15.8 us
    ppermute x10, starting transfers between devices, over_x(): lax.ppermute(x, 'tensor', [(i, (i + step) % parts) for i in range(parts)])  10.2 us
    ppermute x6, starting transfers between devices, over_y(): return lax.ppermute(x, 'expert', [(i, i ^ 1) for i in range(ring)])  7.24 us
    dot_general x9, matrix products, down_product(): results[i].append(jnp.dot(value, downs[expert], preferred_element_type=F32))  6.29 us
    ppermute x3, starting transfers between devices, over_z(): return lax.ppermute(x, 'expert', [(i, (i + 2) % ring) for i in range(ring)])  6.02 us
  transfers between devices with their start and end apart: 27, of which 8 were waited for; matrix products, arithmetic and copies ran while one was open for 24% of the time, Pallas kernels for 16%

profile of v4, /device:TPU:0, one launch (start us, length us, event | category | flops | bytes accessed | tf_op | source)
XLA Modules:
  0.0 144.8 jit_solution(14501236539966708078)
XLA Ops:
  0.5 1.0 copy-done.1
  1.5 0.7 copy-done.2
  2.2 0.7 copy-done.3
  3.4 3.1 %collective-permute-start.1 = (bf16[96,2176]{1,0:T(8,128)(2,1)S(1)}, bf16[96,2176]{1,0:T(8,128)(2,1)S(1)}, u32[]{:S(2)}, u32[]{:S(2)}) collective-permute-start(bf16[96,2176]{1,0:T(8,128)(2,1)S(1)} %shard_map.64.refs_1_.refs_2_.refs_3_), channel_id=1, source_target_pairs={{0,8},{4,12},{8,16},{12,20},{16,24},{20,28},{24,0},{28,4},{1,9},{5... | collective-permute-start | bytes 1253384 | tf_op jit(solution)/shard_map/ppermute | solution.py:284
  6.5 1.5 %collective-permute-start.3 = (bf16[96,2176]{1,0:T(8,128)(2,1)S(1)}, bf16[96,2176]{1,0:T(8,128)(2,1)S(1)}, u32[]{:S(2)}, u32[]{:S(2)}) collective-permute-start(bf16[96,2176]{1,0:T(8,128)(2,1)S(1)} %shard_map.64.refs_1_.refs_2_.refs_3_), channel_id=1, source_target_pairs={{0,4},{4,0},{8,12},{12,8},{16,20},{20,16},{24,28},{28,24},{1,5},{5... | collective-permute-start | bytes 1253384 | tf_op jit(solution)/shard_map/ppermute | solution.py:281
  8.1 1.0 shard_map.65
  9.1 2.5 %fusion.42.refs_2_.refs_3_ = f32[80,768]{1,0:T(8,128)S(1)} fusion(bf16[80,2048]{1,0:T(8,128)(2,1)S(1)} %get-tuple-element.72, bf16[1,2048,768]{2,1,0:T(8,128)(2,1)} %param.10), kind=kOutput, calls=%fused_computation.42 | convolution fusion | flops 251658240 | bytes 3719168 | tf_op jit(solution)/shard_map/dot_general | solution.py:342
  11.6 0.7 fusion.52.refs_1_.refs_2_
  12.9 1.6 %collective-permute-start = (bf16[80,768]{1,0:T(8,128)(2,1)S(1)}, bf16[80,768]{1,0:T(8,128)(2,1)S(1)}, u32[]{:S(2)}, u32[]{:S(2)}) collective-permute-start(bf16[80,768]{1,0:T(8,128)(2,1)S(1)} %get-tuple-element.74), channel_id=1, source_target_pairs={{0,2},{2,0},{1,3},{3,1},{4,6},{6,4},{5,7},{7,5},{8,10},{10,8},{9,1... | collective-permute-start | bytes 368648 | tf_op jit(solution)/shard_map/ppermute | solution.py:296
  14.4 3.4 %collective-permute-done.refs_1_ = bf16[80,768]{1,0:T(8,128)(2,1)S(1)} collective-permute-done((bf16[80,768]{1,0:T(8,128)(2,1)S(1)}, bf16[80,768]{1,0:T(8,128)(2,1)S(1)}, u32[]{:S(2)}, u32[]{:S(2)}) %collective-permute-start) | collective-permute-done | bytes 122912 | tf_op jit(solution)/shard_map/ppermute | solution.py:296
  18.9 1.2 collective-permute-start.6
  20.6 2.1 %shard_map.68 = (bf16[224,2048]{1,0:T(8,128)(2,1)S(1)}, bf16[144,2048]{1,0:T(8,128)(2,1)S(1)}, bf16[1,768,2048]{2,1,0:T(8,128)(2,1)S(1)}, f32[8,128]{1,0:T(8,128)S(1)}) custom-call(s32[4]{0:T(128)S(1)} %pad_add_fusion.refs_0_, bf16[96,2176]{1,0:T(8,128)(2,1)S(1)} %shard_map.64.refs_1_.refs_2_.refs_3_, ...), custom_call_target="tpu_custom_call" | custom-call | flops 1 | bytes 1 | tf_op jit(solution)/shard_map/pallas_call | solution.py:128
  22.7 0.6 fusion.40.refs_4_.refs_5_
  23.4 0.6 fusion.50.refs_3_.refs_4_
  24.1 1.6 %collective-permute-start.2 = (bf16[80,384]{1,0:T(8,128)(2,1)S(1)}, bf16[80,384]{1,0:T(8,128)(2,1)S(1)}, u32[]{:S(2)}, u32[]{:S(2)}) collective-permute-start(bf16[80,384]{1,0:T(8,128)(2,1)S(1)} %get-tuple-element.76.refs_1_), channel_id=1, source_target_pairs={{0,2},{2,0},{1,3},{3,1},{4,6},{6,4},{5,7},{7,5},{8,10},{10,8},{9,1... | collective-permute-start | bytes 184328 | tf_op jit(solution)/shard_map/ppermute | solution.py:296
  25.6 2.8 %fusion.24.refs_2_.refs_3_ = f32[224,768]{1,0:T(8,128)S(1)} fusion(bf16[224,2048]{1,0:T(8,128)(2,1)S(1)} %get-tuple-element.79, bf16[1,2048,768]{2,1,0:T(8,128)(2,1)} %collective-permute-done.5), kind=kOutput, calls=%fused_computation.24 | convolution fusion | flops 704643072 | bytes 4751360 | tf_op jit(solution)/shard_map/dot_general | solution.py:342
  28.4 2.8 %fusion.32.refs_1_.refs_2_ = f32[224,768]{1,0:T(8,128)S(1)} fusion(bf16[224,2048]{1,0:T(8,128)(2,1)S(1)} %get-tuple-element.79, bf16[1,2048,768]{2,1,0:T(8,128)(2,1)} %collective-permute-done.4), kind=kOutput, calls=%fused_computation.32 | convolution fusion | flops 704643072 | bytes 4751360 | tf_op jit(solution)/shard_map/dot_general | solution.py:342
  33.0 0.7 fusion.16.refs_1_
  33.7 1.1 shard_map.71
  34.7 1.8 %collective-permute-start.10 = (bf16[96,2176]{1,0:T(8,128)(2,1)S(1)}, bf16[96,2176]{1,0:T(8,128)(2,1)S(1)}, u32[]{:S(2)}, u32[]{:S(2)}) collective-permute-start(bf16[96,2176]{1,0:T(8,128)(2,1)S(1)} %get-tuple-element.87.refs_2_.refs_4_), channel_id=1, source_target_pairs={{0,8},{4,12},{8,16},{12,20},{16,24},{20,28},{24,0},{28,4},{1,9},{5... | collective-permute-start | bytes 1253384 | tf_op jit(solution)/shard_map/ppermute | solution.py:284
  36.5 1.5 %shard_map.72 = (bf16[144,2048]{1,0:T(8,128)(2,1)S(1)}, bf16[144,2048]{1,0:T(8,128)(2,1)S(1)}, f32[8,128]{1,0:T(8,128)S(1)}) custom-call(s32[4]{0:T(128)S(1)} %pad_add_fusion.refs_0_, bf16[96,2176]{1,0:T(8,128)(2,1)S(1)} %collective-permute-done.8.refs_1_.refs_3_, bf16[96,2176]{1,0:T(8,128)(2,1)S(1)} %get-tuple-element.87.refs_2_.refs_4_, ...), custom_call_target="tpu_custom_call" | custom-call | flops 1 | bytes 1 | tf_op jit(solution)/shard_map/pallas_call | solution.py:128
  39.3 2.5 %fusion.22.refs_4_.refs_5_ = f32[144,768]{1,0:T(8,128)S(1)} fusion(bf16[144,2048]{1,0:T(8,128)(2,1)S(1)} %get-tuple-element.90, bf16[1,2048,768]{2,1,0:T(8,128)(2,1)} %collective-permute-done.5), kind=kOutput, calls=%fused_computation.22 | convolution fusion | flops 452984832 | bytes 4177920 | tf_op jit(solution)/shard_map/dot_general | solution.py:342
  41.9 2.5 %fusion.30.refs_3_.refs_4_ = f32[144,768]{1,0:T(8,128)S(1)} fusion(bf16[144,2048]{1,0:T(8,128)(2,1)S(1)} %get-tuple-element.90, bf16[1,2048,768]{2,1,0:T(8,128)(2,1)} %collective-permute-done.4), kind=kOutput, calls=%fused_computation.30 | convolution fusion | flops 452984832 | bytes 4177920 | tf_op jit(solution)/shard_map/dot_general | solution.py:342
  45.0 1.8 %collective-permute-done.7.refs_1_ = bf16[368,768]{1,0:T(8,128)(2,1)S(1)} collective-permute-done((bf16[368,768]{1,0:T(8,128)(2,1)S(1)}, bf16[368,768]{1,0:T(8,128)(2,1)S(1)}, u32[]{:S(2)}, u32[]{:S(2)}) %collective-permute-start.7) | collective-permute-done | bytes 565280 | tf_op jit(solution)/shard_map/ppermute | solution.py:296
  46.8 0.8 shard_map.74
  48.2 1.5 %collective-permute-start.13 = (bf16[96,2176]{1,0:T(8,128)(2,1)S(1)}, bf16[96,2176]{1,0:T(8,128)(2,1)S(1)}, u32[]{:S(2)}, u32[]{:S(2)}) collective-permute-start(bf16[96,2176]{1,0:T(8,128)(2,1)S(1)} %get-tuple-element.87.refs_2_.refs_4_), channel_id=1, source_target_pairs={{0,4},{4,0},{8,12},{12,8},{16,20},{20,16},{24,28},{28,24},{1,5},{5... | collective-permute-start | bytes 1253384 | tf_op jit(solution)/shard_map/ppermute | solution.py:281
  49.7 1.5 %collective-permute-start.15 = (bf16[288,768]{1,0:T(8,128)(2,1)S(1)}, bf16[288,768]{1,0:T(8,128)(2,1)S(1)}, u32[]{:S(2)}, u32[]{:S(2)}) collective-permute-start(bf16[288,768]{1,0:T(8,128)(2,1)S(1)} %get-tuple-element.101), channel_id=1, source_target_pairs={{0,2},{2,0},{1,3},{3,1},{4,6},{6,4},{5,7},{7,5},{8,10},{10,8},{9,1... | collective-permute-start | bytes 1327112 | tf_op jit(solution)/shard_map/ppermute | solution.py:296
  51.1 6.2 %collective-permute-done.9.refs_2_ = bf16[368,384]{1,0:T(8,128)(2,1)S(1)} collective-permute-done((bf16[368,384]{1,0:T(8,128)(2,1)S(1)}, bf16[368,384]{1,0:T(8,128)(2,1)S(1)}, u32[]{:S(2)}, u32[]{:S(2)}) %collective-permute-start.9) | collective-permute-done | bytes 282656 | tf_op jit(solution)/shard_map/ppermute | solution.py:296
  57.9 1.6 %collective-permute-start.14 = (bf16[96,2176]{1,0:T(8,128)(2,1)S(1)}, bf16[96,2176]{1,0:T(8,128)(2,1)S(1)}, u32[]{:S(2)}, u32[]{:S(2)}) collective-permute-start(bf16[96,2176]{1,0:T(8,128)(2,1)S(1)} %get-tuple-element.100.refs_1_.refs_3_), channel_id=1, source_target_pairs={{0,4},{4,0},{8,12},{12,8},{16,20},{20,16},{24,28},{28,24},{1,5},{5... | collective-permute-start | bytes 1253384 | tf_op jit(solution)/shard_map/ppermute | solution.py:281
  59.5 0.7 fusion.14.refs_2_
  60.1 0.9 fusion.6.refs_1_
  61.1 1.6 %shard_map.76 = (bf16[288,2048]{1,0:T(8,128)(2,1)S(1)}, f32[8,128]{1,0:T(8,128)S(1)}) custom-call(s32[4]{0:T(128)S(1)} %pad_add_fusion.refs_0_, f32[224,2048]{1,0:T(8,128)S(1)} %fusion.6.refs_1_, f32[144,2048]{1,0:T(8,128)S(1)} %fusion.14.refs_2_, bf16[96,2176]{1,0:T(8,128)(2,1)S(1)} %shard_map.64.refs_1_.refs_2_.refs_3_, ...), custom_call_target="tpu_custom_call" | custom-call | flops 1 | bytes 1 | tf_op jit(solution)/shard_map/pallas_call | solution.py:128
  63.4 1.7 %collective-permute-done.15.refs_1_ = bf16[288,768]{1,0:T(8,128)(2,1)S(1)} collective-permute-done((bf16[288,768]{1,0:T(8,128)(2,1)S(1)}, bf16[288,768]{1,0:T(8,128)(2,1)S(1)}, u32[]{:S(2)}, u32[]{:S(2)}) %collective-permute-start.15) | collective-permute-done | bytes 442400 | tf_op jit(solution)/shard_map/ppermute | solution.py:296
  65.1 0.7 shard_map.77
  66.5 4.1 %collective-permute-done.14.refs_2_.refs_4_ = bf16[96,2176]{1,0:T(8,128)(2,1)S(1)} collective-permute-done((bf16[96,2176]{1,0:T(8,128)(2,1)S(1)}, bf16[96,2176]{1,0:T(8,128)(2,1)S(1)}, u32[]{:S(2)}, u32[]{:S(2)}) %collective-permute-start.14) | collective-permute-done | bytes 417824 | tf_op jit(solution)/shard_map/ppermute | solution.py:281
  70.5 1.5 %shard_map.78 = (bf16[144,2048]{1,0:T(8,128)(2,1)S(1)}, bf16[144,2048]{1,0:T(8,128)(2,1)S(1)}, f32[8,128]{1,0:T(8,128)S(1)}) custom-call(s32[4]{0:T(128)S(1)} %pad_add_fusion.refs_0_, bf16[96,2176]{1,0:T(8,128)(2,1)S(1)} %collective-permute-done.13.refs_1_.refs_3_, bf16[96,2176]{1,0:T(8,128)(2,1)S(1)} %collective-permute-done.14.refs_2_.refs_4_, ...), custom_call_target="tpu_custom_call" | custom-call | flops 1 | bytes 1 | tf_op jit(solution)/shard_map/pallas_call | solution.py:128
  73.4 2.5 %fusion.20.refs_4_.refs_5_ = f32[144,768]{1,0:T(8,128)S(1)} fusion(bf16[144,2048]{1,0:T(8,128)(2,1)S(1)} %get-tuple-element.105, bf16[1,2048,768]{2,1,0:T(8,128)(2,1)} %collective-permute-done.5), kind=kOutput, calls=%fused_computation.20 | convolution fusion | flops 452984832 | bytes 4177920 | tf_op jit(solution)/shard_map/dot_general | solution.py:342
  75.9 2.5 %fusion.28.refs_3_.refs_4_ = f32[144,768]{1,0:T(8,128)S(1)} fusion(bf16[144,2048]{1,0:T(8,128)(2,1)S(1)} %get-tuple-element.105, bf16[1,2048,768]{2,1,0:T(8,128)(2,1)} %collective-permute-done.4), kind=kOutput, calls=%fused_computation.28 | convolution fusion | flops 452984832 | bytes 4177920 | tf_op jit(solution)/shard_map/dot_general | solution.py:342
  79.8 0.7 fusion.12.refs_1_
  80.4 0.7 collective-permute-start.18
  81.1 0.7 fusion.4.refs_2_
  81.8 1.4 shard_map.82
  83.3 1.6 %collective-permute-start.21 = (bf16[96,2048]{1,0:T(8,128)(2,1)S(1)}, bf16[96,2048]{1,0:T(8,128)(2,1)S(1)}, u32[]{:S(2)}, u32[]{:S(2)}) collective-permute-start(bf16[96,2048]{1,0:T(8,128)(2,1)S(1)} %get-tuple-element.145), channel_id=1, source_target_pairs={{0,4},{4,0},{8,12},{12,8},{16,20},{20,16},{24,28},{28,24},{1,5},{5... | collective-permute-start | bytes 1179656 | tf_op jit(solution)/shard_map/ppermute | solution.py:281
  84.9 1.2 collective-permute-start.17
  86.1 2.7 %collective-permute-done.18.refs_1_ = bf16[288,768]{1,0:T(8,128)(2,1)S(1)} collective-permute-done((bf16[288,768]{1,0:T(8,128)(2,1)S(1)}, bf16[288,768]{1,0:T(8,128)(2,1)S(1)}, u32[]{:S(2)}, u32[]{:S(2)}) %collective-permute-start.18) | collective-permute-done | bytes 442400 | tf_op jit(solution)/shard_map/ppermute | solution.py:296
  88.8 0.7 shard_map.83
  89.5 1.4 shard_map.84
  91.5 0.6 fusion.44.refs_1_.refs_2_
  92.2 1.0 collective-permute-start.20
  93.1 2.5 %fusion.18.refs_4_.refs_5_ = f32[80,768]{1,0:T(8,128)S(1)} fusion(bf16[80,2048]{1,0:T(8,128)(2,1)S(1)} %get-tuple-element.119, bf16[1,2048,768]{2,1,0:T(8,128)(2,1)} %collective-permute-done.5), kind=kOutput, calls=%fused_computation.18 | convolution fusion | flops 251658240 | bytes 3719168 | tf_op jit(solution)/shard_map/dot_general | solution.py:342
  95.7 2.5 %fusion.26.refs_3_.refs_4_ = f32[80,768]{1,0:T(8,128)S(1)} fusion(bf16[80,2048]{1,0:T(8,128)(2,1)S(1)} %get-tuple-element.119, bf16[1,2048,768]{2,1,0:T(8,128)(2,1)} %collective-permute-done.4), kind=kOutput, calls=%fused_computation.26 | convolution fusion | flops 251658240 | bytes 3719168 | tf_op jit(solution)/shard_map/dot_general | solution.py:342
  98.8 1.4 collective-permute-start.19
  100.3 3.8 %collective-permute-start.22 = (bf16[96,2048]{1,0:T(8,128)(2,1)S(1)}, bf16[96,2048]{1,0:T(8,128)(2,1)S(1)}, u32[]{:S(2)}, u32[]{:S(2)}) collective-permute-start(bf16[96,2048]{1,0:T(8,128)(2,1)S(1)} %get-tuple-element.131), channel_id=1, source_target_pairs={{0,24},{4,28},{8,0},{12,4},{16,8},{20,12},{24,16},{28,20},{1,25},{... | collective-permute-start | bytes 1179656 | tf_op jit(solution)/shard_map/ppermute | solution.py:287
  104.7 0.7 fusion.10.refs_1_
  106.0 1.4 shard_map.88
  107.4 0.6 shard_map.89
  108.1 0.7 collective-permute-start.25
  108.9 1.9 %collective-permute-start.23 = (bf16[96,2048]{1,0:T(8,128)(2,1)S(1)}, bf16[96,2048]{1,0:T(8,128)(2,1)S(1)}, u32[]{:S(2)}, u32[]{:S(2)}) collective-permute-start(bf16[96,2048]{1,0:T(8,128)(2,1)S(1)} %get-tuple-element.142), channel_id=1, source_target_pairs={{0,20},{4,16},{8,28},{12,24},{16,4},{20,0},{24,12},{28,8},{1,21},{... | collective-permute-start | bytes 1179656 | tf_op jit(solution)/shard_map/ppermute | solution.py:290
  110.7 3.0 %collective-permute-start.24 = (bf16[96,2048]{1,0:T(8,128)(2,1)S(1)}, bf16[96,2048]{1,0:T(8,128)(2,1)S(1)}, u32[]{:S(2)}, u32[]{:S(2)}) collective-permute-start(bf16[96,2048]{1,0:T(8,128)(2,1)S(1)} %get-tuple-element.143), channel_id=1, source_target_pairs={{0,12},{4,8},{8,20},{12,16},{16,28},{20,24},{24,4},{28,0},{1,13},{... | collective-permute-start | bytes 1179656 | tf_op jit(solution)/shard_map/ppermute | solution.py:290
  114.4 0.7 fusion.8.refs_1_
  115.1 0.7 fusion.refs_2_
  115.8 1.2 shard_map.92
  117.1 26.7 %collective-permute-done.23 = bf16[96,2048]{1,0:T(8,128)(2,1)S(1)} collective-permute-done((bf16[96,2048]{1,0:T(8,128)(2,1)S(1)}, bf16[96,2048]{1,0:T(8,128)(2,1)S(1)}, u32[]{:S(2)}, u32[]{:S(2)}) %collective-permute-start.23) | collective-permute-done | bytes 393248 | tf_op jit(solution)/shard_map/ppermute | solution.py:290
  143.8 1.0 add_convert_fusion
  (63 shorter events, 15.4 us)
Async XLA Ops:
  0.0 24.1 %collective-permute-start.5 = (bf16[1,2048,768]{2,1,0:T(8,128)(2,1)}, bf16[1,2048,768]{2,1,0:T(8,128)(2,1)}, u32[]{:S(2)}, u32[]{:S(2)}) collective-permute-start(bf16[1,2048,768]{2,1,0:T(8,128)(2,1)} %param.10), channel_id=1, source_target_pairs={{0,1},{1,0},{2,3},{3,2},{4,5},{5,4},{6,7},{7,6},{8,9},{9,8},{10,11... | collective-permute-start | bytes 9437192 | tf_op jit(solution)/shard_map/ppermute | solution.py:293
  0.5 27.9 %collective-permute-start.4 = (bf16[1,2048,768]{2,1,0:T(8,128)(2,1)}, bf16[1,2048,768]{2,1,0:T(8,128)(2,1)}, u32[]{:S(2)}, u32[]{:S(2)}) collective-permute-start(bf16[1,2048,768]{2,1,0:T(8,128)(2,1)} %param.9), channel_id=1, source_target_pairs={{0,1},{1,0},{2,3},{3,2},{4,5},{5,4},{6,7},{7,6},{8,9},{9,8},{10,11... | collective-permute-start | bytes 9437192 | tf_op jit(solution)/shard_map/ppermute | solution.py:293
  0.5 1.0 copy-start.1
  1.5 0.7 copy-start.2
  2.2 0.7 copy-start.3
  3.4 14.9 %collective-permute-start.1 = (bf16[96,2176]{1,0:T(8,128)(2,1)S(1)}, bf16[96,2176]{1,0:T(8,128)(2,1)S(1)}, u32[]{:S(2)}, u32[]{:S(2)}) collective-permute-start(bf16[96,2176]{1,0:T(8,128)(2,1)S(1)} %shard_map.64.refs_1_.refs_2_.refs_3_), channel_id=1, source_target_pairs={{0,8},{4,12},{8,16},{12,20},{16,24},{20,28},{24,0},{28,4},{1,9},{5... | collective-permute-start | bytes 1253384 | tf_op jit(solution)/shard_map/ppermute | solution.py:284
  6.5 5.2 %copy-start.5 = (bf16[1,2048,768]{2,1,0:T(8,128)(2,1)S(1)}, bf16[1,2048,768]{2,1,0:T(8,128)(2,1)}, u32[]{:S(2)}) copy-start(bf16[1,2048,768]{2,1,0:T(8,128)(2,1)} %param.9) | copy-start | bytes 9437188
  6.5 14.0 %collective-permute-start.3 = (bf16[96,2176]{1,0:T(8,128)(2,1)S(1)}, bf16[96,2176]{1,0:T(8,128)(2,1)S(1)}, u32[]{:S(2)}, u32[]{:S(2)}) collective-permute-start(bf16[96,2176]{1,0:T(8,128)(2,1)S(1)} %shard_map.64.refs_1_.refs_2_.refs_3_), channel_id=1, source_target_pairs={{0,4},{4,0},{8,12},{12,8},{16,20},{20,16},{24,28},{28,24},{1,5},{5... | collective-permute-start | bytes 1253384 | tf_op jit(solution)/shard_map/ppermute | solution.py:281
  11.6 8.9 %copy-start = (bf16[1,768,2048]{2,1,0:T(8,128)(2,1)S(1)}, bf16[1,768,2048]{2,1,0:T(8,128)(2,1)}, u32[]{:S(2)}) copy-start(bf16[1,768,2048]{2,1,0:T(8,128)(2,1)} %refs_5_.1) | copy-start | bytes 9437188
  12.3 10.4 %copy-start.4 = (bf16[1,2048,768]{2,1,0:T(8,128)(2,1)S(1)}, bf16[1,2048,768]{2,1,0:T(8,128)(2,1)}, u32[]{:S(2)}) copy-start(bf16[1,2048,768]{2,1,0:T(8,128)(2,1)} %param.10) | copy-start | bytes 9437188
  12.9 4.9 %collective-permute-start = (bf16[80,768]{1,0:T(8,128)(2,1)S(1)}, bf16[80,768]{1,0:T(8,128)(2,1)S(1)}, u32[]{:S(2)}, u32[]{:S(2)}) collective-permute-start(bf16[80,768]{1,0:T(8,128)(2,1)S(1)} %get-tuple-element.74), channel_id=1, source_target_pairs={{0,2},{2,0},{1,3},{3,1},{4,6},{6,4},{5,7},{7,5},{8,10},{10,8},{9,1... | collective-permute-start | bytes 368648 | tf_op jit(solution)/shard_map/ppermute | solution.py:296
  18.9 14.8 %collective-permute-start.6 = (bf16[96,2176]{1,0:T(8,128)(2,1)S(1)}, bf16[96,2176]{1,0:T(8,128)(2,1)S(1)}, u32[]{:S(2)}, u32[]{:S(2)}) collective-permute-start(bf16[96,2176]{1,0:T(8,128)(2,1)S(1)} %get-tuple-element.77.refs_3_.refs_5_), channel_id=1, source_target_pairs={{0,8},{4,12},{8,16},{12,20},{16,24},{20,28},{24,0},{28,4},{1,9},{5... | collective-permute-start | bytes 1253384 | tf_op jit(solution)/shard_map/ppermute | solution.py:284
  20.1 16.5 %collective-permute-start.8 = (bf16[96,2176]{1,0:T(8,128)(2,1)S(1)}, bf16[96,2176]{1,0:T(8,128)(2,1)S(1)}, u32[]{:S(2)}, u32[]{:S(2)}) collective-permute-start(bf16[96,2176]{1,0:T(8,128)(2,1)S(1)} %get-tuple-element.77.refs_3_.refs_5_), channel_id=1, source_target_pairs={{0,4},{4,0},{8,12},{12,8},{16,20},{20,16},{24,28},{28,24},{1,5},{5... | collective-permute-start | bytes 1253384 | tf_op jit(solution)/shard_map/ppermute | solution.py:281
  22.6 37.5 %collective-permute-start.11 = (bf16[1,768,2048]{2,1,0:T(8,128)(2,1)S(1)}, bf16[1,768,2048]{2,1,0:T(8,128)(2,1)S(1)}, u32[]{:S(2)}, u32[]{:S(2)}) collective-permute-start(bf16[1,768,2048]{2,1,0:T(8,128)(2,1)S(1)} %get-tuple-element.96), channel_id=1, source_target_pairs={{0,1},{1,0},{2,3},{3,2},{4,5},{5,4},{6,7},{7,6},{8,9},{9,8},{10,11... | collective-permute-start | bytes 9437192 | tf_op jit(solution)/shard_map/ppermute | solution.py:293
  24.1 8.3 %collective-permute-start.2 = (bf16[80,384]{1,0:T(8,128)(2,1)S(1)}, bf16[80,384]{1,0:T(8,128)(2,1)S(1)}, u32[]{:S(2)}, u32[]{:S(2)}) collective-permute-start(bf16[80,384]{1,0:T(8,128)(2,1)S(1)} %get-tuple-element.76.refs_1_), channel_id=1, source_target_pairs={{0,2},{2,0},{1,3},{3,1},{4,6},{6,4},{5,7},{7,5},{8,10},{10,8},{9,1... | collective-permute-start | bytes 184328 | tf_op jit(solution)/shard_map/ppermute | solution.py:296
  31.8 15.0 %collective-permute-start.7 = (bf16[368,768]{1,0:T(8,128)(2,1)S(1)}, bf16[368,768]{1,0:T(8,128)(2,1)S(1)}, u32[]{:S(2)}, u32[]{:S(2)}) collective-permute-start(bf16[368,768]{1,0:T(8,128)(2,1)S(1)} %get-tuple-element.86), channel_id=1, source_target_pairs={{0,2},{2,0},{1,3},{3,1},{4,6},{6,4},{5,7},{7,5},{8,10},{10,8},{9,1... | collective-permute-start | bytes 1695752 | tf_op jit(solution)/shard_map/ppermute | solution.py:296
  34.7 16.4 %collective-permute-start.10 = (bf16[96,2176]{1,0:T(8,128)(2,1)S(1)}, bf16[96,2176]{1,0:T(8,128)(2,1)S(1)}, u32[]{:S(2)}, u32[]{:S(2)}) collective-permute-start(bf16[96,2176]{1,0:T(8,128)(2,1)S(1)} %get-tuple-element.87.refs_2_.refs_4_), channel_id=1, source_target_pairs={{0,8},{4,12},{8,16},{12,20},{16,24},{20,28},{24,0},{28,4},{1,9},{5... | collective-permute-start | bytes 1253384 | tf_op jit(solution)/shard_map/ppermute | solution.py:284
  47.5 9.7 %collective-permute-start.9 = (bf16[368,384]{1,0:T(8,128)(2,1)S(1)}, bf16[368,384]{1,0:T(8,128)(2,1)S(1)}, u32[]{:S(2)}, u32[]{:S(2)}) collective-permute-start(bf16[368,384]{1,0:T(8,128)(2,1)S(1)} %get-tuple-element.93.refs_1_), channel_id=1, source_target_pairs={{0,2},{2,0},{1,3},{3,1},{4,6},{6,4},{5,7},{7,5},{8,10},{10,8},{9,1... | collective-permute-start | bytes 847880 | tf_op jit(solution)/shard_map/ppermute | solution.py:296
  48.2 18.3 %collective-permute-start.13 = (bf16[96,2176]{1,0:T(8,128)(2,1)S(1)}, bf16[96,2176]{1,0:T(8,128)(2,1)S(1)}, u32[]{:S(2)}, u32[]{:S(2)}) collective-permute-start(bf16[96,2176]{1,0:T(8,128)(2,1)S(1)} %get-tuple-element.87.refs_2_.refs_4_), channel_id=1, source_target_pairs={{0,4},{4,0},{8,12},{12,8},{16,20},{20,16},{24,28},{28,24},{1,5},{5... | collective-permute-start | bytes 1253384 | tf_op jit(solution)/shard_map/ppermute | solution.py:281
  49.7 15.5 %collective-permute-start.15 = (bf16[288,768]{1,0:T(8,128)(2,1)S(1)}, bf16[288,768]{1,0:T(8,128)(2,1)S(1)}, u32[]{:S(2)}, u32[]{:S(2)}) collective-permute-start(bf16[288,768]{1,0:T(8,128)(2,1)S(1)} %get-tuple-element.101), channel_id=1, source_target_pairs={{0,2},{2,0},{1,3},{3,1},{4,6},{6,4},{5,7},{7,5},{8,10},{10,8},{9,1... | collective-permute-start | bytes 1327112 | tf_op jit(solution)/shard_map/ppermute | solution.py:296
  57.9 12.6 %collective-permute-start.14 = (bf16[96,2176]{1,0:T(8,128)(2,1)S(1)}, bf16[96,2176]{1,0:T(8,128)(2,1)S(1)}, u32[]{:S(2)}, u32[]{:S(2)}) collective-permute-start(bf16[96,2176]{1,0:T(8,128)(2,1)S(1)} %get-tuple-element.100.refs_1_.refs_3_), channel_id=1, source_target_pairs={{0,4},{4,0},{8,12},{12,8},{16,20},{20,16},{24,28},{28,24},{1,5},{5... | collective-permute-start | bytes 1253384 | tf_op jit(solution)/shard_map/ppermute | solution.py:281
  62.8 16.2 %collective-permute-start.12 = (bf16[96,2048]{1,0:T(8,128)(2,1)S(1)}, bf16[96,2048]{1,0:T(8,128)(2,1)S(1)}, u32[]{:S(2)}, u32[]{:S(2)}) collective-permute-start(bf16[96,2048]{1,0:T(8,128)(2,1)S(1)} %get-tuple-element.140), channel_id=1, source_target_pairs={{0,4},{4,0},{8,12},{12,8},{16,20},{20,16},{24,28},{28,24},{1,5},{5... | collective-permute-start | bytes 1179656 | tf_op jit(solution)/shard_map/ppermute | solution.py:281
  65.9 13.3 %collective-permute-start.16 = (bf16[288,384]{1,0:T(8,128)(2,1)S(1)}, bf16[288,384]{1,0:T(8,128)(2,1)S(1)}, u32[]{:S(2)}, u32[]{:S(2)}) collective-permute-start(bf16[288,384]{1,0:T(8,128)(2,1)S(1)} %get-tuple-element.109.refs_1_), channel_id=1, source_target_pairs={{0,2},{2,0},{1,3},{3,1},{4,6},{6,4},{5,7},{7,5},{8,10},{10,8},{9,1... | collective-permute-start | bytes 663560 | tf_op jit(solution)/shard_map/ppermute | solution.py:296
  80.4 8.4 %collective-permute-start.18 = (bf16[288,768]{1,0:T(8,128)(2,1)S(1)}, bf16[288,768]{1,0:T(8,128)(2,1)S(1)}, u32[]{:S(2)}, u32[]{:S(2)}) collective-permute-start(bf16[288,768]{1,0:T(8,128)(2,1)S(1)} %get-tuple-element.115), channel_id=1, source_target_pairs={{0,2},{2,0},{1,3},{3,1},{4,6},{6,4},{5,7},{7,5},{8,10},{10,8},{9,1... | collective-permute-start | bytes 1327112 | tf_op jit(solution)/shard_map/ppermute | solution.py:296
  83.3 16.9 %collective-permute-start.21 = (bf16[96,2048]{1,0:T(8,128)(2,1)S(1)}, bf16[96,2048]{1,0:T(8,128)(2,1)S(1)}, u32[]{:S(2)}, u32[]{:S(2)}) collective-permute-start(bf16[96,2048]{1,0:T(8,128)(2,1)S(1)} %get-tuple-element.145), channel_id=1, source_target_pairs={{0,4},{4,0},{8,12},{12,8},{16,20},{20,16},{24,28},{28,24},{1,5},{5... | collective-permute-start | bytes 1179656 | tf_op jit(solution)/shard_map/ppermute | solution.py:281
  84.9 28.9 %collective-permute-start.17 = (bf16[96,2048]{1,0:T(8,128)(2,1)S(1)}, bf16[96,2048]{1,0:T(8,128)(2,1)S(1)}, u32[]{:S(2)}, u32[]{:S(2)}) collective-permute-start(bf16[96,2048]{1,0:T(8,128)(2,1)S(1)} %get-tuple-element.144), channel_id=1, source_target_pairs={{0,16},{4,20},{8,24},{12,28},{16,0},{20,4},{24,8},{28,12},{1,17},{... | collective-permute-start | bytes 1179656 | tf_op jit(solution)/shard_map/ppermute | solution.py:287
  92.2 11.9 %collective-permute-start.20 = (bf16[288,384]{1,0:T(8,128)(2,1)S(1)}, bf16[288,384]{1,0:T(8,128)(2,1)S(1)}, u32[]{:S(2)}, u32[]{:S(2)}) collective-permute-start(bf16[288,384]{1,0:T(8,128)(2,1)S(1)} %get-tuple-element.122.refs_1_), channel_id=1, source_target_pairs={{0,2},{2,0},{1,3},{3,1},{4,6},{6,4},{5,7},{7,5},{8,10},{10,8},{9,1... | collective-permute-start | bytes 663560 | tf_op jit(solution)/shard_map/ppermute | solution.py:296
  98.8 8.6 %collective-permute-start.19 = (bf16[160,768]{1,0:T(8,128)(2,1)S(1)}, bf16[160,768]{1,0:T(8,128)(2,1)S(1)}, u32[]{:S(2)}, u32[]{:S(2)}) collective-permute-start(bf16[160,768]{1,0:T(8,128)(2,1)S(1)} %get-tuple-element.121), channel_id=1, source_target_pairs={{0,2},{2,0},{1,3},{3,1},{4,6},{6,4},{5,7},{7,5},{8,10},{10,8},{9,1... | collective-permute-start | bytes 737288 | tf_op jit(solution)/shard_map/ppermute | solution.py:296
  100.3 16.7 %collective-permute-start.22 = (bf16[96,2048]{1,0:T(8,128)(2,1)S(1)}, bf16[96,2048]{1,0:T(8,128)(2,1)S(1)}, u32[]{:S(2)}, u32[]{:S(2)}) collective-permute-start(bf16[96,2048]{1,0:T(8,128)(2,1)S(1)} %get-tuple-element.131), channel_id=1, source_target_pairs={{0,24},{4,28},{8,0},{12,4},{16,8},{20,12},{24,16},{28,20},{1,25},{... | collective-permute-start | bytes 1179656 | tf_op jit(solution)/shard_map/ppermute | solution.py:287
  108.1 5.7 %collective-permute-start.25 = (bf16[160,384]{1,0:T(8,128)(2,1)S(1)}, bf16[160,384]{1,0:T(8,128)(2,1)S(1)}, u32[]{:S(2)}, u32[]{:S(2)}) collective-permute-start(bf16[160,384]{1,0:T(8,128)(2,1)S(1)} %get-tuple-element.133.refs_1_), channel_id=1, source_target_pairs={{0,2},{2,0},{1,3},{3,1},{4,6},{6,4},{5,7},{7,5},{8,10},{10,8},{9,1... | collective-permute-start | bytes 368648 | tf_op jit(solution)/shard_map/ppermute | solution.py:296
  108.9 34.9 %collective-permute-start.23 = (bf16[96,2048]{1,0:T(8,128)(2,1)S(1)}, bf16[96,2048]{1,0:T(8,128)(2,1)S(1)}, u32[]{:S(2)}, u32[]{:S(2)}) collective-permute-start(bf16[96,2048]{1,0:T(8,128)(2,1)S(1)} %get-tuple-element.142), channel_id=1, source_target_pairs={{0,20},{4,16},{8,28},{12,24},{16,4},{20,0},{24,12},{28,8},{1,21},{... | collective-permute-start | bytes 1179656 | tf_op jit(solution)/shard_map/ppermute | solution.py:290
  110.7 33.1 %collective-permute-start.24 = (bf16[96,2048]{1,0:T(8,128)(2,1)S(1)}, bf16[96,2048]{1,0:T(8,128)(2,1)S(1)}, u32[]{:S(2)}, u32[]{:S(2)}) collective-permute-start(bf16[96,2048]{1,0:T(8,128)(2,1)S(1)} %get-tuple-element.143), channel_id=1, source_target_pairs={{0,12},{4,8},{8,20},{12,16},{16,28},{20,24},{24,4},{28,0},{1,13},{... | collective-permute-start | bytes 1179656 | tf_op jit(solution)/shard_map/ppermute | solution.py:290
  117.0 26.8 %collective-permute-start.26 = (bf16[96,2048]{1,0:T(8,128)(2,1)S(1)}, bf16[96,2048]{1,0:T(8,128)(2,1)S(1)}, u32[]{:S(2)}, u32[]{:S(2)}) collective-permute-start(bf16[96,2048]{1,0:T(8,128)(2,1)S(1)} %get-tuple-element.138), channel_id=1, source_target_pairs={{0,8},{4,12},{8,16},{12,20},{16,24},{20,28},{24,0},{28,4},{1,9},{5... | collective-permute-start | bytes 1179656 | tf_op jit(solution)/shard_map/ppermute | solution.py:287

commit v5 on v3

--- a/solution.py
+++ b/solution.py
@@ -10,9 +10,10 @@
 F32 = jnp.float32
 BF16 = jnp.bfloat16
 LANES = 128
-VMEM = 24 * 1024 * 1024
+VMEM = 12 * 1024 * 1024
 SMEM = pl.BlockSpec(memory_space=pltpu.SMEM)
 ANY = pl.BlockSpec(memory_space=pl.ANY)
+HBM = pl.BlockSpec(memory_space=pltpu.HBM)
 
 
 def tile(extent, choices):
@@ -34,11 +35,19 @@
     return pl.CostEstimate(flops=1, bytes_accessed=1, transcendentals=0)
 
 
-def block_kernel(experts, tokens_ref, ids_ref, route_ref, out_ref):
+def block_kernel(experts, tokens_ref, ids_ref, route_ref, out_ref, ids_buffer, route_buffer, sems):
     rows, width = tokens_ref.shape
-    out_ref[:, :width] = tokens_ref[...]
-    ids = ids_ref[...].T
-    route = route_ref[...].T
+    copies = [
+        pltpu.make_async_copy(ids_ref, ids_buffer, sems.at[0]),
+        pltpu.make_async_copy(route_ref, route_buffer, sems.at[1]),
+        pltpu.make_async_copy(tokens_ref, out_ref.at[:, :width], sems.at[2]),
+    ]
+    for copy in copies:
+        copy.start()
+    copies[0].wait()
+    copies[1].wait()
+    ids = ids_buffer[...].T
+    route = route_buffer[...].T
     column = lax.broadcasted_iota(jnp.int32, (rows, out_ref.shape[1] - width), 1)
     expert = jnp.where(column < experts, column, column - experts)
     value = jnp.zeros(column.shape, F32)
@@ -46,6 +55,7 @@
         value = value + jnp.where(expert == ids[:, k:k + 1], route[:, k:k + 1], 0.0)
     high = value.astype(BF16).astype(F32)
     out_ref[:, width:] = jnp.where(column < experts, high, value - high).astype(BF16)
+    copies[2].wait()
 
 
 def make_block(tokens, expert_ids, route_weights, experts):
@@ -56,8 +66,13 @@
         functools.partial(block_kernel, experts),
         grid=(1,),
         out_shape=jax.ShapeDtypeStruct((rows, padded), BF16),
-        in_specs=[whole(a) for a in args],
+        in_specs=[HBM] * 3,
         out_specs=pl.BlockSpec((rows, padded), lambda i: (0, 0)),
+        scratch_shapes=[
+            pltpu.VMEM(args[1].shape, jnp.int32),
+            pltpu.VMEM(args[2].shape, F32),
+            pltpu.SemaphoreType.DMA((3,)),
+        ],
         compiler_params=params(),
         cost_estimate=cost(),
     )(*args)
@@ -123,14 +138,9 @@
         out_ref[rows, units + full:] = y[:, units - full:]
 
 
-def pick_kernel(width, experts, capacity, units, groups, count, kinds, split, copied, scalars, *refs):
+def pick_kernel(width, experts, capacity, units, groups, count, kinds, split, scalars, *refs):
     blocks, weights = refs[:count], refs[count:]
-    if copied:
-        *_, source_ref, chosen_ref, part_ref, target_ref, sem = refs
-        copy = pltpu.make_async_copy(source_ref, target_ref, sem)
-        copy.start()
-    else:
-        chosen_ref, part_ref = refs[-2:]
+    chosen_ref, part_ref = refs[-2:]
     rows = blocks[0].shape[0]
     offsets = layout(groups, capacity)
     step = tile(width, (512, 256))
@@ -147,35 +157,25 @@
     for g in range(len(groups)):
         mine = weights[kinds * g:kinds * (g + 1)]
         multiply(chosen_ref, slice(offsets[g], offsets[g + 1]), mine, scalars[2] if split else None, units, part_ref)
-    if copied:
-        copy.wait()
-
-
-def pick_rows(scalars, groups, blocks, weights, split, copying, after, width, experts, capacity, units):
+
+
+def pick_rows(scalars, groups, blocks, weights, split, after, width, experts, capacity, units):
     columns = 2 * units if split else weights[0][0].shape[1]
     taken = layout(groups, capacity)[-1]
     flat = [w for expert, _ in groups for w in weights[expert]]
-    kinds = len(weights[0])
-    copied = len(copying)
-    kernel = functools.partial(pick_kernel, width, experts, capacity, units, groups, len(blocks), kinds, split, copied)
+    kernel = functools.partial(
+        pick_kernel, width, experts, capacity, units, groups, len(blocks), len(weights[0]), split
+    )
+    out = (jax.ShapeDtypeStruct((taken, width), BF16), jax.ShapeDtypeStruct((taken, columns), BF16))
     return pl.pallas_call(
         kernel,
         grid=(1,),
-        out_shape=(
-            jax.ShapeDtypeStruct((taken, width), BF16),
-            jax.ShapeDtypeStruct((taken, columns), BF16),
-            *[jax.ShapeDtypeStruct(a.shape, a.dtype) for a in copying],
-        ),
-        in_specs=[SMEM] + [whole(x) for x in (*blocks, *flat)] + [ANY] * (len(after) + copied),
-        out_specs=(
-            pl.BlockSpec((taken, width), lambda i: (0, 0)),
-            pl.BlockSpec((taken, columns), lambda i: (0, 0)),
-            *[ANY] * copied,
-        ),
-        scratch_shapes=[pltpu.SemaphoreType.DMA] * copied,
+        out_shape=out,
+        in_specs=[SMEM] + [whole(x) for x in (*blocks, *flat)] + [ANY] * len(after),
+        out_specs=tuple(whole(o) for o in out),
         compiler_params=params(),
         cost_estimate=cost(),
-    )(scalars, *blocks, *flat, *after, *copying)
+    )(scalars, *blocks, *flat, *after)
 
 
 def home_kernel(capacity, units, groups, kinds, split, passed, scalars, x_ref, *refs):
@@ -277,6 +277,27 @@
     return result[0], result[1:]
 
 
+def add_kernel(count, *refs):
+    out_ref = refs[-1]
+    total = refs[0][...].astype(F32)
+    for ref in refs[1:count]:
+        total = total + ref[...].astype(F32)
+    out_ref[...] = total.astype(out_ref.dtype)
+
+
+def added(terms, kind, after):
+    out = jax.ShapeDtypeStruct(terms[0].shape, kind)
+    return pl.pallas_call(
+        functools.partial(add_kernel, len(terms)),
+        grid=(1,),
+        out_shape=out,
+        in_specs=[whole(t) for t in terms] + [ANY] * len(after),
+        out_specs=whole(out),
+        compiler_params=params(),
+        cost_estimate=cost(),
+    )(*terms, *after)
+
+
 def on_device(tokens, expert_ids, route_weights, w_gate, w_up, w_down):
     rows, width = tokens.shape
     top = expert_ids.shape[1]
@@ -330,32 +351,35 @@
 
     both = ((0, (0, 1)), (1, (0, 1)))
     one = ((0, (0,)), (1, (0,)))
-    plan = [([(0, "s")], ((0, (0,)),)), ([(0, "s"), (0, "b")], ((1, (0, 1)), (0, (1,)))), ([(1, "s")], one)]
-    plan += [([(hop, "b"), (hop + 1, "s")], both) for hop in range(1, hops - 2)]
-    plan += [([(hops - 2, "b"), (hops - 1, "b")], both), ([(hops - 1, "s")], one)]
+    plan = [([(0, "s")], ((0, (0,)),)), ([(0, "s"), (0, "b"), (1, "s")], ((1, (0, 1, 2)), (0, (1, 2))))]
+    plan += [([(hop - 1, "b"), (hop, "s")], both) for hop in range(2, hops)]
+    plan += [([(hops - 1, "b")], one)]
     count = len(plan)
-    chosen, parts_in, totals, hidden, returned = {}, {}, {}, {}, {}
-    downs = [w_down[0]]
+    chosen, parts_in, totals, hidden, returned, carried, gathered = {}, {}, {}, {}, {}, {}, []
+    downs = [w_down[0], over_core(w_down)[0]]
     order = [scalars]
+
+    def passing(hop):
+        return [arrived[hop]] if hop in arrived else []
+
+    def take_on(hop, passed):
+        if passed:
+            blocks[hop, "s"] = passed[0]
+            send_on(hop)
 
     def pick(i):
         keys, groups = plan[i]
         mine = [blocks[k] for k in keys]
-        copying = [w_down] if i == 1 else []
-        chosen[i], part, *copies = pick_rows(
-            scalars, groups, mine, away, split, copying, order, width, experts, capacity, units
-        )
-        downs.extend(over_core(c)[0] for c in copies)
+        chosen[i], part = pick_rows(scalars, groups, mine, away, split, order, width, experts, capacity, units)
         parts_in[i] = [over_x(part[:, 2 * units * (s - 1):2 * units * s], s) for s in range(1, parts)]
         order[:] = [part]
 
-    def home_product(i, hop):
-        passing = [arrived[hop]] if hop in arrived else []
-        totals[i], passed = home_rows(scalars, plan[i][1], chosen[i], home, split, passing, order, capacity, units)
+    def home_product(i, hop=None):
+        totals[i], passed = home_rows(
+            scalars, plan[i][1], chosen[i], home, split, passing(hop), order, capacity, units
+        )
         order[:] = [totals[i]]
-        if passing:
-            blocks[hop, "s"] = passed[0]
-            send_on(hop)
+        take_on(hop, passed)
 
     def activate(i):
         total = totals[i]
@@ -365,53 +389,83 @@
         hidden[i] = [value] + [over_x(value, s) for s in range(1, parts)]
         order.append(value)
 
-    def down_product(i, hop):
+    def down_product(i, hop=None):
         keys, groups = plan[i]
         mine = [blocks[k] for k in keys]
-        passing = [arrived[hop]] if hop in arrived else []
         term, passed = down_rows(
-            scalars, groups, hidden[i], mine, downs, passing, order, width, experts, capacity
+            scalars, groups, hidden[i], mine, downs, passing(hop), order, width, experts, capacity
         )
         order[:] = [term]
-        if passing:
-            blocks[hop, "s"] = passed[0]
-            send_on(hop)
+        take_on(hop, passed)
         for k, (at, kind) in enumerate(keys):
             piece = term[k * rows:(k + 1) * rows]
             if kind == "b":
-                piece = over_y(piece)
-            returned.setdefault(at, []).append(piece)
-
-    arriving = []
+                returned[at, "b"] = over_y(piece)
+            elif at == 0:
+                gathered.append(piece)
+            else:
+                returned[at, "s"] = piece
 
     def add_hop(hop):
-        total = sum(x.astype(F32) for x in returned[hop])
-        if hop > 0:
-            total = total.astype(BF16)
-            arriving.append(lax.ppermute(total, "expert", [(i, (i - 2 * hop) % ring) for i in range(ring)]))
+        if hop == 0:
+            gathered[:] = [added(gathered + [returned[hop, "b"]], F32, order)]
+            order[:] = [gathered[0]]
         else:
-            arriving.append(total)
-        order.append(total)
+            terms = [returned[hop, "s"], returned[hop, "b"]] + ([carried[hop]] if hop in carried else [])
+            total = added(terms, BF16, order)
+            order[:] = [total]
+            carried[hop + 1] = over_z(total)
+
+    def await_beside(hop):
+        if (hop, "b") in blocks:
+            order.append(blocks[hop, "b"])
 
     send_on(0)
-    added = 0
-    for i in range(count + 2):
-        if i == 1:
-            activate(0)
-        if i < count:
+    if hops == 4:
+        pick(0)
+        order.extend([gates[1], ups[1]])
+        home_product(0, 1)
+        pick(1)
+        activate(0)
+        order.append(downs[1])
+        home_product(1, 2)
+        pick(2)
+        activate(1)
+        home_product(2, 3)
+        order.append(blocks[2, "b"])
+        down_product(0, None)
+        activate(2)
+        pick(3)
+        home_product(3, None)
+        down_product(1, None)
+        down_product(2, None)
+        pick(4)
+        home_product(4, None)
+        activate(3)
+        down_product(3, None)
+        add_hop(1)
+        add_hop(0)
+        activate(4)
+        down_product(4, None)
+        add_hop(2)
+        add_hop(3)
+    else:
+        pick(0)
+        home_product(0, 1)
+        activate(0)
+        for i in range(1, count):
+            if i > 1:
+                activate(i - 1)
             pick(i)
-        if 1 <= i - 1 < count:
-            activate(i - 1)
-        if i < count:
-            home_product(i, {0: 1, 2: 2}.get(i))
-        if (5 <= i < count or i > count) and added < hops - 2:
-            add_hop(added)
-            added += 1
-        if 0 <= i - 2 < count:
-            down_product(i - 2, i if i >= 3 else None)
-    for hop in range(added, hops):
-        add_hop(hop)
-    return sum(x.astype(F32) for x in arriving).astype(BF16)
+            home_product(i, i + 1)
+            down_product(i - 1)
+            if i >= 3:
+                add_hop(i - 3)
+        activate(count - 1)
+        down_product(count - 1)
+        for hop in range(count - 3, hops):
+            add_hop(hop)
+    return (gathered[0] + carried[hops].astype(F32)).astype(BF16)
 
 
 def solution(mesh):

time: 156 us -> 138 us (0.88)
  waiting for transfers between devices: 52 us -> 43.9 us
  starting transfers between devices: 31.2 us -> 25.8 us
  Pallas kernels: 62.6 us -> 59.3 us
    ppermute x3 -> x6, waiting for transfers between devices: 5.38 us -> 34.3 us  [over_z(): return lax.ppermute(x, 'expert', [(i, (i + 2) % ring) for i in range(ring)])]
    ppermute x3 -> x0, waiting for transfers between devices: 20 us -> none  [add_hop(): lax.ppermute(total, 'expert', [(i, (i - 2 * hop) % ring) for i in range(r...]
    ppermute x8, waiting for transfers between devices: 25.8 us -> 6.21 us  [over_y(): return lax.ppermute(x, 'expert', [(i, i ^ 1) for i in range(ring)])]
    ppermute x3 -> x0, starting transfers between devices: 4.43 us -> none  [add_hop(): lax.ppermute(total, 'expert', [(i, (i - 2 * hop) % ring) for i in range(r...]
    pallas_call x6 -> x9, Pallas kernels: 22 us -> 19.3 us  [the longest x5 18.7 us: pick_rows(): pl.pallas_call(kernel, grid=(1,), out_shape=out, in_specs=[SMEM] + [whole...]
    pallas_call x6 -> x5, Pallas kernels: 16.6 us -> 13.9 us  [home_rows(): pl.pallas_call(functools.partial(home_kernel, capacity, units, groups, le...]
    ppermute x12 -> x10, waiting for transfers between devices: 0.79 us -> 3.37 us  [over_x(): lax.ppermute(x, 'tensor', [(i, (i + step) % parts) for i in range(parts)])]
    pallas_call x6 -> x5, Pallas kernels: 22.7 us -> 24.9 us  [down_rows(): pl.pallas_call(functools.partial(down_kernel, experts, capacity, groups,...]
  transfers between devices with their start and end apart: 29 -> 27, of which waited for: 11 -> 7; matrix products, arithmetic and copies ran while one was open for 1% -> 1% of each run, Pallas kernels for 38% -> 43%
where the time goes in v5:
time: 138 us
  Pallas kernels  59.3 us (43%)
  waiting for transfers between devices  43.9 us (32%)
  starting transfers between devices  25.8 us (19%)
  local copies, waits for them, and re-layouts  6.45 us (5%)
  other arithmetic  1.75 us (1%)
    ppermute x6, waiting for transfers between devices, over_z(): return lax.ppermute(x, 'expert', [(i, (i + 2) % ring) for i in range(ring)])  34.3 us
    pallas_call x5, Pallas kernels, down_rows(): pl.pallas_call(functools.partial(down_kernel, experts, capacity, groups,...  24.9 us
    pallas_call x5, Pallas kernels, pick_rows(): pl.pallas_call(kernel, grid=(1,), out_shape=out, in_specs=[SMEM] + [whole...  18.7 us
    pallas_call x5, Pallas kernels, home_rows(): pl.pallas_call(functools.partial(home_kernel, capacity, units, groups, le...  13.9 us
    ppermute x10, starting transfers between devices, over_x(): lax.ppermute(x, 'tensor', [(i, (i + step) % parts) for i in range(parts)])  11.2 us
    ppermute x8, starting transfers between devices, over_y(): return lax.ppermute(x, 'expert', [(i, i ^ 1) for i in range(ring)])  10.4 us
    ppermute x8, waiting for transfers between devices, over_y(): return lax.ppermute(x, 'expert', [(i, i ^ 1) for i in range(ring)])  6.21 us
    unnamed x16, local copies, waits for them, and re-layouts  6.16 us
  transfers between devices with their start and end apart: 27, of which 7 were waited for; matrix products, arithmetic and copies ran while one was open for 1% of the time, Pallas kernels for 43%

profile of v5, /device:TPU:0, one launch (start us, length us, event | category | flops | bytes accessed | tf_op | source)
XLA Modules:
  0.0 137.5 jit_solution(9807526037674850591)
XLA Ops:
  0.0 0.5 collective-permute-start.1
  0.5 0.5 collective-permute-start.7
  1.0 1.0 copy-done.5
  2.0 0.7 copy-done.6
  2.7 0.7 copy-done.7
  3.3 1.2 shard_map.64.refs_0_.refs_2_
  4.6 2.6 %collective-permute-start.2 = (bf16[96,2176]{1,0:T(8,128)(2,1)}, bf16[96,2176]{1,0:T(8,128)(2,1)}, u32[]{:S(2)}, u32[]{:S(2)}) collective-permute-start(bf16[96,2176]{1,0:T(8,128)(2,1)} %shard_map.64.refs_0_.refs_2_), channel_id=1, source_target_pairs={{0,8},{4,12},{8,16},{12,20},{16,24},{20,28},{24,0},{28,4},{1,9},{5... | collective-permute-start | bytes 1253384 | tf_op jit(solution)/shard_map/ppermute | solution.py:317
  7.2 1.5 %collective-permute-start.6 = (bf16[96,2176]{1,0:T(8,128)(2,1)}, bf16[96,2176]{1,0:T(8,128)(2,1)}, u32[]{:S(2)}, u32[]{:S(2)}) collective-permute-start(bf16[96,2176]{1,0:T(8,128)(2,1)} %shard_map.64.refs_0_.refs_2_), channel_id=1, source_target_pairs={{0,4},{4,0},{8,12},{12,8},{16,20},{20,16},{24,28},{28,24},{1,5},{5... | collective-permute-start | bytes 1253384 | tf_op jit(solution)/shard_map/ppermute | solution.py:314
  8.7 0.1 stack.24.scalars.refs_3_
  8.8 1.9 %copy-done = bf16[1,2048,768]{2,1,0:T(8,128)(2,1)S(1)} copy-done((bf16[1,2048,768]{2,1,0:T(8,128)(2,1)S(1)}, bf16[1,2048,768]{2,1,0:T(8,128)(2,1)}, u32[]{:S(2)}) %copy-start) | copy-done | bytes 3145752
  10.7 1.9 %copy-done.2 = bf16[1,2048,768]{2,1,0:T(8,128)(2,1)S(1)} copy-done((bf16[1,2048,768]{2,1,0:T(8,128)(2,1)S(1)}, bf16[1,2048,768]{2,1,0:T(8,128)(2,1)}, u32[]{:S(2)}) %copy-start.2) | copy-done | bytes 3145752
  12.6 2.2 %shard_map.65 = (bf16[80,2048]{1,0:T(8,128)(2,1)S(1)}, bf16[80,768]{1,0:T(8,128)(2,1)S(1)}) custom-call(s32[6]{0:T(128)S(1)} %stack.24.scalars.refs_3_, bf16[96,2176]{1,0:T(8,128)(2,1)} %shard_map.64.refs_0_.refs_2_, bf16[2048,768]{1,0:T(8,128)(2,1)S(1)} %bitcast.13, bf16[2048,768]{1,0:T(8,128)(2,1)S(1)} %bitcast.23, s32[6]{0:T(128)S(1)} %stack.24.scalars.refs_3_), custom_call_target="tpu_custom_call" | custom-call | flops 1 | bytes 1 | tf_op jit(solution)/shard_map/pallas_call | solution.py:170
  14.9 5.0 %collective-permute-done.2.refs_5_ = bf16[96,2176]{1,0:T(8,128)(2,1)} collective-permute-done((bf16[96,2176]{1,0:T(8,128)(2,1)}, bf16[96,2176]{1,0:T(8,128)(2,1)}, u32[]{:S(2)}, u32[]{:S(2)}) %collective-permute-start.2) | collective-permute-done | bytes 417824 | tf_op jit(solution)/shard_map/ppermute | solution.py:317
  19.9 1.5 %collective-permute-start.3 = (bf16[80,768]{1,0:T(8,128)(2,1)S(1)}, bf16[80,768]{1,0:T(8,128)(2,1)S(1)}, u32[]{:S(2)}, u32[]{:S(2)}) collective-permute-start(bf16[80,768]{1,0:T(8,128)(2,1)S(1)} %get-tuple-element.22.refs_2_), channel_id=1, source_target_pairs={{0,2},{2,0},{1,3},{3,1},{4,6},{6,4},{5,7},{7,5},{8,10},{10,8},{9,1... | collective-permute-start | bytes 368648 | tf_op jit(solution)/shard_map/ppermute | solution.py:323
  21.4 1.2 shard_map.66
  22.6 4.9 %shard_map.67 = (bf16[368,2048]{1,0:T(8,128)(2,1)S(1)}, bf16[368,768]{1,0:T(8,128)(2,1)S(1)}) custom-call(s32[6]{0:T(128)S(1)} %stack.24.scalars.refs_3_, bf16[96,2176]{1,0:T(8,128)(2,1)} %shard_map.64.refs_0_.refs_2_, bf16[96,2176]{1,0:T(8,128)(2,1)} %collective-permute-done.6.refs_1_.refs_3_, bf16[96,2176]{1,0:T(8,128)(2,1)} %get-tuple-element.24.refs_2_.refs_4_, ...), custom_call_target="tpu_custom_call" | custom-call | flops 1 | bytes 1 | tf_op jit(solution)/shard_map/pallas_call | solution.py:170
  27.5 0.6 collective-permute-start.9
  28.1 1.5 %collective-permute-start.5 = (bf16[96,2176]{1,0:T(8,128)(2,1)}, bf16[96,2176]{1,0:T(8,128)(2,1)S(1)}, u32[]{:S(2)}, u32[]{:S(2)}) collective-permute-start(bf16[96,2176]{1,0:T(8,128)(2,1)} %get-tuple-element.24.refs_2_.refs_4_), channel_id=1, source_target_pairs={{0,4},{4,0},{8,12},{12,8},{16,20},{20,16},{24,28},{28,24},{1,5},{5... | collective-permute-start | bytes 1253384 | tf_op jit(solution)/shard_map/ppermute | solution.py:314
  29.7 1.6 %collective-permute-start.4 = (bf16[80,384]{1,0:T(8,128)(2,1)S(1)}, bf16[80,384]{1,0:T(8,128)(2,1)S(1)}, u32[]{:S(2)}, u32[]{:S(2)}) collective-permute-start(bf16[80,384]{1,0:T(8,128)(2,1)S(1)} %fusion.4.refs_5_.refs_0_), channel_id=1, source_target_pairs={{0,2},{2,0},{1,3},{3,1},{4,6},{6,4},{5,7},{7,5},{8,10},{10,8},{9,1... | collective-permute-start | bytes 184328 | tf_op jit(solution)/shard_map/ppermute | solution.py:323
  31.3 9.7 %collective-permute-done.8.refs_7_ = bf16[96,2176]{1,0:T(8,128)(2,1)S(1)} collective-permute-done((bf16[96,2176]{1,0:T(8,128)(2,1)}, bf16[96,2176]{1,0:T(8,128)(2,1)S(1)}, u32[]{:S(2)}, u32[]{:S(2)}) %collective-permute-start.8) | collective-permute-done | bytes 417824 | tf_op jit(solution)/shard_map/ppermute | solution.py:317
  41.0 3.3 %shard_map.68 = (f32[368,768]{1,0:T(8,128)S(1)}, bf16[96,2176]{1,0:T(8,128)(2,1)S(1)}) custom-call(s32[6]{0:T(128)S(1)} %stack.24.scalars.refs_3_, bf16[368,2048]{1,0:T(8,128)(2,1)S(1)} %get-tuple-element.25.x_ref, bf16[2048,768]{1,0:T(8,128)(2,1)} %bitcast.9.refs_3_.refs_0_.refs_4_.refs_2_, ...), custom_call_target="tpu_custom_call", output_to_operand_aliasing={{1}: (9, {})} | custom-call | flops 1 | bytes 1 | tf_op jit(solution)/shard_map/pallas_call | solution.py:193
  44.3 0.2 collective-permute-start.10
  44.5 1.5 %collective-permute-start.11 = (bf16[96,2176]{1,0:T(8,128)(2,1)S(1)}, bf16[96,2176]{1,0:T(8,128)(2,1)S(1)}, u32[]{:S(2)}, u32[]{:S(2)}) collective-permute-start(bf16[96,2176]{1,0:T(8,128)(2,1)S(1)} %get-tuple-element.27.refs_1_.refs_3_), channel_id=1, source_target_pairs={{0,4},{4,0},{8,12},{12,8},{16,20},{20,16},{24,28},{28,24},{1,5},{5... | collective-permute-start | bytes 1253384 | tf_op jit(solution)/shard_map/ppermute | solution.py:314
  46.0 3.9 %shard_map.69 = (bf16[288,2048]{1,0:T(8,128)(2,1)S(1)}, bf16[288,768]{1,0:T(8,128)(2,1)S(1)}) custom-call(s32[6]{0:T(128)S(1)} %stack.24.scalars.refs_3_, bf16[96,2176]{1,0:T(8,128)(2,1)S(1)} %collective-permute-done.5.refs_0_.refs_2_, bf16[96,2176]{1,0:T(8,128)(2,1)S(1)} %get-tuple-element.27.refs_1_.refs_3_, bf16[2048,768]{1,0:T(8,128)(2,1)S(1)} %bitcast.17, ...), custom_call_target="tpu_custom_call" | custom-call | flops 1 | bytes 1 | tf_op jit(solution)/shard_map/pallas_call | solution.py:170
  49.9 1.6 %collective-permute-start.13 = (bf16[288,768]{1,0:T(8,128)(2,1)S(1)}, bf16[288,768]{1,0:T(8,128)(2,1)S(1)}, u32[]{:S(2)}, u32[]{:S(2)}) collective-permute-start(bf16[288,768]{1,0:T(8,128)(2,1)S(1)} %get-tuple-element.30.refs_4_), channel_id=1, source_target_pairs={{0,2},{2,0},{1,3},{3,1},{4,6},{6,4},{5,7},{7,5},{8,10},{10,8},{9,1... | collective-permute-start | bytes 1327112 | tf_op jit(solution)/shard_map/ppermute | solution.py:323
  51.5 0.1 convert_add_fusion
  51.6 0.2 fusion.refs_5_.refs_0_
  51.7 0.6 collective-permute-start.12
  52.3 4.0 %collective-permute-done.10.refs_6_ = bf16[96,2176]{1,0:T(8,128)(2,1)S(1)} collective-permute-done((bf16[96,2176]{1,0:T(8,128)(2,1)S(1)}, bf16[96,2176]{1,0:T(8,128)(2,1)S(1)}, u32[]{:S(2)}, u32[]{:S(2)}) %collective-permute-start.10) | collective-permute-done | bytes 417824 | tf_op jit(solution)/shard_map/ppermute | solution.py:317
  56.3 3.2 %shard_map.70 = (f32[288,768]{1,0:T(8,128)S(1)}, bf16[96,2176]{1,0:T(8,128)(2,1)S(1)}) custom-call(s32[6]{0:T(128)S(1)} %stack.24.scalars.refs_3_, bf16[288,2048]{1,0:T(8,128)(2,1)S(1)} %get-tuple-element.29.x_ref, bf16[2048,768]{1,0:T(8,128)(2,1)S(1)} %bitcast.18, bf16[2048,768]{1,0:T(8,128)(2,1)S(1)} %bitcast.28, ...), custom_call_target="tpu_custom_call", output_to_operand_aliasing={{1}: (8, {})} | custom-call | flops 1 | bytes 1 | tf_op jit(solution)/shard_map/pallas_call | solution.py:193
  59.5 1.3 collective-permute-start.19
  60.9 3.0 %shard_map.71.refs_6_.refs_0_ = bf16[96,2048]{1,0:T(8,128)(2,1)S(1)} custom-call(s32[6]{0:T(128)S(1)} %stack.24.scalars.refs_3_, bf16[80,384]{1,0:T(8,128)(2,1)S(1)} %fusion.4.refs_5_.refs_0_, bf16[80,384]{1,0:T(8,128)(2,1)S(1)} %collective-permute-done.4.refs_1_, bf16[96,2176]{1,0:T(8,128)(2,1)} %shard_map.64.refs_0_.refs_2_, ...), custom_call_target="tpu_custom_call" | custom-call | flops 1 | bytes 1 | tf_op jit(solution)/shard_map/pallas_call | solution.py:265
  63.9 0.1 fusion.2.refs_7_.refs_0_
  64.1 1.6 %collective-permute-start.15 = (bf16[288,384]{1,0:T(8,128)(2,1)S(1)}, bf16[288,384]{1,0:T(8,128)(2,1)S(1)}, u32[]{:S(2)}, u32[]{:S(2)}) collective-permute-start(bf16[288,384]{1,0:T(8,128)(2,1)S(1)} %fusion.2.refs_7_.refs_0_), channel_id=1, source_target_pairs={{0,2},{2,0},{1,3},{3,1},{4,6},{6,4},{5,7},{7,5},{8,10},{10,8},{9,1... | collective-permute-start | bytes 663560 | tf_op jit(solution)/shard_map/ppermute | solution.py:323
  65.7 3.9 %shard_map.72 = (bf16[288,2048]{1,0:T(8,128)(2,1)S(1)}, bf16[288,768]{1,0:T(8,128)(2,1)S(1)}) custom-call(s32[6]{0:T(128)S(1)} %stack.24.scalars.refs_3_, bf16[96,2176]{1,0:T(8,128)(2,1)S(1)} %collective-permute-done.11.refs_5_.refs_0_.refs_2_, bf16[96,2176]{1,0:T(8,128)(2,1)S(1)} %get-tuple-element.32.refs_1_.refs_3_, bf16[2048,768]{1,0:T(8,128)(2,1)S(1)} %bitcast.19, ...), custom_call_target="tpu_custom_call" | custom-call | flops 1 | bytes 1 | tf_op jit(solution)/shard_map/pallas_call | solution.py:170
  69.6 0.5 collective-permute-start.17
  70.1 3.0 %shard_map.73.refs_7_ = f32[288,768]{1,0:T(8,128)S(1)} custom-call(s32[6]{0:T(128)S(1)} %stack.24.scalars.refs_3_, bf16[288,2048]{1,0:T(8,128)(2,1)S(1)} %get-tuple-element.33.x_ref, bf16[2048,768]{1,0:T(8,128)(2,1)S(1)} %bitcast.20, bf16[2048,768]{1,0:T(8,128)(2,1)S(1)} %bitcast.30, bf16[2048,768]{1,0:T(8,128)(2,1)} %bitcast.9.refs_3_.refs_0_.refs_4_.refs_2_, ...), custom_call_target="tpu_custom_call" | custom-call | flops 1 | bytes 1 | tf_op jit(solution)/shard_map/pallas_call | solution.py:193
  73.1 6.0 %shard_map.74.refs_6_ = bf16[288,2048]{1,0:T(8,128)(2,1)S(1)} custom-call(s32[6]{0:T(128)S(1)} %stack.24.scalars.refs_3_, bf16[368,384]{1,0:T(8,128)(2,1)S(1)} %fusion.refs_5_.refs_0_, bf16[368,384]{1,0:T(8,128)(2,1)S(1)} %collective-permute-done.12.refs_1_, bf16[96,2176]{1,0:T(8,128)(2,1)} %shard_map.64.refs_0_.refs_2_, ...), custom_call_target="tpu_custom_call" | custom-call | flops 1 | bytes 1 | tf_op jit(solution)/shard_map/pallas_call | solution.py:265
  79.2 0.1 fusion.5
  79.3 0.8 collective-permute-start.14
  80.1 5.5 %shard_map.75.refs_5_ = bf16[192,2048]{1,0:T(8,128)(2,1)S(1)} custom-call(s32[6]{0:T(128)S(1)} %stack.24.scalars.refs_3_, bf16[288,384]{1,0:T(8,128)(2,1)S(1)} %fusion.2.refs_7_.refs_0_, bf16[288,384]{1,0:T(8,128)(2,1)S(1)} %collective-permute-done.15.refs_1_, bf16[96,2176]{1,0:T(8,128)(2,1)S(1)} %collective-permute-done.5.refs_0_.refs_2_, ...), custom_call_target="tpu_custom_call" | custom-call | flops 1 | bytes 1 | tf_op jit(solution)/shard_map/pallas_call | solution.py:265
  85.6 0.1 convert_add_fusion.1
  85.7 0.1 fusion.1.refs_0_.refs_7_
  85.9 1.4 %collective-permute-start.18 = (bf16[288,384]{1,0:T(8,128)(2,1)S(1)}, bf16[288,384]{1,0:T(8,128)(2,1)S(1)}, u32[]{:S(2)}, u32[]{:S(2)}) collective-permute-start(bf16[288,384]{1,0:T(8,128)(2,1)S(1)} %fusion.1.refs_0_.refs_7_), channel_id=1, source_target_pairs={{0,2},{2,0},{1,3},{3,1},{4,6},{6,4},{5,7},{7,5},{8,10},{10,8},{9,1... | collective-permute-start | bytes 663560 | tf_op jit(solution)/shard_map/ppermute | solution.py:323
  87.3 1.6 %collective-permute-start.16 = (bf16[96,2048]{1,0:T(8,128)(2,1)S(1)}, bf16[96,2048]{1,0:T(8,128)(2,1)S(1)}, u32[]{:S(2)}, u32[]{:S(2)}) collective-permute-start(bf16[96,2048]{1,0:T(8,128)(2,1)S(1)} %get-tuple-element.43), channel_id=1, source_target_pairs={{0,4},{4,0},{8,12},{12,8},{16,20},{20,16},{24,28},{28,24},{1,5},{5... | collective-permute-start | bytes 1179656 | tf_op jit(solution)/shard_map/ppermute | solution.py:314
  88.9 3.8 %shard_map.76 = (bf16[160,2048]{1,0:T(8,128)(2,1)S(1)}, bf16[160,768]{1,0:T(8,128)(2,1)S(1)}) custom-call(s32[6]{0:T(128)S(1)} %stack.24.scalars.refs_3_, bf16[96,2176]{1,0:T(8,128)(2,1)S(1)} %collective-permute-done.19.refs_0_.refs_2_, bf16[2048,768]{1,0:T(8,128)(2,1)S(1)} %bitcast.21, bf16[2048,768]{1,0:T(8,128)(2,1)S(1)} %bitcast.31, ...), custom_call_target="tpu_custom_call" | custom-call | flops 1 | bytes 1 | tf_op jit(solution)/shard_map/pallas_call | solution.py:170
  92.8 0.5 collective-permute-start.20
  93.2 3.1 %shard_map.77.refs_6_ = f32[160,768]{1,0:T(8,128)S(1)} custom-call(s32[6]{0:T(128)S(1)} %stack.24.scalars.refs_3_, bf16[160,2048]{1,0:T(8,128)(2,1)S(1)} %get-tuple-element.35.x_ref, bf16[2048,768]{1,0:T(8,128)(2,1)S(1)} %bitcast.22, bf16[2048,768]{1,0:T(8,128)(2,1)S(1)} %bitcast.32, bf16[2048,768]{1,0:T(8,128)(2,1)} %bitcast.9.refs_3_.refs_0_.refs_4_.refs_2_, ...), custom_call_target="tpu_custom_call" | custom-call | flops 1 | bytes 1 | tf_op jit(solution)/shard_map/pallas_call | solution.py:193
  96.4 5.5 %shard_map.78.refs_2_ = bf16[192,2048]{1,0:T(8,128)(2,1)S(1)} custom-call(s32[6]{0:T(128)S(1)} %stack.24.scalars.refs_3_, bf16[288,384]{1,0:T(8,128)(2,1)S(1)} %fusion.1.refs_0_.refs_7_, bf16[288,384]{1,0:T(8,128)(2,1)S(1)} %collective-permute-done.18.refs_1_, bf16[96,2176]{1,0:T(8,128)(2,1)S(1)} %collective-permute-done.11.refs_5_.refs_0_.refs_2_, ...), custom_call_target="tpu_custom_call" | custom-call | flops 1 | bytes 1 | tf_op jit(solution)/shard_map/pallas_call | solution.py:265
  101.9 0.8 collective-permute-start.23
  102.8 0.1 shard_map.79.refs_3_
  103.0 0.1 fusion.3.refs_0_.refs_6_
  103.1 1.4 %collective-permute-start.21 = (bf16[160,384]{1,0:T(8,128)(2,1)S(1)}, bf16[160,384]{1,0:T(8,128)(2,1)S(1)}, u32[]{:S(2)}, u32[]{:S(2)}) collective-permute-start(bf16[160,384]{1,0:T(8,128)(2,1)S(1)} %fusion.3.refs_0_.refs_6_), channel_id=1, source_target_pairs={{0,2},{2,0},{1,3},{3,1},{4,6},{6,4},{5,7},{7,5},{8,10},{10,8},{9,1... | collective-permute-start | bytes 368648 | tf_op jit(solution)/shard_map/ppermute | solution.py:323
  104.5 0.2 shard_map.80.refs_5_
  104.7 3.3 %collective-permute-done.21.refs_1_ = bf16[160,384]{1,0:T(8,128)(2,1)S(1)} collective-permute-done((bf16[160,384]{1,0:T(8,128)(2,1)S(1)}, bf16[160,384]{1,0:T(8,128)(2,1)S(1)}, u32[]{:S(2)}, u32[]{:S(2)}) %collective-permute-start.21) | collective-permute-done | bytes 122912 | tf_op jit(solution)/shard_map/ppermute | solution.py:323
  108.0 5.0 %shard_map.81.refs_3_ = bf16[96,2048]{1,0:T(8,128)(2,1)S(1)} custom-call(s32[6]{0:T(128)S(1)} %stack.24.scalars.refs_3_, bf16[160,384]{1,0:T(8,128)(2,1)S(1)} %fusion.3.refs_0_.refs_6_, bf16[160,384]{1,0:T(8,128)(2,1)S(1)} %collective-permute-done.21.refs_1_, bf16[96,2176]{1,0:T(8,128)(2,1)S(1)} %collective-permute-done.19.refs_0_.refs_2_, ...), custom_call_target="tpu_custom_call" | custom-call | flops 1 | bytes 1 | tf_op jit(solution)/shard_map/pallas_call | solution.py:265
  113.0 1.3 collective-permute-start.22
  114.4 0.1 shard_map.82.refs_3_
  114.5 0.2 collective-permute-start.25
  114.7 6.2 %collective-permute-done.22.refs_1_ = bf16[96,2048]{1,0:T(8,128)(2,1)S(1)} collective-permute-done((bf16[96,2048]{1,0:T(8,128)(2,1)S(1)}, bf16[96,2048]{1,0:T(8,128)(2,1)S(1)}, u32[]{:S(2)}, u32[]{:S(2)}) %collective-permute-start.22) | collective-permute-done | bytes 393248 | tf_op jit(solution)/shard_map/ppermute | solution.py:314
  120.9 6.0 %collective-permute-done.25.refs_2_ = bf16[96,2048]{1,0:T(8,128)(2,1)S(1)} collective-permute-done((bf16[96,2048]{1,0:T(8,128)(2,1)S(1)}, bf16[96,2048]{1,0:T(8,128)(2,1)S(1)}, u32[]{:S(2)}, u32[]{:S(2)}) %collective-permute-start.25) | collective-permute-done | bytes 393248 | tf_op jit(solution)/shard_map/ppermute | solution.py:317
  126.9 0.2 shard_map.83
  127.1 9.6 %collective-permute-done.26 = bf16[96,2048]{1,0:T(8,128)(2,1)S(1)} collective-permute-done((bf16[96,2048]{1,0:T(8,128)(2,1)S(1)}, bf16[96,2048]{1,0:T(8,128)(2,1)S(1)}, u32[]{:S(2)}, u32[]{:S(2)}) %collective-permute-start.26) | collective-permute-done | bytes 393248 | tf_op jit(solution)/shard_map/ppermute | solution.py:317
  136.7 0.8 add_convert_fusion
  (41 shorter events, 0.5 us)
Async XLA Ops:
  0.0 21.4 %collective-permute-start.1 = (bf16[1,2048,768]{2,1,0:T(8,128)(2,1)}, bf16[1,2048,768]{2,1,0:T(8,128)(2,1)S(1)}, u32[]{:S(2)}, u32[]{:S(2)}) collective-permute-start(bf16[1,2048,768]{2,1,0:T(8,128)(2,1)} %param.10), channel_id=1, source_target_pairs={{0,1},{1,0},{2,3},{3,2},{4,5},{5,4},{6,7},{7,6},{8,9},{9,8},{10,11... | collective-permute-start | bytes 9437192 | tf_op jit(solution)/shard_map/ppermute | solution.py:320
  0.5 20.9 %collective-permute-start = (bf16[1,2048,768]{2,1,0:T(8,128)(2,1)}, bf16[1,2048,768]{2,1,0:T(8,128)(2,1)}, u32[]{:S(2)}, u32[]{:S(2)}) collective-permute-start(bf16[1,2048,768]{2,1,0:T(8,128)(2,1)} %param.9), channel_id=1, source_target_pairs={{0,1},{1,0},{2,3},{3,2},{4,5},{5,4},{6,7},{7,6},{8,9},{9,8},{10,11... | collective-permute-start | bytes 9437192 | tf_op jit(solution)/shard_map/ppermute | solution.py:320
  0.5 30.7 %collective-permute-start.7 = (bf16[1,768,2048]{2,1,0:T(8,128)(2,1)}, bf16[1,768,2048]{2,1,0:T(8,128)(2,1)}, u32[]{:S(2)}, u32[]{:S(2)}) collective-permute-start(bf16[1,768,2048]{2,1,0:T(8,128)(2,1)} %param.11), channel_id=1, source_target_pairs={{0,1},{1,0},{2,3},{3,2},{4,5},{5,4},{6,7},{7,6},{8,9},{9,8},{10,11... | collective-permute-start | bytes 9437192 | tf_op jit(solution)/shard_map/ppermute | solution.py:320
  1.0 1.0 copy-start.5
  2.0 0.7 copy-start.6
  2.6 0.7 copy-start.7
  4.6 15.3 %collective-permute-start.2 = (bf16[96,2176]{1,0:T(8,128)(2,1)}, bf16[96,2176]{1,0:T(8,128)(2,1)}, u32[]{:S(2)}, u32[]{:S(2)}) collective-permute-start(bf16[96,2176]{1,0:T(8,128)(2,1)} %shard_map.64.refs_0_.refs_2_), channel_id=1, source_target_pairs={{0,8},{4,12},{8,16},{12,20},{16,24},{20,28},{24,0},{28,4},{1,9},{5... | collective-permute-start | bytes 1253384 | tf_op jit(solution)/shard_map/ppermute | solution.py:317
  7.2 15.4 %collective-permute-start.6 = (bf16[96,2176]{1,0:T(8,128)(2,1)}, bf16[96,2176]{1,0:T(8,128)(2,1)}, u32[]{:S(2)}, u32[]{:S(2)}) collective-permute-start(bf16[96,2176]{1,0:T(8,128)(2,1)} %shard_map.64.refs_0_.refs_2_), channel_id=1, source_target_pairs={{0,4},{4,0},{8,12},{12,8},{16,20},{20,16},{24,28},{28,24},{1,5},{5... | collective-permute-start | bytes 1253384 | tf_op jit(solution)/shard_map/ppermute | solution.py:314
  8.8 1.9 %copy-start = (bf16[1,2048,768]{2,1,0:T(8,128)(2,1)S(1)}, bf16[1,2048,768]{2,1,0:T(8,128)(2,1)}, u32[]{:S(2)}) copy-start(bf16[1,2048,768]{2,1,0:T(8,128)(2,1)} %param.9) | copy-start | bytes 9437188
  10.7 1.9 %copy-start.2 = (bf16[1,2048,768]{2,1,0:T(8,128)(2,1)S(1)}, bf16[1,2048,768]{2,1,0:T(8,128)(2,1)}, u32[]{:S(2)}) copy-start(bf16[1,2048,768]{2,1,0:T(8,128)(2,1)} %param.10) | copy-start | bytes 9437188
  12.6 8.8 %copy-start.1 = (bf16[1,2048,768]{2,1,0:T(8,128)(2,1)S(1)}, bf16[1,2048,768]{2,1,0:T(8,128)(2,1)}, u32[]{:S(2)}) copy-start(bf16[1,2048,768]{2,1,0:T(8,128)(2,1)} %param.9) | copy-start | bytes 9437188
  12.6 8.8 %copy-start.3 = (bf16[1,2048,768]{2,1,0:T(8,128)(2,1)S(1)}, bf16[1,2048,768]{2,1,0:T(8,128)(2,1)}, u32[]{:S(2)}) copy-start(bf16[1,2048,768]{2,1,0:T(8,128)(2,1)} %param.10) | copy-start | bytes 9437188
  19.9 9.7 %collective-permute-start.3 = (bf16[80,768]{1,0:T(8,128)(2,1)S(1)}, bf16[80,768]{1,0:T(8,128)(2,1)S(1)}, u32[]{:S(2)}, u32[]{:S(2)}) collective-permute-start(bf16[80,768]{1,0:T(8,128)(2,1)S(1)} %get-tuple-element.22.refs_2_), channel_id=1, source_target_pairs={{0,2},{2,0},{1,3},{3,1},{4,6},{6,4},{5,7},{7,5},{8,10},{10,8},{9,1... | collective-permute-start | bytes 368648 | tf_op jit(solution)/shard_map/ppermute | solution.py:323
  27.5 24.0 %collective-permute-start.9 = (bf16[368,768]{1,0:T(8,128)(2,1)S(1)}, bf16[368,768]{1,0:T(8,128)(2,1)S(1)}, u32[]{:S(2)}, u32[]{:S(2)}) collective-permute-start(bf16[368,768]{1,0:T(8,128)(2,1)S(1)} %get-tuple-element.26.refs_4_), channel_id=1, source_target_pairs={{0,2},{2,0},{1,3},{3,1},{4,6},{6,4},{5,7},{7,5},{8,10},{10,8},{9,1... | collective-permute-start | bytes 1695752 | tf_op jit(solution)/shard_map/ppermute | solution.py:323
  28.1 12.9 %collective-permute-start.8 = (bf16[96,2176]{1,0:T(8,128)(2,1)}, bf16[96,2176]{1,0:T(8,128)(2,1)S(1)}, u32[]{:S(2)}, u32[]{:S(2)}) collective-permute-start(bf16[96,2176]{1,0:T(8,128)(2,1)} %get-tuple-element.24.refs_2_.refs_4_), channel_id=1, source_target_pairs={{0,8},{4,12},{8,16},{12,20},{16,24},{20,28},{24,0},{28,4},{1,9},{5... | collective-permute-start | bytes 1253384 | tf_op jit(solution)/shard_map/ppermute | solution.py:317
  28.1 17.9 %collective-permute-start.5 = (bf16[96,2176]{1,0:T(8,128)(2,1)}, bf16[96,2176]{1,0:T(8,128)(2,1)S(1)}, u32[]{:S(2)}, u32[]{:S(2)}) collective-permute-start(bf16[96,2176]{1,0:T(8,128)(2,1)} %get-tuple-element.24.refs_2_.refs_4_), channel_id=1, source_target_pairs={{0,4},{4,0},{8,12},{12,8},{16,20},{20,16},{24,28},{28,24},{1,5},{5... | collective-permute-start | bytes 1253384 | tf_op jit(solution)/shard_map/ppermute | solution.py:314
  29.7 31.2 %collective-permute-start.4 = (bf16[80,384]{1,0:T(8,128)(2,1)S(1)}, bf16[80,384]{1,0:T(8,128)(2,1)S(1)}, u32[]{:S(2)}, u32[]{:S(2)}) collective-permute-start(bf16[80,384]{1,0:T(8,128)(2,1)S(1)} %fusion.4.refs_5_.refs_0_), channel_id=1, source_target_pairs={{0,2},{2,0},{1,3},{3,1},{4,6},{6,4},{5,7},{7,5},{8,10},{10,8},{9,1... | collective-permute-start | bytes 184328 | tf_op jit(solution)/shard_map/ppermute | solution.py:323
  44.3 12.0 %collective-permute-start.10 = (bf16[96,2176]{1,0:T(8,128)(2,1)S(1)}, bf16[96,2176]{1,0:T(8,128)(2,1)S(1)}, u32[]{:S(2)}, u32[]{:S(2)}) collective-permute-start(bf16[96,2176]{1,0:T(8,128)(2,1)S(1)} %get-tuple-element.27.refs_1_.refs_3_), channel_id=1, source_target_pairs={{0,8},{4,12},{8,16},{12,20},{16,24},{20,28},{24,0},{28,4},{1,9},{5... | collective-permute-start | bytes 1253384 | tf_op jit(solution)/shard_map/ppermute | solution.py:317
  44.5 16.3 %collective-permute-start.11 = (bf16[96,2176]{1,0:T(8,128)(2,1)S(1)}, bf16[96,2176]{1,0:T(8,128)(2,1)S(1)}, u32[]{:S(2)}, u32[]{:S(2)}) collective-permute-start(bf16[96,2176]{1,0:T(8,128)(2,1)S(1)} %get-tuple-element.27.refs_1_.refs_3_), channel_id=1, source_target_pairs={{0,4},{4,0},{8,12},{12,8},{16,20},{20,16},{24,28},{28,24},{1,5},{5... | collective-permute-start | bytes 1253384 | tf_op jit(solution)/shard_map/ppermute | solution.py:314
  49.9 13.9 %collective-permute-start.13 = (bf16[288,768]{1,0:T(8,128)(2,1)S(1)}, bf16[288,768]{1,0:T(8,128)(2,1)S(1)}, u32[]{:S(2)}, u32[]{:S(2)}) collective-permute-start(bf16[288,768]{1,0:T(8,128)(2,1)S(1)} %get-tuple-element.30.refs_4_), channel_id=1, source_target_pairs={{0,2},{2,0},{1,3},{3,1},{4,6},{6,4},{5,7},{7,5},{8,10},{10,8},{9,1... | collective-permute-start | bytes 1327112 | tf_op jit(solution)/shard_map/ppermute | solution.py:323
  51.7 21.4 %collective-permute-start.12 = (bf16[368,384]{1,0:T(8,128)(2,1)S(1)}, bf16[368,384]{1,0:T(8,128)(2,1)S(1)}, u32[]{:S(2)}, u32[]{:S(2)}) collective-permute-start(bf16[368,384]{1,0:T(8,128)(2,1)S(1)} %fusion.refs_5_.refs_0_), channel_id=1, source_target_pairs={{0,2},{2,0},{1,3},{3,1},{4,6},{6,4},{5,7},{7,5},{8,10},{10,8},{9,1... | collective-permute-start | bytes 847880 | tf_op jit(solution)/shard_map/ppermute | solution.py:323
  56.3 4.5 %copy-start.4 = (bf16[1,768,2048]{2,1,0:T(8,128)(2,1)S(1)}, bf16[1,768,2048]{2,1,0:T(8,128)(2,1)}, u32[]{:S(2)}) copy-start(bf16[1,768,2048]{2,1,0:T(8,128)(2,1)} %param.11) | copy-start | bytes 9437188
  59.5 29.4 %collective-permute-start.19 = (bf16[96,2176]{1,0:T(8,128)(2,1)S(1)}, bf16[96,2176]{1,0:T(8,128)(2,1)S(1)}, u32[]{:S(2)}, u32[]{:S(2)}) collective-permute-start(bf16[96,2176]{1,0:T(8,128)(2,1)S(1)} %get-tuple-element.32.refs_1_.refs_3_), channel_id=1, source_target_pairs={{0,4},{4,0},{8,12},{12,8},{16,20},{20,16},{24,28},{28,24},{1,5},{5... | collective-permute-start | bytes 1253384 | tf_op jit(solution)/shard_map/ppermute | solution.py:314
  64.1 16.0 %collective-permute-start.15 = (bf16[288,384]{1,0:T(8,128)(2,1)S(1)}, bf16[288,384]{1,0:T(8,128)(2,1)S(1)}, u32[]{:S(2)}, u32[]{:S(2)}) collective-permute-start(bf16[288,384]{1,0:T(8,128)(2,1)S(1)} %fusion.2.refs_7_.refs_0_), channel_id=1, source_target_pairs={{0,2},{2,0},{1,3},{3,1},{4,6},{6,4},{5,7},{7,5},{8,10},{10,8},{9,1... | collective-permute-start | bytes 663560 | tf_op jit(solution)/shard_map/ppermute | solution.py:323
  69.6 16.0 %collective-permute-start.17 = (bf16[288,768]{1,0:T(8,128)(2,1)S(1)}, bf16[288,768]{1,0:T(8,128)(2,1)S(1)}, u32[]{:S(2)}, u32[]{:S(2)}) collective-permute-start(bf16[288,768]{1,0:T(8,128)(2,1)S(1)} %get-tuple-element.34.refs_4_), channel_id=1, source_target_pairs={{0,2},{2,0},{1,3},{3,1},{4,6},{6,4},{5,7},{7,5},{8,10},{10,8},{9,1... | collective-permute-start | bytes 1327112 | tf_op jit(solution)/shard_map/ppermute | solution.py:323
  79.3 25.2 %collective-permute-start.14 = (bf16[96,2048]{1,0:T(8,128)(2,1)S(1)}, bf16[96,2048]{1,0:T(8,128)(2,1)S(1)}, u32[]{:S(2)}, u32[]{:S(2)}) collective-permute-start(bf16[96,2048]{1,0:T(8,128)(2,1)S(1)} %get-tuple-element.38), channel_id=1, source_target_pairs={{0,4},{4,0},{8,12},{12,8},{16,20},{20,16},{24,28},{28,24},{1,5},{5... | collective-permute-start | bytes 1179656 | tf_op jit(solution)/shard_map/ppermute | solution.py:314
  85.9 10.5 %collective-permute-start.18 = (bf16[288,384]{1,0:T(8,128)(2,1)S(1)}, bf16[288,384]{1,0:T(8,128)(2,1)S(1)}, u32[]{:S(2)}, u32[]{:S(2)}) collective-permute-start(bf16[288,384]{1,0:T(8,128)(2,1)S(1)} %fusion.1.refs_0_.refs_7_), channel_id=1, source_target_pairs={{0,2},{2,0},{1,3},{3,1},{4,6},{6,4},{5,7},{7,5},{8,10},{10,8},{9,1... | collective-permute-start | bytes 663560 | tf_op jit(solution)/shard_map/ppermute | solution.py:323
  87.3 15.4 %collective-permute-start.16 = (bf16[96,2048]{1,0:T(8,128)(2,1)S(1)}, bf16[96,2048]{1,0:T(8,128)(2,1)S(1)}, u32[]{:S(2)}, u32[]{:S(2)}) collective-permute-start(bf16[96,2048]{1,0:T(8,128)(2,1)S(1)} %get-tuple-element.43), channel_id=1, source_target_pairs={{0,4},{4,0},{8,12},{12,8},{16,20},{20,16},{24,28},{28,24},{1,5},{5... | collective-permute-start | bytes 1179656 | tf_op jit(solution)/shard_map/ppermute | solution.py:314
  92.8 10.2 %collective-permute-start.20 = (bf16[160,768]{1,0:T(8,128)(2,1)S(1)}, bf16[160,768]{1,0:T(8,128)(2,1)S(1)}, u32[]{:S(2)}, u32[]{:S(2)}) collective-permute-start(bf16[160,768]{1,0:T(8,128)(2,1)S(1)} %get-tuple-element.36.refs_4_), channel_id=1, source_target_pairs={{0,2},{2,0},{1,3},{3,1},{4,6},{6,4},{5,7},{7,5},{8,10},{10,8},{9,1... | collective-permute-start | bytes 737288 | tf_op jit(solution)/shard_map/ppermute | solution.py:323
  101.9 12.4 %collective-permute-start.23 = (bf16[96,2048]{1,0:T(8,128)(2,1)S(1)}, bf16[96,2048]{1,0:T(8,128)(2,1)S(1)}, u32[]{:S(2)}, u32[]{:S(2)}) collective-permute-start(bf16[96,2048]{1,0:T(8,128)(2,1)S(1)} %get-tuple-element.40), channel_id=1, source_target_pairs={{0,4},{4,0},{8,12},{12,8},{16,20},{20,16},{24,28},{28,24},{1,5},{5... | collective-permute-start | bytes 1179656 | tf_op jit(solution)/shard_map/ppermute | solution.py:314
  102.9 11.5 %collective-permute-start.24 = (bf16[96,2048]{1,0:T(8,128)(2,1)S(1)}, bf16[96,2048]{1,0:T(8,128)(2,1)S(1)}, u32[]{:S(2)}, u32[]{:S(2)}) collective-permute-start(bf16[96,2048]{1,0:T(8,128)(2,1)S(1)} %shard_map.79.refs_3_), channel_id=1, source_target_pairs={{0,8},{4,12},{8,16},{12,20},{16,24},{20,28},{24,0},{28,4},{1,9},{5... | collective-permute-start | bytes 1179656 | tf_op jit(solution)/shard_map/ppermute | solution.py:317
  103.1 4.9 %collective-permute-start.21 = (bf16[160,384]{1,0:T(8,128)(2,1)S(1)}, bf16[160,384]{1,0:T(8,128)(2,1)S(1)}, u32[]{:S(2)}, u32[]{:S(2)}) collective-permute-start(bf16[160,384]{1,0:T(8,128)(2,1)S(1)} %fusion.3.refs_0_.refs_6_), channel_id=1, source_target_pairs={{0,2},{2,0},{1,3},{3,1},{4,6},{6,4},{5,7},{7,5},{8,10},{10,8},{9,1... | collective-permute-start | bytes 368648 | tf_op jit(solution)/shard_map/ppermute | solution.py:323
  113.0 7.8 %collective-permute-start.22 = (bf16[96,2048]{1,0:T(8,128)(2,1)S(1)}, bf16[96,2048]{1,0:T(8,128)(2,1)S(1)}, u32[]{:S(2)}, u32[]{:S(2)}) collective-permute-start(bf16[96,2048]{1,0:T(8,128)(2,1)S(1)} %shard_map.81.refs_3_), channel_id=1, source_target_pairs={{0,4},{4,0},{8,12},{12,8},{16,20},{20,16},{24,28},{28,24},{1,5},{5... | collective-permute-start | bytes 1179656 | tf_op jit(solution)/shard_map/ppermute | solution.py:314
  114.5 12.4 %collective-permute-start.25 = (bf16[96,2048]{1,0:T(8,128)(2,1)S(1)}, bf16[96,2048]{1,0:T(8,128)(2,1)S(1)}, u32[]{:S(2)}, u32[]{:S(2)}) collective-permute-start(bf16[96,2048]{1,0:T(8,128)(2,1)S(1)} %shard_map.82.refs_3_), channel_id=1, source_target_pairs={{0,8},{4,12},{8,16},{12,20},{16,24},{20,28},{24,0},{28,4},{1,9},{5... | collective-permute-start | bytes 1179656 | tf_op jit(solution)/shard_map/ppermute | solution.py:317
  127.0 9.6 %collective-permute-start.26 = (bf16[96,2048]{1,0:T(8,128)(2,1)S(1)}, bf16[96,2048]{1,0:T(8,128)(2,1)S(1)}, u32[]{:S(2)}, u32[]{:S(2)}) collective-permute-start(bf16[96,2048]{1,0:T(8,128)(2,1)S(1)} %shard_map.83), channel_id=1, source_target_pairs={{0,8},{4,12},{8,16},{12,20},{16,24},{20,28},{24,0},{28,4},{1,9},{5... | collective-permute-start | bytes 1179656 | tf_op jit(solution)/shard_map/ppermute | solution.py:317

commit v6 on v5

--- a/solution.py
+++ b/solution.py
@@ -10,8 +10,7 @@
 F32 = jnp.float32
 BF16 = jnp.bfloat16
 LANES = 128
-VMEM = 12 * 1024 * 1024
-SMEM = pl.BlockSpec(memory_space=pltpu.SMEM)
+VMEM = 10 * 1024 * 1024
 ANY = pl.BlockSpec(memory_space=pl.ANY)
 HBM = pl.BlockSpec(memory_space=pltpu.HBM)
 
@@ -138,15 +137,23 @@
         out_ref[rows, units + full:] = y[:, units - full:]
 
 
-def pick_kernel(width, experts, capacity, units, groups, count, kinds, split, scalars, *refs):
+def position(units):
+    core, rank, parts = lax.axis_index("dp"), lax.axis_index("tensor"), lax.axis_size("tensor")
+    first = lax.axis_index("expert") * 2
+    places = [(rank + parts - s) % parts * units for s in range(parts)]
+    return (first + core, first + 1 - core), (rank + 1) % parts * units, rank * units, places
+
+
+def pick_kernel(width, experts, capacity, units, groups, count, kinds, split, *refs):
     blocks, weights = refs[:count], refs[count:]
     chosen_ref, part_ref = refs[-2:]
     rows = blocks[0].shape[0]
+    mine_and_other, start, _, _ = position(units)
     offsets = layout(groups, capacity)
     step = tile(width, (512, 256))
     for g, (expert, members) in enumerate(groups):
         tails = jnp.concatenate([blocks[m][:, width:] for m in members], axis=0)
-        slot = slot_row(tails, scalars[expert], experts, rows, capacity)
+        slot = slot_row(tails, mine_and_other[expert], experts, rows, capacity)
         here = offsets[g + 1] - offsets[g]
         place = lax.broadcasted_iota(jnp.int32, (here, len(members) * rows), 0)
         pick = jnp.where(place == slot, 1.0, 0.0).astype(BF16)
@@ -156,10 +163,10 @@
             chosen_ref[offsets[g]:offsets[g + 1], column:column + step] = value
     for g in range(len(groups)):
         mine = weights[kinds * g:kinds * (g + 1)]
-        multiply(chosen_ref, slice(offsets[g], offsets[g + 1]), mine, scalars[2] if split else None, units, part_ref)
-
-
-def pick_rows(scalars, groups, blocks, weights, split, after, width, experts, capacity, units):
+        multiply(chosen_ref, slice(offsets[g], offsets[g + 1]), mine, start if split else None, units, part_ref)
+
+
+def pick_rows(groups, blocks, weights, split, after, width, experts, capacity, units):
     columns = 2 * units if split else weights[0][0].shape[1]
     taken = layout(groups, capacity)[-1]
     flat = [w for expert, _ in groups for w in weights[expert]]
@@ -171,30 +178,31 @@
         kernel,
         grid=(1,),
         out_shape=out,
-        in_specs=[SMEM] + [whole(x) for x in (*blocks, *flat)] + [ANY] * len(after),
+        in_specs=[whole(x) for x in (*blocks, *flat)] + [ANY] * len(after),
         out_specs=tuple(whole(o) for o in out),
         compiler_params=params(),
         cost_estimate=cost(),
-    )(scalars, *blocks, *flat, *after)
-
-
-def home_kernel(capacity, units, groups, kinds, split, passed, scalars, x_ref, *refs):
+    )(*blocks, *flat, *after)
+
+
+def home_kernel(capacity, units, groups, kinds, split, passed, x_ref, *refs):
+    _, _, start, _ = position(units)
     out_ref = refs[-1 - passed]
     offsets = layout(groups, capacity)
     for g in range(len(groups)):
         mine = refs[kinds * g:kinds * (g + 1)]
-        multiply(x_ref, slice(offsets[g], offsets[g + 1]), mine, scalars[3] if split else None, units, out_ref)
-
-
-def home_rows(scalars, groups, chosen, weights, split, passing, after, capacity, units):
+        multiply(x_ref, slice(offsets[g], offsets[g + 1]), mine, start if split else None, units, out_ref)
+
+
+def home_rows(groups, chosen, weights, split, passing, after, capacity, units):
     flat = [w for expert, _ in groups for w in weights[expert]]
     out = jax.ShapeDtypeStruct((chosen.shape[0], 2 * units), F32)
-    args = (scalars, chosen, *flat, *after, *passing)
+    args = (chosen, *flat, *after, *passing)
     result = pl.pallas_call(
         functools.partial(home_kernel, capacity, units, groups, len(weights[0]), split, len(passing)),
         grid=(1,),
         out_shape=(out, *[jax.ShapeDtypeStruct(p.shape, p.dtype) for p in passing]),
-        in_specs=[SMEM, whole(chosen)] + [whole(w) for w in flat] + [ANY] * (len(after) + len(passing)),
+        in_specs=[whole(chosen)] + [whole(w) for w in flat] + [ANY] * (len(after) + len(passing)),
         out_specs=(whole(out), *[ANY] * len(passing)),
         input_output_aliases={len(args) - len(passing) + i: 1 + i for i in range(len(passing))},
         compiler_params=params(),
@@ -203,54 +211,50 @@
     return result[0], result[1:]
 
 
-def down_kernel(experts, capacity, groups, count, pieces, wide, passed, scalars, *refs):
+def down_kernel(experts, capacity, groups, count, pieces, wide, passed, *refs):
     hiddens, refs = refs[:pieces], refs[pieces:]
     tail_refs, weights = refs[:count], refs[count:]
-    scratch = refs[-2 * len(groups):]
-    out_ref = refs[-2 * len(groups) - 1 - passed]
+    scratch = refs[-len(groups):]
+    out_ref = refs[-len(groups) - 1 - passed]
     rows = tail_refs[0].shape[0]
     units = hiddens[0].shape[1]
+    mine_and_other, _, _, starts = position(units)
     offsets = layout(groups, capacity)
-    starts = [scalars[4 + s] for s in range(pieces)]
+    width = out_ref.shape[1]
+    step = tile(width, (256,))
+    shares = []
     for g, (expert, members) in enumerate(groups):
-        spread_ref, weight_ref = scratch[2 * g:2 * g + 2]
         tails = jnp.concatenate([tail_refs[m][...] for m in members], axis=0)
-        slot, weight = slot_column(tails, scalars[expert], experts, rows, capacity)
-        weight_ref[...] = weight
+        slot, weight = slot_column(tails, mine_and_other[expert], experts, rows, capacity)
+        shares.append(jnp.broadcast_to(weight, (len(members) * rows, step)))
         place = lax.broadcasted_iota(jnp.int32, (len(members) * rows, offsets[g + 1] - offsets[g]), 1)
         spread = jnp.where(place == slot, 1.0, 0.0).astype(BF16)
         for s, ref in enumerate(hiddens):
             value = jnp.dot(spread, ref[offsets[g]:offsets[g + 1], :], preferred_element_type=F32).astype(BF16)
             if wide:
-                spread_ref[:, pl.ds(pl.multiple_of(starts[s], LANES), units)] = value
+                scratch[g][:, pl.ds(pl.multiple_of(starts[s], LANES), units)] = value
             else:
-                spread_ref[s] = value
-    width = out_ref.shape[1]
-    step = tile(width, (256,))
-
-    @pl.loop(0, width // step)
-    def _(i):
-        span = pl.ds(pl.multiple_of(i * step, LANES), step)
+                scratch[g][s] = value
+    for column in range(0, width, step):
         sums = [None] * count
         for g, (expert, members) in enumerate(groups):
-            spread_ref, weight_ref = scratch[2 * g:2 * g + 2]
             w_ref = weights[g]
             if wide:
-                result = jnp.dot(spread_ref[...], w_ref[:, span], preferred_element_type=F32)
+                result = jnp.dot(scratch[g][...], w_ref[:, column:column + step], preferred_element_type=F32)
             else:
                 result = jnp.zeros((len(members) * rows, step), F32)
                 for s in range(pieces):
-                    w = w_ref[pl.ds(pl.multiple_of(starts[s], 16), units), span]
-                    result = result + jnp.dot(spread_ref[s], w, preferred_element_type=F32)
-            result = result * weight_ref[...]
+                    w = w_ref[pl.ds(pl.multiple_of(starts[s], 16), units), column:column + step]
+                    result = result + jnp.dot(scratch[g][s], w, preferred_element_type=F32)
+            result = result * shares[g]
             for k, m in enumerate(members):
                 part = result[k * rows:(k + 1) * rows]
                 sums[m] = part if sums[m] is None else sums[m] + part
         for m, value in enumerate(sums):
-            out_ref[m * rows:(m + 1) * rows, span] = value.astype(BF16)
-
-
-def down_rows(scalars, groups, hiddens, blocks, weights, passing, after, width, experts, capacity):
+            out_ref[m * rows:(m + 1) * rows, column:column + step] = value.astype(BF16)
+
+
+def down_rows(groups, hiddens, blocks, weights, passing, after, width, experts, capacity):
     rows, padded = blocks[0].shape
     units = hiddens[0].shape[1]
     pieces = len(hiddens)
@@ -259,14 +263,14 @@
     scratch = []
     for _, members in groups:
         spread = (len(members) * rows, pieces * units) if wide else (pieces, len(members) * rows, units)
-        scratch += [pltpu.VMEM(spread, BF16), pltpu.VMEM((len(members) * rows, 1), F32)]
+        scratch.append(pltpu.VMEM(spread, BF16))
     out = jax.ShapeDtypeStruct((len(blocks) * rows, width), BF16)
-    args = (scalars, *hiddens, *blocks, *[weights[e] for e, _ in groups], *after, *passing)
+    args = (*hiddens, *blocks, *[weights[e] for e, _ in groups], *after, *passing)
     result = pl.pallas_call(
         functools.partial(down_kernel, experts, capacity, groups, len(blocks), pieces, wide, len(passing)),
         grid=(1,),
         out_shape=(out, *[jax.ShapeDtypeStruct(p.shape, p.dtype) for p in passing]),
-        in_specs=[SMEM] + [whole(h) for h in hiddens] + [tail] * len(blocks)
+        in_specs=[whole(h) for h in hiddens] + [tail] * len(blocks)
         + [whole(weights[0])] * len(groups) + [ANY] * (len(after) + len(passing)),
         out_specs=(whole(out), *[ANY] * len(passing)),
         input_output_aliases={len(args) - len(passing) + i: 1 + i for i in range(len(passing))},
@@ -306,7 +310,6 @@
     capacity = min(rows, max(2, 3 * rows * top // (2 * experts)))
     parts = lax.axis_size("tensor")
     units = w_gate.shape[2] // parts
-    core = lax.axis_index("dp")
     rank = lax.axis_index("tensor")
     hops = ring // 2
 
@@ -322,10 +325,6 @@
     def over_x(x, step):
         return lax.ppermute(x, "tensor", [(i, (i + step) % parts) for i in range(parts)])
 
-    first = lax.axis_index("expert") * 2
-    scalars = [first + core, first + 1 - core, (rank + 1) % parts * units, rank * units]
-    scalars += [(rank + parts - s) % parts * units for s in range(parts)]
-    scalars = jnp.stack([jnp.asarray(s, jnp.int32) for s in scalars])
     gates = (w_gate[0], over_core(w_gate)[0])
     ups = (w_up[0], over_core(w_up)[0])
     split = parts == 2 and units % LANES == 0
@@ -357,7 +356,7 @@
     count = len(plan)
     chosen, parts_in, totals, hidden, returned, carried, gathered = {}, {}, {}, {}, {}, {}, []
     downs = [w_down[0], over_core(w_down)[0]]
-    order = [scalars]
+    order = []
 
     def passing(hop):
         return [arrived[hop]] if hop in arrived else []
@@ -370,13 +369,13 @@
     def pick(i):
         keys, groups = plan[i]
         mine = [blocks[k] for k in keys]
-        chosen[i], part = pick_rows(scalars, groups, mine, away, split, order, width, experts, capacity, units)
+        chosen[i], part = pick_rows(groups, mine, away, split, order, width, experts, capacity, units)
         parts_in[i] = [over_x(part[:, 2 * units * (s - 1):2 * units * s], s) for s in range(1, parts)]
         order[:] = [part]
 
     def home_product(i, hop=None):
         totals[i], passed = home_rows(
-            scalars, plan[i][1], chosen[i], home, split, passing(hop), order, capacity, units
+            plan[i][1], chosen[i], home, split, passing(hop), order, capacity, units
         )
         order[:] = [totals[i]]
         take_on(hop, passed)
@@ -393,7 +392,7 @@
         keys, groups = plan[i]
         mine = [blocks[k] for k in keys]
         term, passed = down_rows(
-            scalars, groups, hidden[i], mine, downs, passing(hop), order, width, experts, capacity
+            groups, hidden[i], mine, downs, passing(hop), order, width, experts, capacity
         )
         order[:] = [term]
         take_on(hop, passed)

time: 138 us -> 118 us (0.86)
  Pallas kernels: 59.3 us -> 26.1 us
  waiting for transfers between devices: 43.9 us -> 58.2 us
    pallas_call x5, Pallas kernels: 24.9 us -> 10 us  [down_rows(): pl.pallas_call(functools.partial(down_kernel, experts, capacity, groups,...]
    pallas_call x5, Pallas kernels: 18.7 us -> 9.52 us  [pick_rows(): pl.pallas_call(kernel, grid=(1,), out_shape=out, in_specs=[whole(x) for x...]
    ppermute x10, waiting for transfers between devices: 3.37 us -> 12.3 us  [over_x(): lax.ppermute(x, 'tensor', [(i, (i + step) % parts) for i in range(parts)])]
    pallas_call x5, Pallas kernels: 13.9 us -> 5.57 us  [home_rows(): pl.pallas_call(functools.partial(home_kernel, capacity, units, groups, le...]
    ppermute x6, waiting for transfers between devices: 34.3 us -> 41.4 us  [over_z(): return lax.ppermute(x, 'expert', [(i, (i + 2) % ring) for i in range(ring)])]
    ppermute x8, waiting for transfers between devices: 6.21 us -> 4.54 us  [over_y(): return lax.ppermute(x, 'expert', [(i, i ^ 1) for i in range(ring)])]
  transfers between devices with their start and end apart: 27 -> 27, of which waited for: 7 -> 15; matrix products, arithmetic and copies ran while one was open for 1% -> 1% of each run, Pallas kernels for 43% -> 22%
where the time goes in v6:
time: 118 us
  waiting for transfers between devices  58.2 us (49%)
  Pallas kernels  26.1 us (22%)
  starting transfers between devices  25.3 us (21%)
  local copies, waits for them, and re-layouts  6.35 us (5%)
  other arithmetic  1.75 us (1%)
    ppermute x6, waiting for transfers between devices, over_z(): return lax.ppermute(x, 'expert', [(i, (i + 2) % ring) for i in range(ring)])  41.4 us
    ppermute x10, waiting for transfers between devices, over_x(): lax.ppermute(x, 'tensor', [(i, (i + step) % parts) for i in range(parts)])  12.3 us
    ppermute x10, starting transfers between devices, over_x(): lax.ppermute(x, 'tensor', [(i, (i + step) % parts) for i in range(parts)])  12.2 us
    pallas_call x5, Pallas kernels, down_rows(): pl.pallas_call(functools.partial(down_kernel, experts, capacity, groups,...  10 us
    pallas_call x5, Pallas kernels, pick_rows(): pl.pallas_call(kernel, grid=(1,), out_shape=out, in_specs=[whole(x) for x...  9.52 us
    ppermute x8, starting transfers between devices, over_y(): return lax.ppermute(x, 'expert', [(i, i ^ 1) for i in range(ring)])  9.04 us
    unnamed x16, local copies, waits for them, and re-layouts  6.16 us
    pallas_call x5, Pallas kernels, home_rows(): pl.pallas_call(functools.partial(home_kernel, capacity, units, groups, le...  5.57 us
  transfers between devices with their start and end apart: 27, of which 15 were waited for; matrix products, arithmetic and copies ran while one was open for 1% of the time, Pallas kernels for 22%

profile of v6, /device:TPU:0, one launch (start us, length us, event | category | flops | bytes accessed | tf_op | source)
XLA Modules:
  0.0 118.0 jit_solution(15446524368450778509)
XLA Ops:
  0.0 0.5 collective-permute-start
  0.5 0.5 collective-permute-start.7
  1.0 1.0 copy-done.5
  2.0 0.7 copy-done.6
  2.7 0.7 copy-done.7
  3.3 0.5 shard_map.64.refs_0_.refs_2_
  3.8 2.6 %collective-permute-start.2 = (bf16[96,2176]{1,0:T(8,128)(2,1)S(1)}, bf16[96,2176]{1,0:T(8,128)(2,1)S(1)}, u32[]{:S(2)}, u32[]{:S(2)}) collective-permute-start(bf16[96,2176]{1,0:T(8,128)(2,1)S(1)} %shard_map.64.refs_0_.refs_2_), channel_id=1, source_target_pairs={{0,8},{4,12},{8,16},{12,20},{16,24},{20,28},{24,0},{28,4},{1,9},{5... | collective-permute-start | bytes 1253384 | tf_op jit(solution)/shard_map/ppermute | solution.py:320
  6.5 1.5 %collective-permute-start.6 = (bf16[96,2176]{1,0:T(8,128)(2,1)S(1)}, bf16[96,2176]{1,0:T(8,128)(2,1)S(1)}, u32[]{:S(2)}, u32[]{:S(2)}) collective-permute-start(bf16[96,2176]{1,0:T(8,128)(2,1)S(1)} %shard_map.64.refs_0_.refs_2_), channel_id=1, source_target_pairs={{0,4},{4,0},{8,12},{12,8},{16,20},{20,16},{24,28},{28,24},{1,5},{5... | collective-permute-start | bytes 1253384 | tf_op jit(solution)/shard_map/ppermute | solution.py:317
  8.0 1.9 %copy-done = bf16[1,2048,768]{2,1,0:T(8,128)(2,1)S(1)} copy-done((bf16[1,2048,768]{2,1,0:T(8,128)(2,1)S(1)}, bf16[1,2048,768]{2,1,0:T(8,128)(2,1)}, u32[]{:S(2)}) %copy-start) | copy-done | bytes 3145752
  9.9 1.9 %copy-done.2 = bf16[1,2048,768]{2,1,0:T(8,128)(2,1)S(1)} copy-done((bf16[1,2048,768]{2,1,0:T(8,128)(2,1)S(1)}, bf16[1,2048,768]{2,1,0:T(8,128)(2,1)}, u32[]{:S(2)}) %copy-start.2) | copy-done | bytes 3145752
  11.8 1.1 shard_map.65
  12.8 5.9 %collective-permute-done.2.refs_5_ = bf16[96,2176]{1,0:T(8,128)(2,1)S(1)} collective-permute-done((bf16[96,2176]{1,0:T(8,128)(2,1)S(1)}, bf16[96,2176]{1,0:T(8,128)(2,1)S(1)}, u32[]{:S(2)}, u32[]{:S(2)}) %collective-permute-start.2) | collective-permute-done | bytes 417824 | tf_op jit(solution)/shard_map/ppermute | solution.py:320
  18.8 1.5 %collective-permute-start.3 = (bf16[80,768]{1,0:T(8,128)(2,1)S(1)}, bf16[80,768]{1,0:T(8,128)(2,1)S(1)}, u32[]{:S(2)}, u32[]{:S(2)}) collective-permute-start(bf16[80,768]{1,0:T(8,128)(2,1)S(1)} %get-tuple-element.22.refs_2_), channel_id=1, source_target_pairs={{0,2},{2,0},{1,3},{3,1},{4,6},{6,4},{5,7},{7,5},{8,10},{10,8},{9,1... | collective-permute-start | bytes 368648 | tf_op jit(solution)/shard_map/ppermute | solution.py:326
  20.3 0.7 shard_map.66
  21.0 2.6 %shard_map.67 = (bf16[368,2048]{1,0:T(8,128)(2,1)S(1)}, bf16[368,768]{1,0:T(8,128)(2,1)S(1)}) custom-call(bf16[96,2176]{1,0:T(8,128)(2,1)S(1)} %shard_map.64.refs_0_.refs_2_, bf16[96,2176]{1,0:T(8,128)(2,1)S(1)} %collective-permute-done.6.refs_1_.refs_3_, bf16[96,2176]{1,0:T(8,128)(2,1)S(1)} %get-tuple-element.24.refs_2_.refs_4_, ...), custom_call_target="tpu_custom_call" | custom-call | flops 1 | bytes 1 | tf_op jit(solution)/shard_map/pallas_call | solution.py:177
  23.6 0.6 collective-permute-start.9
  24.2 1.5 %collective-permute-start.5 = (bf16[96,2176]{1,0:T(8,128)(2,1)S(1)}, bf16[96,2176]{1,0:T(8,128)(2,1)S(1)}, u32[]{:S(2)}, u32[]{:S(2)}) collective-permute-start(bf16[96,2176]{1,0:T(8,128)(2,1)S(1)} %get-tuple-element.24.refs_2_.refs_4_), channel_id=1, source_target_pairs={{0,4},{4,0},{8,12},{12,8},{16,20},{20,16},{24,28},{28,24},{1,5},{5... | collective-permute-start | bytes 1253384 | tf_op jit(solution)/shard_map/ppermute | solution.py:317
  25.8 1.6 %collective-permute-start.4 = (bf16[80,384]{1,0:T(8,128)(2,1)S(1)}, bf16[80,384]{1,0:T(8,128)(2,1)S(1)}, u32[]{:S(2)}, u32[]{:S(2)}) collective-permute-start(bf16[80,384]{1,0:T(8,128)(2,1)S(1)} %fusion.4.refs_5_.refs_0_), channel_id=1, source_target_pairs={{0,2},{2,0},{1,3},{3,1},{4,6},{6,4},{5,7},{7,5},{8,10},{10,8},{9,1... | collective-permute-start | bytes 184328 | tf_op jit(solution)/shard_map/ppermute | solution.py:326
  27.3 9.5 %collective-permute-done.8.refs_7_ = bf16[96,2176]{1,0:T(8,128)(2,1)S(1)} collective-permute-done((bf16[96,2176]{1,0:T(8,128)(2,1)S(1)}, bf16[96,2176]{1,0:T(8,128)(2,1)S(1)}, u32[]{:S(2)}, u32[]{:S(2)}) %collective-permute-start.8) | collective-permute-done | bytes 417824 | tf_op jit(solution)/shard_map/ppermute | solution.py:320
  36.9 1.4 %shard_map.68 = (f32[368,768]{1,0:T(8,128)S(1)}, bf16[96,2176]{1,0:T(8,128)(2,1)S(1)}) custom-call(bf16[368,2048]{1,0:T(8,128)(2,1)S(1)} %get-tuple-element.25.x_ref, bf16[2048,768]{1,0:T(8,128)(2,1)S(1)} %bitcast.30, bf16[2048,768]{1,0:T(8,128)(2,1)S(1)} %bitcast.39, bf16[2048,768]{1,0:T(8,128)(2,1)S(1)} %bitcast.11, ...), custom_call_target="tpu_custom_call", output_to_operand_aliasing={{1}: (8, {})} | custom-call | flops 1 | bytes 1 | tf_op jit(solution)/shard_map/pallas_call | solution.py:201
  38.3 0.2 collective-permute-start.10
  38.5 1.5 %collective-permute-start.11 = (bf16[96,2176]{1,0:T(8,128)(2,1)S(1)}, bf16[96,2176]{1,0:T(8,128)(2,1)S(1)}, u32[]{:S(2)}, u32[]{:S(2)}) collective-permute-start(bf16[96,2176]{1,0:T(8,128)(2,1)S(1)} %get-tuple-element.27.refs_1_.refs_3_), channel_id=1, source_target_pairs={{0,4},{4,0},{8,12},{12,8},{16,20},{20,16},{24,28},{28,24},{1,5},{5... | collective-permute-start | bytes 1253384 | tf_op jit(solution)/shard_map/ppermute | solution.py:317
  40.0 2.0 %shard_map.69 = (bf16[288,2048]{1,0:T(8,128)(2,1)S(1)}, bf16[288,768]{1,0:T(8,128)(2,1)S(1)}) custom-call(bf16[96,2176]{1,0:T(8,128)(2,1)S(1)} %collective-permute-done.5.refs_0_.refs_2_, bf16[96,2176]{1,0:T(8,128)(2,1)S(1)} %get-tuple-element.27.refs_1_.refs_3_, bf16[2048,768]{1,0:T(8,128)(2,1)S(1)} %bitcast.12, bf16[2048,768]{1,0:T(8,128)(2,1)S(1)} %bitcast.22, ...), custom_call_target="tpu_custom_call" | custom-call | flops 1 | bytes 1 | tf_op jit(solution)/shard_map/pallas_call | solution.py:177
  41.9 1.5 %collective-permute-start.13 = (bf16[288,768]{1,0:T(8,128)(2,1)S(1)}, bf16[288,768]{1,0:T(8,128)(2,1)S(1)}, u32[]{:S(2)}, u32[]{:S(2)}) collective-permute-start(bf16[288,768]{1,0:T(8,128)(2,1)S(1)} %get-tuple-element.30.refs_4_), channel_id=1, source_target_pairs={{0,2},{2,0},{1,3},{3,1},{4,6},{6,4},{5,7},{7,5},{8,10},{10,8},{9,1... | collective-permute-start | bytes 1327112 | tf_op jit(solution)/shard_map/ppermute | solution.py:326
  43.6 0.2 fusion.refs_5_.refs_0_
  43.8 0.6 collective-permute-start.12
  44.4 5.9 %collective-permute-done.10.refs_6_ = bf16[96,2176]{1,0:T(8,128)(2,1)S(1)} collective-permute-done((bf16[96,2176]{1,0:T(8,128)(2,1)S(1)}, bf16[96,2176]{1,0:T(8,128)(2,1)S(1)}, u32[]{:S(2)}, u32[]{:S(2)}) %collective-permute-start.10) | collective-permute-done | bytes 417824 | tf_op jit(solution)/shard_map/ppermute | solution.py:320
  50.3 1.1 shard_map.70
  51.4 1.3 %collective-permute-start.19 = (bf16[96,2176]{1,0:T(8,128)(2,1)S(1)}, bf16[96,2176]{1,0:T(8,128)(2,1)S(1)}, u32[]{:S(2)}, u32[]{:S(2)}) collective-permute-start(bf16[96,2176]{1,0:T(8,128)(2,1)S(1)} %get-tuple-element.32.refs_1_.refs_3_), channel_id=1, source_target_pairs={{0,4},{4,0},{8,12},{12,8},{16,20},{20,16},{24,28},{28,24},{1,5},{5... | collective-permute-start | bytes 1253384 | tf_op jit(solution)/shard_map/ppermute | solution.py:317
  52.8 1.1 shard_map.71.refs_6_.refs_0_
  53.9 1.3 %collective-permute-done.13 = bf16[288,768]{1,0:T(8,128)(2,1)S(1)} collective-permute-done((bf16[288,768]{1,0:T(8,128)(2,1)S(1)}, bf16[288,768]{1,0:T(8,128)(2,1)S(1)}, u32[]{:S(2)}, u32[]{:S(2)}) %collective-permute-start.13) | collective-permute-done | bytes 442400 | tf_op jit(solution)/shard_map/ppermute | solution.py:326
  55.2 0.1 fusion.2.refs_7_.refs_0_
  55.3 1.5 %collective-permute-start.15 = (bf16[288,384]{1,0:T(8,128)(2,1)S(1)}, bf16[288,384]{1,0:T(8,128)(2,1)S(1)}, u32[]{:S(2)}, u32[]{:S(2)}) collective-permute-start(bf16[288,384]{1,0:T(8,128)(2,1)S(1)} %fusion.2.refs_7_.refs_0_), channel_id=1, source_target_pairs={{0,2},{2,0},{1,3},{3,1},{4,6},{6,4},{5,7},{7,5},{8,10},{10,8},{9,1... | collective-permute-start | bytes 663560 | tf_op jit(solution)/shard_map/ppermute | solution.py:326
  56.9 2.0 %shard_map.72 = (bf16[288,2048]{1,0:T(8,128)(2,1)S(1)}, bf16[288,768]{1,0:T(8,128)(2,1)S(1)}) custom-call(bf16[96,2176]{1,0:T(8,128)(2,1)S(1)} %collective-permute-done.11.refs_5_.refs_0_.refs_2_, bf16[96,2176]{1,0:T(8,128)(2,1)S(1)} %get-tuple-element.32.refs_1_.refs_3_, bf16[2048,768]{1,0:T(8,128)(2,1)S(1)} %bitcast.14, bf16[2048,768]{1,0:T(8,128)(2,1)S(1)} %bitcast.24, ...), custom_call_target="tpu_custom_call" | custom-call | flops 1 | bytes 1 | tf_op jit(solution)/shard_map/pallas_call | solution.py:177
  58.9 0.6 collective-permute-start.17
  59.5 1.1 shard_map.73.refs_7_
  60.6 0.6 collective-permute-done.12.refs_1_
  61.2 2.7 %shard_map.74.refs_6_ = bf16[288,2048]{1,0:T(8,128)(2,1)S(1)} custom-call(bf16[368,384]{1,0:T(8,128)(2,1)S(1)} %fusion.refs_5_.refs_0_, bf16[368,384]{1,0:T(8,128)(2,1)S(1)} %collective-permute-done.12.refs_1_, bf16[96,2176]{1,0:T(8,128)(2,1)S(1)} %shard_map.64.refs_0_.refs_2_, bf16[96,2176]{1,0:T(8,128)(2,1)S(1)} %collective-permute-done.6.refs_1_.refs_3_, ...), custom_call_target="tpu_custom_call" | custom-call | flops 1 | bytes 1 | tf_op jit(solution)/shard_map/pallas_call | solution.py:269
  64.0 0.7 collective-permute-start.14
  64.7 1.3 %collective-permute-done.15.refs_1_ = bf16[288,384]{1,0:T(8,128)(2,1)S(1)} collective-permute-done((bf16[288,384]{1,0:T(8,128)(2,1)S(1)}, bf16[288,384]{1,0:T(8,128)(2,1)S(1)}, u32[]{:S(2)}, u32[]{:S(2)}) %collective-permute-start.15) | collective-permute-done | bytes 221216 | tf_op jit(solution)/shard_map/ppermute | solution.py:326
  65.9 2.3 %shard_map.75.refs_5_ = bf16[192,2048]{1,0:T(8,128)(2,1)S(1)} custom-call(bf16[288,384]{1,0:T(8,128)(2,1)S(1)} %fusion.2.refs_7_.refs_0_, bf16[288,384]{1,0:T(8,128)(2,1)S(1)} %collective-permute-done.15.refs_1_, bf16[96,2176]{1,0:T(8,128)(2,1)S(1)} %collective-permute-done.5.refs_0_.refs_2_, bf16[96,2176]{1,0:T(8,128)(2,1)S(1)} %get-tuple-element.27.refs_1_.refs_3_, ...), custom_call_target="tpu_custom_call" | custom-call | flops 1 | bytes 1 | tf_op jit(solution)/shard_map/pallas_call | solution.py:269
  68.2 4.2 %collective-permute-done.17 = bf16[288,768]{1,0:T(8,128)(2,1)S(1)} collective-permute-done((bf16[288,768]{1,0:T(8,128)(2,1)S(1)}, bf16[288,768]{1,0:T(8,128)(2,1)S(1)}, u32[]{:S(2)}, u32[]{:S(2)}) %collective-permute-start.17) | collective-permute-done | bytes 442400 | tf_op jit(solution)/shard_map/ppermute | solution.py:326
  72.5 0.1 fusion.1.refs_0_.refs_7_
  72.6 1.5 %collective-permute-start.18 = (bf16[288,384]{1,0:T(8,128)(2,1)S(1)}, bf16[288,384]{1,0:T(8,128)(2,1)S(1)}, u32[]{:S(2)}, u32[]{:S(2)}) collective-permute-start(bf16[288,384]{1,0:T(8,128)(2,1)S(1)} %fusion.1.refs_0_.refs_7_), channel_id=1, source_target_pairs={{0,2},{2,0},{1,3},{3,1},{4,6},{6,4},{5,7},{7,5},{8,10},{10,8},{9,1... | collective-permute-start | bytes 663560 | tf_op jit(solution)/shard_map/ppermute | solution.py:326
  74.2 0.6 collective-permute-start.16
  74.8 1.9 %shard_map.76 = (bf16[160,2048]{1,0:T(8,128)(2,1)S(1)}, bf16[160,768]{1,0:T(8,128)(2,1)S(1)}) custom-call(bf16[96,2176]{1,0:T(8,128)(2,1)S(1)} %collective-permute-done.19.refs_0_.refs_2_, bf16[2048,768]{1,0:T(8,128)(2,1)S(1)} %bitcast.16, bf16[2048,768]{1,0:T(8,128)(2,1)S(1)} %bitcast.26, bf16[2048,768]{1,0:T(8,128)(2,1)S(1)} %bitcast.35, ...), custom_call_target="tpu_custom_call" | custom-call | flops 1 | bytes 1 | tf_op jit(solution)/shard_map/pallas_call | solution.py:177
  76.7 1.1 collective-permute-start.20
  77.8 1.2 %shard_map.77.refs_6_ = f32[160,768]{1,0:T(8,128)S(1)} custom-call(bf16[160,2048]{1,0:T(8,128)(2,1)S(1)} %get-tuple-element.35.x_ref, bf16[2048,768]{1,0:T(8,128)(2,1)S(1)} %bitcast.17, bf16[2048,768]{1,0:T(8,128)(2,1)S(1)} %bitcast.27, bf16[2048,768]{1,0:T(8,128)(2,1)S(1)} %bitcast.36, bf16[2048,768]{1,0:T(8,128)(2,1)S(1)} %bitcast.45, ...), custom_call_target="tpu_custom_call" | custom-call | flops 1 | bytes 1 | tf_op jit(solution)/shard_map/pallas_call | solution.py:201
  79.1 1.9 %collective-permute-done.18.refs_1_ = bf16[288,384]{1,0:T(8,128)(2,1)S(1)} collective-permute-done((bf16[288,384]{1,0:T(8,128)(2,1)S(1)}, bf16[288,384]{1,0:T(8,128)(2,1)S(1)}, u32[]{:S(2)}, u32[]{:S(2)}) %collective-permute-start.18) | collective-permute-done | bytes 221216 | tf_op jit(solution)/shard_map/ppermute | solution.py:326
  81.0 2.3 %shard_map.78.refs_2_ = bf16[192,2048]{1,0:T(8,128)(2,1)S(1)} custom-call(bf16[288,384]{1,0:T(8,128)(2,1)S(1)} %fusion.1.refs_0_.refs_7_, bf16[288,384]{1,0:T(8,128)(2,1)S(1)} %collective-permute-done.18.refs_1_, bf16[96,2176]{1,0:T(8,128)(2,1)S(1)} %collective-permute-done.11.refs_5_.refs_0_.refs_2_, ...), custom_call_target="tpu_custom_call" | custom-call | flops 1 | bytes 1 | tf_op jit(solution)/shard_map/pallas_call | solution.py:269
  83.3 0.2 collective-permute-start.23
  83.5 0.2 collective-permute-done.16.refs_1_
  84.1 1.7 %collective-permute-start.21 = (bf16[160,384]{1,0:T(8,128)(2,1)S(1)}, bf16[160,384]{1,0:T(8,128)(2,1)S(1)}, u32[]{:S(2)}, u32[]{:S(2)}) collective-permute-start(bf16[160,384]{1,0:T(8,128)(2,1)S(1)} %fusion.3.refs_0_.refs_6_), channel_id=1, source_target_pairs={{0,2},{2,0},{1,3},{3,1},{4,6},{6,4},{5,7},{7,5},{8,10},{10,8},{9,1... | collective-permute-start | bytes 368648 | tf_op jit(solution)/shard_map/ppermute | solution.py:326
  85.8 0.2 shard_map.80.refs_5_
  85.9 3.1 %collective-permute-done.21.refs_1_ = bf16[160,384]{1,0:T(8,128)(2,1)S(1)} collective-permute-done((bf16[160,384]{1,0:T(8,128)(2,1)S(1)}, bf16[160,384]{1,0:T(8,128)(2,1)S(1)}, u32[]{:S(2)}, u32[]{:S(2)}) %collective-permute-start.21) | collective-permute-done | bytes 122912 | tf_op jit(solution)/shard_map/ppermute | solution.py:326
  89.0 1.7 %shard_map.81.refs_3_ = bf16[96,2048]{1,0:T(8,128)(2,1)S(1)} custom-call(bf16[160,384]{1,0:T(8,128)(2,1)S(1)} %fusion.3.refs_0_.refs_6_, bf16[160,384]{1,0:T(8,128)(2,1)S(1)} %collective-permute-done.21.refs_1_, bf16[96,2176]{1,0:T(8,128)(2,1)S(1)} %collective-permute-done.19.refs_0_.refs_2_, bf16[768,2048]{1,0:T(8,128)(2,1)S(1)} %bitcast.50, ...), custom_call_target="tpu_custom_call" | custom-call | flops 1 | bytes 1 | tf_op jit(solution)/shard_map/pallas_call | solution.py:269
  90.7 1.7 %collective-permute-start.22 = (bf16[96,2048]{1,0:T(8,128)(2,1)S(1)}, bf16[96,2048]{1,0:T(8,128)(2,1)S(1)}, u32[]{:S(2)}, u32[]{:S(2)}) collective-permute-start(bf16[96,2048]{1,0:T(8,128)(2,1)S(1)} %shard_map.81.refs_3_), channel_id=1, source_target_pairs={{0,4},{4,0},{8,12},{12,8},{16,20},{20,16},{24,28},{28,24},{1,5},{5... | collective-permute-start | bytes 1179656 | tf_op jit(solution)/shard_map/ppermute | solution.py:317
  92.5 2.6 %collective-permute-done.24.refs_2_ = bf16[96,2048]{1,0:T(8,128)(2,1)S(1)} collective-permute-done((bf16[96,2048]{1,0:T(8,128)(2,1)S(1)}, bf16[96,2048]{1,0:T(8,128)(2,1)S(1)}, u32[]{:S(2)}, u32[]{:S(2)}) %collective-permute-start.24) | collective-permute-done | bytes 393248 | tf_op jit(solution)/shard_map/ppermute | solution.py:320
  95.1 0.1 shard_map.82.refs_3_
  95.3 4.3 %collective-permute-done.22.refs_1_ = bf16[96,2048]{1,0:T(8,128)(2,1)S(1)} collective-permute-done((bf16[96,2048]{1,0:T(8,128)(2,1)S(1)}, bf16[96,2048]{1,0:T(8,128)(2,1)S(1)}, u32[]{:S(2)}, u32[]{:S(2)}) %collective-permute-start.22) | collective-permute-done | bytes 393248 | tf_op jit(solution)/shard_map/ppermute | solution.py:317
  99.6 7.8 %collective-permute-done.25.refs_2_ = bf16[96,2048]{1,0:T(8,128)(2,1)S(1)} collective-permute-done((bf16[96,2048]{1,0:T(8,128)(2,1)S(1)}, bf16[96,2048]{1,0:T(8,128)(2,1)S(1)}, u32[]{:S(2)}, u32[]{:S(2)}) %collective-permute-start.25) | collective-permute-done | bytes 393248 | tf_op jit(solution)/shard_map/ppermute | solution.py:320
  107.4 0.1 shard_map.83
  107.6 9.6 %collective-permute-done.26 = bf16[96,2048]{1,0:T(8,128)(2,1)S(1)} collective-permute-done((bf16[96,2048]{1,0:T(8,128)(2,1)S(1)}, bf16[96,2048]{1,0:T(8,128)(2,1)S(1)}, u32[]{:S(2)}, u32[]{:S(2)}) %collective-permute-start.26) | collective-permute-done | bytes 393248 | tf_op jit(solution)/shard_map/ppermute | solution.py:320
  117.2 0.8 add_convert_fusion
  (40 shorter events, 1.1 us)
Async XLA Ops:
  0.0 20.3 %collective-permute-start = (bf16[1,2048,768]{2,1,0:T(8,128)(2,1)}, bf16[1,2048,768]{2,1,0:T(8,128)(2,1)S(1)}, u32[]{:S(2)}, u32[]{:S(2)}) collective-permute-start(bf16[1,2048,768]{2,1,0:T(8,128)(2,1)} %param.9), channel_id=1, source_target_pairs={{0,1},{1,0},{2,3},{3,2},{4,5},{5,4},{6,7},{7,6},{8,9},{9,8},{10,11... | collective-permute-start | bytes 9437192 | tf_op jit(solution)/shard_map/ppermute | solution.py:323
  0.5 19.8 %collective-permute-start.1 = (bf16[1,2048,768]{2,1,0:T(8,128)(2,1)}, bf16[1,2048,768]{2,1,0:T(8,128)(2,1)S(1)}, u32[]{:S(2)}, u32[]{:S(2)}) collective-permute-start(bf16[1,2048,768]{2,1,0:T(8,128)(2,1)} %param.10), channel_id=1, source_target_pairs={{0,1},{1,0},{2,3},{3,2},{4,5},{5,4},{6,7},{7,6},{8,9},{9,8},{10,11... | collective-permute-start | bytes 9437192 | tf_op jit(solution)/shard_map/ppermute | solution.py:323
  0.5 26.8 %collective-permute-start.7 = (bf16[1,768,2048]{2,1,0:T(8,128)(2,1)}, bf16[1,768,2048]{2,1,0:T(8,128)(2,1)S(1)}, u32[]{:S(2)}, u32[]{:S(2)}) collective-permute-start(bf16[1,768,2048]{2,1,0:T(8,128)(2,1)} %param.11), channel_id=1, source_target_pairs={{0,1},{1,0},{2,3},{3,2},{4,5},{5,4},{6,7},{7,6},{8,9},{9,8},{10,11... | collective-permute-start | bytes 9437192 | tf_op jit(solution)/shard_map/ppermute | solution.py:323
  1.0 1.0 copy-start.5
  2.0 0.7 copy-start.6
  2.6 0.7 copy-start.7
  3.8 15.0 %collective-permute-start.2 = (bf16[96,2176]{1,0:T(8,128)(2,1)S(1)}, bf16[96,2176]{1,0:T(8,128)(2,1)S(1)}, u32[]{:S(2)}, u32[]{:S(2)}) collective-permute-start(bf16[96,2176]{1,0:T(8,128)(2,1)S(1)} %shard_map.64.refs_0_.refs_2_), channel_id=1, source_target_pairs={{0,8},{4,12},{8,16},{12,20},{16,24},{20,28},{24,0},{28,4},{1,9},{5... | collective-permute-start | bytes 1253384 | tf_op jit(solution)/shard_map/ppermute | solution.py:320
  6.5 14.5 %collective-permute-start.6 = (bf16[96,2176]{1,0:T(8,128)(2,1)S(1)}, bf16[96,2176]{1,0:T(8,128)(2,1)S(1)}, u32[]{:S(2)}, u32[]{:S(2)}) collective-permute-start(bf16[96,2176]{1,0:T(8,128)(2,1)S(1)} %shard_map.64.refs_0_.refs_2_), channel_id=1, source_target_pairs={{0,4},{4,0},{8,12},{12,8},{16,20},{20,16},{24,28},{28,24},{1,5},{5... | collective-permute-start | bytes 1253384 | tf_op jit(solution)/shard_map/ppermute | solution.py:317
  8.0 1.9 %copy-start = (bf16[1,2048,768]{2,1,0:T(8,128)(2,1)S(1)}, bf16[1,2048,768]{2,1,0:T(8,128)(2,1)}, u32[]{:S(2)}) copy-start(bf16[1,2048,768]{2,1,0:T(8,128)(2,1)} %param.9) | copy-start | bytes 9437188
  9.9 1.9 %copy-start.2 = (bf16[1,2048,768]{2,1,0:T(8,128)(2,1)S(1)}, bf16[1,2048,768]{2,1,0:T(8,128)(2,1)}, u32[]{:S(2)}) copy-start(bf16[1,2048,768]{2,1,0:T(8,128)(2,1)} %param.10) | copy-start | bytes 9437188
  11.8 8.5 %copy-start.1 = (bf16[1,2048,768]{2,1,0:T(8,128)(2,1)S(1)}, bf16[1,2048,768]{2,1,0:T(8,128)(2,1)}, u32[]{:S(2)}) copy-start(bf16[1,2048,768]{2,1,0:T(8,128)(2,1)} %param.9) | copy-start | bytes 9437188
  11.8 8.5 %copy-start.3 = (bf16[1,2048,768]{2,1,0:T(8,128)(2,1)S(1)}, bf16[1,2048,768]{2,1,0:T(8,128)(2,1)}, u32[]{:S(2)}) copy-start(bf16[1,2048,768]{2,1,0:T(8,128)(2,1)} %param.10) | copy-start | bytes 9437188
  18.8 6.9 %collective-permute-start.3 = (bf16[80,768]{1,0:T(8,128)(2,1)S(1)}, bf16[80,768]{1,0:T(8,128)(2,1)S(1)}, u32[]{:S(2)}, u32[]{:S(2)}) collective-permute-start(bf16[80,768]{1,0:T(8,128)(2,1)S(1)} %get-tuple-element.22.refs_2_), channel_id=1, source_target_pairs={{0,2},{2,0},{1,3},{3,1},{4,6},{6,4},{5,7},{7,5},{8,10},{10,8},{9,1... | collective-permute-start | bytes 368648 | tf_op jit(solution)/shard_map/ppermute | solution.py:326
  23.6 19.9 %collective-permute-start.9 = (bf16[368,768]{1,0:T(8,128)(2,1)S(1)}, bf16[368,768]{1,0:T(8,128)(2,1)S(1)}, u32[]{:S(2)}, u32[]{:S(2)}) collective-permute-start(bf16[368,768]{1,0:T(8,128)(2,1)S(1)} %get-tuple-element.26.refs_4_), channel_id=1, source_target_pairs={{0,2},{2,0},{1,3},{3,1},{4,6},{6,4},{5,7},{7,5},{8,10},{10,8},{9,1... | collective-permute-start | bytes 1695752 | tf_op jit(solution)/shard_map/ppermute | solution.py:326
  24.2 12.7 %collective-permute-start.8 = (bf16[96,2176]{1,0:T(8,128)(2,1)S(1)}, bf16[96,2176]{1,0:T(8,128)(2,1)S(1)}, u32[]{:S(2)}, u32[]{:S(2)}) collective-permute-start(bf16[96,2176]{1,0:T(8,128)(2,1)S(1)} %get-tuple-element.24.refs_2_.refs_4_), channel_id=1, source_target_pairs={{0,8},{4,12},{8,16},{12,20},{16,24},{20,28},{24,0},{28,4},{1,9},{5... | collective-permute-start | bytes 1253384 | tf_op jit(solution)/shard_map/ppermute | solution.py:320
  24.2 15.8 %collective-permute-start.5 = (bf16[96,2176]{1,0:T(8,128)(2,1)S(1)}, bf16[96,2176]{1,0:T(8,128)(2,1)S(1)}, u32[]{:S(2)}, u32[]{:S(2)}) collective-permute-start(bf16[96,2176]{1,0:T(8,128)(2,1)S(1)} %get-tuple-element.24.refs_2_.refs_4_), channel_id=1, source_target_pairs={{0,4},{4,0},{8,12},{12,8},{16,20},{20,16},{24,28},{28,24},{1,5},{5... | collective-permute-start | bytes 1253384 | tf_op jit(solution)/shard_map/ppermute | solution.py:317
  25.8 27.0 %collective-permute-start.4 = (bf16[80,384]{1,0:T(8,128)(2,1)S(1)}, bf16[80,384]{1,0:T(8,128)(2,1)S(1)}, u32[]{:S(2)}, u32[]{:S(2)}) collective-permute-start(bf16[80,384]{1,0:T(8,128)(2,1)S(1)} %fusion.4.refs_5_.refs_0_), channel_id=1, source_target_pairs={{0,2},{2,0},{1,3},{3,1},{4,6},{6,4},{5,7},{7,5},{8,10},{10,8},{9,1... | collective-permute-start | bytes 184328 | tf_op jit(solution)/shard_map/ppermute | solution.py:326
  38.3 12.0 %collective-permute-start.10 = (bf16[96,2176]{1,0:T(8,128)(2,1)S(1)}, bf16[96,2176]{1,0:T(8,128)(2,1)S(1)}, u32[]{:S(2)}, u32[]{:S(2)}) collective-permute-start(bf16[96,2176]{1,0:T(8,128)(2,1)S(1)} %get-tuple-element.27.refs_1_.refs_3_), channel_id=1, source_target_pairs={{0,8},{4,12},{8,16},{12,20},{16,24},{20,28},{24,0},{28,4},{1,9},{5... | collective-permute-start | bytes 1253384 | tf_op jit(solution)/shard_map/ppermute | solution.py:320
  38.5 14.3 %collective-permute-start.11 = (bf16[96,2176]{1,0:T(8,128)(2,1)S(1)}, bf16[96,2176]{1,0:T(8,128)(2,1)S(1)}, u32[]{:S(2)}, u32[]{:S(2)}) collective-permute-start(bf16[96,2176]{1,0:T(8,128)(2,1)S(1)} %get-tuple-element.27.refs_1_.refs_3_), channel_id=1, source_target_pairs={{0,4},{4,0},{8,12},{12,8},{16,20},{20,16},{24,28},{28,24},{1,5},{5... | collective-permute-start | bytes 1253384 | tf_op jit(solution)/shard_map/ppermute | solution.py:317
  41.9 13.2 %collective-permute-start.13 = (bf16[288,768]{1,0:T(8,128)(2,1)S(1)}, bf16[288,768]{1,0:T(8,128)(2,1)S(1)}, u32[]{:S(2)}, u32[]{:S(2)}) collective-permute-start(bf16[288,768]{1,0:T(8,128)(2,1)S(1)} %get-tuple-element.30.refs_4_), channel_id=1, source_target_pairs={{0,2},{2,0},{1,3},{3,1},{4,6},{6,4},{5,7},{7,5},{8,10},{10,8},{9,1... | collective-permute-start | bytes 1327112 | tf_op jit(solution)/shard_map/ppermute | solution.py:326
  43.8 17.4 %collective-permute-start.12 = (bf16[368,384]{1,0:T(8,128)(2,1)S(1)}, bf16[368,384]{1,0:T(8,128)(2,1)S(1)}, u32[]{:S(2)}, u32[]{:S(2)}) collective-permute-start(bf16[368,384]{1,0:T(8,128)(2,1)S(1)} %fusion.refs_5_.refs_0_), channel_id=1, source_target_pairs={{0,2},{2,0},{1,3},{3,1},{4,6},{6,4},{5,7},{7,5},{8,10},{10,8},{9,1... | collective-permute-start | bytes 847880 | tf_op jit(solution)/shard_map/ppermute | solution.py:326
  50.3 2.5 %copy-start.4 = (bf16[1,768,2048]{2,1,0:T(8,128)(2,1)S(1)}, bf16[1,768,2048]{2,1,0:T(8,128)(2,1)}, u32[]{:S(2)}) copy-start(bf16[1,768,2048]{2,1,0:T(8,128)(2,1)} %param.11) | copy-start | bytes 9437188
  51.4 23.4 %collective-permute-start.19 = (bf16[96,2176]{1,0:T(8,128)(2,1)S(1)}, bf16[96,2176]{1,0:T(8,128)(2,1)S(1)}, u32[]{:S(2)}, u32[]{:S(2)}) collective-permute-start(bf16[96,2176]{1,0:T(8,128)(2,1)S(1)} %get-tuple-element.32.refs_1_.refs_3_), channel_id=1, source_target_pairs={{0,4},{4,0},{8,12},{12,8},{16,20},{20,16},{24,28},{28,24},{1,5},{5... | collective-permute-start | bytes 1253384 | tf_op jit(solution)/shard_map/ppermute | solution.py:317
  55.3 10.6 %collective-permute-start.15 = (bf16[288,384]{1,0:T(8,128)(2,1)S(1)}, bf16[288,384]{1,0:T(8,128)(2,1)S(1)}, u32[]{:S(2)}, u32[]{:S(2)}) collective-permute-start(bf16[288,384]{1,0:T(8,128)(2,1)S(1)} %fusion.2.refs_7_.refs_0_), channel_id=1, source_target_pairs={{0,2},{2,0},{1,3},{3,1},{4,6},{6,4},{5,7},{7,5},{8,10},{10,8},{9,1... | collective-permute-start | bytes 663560 | tf_op jit(solution)/shard_map/ppermute | solution.py:326
  58.9 13.5 %collective-permute-start.17 = (bf16[288,768]{1,0:T(8,128)(2,1)S(1)}, bf16[288,768]{1,0:T(8,128)(2,1)S(1)}, u32[]{:S(2)}, u32[]{:S(2)}) collective-permute-start(bf16[288,768]{1,0:T(8,128)(2,1)S(1)} %get-tuple-element.34.refs_4_), channel_id=1, source_target_pairs={{0,2},{2,0},{1,3},{3,1},{4,6},{6,4},{5,7},{7,5},{8,10},{10,8},{9,1... | collective-permute-start | bytes 1327112 | tf_op jit(solution)/shard_map/ppermute | solution.py:326
  64.0 21.8 %collective-permute-start.14 = (bf16[96,2048]{1,0:T(8,128)(2,1)S(1)}, bf16[96,2048]{1,0:T(8,128)(2,1)S(1)}, u32[]{:S(2)}, u32[]{:S(2)}) collective-permute-start(bf16[96,2048]{1,0:T(8,128)(2,1)S(1)} %get-tuple-element.38), channel_id=1, source_target_pairs={{0,4},{4,0},{8,12},{12,8},{16,20},{20,16},{24,28},{28,24},{1,5},{5... | collective-permute-start | bytes 1179656 | tf_op jit(solution)/shard_map/ppermute | solution.py:317
  72.6 8.4 %collective-permute-start.18 = (bf16[288,384]{1,0:T(8,128)(2,1)S(1)}, bf16[288,384]{1,0:T(8,128)(2,1)S(1)}, u32[]{:S(2)}, u32[]{:S(2)}) collective-permute-start(bf16[288,384]{1,0:T(8,128)(2,1)S(1)} %fusion.1.refs_0_.refs_7_), channel_id=1, source_target_pairs={{0,2},{2,0},{1,3},{3,1},{4,6},{6,4},{5,7},{7,5},{8,10},{10,8},{9,1... | collective-permute-start | bytes 663560 | tf_op jit(solution)/shard_map/ppermute | solution.py:326
  74.2 9.5 %collective-permute-start.16 = (bf16[96,2048]{1,0:T(8,128)(2,1)S(1)}, bf16[96,2048]{1,0:T(8,128)(2,1)S(1)}, u32[]{:S(2)}, u32[]{:S(2)}) collective-permute-start(bf16[96,2048]{1,0:T(8,128)(2,1)S(1)} %get-tuple-element.43), channel_id=1, source_target_pairs={{0,4},{4,0},{8,12},{12,8},{16,20},{20,16},{24,28},{28,24},{1,5},{5... | collective-permute-start | bytes 1179656 | tf_op jit(solution)/shard_map/ppermute | solution.py:317
  76.7 7.2 %collective-permute-start.20 = (bf16[160,768]{1,0:T(8,128)(2,1)S(1)}, bf16[160,768]{1,0:T(8,128)(2,1)S(1)}, u32[]{:S(2)}, u32[]{:S(2)}) collective-permute-start(bf16[160,768]{1,0:T(8,128)(2,1)S(1)} %get-tuple-element.36.refs_4_), channel_id=1, source_target_pairs={{0,2},{2,0},{1,3},{3,1},{4,6},{6,4},{5,7},{7,5},{8,10},{10,8},{9,1... | collective-permute-start | bytes 737288 | tf_op jit(solution)/shard_map/ppermute | solution.py:326
  83.3 9.2 %collective-permute-start.23 = (bf16[96,2048]{1,0:T(8,128)(2,1)S(1)}, bf16[96,2048]{1,0:T(8,128)(2,1)S(1)}, u32[]{:S(2)}, u32[]{:S(2)}) collective-permute-start(bf16[96,2048]{1,0:T(8,128)(2,1)S(1)} %get-tuple-element.40), channel_id=1, source_target_pairs={{0,4},{4,0},{8,12},{12,8},{16,20},{20,16},{24,28},{28,24},{1,5},{5... | collective-permute-start | bytes 1179656 | tf_op jit(solution)/shard_map/ppermute | solution.py:317
  83.8 11.3 %collective-permute-start.24 = (bf16[96,2048]{1,0:T(8,128)(2,1)S(1)}, bf16[96,2048]{1,0:T(8,128)(2,1)S(1)}, u32[]{:S(2)}, u32[]{:S(2)}) collective-permute-start(bf16[96,2048]{1,0:T(8,128)(2,1)S(1)} %shard_map.79.refs_3_), channel_id=1, source_target_pairs={{0,8},{4,12},{8,16},{12,20},{16,24},{20,28},{24,0},{28,4},{1,9},{5... | collective-permute-start | bytes 1179656 | tf_op jit(solution)/shard_map/ppermute | solution.py:320
  84.1 4.9 %collective-permute-start.21 = (bf16[160,384]{1,0:T(8,128)(2,1)S(1)}, bf16[160,384]{1,0:T(8,128)(2,1)S(1)}, u32[]{:S(2)}, u32[]{:S(2)}) collective-permute-start(bf16[160,384]{1,0:T(8,128)(2,1)S(1)} %fusion.3.refs_0_.refs_6_), channel_id=1, source_target_pairs={{0,2},{2,0},{1,3},{3,1},{4,6},{6,4},{5,7},{7,5},{8,10},{10,8},{9,1... | collective-permute-start | bytes 368648 | tf_op jit(solution)/shard_map/ppermute | solution.py:326
  90.7 8.9 %collective-permute-start.22 = (bf16[96,2048]{1,0:T(8,128)(2,1)S(1)}, bf16[96,2048]{1,0:T(8,128)(2,1)S(1)}, u32[]{:S(2)}, u32[]{:S(2)}) collective-permute-start(bf16[96,2048]{1,0:T(8,128)(2,1)S(1)} %shard_map.81.refs_3_), channel_id=1, source_target_pairs={{0,4},{4,0},{8,12},{12,8},{16,20},{20,16},{24,28},{28,24},{1,5},{5... | collective-permute-start | bytes 1179656 | tf_op jit(solution)/shard_map/ppermute | solution.py:317
  95.3 12.1 %collective-permute-start.25 = (bf16[96,2048]{1,0:T(8,128)(2,1)S(1)}, bf16[96,2048]{1,0:T(8,128)(2,1)S(1)}, u32[]{:S(2)}, u32[]{:S(2)}) collective-permute-start(bf16[96,2048]{1,0:T(8,128)(2,1)S(1)} %shard_map.82.refs_3_), channel_id=1, source_target_pairs={{0,8},{4,12},{8,16},{12,20},{16,24},{20,28},{24,0},{28,4},{1,9},{5... | collective-permute-start | bytes 1179656 | tf_op jit(solution)/shard_map/ppermute | solution.py:320
  107.6 9.6 %collective-permute-start.26 = (bf16[96,2048]{1,0:T(8,128)(2,1)S(1)}, bf16[96,2048]{1,0:T(8,128)(2,1)S(1)}, u32[]{:S(2)}, u32[]{:S(2)}) collective-permute-start(bf16[96,2048]{1,0:T(8,128)(2,1)S(1)} %shard_map.83), channel_id=1, source_target_pairs={{0,8},{4,12},{8,16},{12,20},{16,24},{20,28},{24,0},{28,4},{1,9},{5... | collective-permute-start | bytes 1179656 | tf_op jit(solution)/shard_map/ppermute | solution.py:320

commit v7 on v6

--- a/solution.py
+++ b/solution.py
@@ -144,9 +144,14 @@
     return (first + core, first + 1 - core), (rank + 1) % parts * units, rank * units, places
 
 
-def pick_kernel(width, experts, capacity, units, groups, count, kinds, split, *refs):
+def pick_kernel(width, experts, capacity, units, groups, count, kinds, split, copied, *refs):
     blocks, weights = refs[:count], refs[count:]
-    chosen_ref, part_ref = refs[-2:]
+    if copied:
+        *_, source_ref, chosen_ref, part_ref, target_ref, sem = refs
+        copy = pltpu.make_async_copy(source_ref, target_ref, sem)
+        copy.start()
+    else:
+        chosen_ref, part_ref = refs[-2:]
     rows = blocks[0].shape[0]
     mine_and_other, start, _, _ = position(units)
     offsets = layout(groups, capacity)
@@ -164,25 +169,29 @@
     for g in range(len(groups)):
         mine = weights[kinds * g:kinds * (g + 1)]
         multiply(chosen_ref, slice(offsets[g], offsets[g + 1]), mine, start if split else None, units, part_ref)
-
-
-def pick_rows(groups, blocks, weights, split, after, width, experts, capacity, units):
+    if copied:
+        copy.wait()
+
+
+def pick_rows(groups, blocks, weights, split, copying, after, width, experts, capacity, units):
     columns = 2 * units if split else weights[0][0].shape[1]
     taken = layout(groups, capacity)[-1]
     flat = [w for expert, _ in groups for w in weights[expert]]
+    copied = len(copying)
     kernel = functools.partial(
-        pick_kernel, width, experts, capacity, units, groups, len(blocks), len(weights[0]), split
+        pick_kernel, width, experts, capacity, units, groups, len(blocks), len(weights[0]), split, copied
     )
     out = (jax.ShapeDtypeStruct((taken, width), BF16), jax.ShapeDtypeStruct((taken, columns), BF16))
     return pl.pallas_call(
         kernel,
         grid=(1,),
-        out_shape=out,
-        in_specs=[whole(x) for x in (*blocks, *flat)] + [ANY] * len(after),
-        out_specs=tuple(whole(o) for o in out),
+        out_shape=(*out, *[jax.ShapeDtypeStruct(a.shape, a.dtype) for a in copying]),
+        in_specs=[whole(x) for x in (*blocks, *flat)] + [ANY] * (len(after) + copied),
+        out_specs=(*[whole(o) for o in out], *[ANY] * copied),
+        scratch_shapes=[pltpu.SemaphoreType.DMA] * copied,
         compiler_params=params(),
         cost_estimate=cost(),
-    )(*blocks, *flat, *after)
+    )(*blocks, *flat, *after, *copying)
 
 
 def home_kernel(capacity, units, groups, kinds, split, passed, x_ref, *refs):
@@ -319,6 +328,9 @@
     def over_z(x):
         return lax.ppermute(x, "expert", [(i, (i + 2) % ring) for i in range(ring)])
 
+    def home_over_both(x, hop):
+        return lax.ppermute(x, "expert", [(i, ((i - 2 * hop) % ring) ^ 1) for i in range(ring)])
+
     def over_core(x):
         return lax.ppermute(x, "dp", [(0, 1), (1, 0)])
 
@@ -341,6 +353,7 @@
             home.append((jnp.concatenate(pairs[0], axis=1),))
 
     blocks, arrived = {(0, "s"): make_block(tokens, expert_ids, route_weights, experts)}, {}
+    blocks[0, "c"] = over_core(blocks[0, "s"])
 
     def send_on(hop):
         block = blocks[hop, "s"]
@@ -351,11 +364,12 @@
     both = ((0, (0, 1)), (1, (0, 1)))
     one = ((0, (0,)), (1, (0,)))
     plan = [([(0, "s")], ((0, (0,)),)), ([(0, "s"), (0, "b"), (1, "s")], ((1, (0, 1, 2)), (0, (1, 2))))]
-    plan += [([(hop - 1, "b"), (hop, "s")], both) for hop in range(2, hops)]
-    plan += [([(hops - 1, "b")], one)]
+    plan += [([(1, "b")], one)] + [([(hop, "b"), (hop, "s")], both) for hop in range(2, hops - 1)]
+    plan += [([(hops - 1, "b")], one), ([(hops - 1, "s")], one)]
     count = len(plan)
+    straight = ()
     chosen, parts_in, totals, hidden, returned, carried, gathered = {}, {}, {}, {}, {}, {}, []
-    downs = [w_down[0], over_core(w_down)[0]]
+    downs = [w_down[0]]
     order = []
 
     def passing(hop):
@@ -369,7 +383,11 @@
     def pick(i):
         keys, groups = plan[i]
         mine = [blocks[k] for k in keys]
-        chosen[i], part = pick_rows(groups, mine, away, split, order, width, experts, capacity, units)
+        copying = [w_down] if i == 1 else []
+        chosen[i], part, *copies = pick_rows(
+            groups, mine, away, split, copying, order, width, experts, capacity, units
+        )
+        downs.extend(over_core(c)[0] for c in copies)
         parts_in[i] = [over_x(part[:, 2 * units * (s - 1):2 * units * s], s) for s in range(1, parts)]
         order[:] = [part]
 
@@ -398,8 +416,12 @@
         take_on(hop, passed)
         for k, (at, kind) in enumerate(keys):
             piece = term[k * rows:(k + 1) * rows]
-            if kind == "b":
+            if kind == "b" and at in straight:
+                gathered.append(home_over_both(piece, at))
+            elif kind == "b":
                 returned[at, "b"] = over_y(piece)
+            elif kind == "c":
+                gathered.append(over_core(piece))
             elif at == 0:
                 gathered.append(piece)
             else:
@@ -410,7 +432,8 @@
             gathered[:] = [added(gathered + [returned[hop, "b"]], F32, order)]
             order[:] = [gathered[0]]
         else:
-            terms = [returned[hop, "s"], returned[hop, "b"]] + ([carried[hop]] if hop in carried else [])
+            terms = [returned[hop, "s"]] + ([returned[hop, "b"]] if hop not in straight else [])
+            terms += [carried[hop]] if hop in carried else []
             total = added(terms, BF16, order)
             order[:] = [total]
             carried[hop + 1] = over_z(total)
@@ -422,49 +445,49 @@
     send_on(0)
     if hops == 4:
         pick(0)
-        order.extend([gates[1], ups[1]])
+        order.append(blocks[0, "b"])
         home_product(0, 1)
+        activate(0)
         pick(1)
-        activate(0)
-        order.append(downs[1])
+        order.extend(downs[1:])
         home_product(1, 2)
         pick(2)
-        activate(1)
         home_product(2, 3)
-        order.append(blocks[2, "b"])
-        down_product(0, None)
+        down_product(0)
         activate(2)
         pick(3)
-        home_product(3, None)
-        down_product(1, None)
-        down_product(2, None)
+        activate(1)
+        down_product(1)
+        down_product(2)
         pick(4)
-        home_product(4, None)
+        home_product(3)
+        home_product(4)
         activate(3)
-        down_product(3, None)
+        pick(5)
+        home_product(5)
+        order.append(blocks[2, "b"])
+        add_hop(0)
+        down_product(3)
         add_hop(1)
-        add_hop(0)
+        order.append(blocks[2, "b"])
         activate(4)
-        down_product(4, None)
+        down_product(4)
+        activate(5)
         add_hop(2)
+        down_product(5)
         add_hop(3)
     else:
-        pick(0)
-        home_product(0, 1)
-        activate(0)
-        for i in range(1, count):
-            if i > 1:
-                activate(i - 1)
+        for i in range(count):
             pick(i)
             home_product(i, i + 1)
-            down_product(i - 1)
-            if i >= 3:
-                add_hop(i - 3)
+            if i > 0:
+                activate(i - 1)
+                down_product(i - 1)
         activate(count - 1)
         down_product(count - 1)
-        for hop in range(count - 3, hops):
+        for hop in range(hops):
             add_hop(hop)
-    return (gathered[0] + carried[hops].astype(F32)).astype(BF16)
+    return sum(x.astype(F32) for x in gathered + [carried[hops]]).astype(BF16)
 
 
 def solution(mesh):

time: 118 us -> 115 us (0.975)
  waiting for transfers between devices: 58.2 us -> 48.8 us
  Pallas kernels: 26.1 us -> 31.1 us
    ppermute x6, waiting for transfers between devices: 41.4 us -> 37.3 us  [over_z(): return lax.ppermute(x, 'expert', [(i, (i + 2) % ring) for i in range(ring)])]
    ppermute x10 -> x12, waiting for transfers between devices: 12.3 us -> 9.02 us  [over_x(): lax.ppermute(x, 'tensor', [(i, (i + step) % parts) for i in range(parts)])]
    pallas_call x5 -> x6, Pallas kernels: 9.52 us -> 11.9 us  [pick_rows(): pl.pallas_call(kernel, grid=(1,), out_shape=(*out, *[jax.ShapeDtypeStruct...]
    ppermute x8, waiting for transfers between devices: 4.54 us -> 2.5 us  [over_y(): return lax.ppermute(x, 'expert', [(i, i ^ 1) for i in range(ring)])]
    pallas_call x5 -> x6, Pallas kernels: 10 us -> 11.4 us  [down_rows(): pl.pallas_call(functools.partial(down_kernel, experts, capacity, groups,...]
    pallas_call x5 -> x6, Pallas kernels: 5.57 us -> 6.91 us  [home_rows(): pl.pallas_call(functools.partial(home_kernel, capacity, units, groups, le...]
    ppermute x10 -> x12, starting transfers between devices: 12.2 us -> 12 us  [over_x(): lax.ppermute(x, 'tensor', [(i, (i + step) % parts) for i in range(parts)])]
  transfers between devices with their start and end apart: 27 -> 29, of which waited for: 15 -> 12; matrix products, arithmetic and copies ran while one was open for 1% -> 1% of each run, Pallas kernels for 22% -> 25%
where the time goes in v7:
time: 115 us; the launch traced here: 114 us
  waiting for transfers between devices  48.8 us (42%)
  Pallas kernels  31.1 us (27%)
  starting transfers between devices  24.8 us (22%)
  local copies, waits for them, and re-layouts  7.38 us (6%)
  other arithmetic  1.8 us (2%)
    ppermute x6, waiting for transfers between devices, over_z(): return lax.ppermute(x, 'expert', [(i, (i + 2) % ring) for i in range(ring)])  37.3 us
    ppermute x12, starting transfers between devices, over_x(): lax.ppermute(x, 'tensor', [(i, (i + step) % parts) for i in range(parts)])  12 us
    pallas_call x6, Pallas kernels, pick_rows(): pl.pallas_call(kernel, grid=(1,), out_shape=(*out, *[jax.ShapeDtypeStruct...  11.9 us
    pallas_call x6, Pallas kernels, down_rows(): pl.pallas_call(functools.partial(down_kernel, experts, capacity, groups,...  11.4 us
    ppermute x8, starting transfers between devices, over_y(): return lax.ppermute(x, 'expert', [(i, i ^ 1) for i in range(ring)])  10.2 us
    ppermute x12, waiting for transfers between devices, over_x(): lax.ppermute(x, 'tensor', [(i, (i + step) % parts) for i in range(parts)])  9.02 us
    unnamed x16, local copies, waits for them, and re-layouts  7.24 us
    pallas_call x6, Pallas kernels, home_rows(): pl.pallas_call(functools.partial(home_kernel, capacity, units, groups, le...  6.91 us
  transfers between devices with their start and end apart: 29, of which 12 were waited for; matrix products, arithmetic and copies ran while one was open for 1% of the time, Pallas kernels for 25%

profile of v7, /device:TPU:0, one launch (start us, length us, event | category | flops | bytes accessed | tf_op | source)
XLA Modules:
  0.0 114.2 jit_solution(16685853470907293790)
XLA Ops:
  0.0 0.5 collective-permute-start.5
  0.5 1.0 copy-done.5
  1.5 0.7 copy-done.6
  2.2 0.7 copy-done.7
  2.9 0.5 shard_map.64.refs_0_.refs_2_
  3.4 3.0 %collective-permute-start = (bf16[96,2176]{1,0:T(8,128)(2,1)S(1)}, bf16[96,2176]{1,0:T(8,128)(2,1)S(1)}, u32[]{:S(2)}, u32[]{:S(2)}) collective-permute-start(bf16[96,2176]{1,0:T(8,128)(2,1)S(1)} %shard_map.64.refs_0_.refs_2_), channel_id=1, source_target_pairs={{0,4},{4,0},{8,12},{12,8},{16,20},{20,16},{24,28},{28,24},{1,5},{5... | collective-permute-start | bytes 1253384 | tf_op jit(solution)/shard_map/ppermute | solution.py:326
  6.4 1.6 %collective-permute-start.1 = (bf16[96,2176]{1,0:T(8,128)(2,1)S(1)}, bf16[96,2176]{1,0:T(8,128)(2,1)S(1)}, u32[]{:S(2)}, u32[]{:S(2)}) collective-permute-start(bf16[96,2176]{1,0:T(8,128)(2,1)S(1)} %shard_map.64.refs_0_.refs_2_), channel_id=1, source_target_pairs={{0,8},{4,12},{8,16},{12,20},{16,24},{20,28},{24,0},{28,4},{1,9},{5... | collective-permute-start | bytes 1253384 | tf_op jit(solution)/shard_map/ppermute | solution.py:329
  8.0 1.9 %copy-done = bf16[1,2048,768]{2,1,0:T(8,128)(2,1)S(1)} copy-done((bf16[1,2048,768]{2,1,0:T(8,128)(2,1)S(1)}, bf16[1,2048,768]{2,1,0:T(8,128)(2,1)}, u32[]{:S(2)}) %copy-start) | copy-done | bytes 3145752
  9.9 1.9 %copy-done.2 = bf16[1,2048,768]{2,1,0:T(8,128)(2,1)S(1)} copy-done((bf16[1,2048,768]{2,1,0:T(8,128)(2,1)S(1)}, bf16[1,2048,768]{2,1,0:T(8,128)(2,1)}, u32[]{:S(2)}) %copy-start.2) | copy-done | bytes 3145752
  11.8 1.1 shard_map.65
  12.9 1.6 %collective-permute-start.2 = (bf16[80,768]{1,0:T(8,128)(2,1)S(1)}, bf16[80,768]{1,0:T(8,128)(2,1)S(1)}, u32[]{:S(2)}, u32[]{:S(2)}) collective-permute-start(bf16[80,768]{1,0:T(8,128)(2,1)S(1)} %get-tuple-element.25.refs_2_), channel_id=1, source_target_pairs={{0,2},{2,0},{1,3},{3,1},{4,6},{6,4},{5,7},{7,5},{8,10},{10,8},{9,1... | collective-permute-start | bytes 368648 | tf_op jit(solution)/shard_map/ppermute | solution.py:338
  14.4 1.8 %collective-permute-done.refs_3_.refs_1_ = bf16[96,2176]{1,0:T(8,128)(2,1)S(1)} collective-permute-done((bf16[96,2176]{1,0:T(8,128)(2,1)S(1)}, bf16[96,2176]{1,0:T(8,128)(2,1)S(1)}, u32[]{:S(2)}, u32[]{:S(2)}) %collective-permute-start) | collective-permute-done | bytes 417824 | tf_op jit(solution)/shard_map/ppermute | solution.py:326
  16.2 3.3 %collective-permute-done.1.refs_4_ = bf16[96,2176]{1,0:T(8,128)(2,1)S(1)} collective-permute-done((bf16[96,2176]{1,0:T(8,128)(2,1)S(1)}, bf16[96,2176]{1,0:T(8,128)(2,1)S(1)}, u32[]{:S(2)}, u32[]{:S(2)}) %collective-permute-start.1) | collective-permute-done | bytes 417824 | tf_op jit(solution)/shard_map/ppermute | solution.py:329
  19.5 0.7 shard_map.66
  20.3 1.1 copy-done.4
  21.4 2.8 %shard_map.67 = (bf16[368,2048]{1,0:T(8,128)(2,1)S(1)}, bf16[368,768]{1,0:T(8,128)(2,1)S(1)}, bf16[1,768,2048]{2,1,0:T(8,128)(2,1)S(1)}) custom-call(bf16[96,2176]{1,0:T(8,128)(2,1)S(1)} %shard_map.64.refs_0_.refs_2_, bf16[96,2176]{1,0:T(8,128)(2,1)S(1)} %collective-permute-done.refs_3_.refs_1_, bf16[96,2176]{1,0:T(8,128)(2,1)S(1)} %get-tuple-element.27.refs_2_.refs_4_, ...), custom_call_target="tpu_custom_call" | custom-call | flops 1 | bytes 1 | tf_op jit(solution)/shard_map/pallas_call | solution.py:185
  24.3 1.6 %collective-permute-start.10 = (bf16[368,768]{1,0:T(8,128)(2,1)S(1)}, bf16[368,768]{1,0:T(8,128)(2,1)S(1)}, u32[]{:S(2)}, u32[]{:S(2)}) collective-permute-start(bf16[368,768]{1,0:T(8,128)(2,1)S(1)} %get-tuple-element.29.refs_4_), channel_id=1, source_target_pairs={{0,2},{2,0},{1,3},{3,1},{4,6},{6,4},{5,7},{7,5},{8,10},{10,8},{9,1... | collective-permute-start | bytes 1695752 | tf_op jit(solution)/shard_map/ppermute | solution.py:338
  25.9 0.5 collective-permute-start.4
  26.4 0.5 collective-permute-start.3
  26.9 12.5 %collective-permute-done.8.refs_6_ = bf16[96,2176]{1,0:T(8,128)(2,1)S(1)} collective-permute-done((bf16[96,2176]{1,0:T(8,128)(2,1)S(1)}, bf16[96,2176]{1,0:T(8,128)(2,1)S(1)}, u32[]{:S(2)}, u32[]{:S(2)}) %collective-permute-start.8) | collective-permute-done | bytes 417824 | tf_op jit(solution)/shard_map/ppermute | solution.py:329
  39.4 1.4 %shard_map.68 = (f32[368,768]{1,0:T(8,128)S(1)}, bf16[96,2176]{1,0:T(8,128)(2,1)S(1)}) custom-call(bf16[368,2048]{1,0:T(8,128)(2,1)S(1)} %get-tuple-element.28.x_ref, bf16[2048,768]{1,0:T(8,128)(2,1)S(1)} %bitcast.33, bf16[2048,768]{1,0:T(8,128)(2,1)S(1)} %bitcast.43, bf16[2048,768]{1,0:T(8,128)(2,1)S(1)} %bitcast.11, ...), custom_call_target="tpu_custom_call", output_to_operand_aliasing={{1}: (7, {})} | custom-call | flops 1 | bytes 1 | tf_op jit(solution)/shard_map/pallas_call | solution.py:210
  40.8 0.2 collective-permute-start.9
  41.0 0.6 collective-permute-start.12
  41.6 1.9 %shard_map.69 = (bf16[160,2048]{1,0:T(8,128)(2,1)S(1)}, bf16[160,768]{1,0:T(8,128)(2,1)S(1)}) custom-call(bf16[96,2176]{1,0:T(8,128)(2,1)S(1)} %collective-permute-done.4.refs_0_.refs_2_, bf16[2048,768]{1,0:T(8,128)(2,1)S(1)} %bitcast.12, bf16[2048,768]{1,0:T(8,128)(2,1)S(1)} %bitcast.24, bf16[2048,768]{1,0:T(8,128)(2,1)S(1)} %bitcast.34, ...), custom_call_target="tpu_custom_call" | custom-call | flops 1 | bytes 1 | tf_op jit(solution)/shard_map/pallas_call | solution.py:185
  43.5 0.6 collective-permute-start.13
  44.2 0.2 fusion.refs_0_.refs_8_
  44.4 1.6 %collective-permute-start.11 = (bf16[368,384]{1,0:T(8,128)(2,1)S(1)}, bf16[368,384]{1,0:T(8,128)(2,1)S(1)}, u32[]{:S(2)}, u32[]{:S(2)}) collective-permute-start(bf16[368,384]{1,0:T(8,128)(2,1)S(1)} %fusion.refs_0_.refs_8_), channel_id=1, source_target_pairs={{0,2},{2,0},{1,3},{3,1},{4,6},{6,4},{5,7},{7,5},{8,10},{10,8},{9,1... | collective-permute-start | bytes 847880 | tf_op jit(solution)/shard_map/ppermute | solution.py:338
  46.0 7.7 %collective-permute-done.9.refs_5_ = bf16[96,2176]{1,0:T(8,128)(2,1)S(1)} collective-permute-done((bf16[96,2176]{1,0:T(8,128)(2,1)S(1)}, bf16[96,2176]{1,0:T(8,128)(2,1)S(1)}, u32[]{:S(2)}, u32[]{:S(2)}) %collective-permute-start.9) | collective-permute-done | bytes 417824 | tf_op jit(solution)/shard_map/ppermute | solution.py:329
  53.7 1.2 %shard_map.70 = (f32[160,768]{1,0:T(8,128)S(1)}, bf16[96,2176]{1,0:T(8,128)(2,1)S(1)}) custom-call(bf16[160,2048]{1,0:T(8,128)(2,1)S(1)} %get-tuple-element.32.x_ref, bf16[2048,768]{1,0:T(8,128)(2,1)S(1)} %bitcast.13, bf16[2048,768]{1,0:T(8,128)(2,1)S(1)} %bitcast.25, bf16[2048,768]{1,0:T(8,128)(2,1)S(1)} %bitcast.35, ...), custom_call_target="tpu_custom_call", output_to_operand_aliasing={{1}: (6, {})} | custom-call | flops 1 | bytes 1 | tf_op jit(solution)/shard_map/pallas_call | solution.py:210
  55.1 0.6 collective-permute-start.15
  55.6 0.5 collective-permute-start.16
  56.2 1.1 shard_map.71.refs_6_.refs_0_
  57.3 2.0 %shard_map.72 = (bf16[288,2048]{1,0:T(8,128)(2,1)S(1)}, bf16[288,768]{1,0:T(8,128)(2,1)S(1)}) custom-call(bf16[96,2176]{1,0:T(8,128)(2,1)S(1)} %collective-permute-done.12.refs_0_.refs_4_.refs_2_.refs_6_, bf16[96,2176]{1,0:T(8,128)(2,1)S(1)} %get-tuple-element.34.refs_1_.refs_3_, bf16[2048,768]{1,0:T(8,128)(2,1)S(1)} %bitcast.14, ...), custom_call_target="tpu_custom_call" | custom-call | flops 1 | bytes 1 | tf_op jit(solution)/shard_map/pallas_call | solution.py:185
  59.3 1.5 %collective-permute-start.17 = (bf16[288,768]{1,0:T(8,128)(2,1)S(1)}, bf16[288,768]{1,0:T(8,128)(2,1)S(1)}, u32[]{:S(2)}, u32[]{:S(2)}) collective-permute-start(bf16[288,768]{1,0:T(8,128)(2,1)S(1)} %get-tuple-element.36.refs_7_), channel_id=1, source_target_pairs={{0,2},{2,0},{1,3},{3,1},{4,6},{6,4},{5,7},{7,5},{8,10},{10,8},{9,1... | collective-permute-start | bytes 1327112 | tf_op jit(solution)/shard_map/ppermute | solution.py:338
  60.8 2.6 %shard_map.73.refs_5_ = bf16[288,2048]{1,0:T(8,128)(2,1)S(1)} custom-call(bf16[368,384]{1,0:T(8,128)(2,1)S(1)} %fusion.refs_0_.refs_8_, bf16[368,384]{1,0:T(8,128)(2,1)S(1)} %collective-permute-done.11.refs_1_, bf16[96,2176]{1,0:T(8,128)(2,1)S(1)} %shard_map.64.refs_0_.refs_2_, bf16[96,2176]{1,0:T(8,128)(2,1)S(1)} %collective-permute-done.refs_3_.refs_1_, ...), custom_call_target="tpu_custom_call" | custom-call | flops 1 | bytes 1 | tf_op jit(solution)/shard_map/pallas_call | solution.py:278
  63.5 1.6 %collective-permute-start.14 = (bf16[96,2048]{1,0:T(8,128)(2,1)S(1)}, bf16[96,2048]{1,0:T(8,128)(2,1)S(1)}, u32[]{:S(2)}, u32[]{:S(2)}) collective-permute-start(bf16[96,2048]{1,0:T(8,128)(2,1)S(1)} %get-tuple-element.44), channel_id=1, source_target_pairs={{0,4},{4,0},{8,12},{12,8},{16,20},{20,16},{24,28},{28,24},{1,5},{5... | collective-permute-start | bytes 1179656 | tf_op jit(solution)/shard_map/ppermute | solution.py:326
  65.1 1.8 %shard_map.74.refs_5_ = bf16[96,2048]{1,0:T(8,128)(2,1)S(1)} custom-call(bf16[160,384]{1,0:T(8,128)(2,1)S(1)} %fusion.4.refs_7_.refs_0_, bf16[160,384]{1,0:T(8,128)(2,1)S(1)} %collective-permute-done.16.refs_1_, bf16[96,2176]{1,0:T(8,128)(2,1)S(1)} %collective-permute-done.4.refs_0_.refs_2_, bf16[768,2048]{1,0:T(8,128)(2,1)S(1)} %bitcast.54, ...), custom_call_target="tpu_custom_call" | custom-call | flops 1 | bytes 1 | tf_op jit(solution)/shard_map/pallas_call | solution.py:278
  66.9 1.9 %shard_map.75 = (bf16[160,2048]{1,0:T(8,128)(2,1)S(1)}, bf16[160,768]{1,0:T(8,128)(2,1)S(1)}) custom-call(bf16[96,2176]{1,0:T(8,128)(2,1)S(1)} %collective-permute-done.15.refs_0_.refs_2_, bf16[2048,768]{1,0:T(8,128)(2,1)S(1)} %bitcast.15, bf16[2048,768]{1,0:T(8,128)(2,1)S(1)} %bitcast.27, bf16[2048,768]{1,0:T(8,128)(2,1)S(1)} %bitcast.37, ...), custom_call_target="tpu_custom_call" | custom-call | flops 1 | bytes 1 | tf_op jit(solution)/shard_map/pallas_call | solution.py:185
  68.9 1.2 %shard_map.76.refs_4_ = f32[288,768]{1,0:T(8,128)S(1)} custom-call(bf16[288,2048]{1,0:T(8,128)(2,1)S(1)} %get-tuple-element.39.x_ref, bf16[2048,768]{1,0:T(8,128)(2,1)S(1)} %bitcast.16, bf16[2048,768]{1,0:T(8,128)(2,1)S(1)} %bitcast.28, bf16[2048,768]{1,0:T(8,128)(2,1)S(1)} %bitcast.38, bf16[2048,768]{1,0:T(8,128)(2,1)S(1)} %bitcast.48, ...), custom_call_target="tpu_custom_call" | custom-call | flops 1 | bytes 1 | tf_op jit(solution)/shard_map/pallas_call | solution.py:210
  70.3 0.7 collective-permute-start.20
  71.0 1.5 %collective-permute-start.22 = (bf16[96,2048]{1,0:T(8,128)(2,1)S(1)}, bf16[96,2048]{1,0:T(8,128)(2,1)S(1)}, u32[]{:S(2)}, u32[]{:S(2)}) collective-permute-start(bf16[96,2048]{1,0:T(8,128)(2,1)S(1)} %shard_map.74.refs_5_), channel_id=1, source_target_pairs={{0,4},{4,0},{8,12},{12,8},{16,20},{20,16},{24,28},{28,24},{1,5},{5... | collective-permute-start | bytes 1179656 | tf_op jit(solution)/shard_map/ppermute | solution.py:326
  72.5 1.2 %shard_map.77.refs_5_ = f32[160,768]{1,0:T(8,128)S(1)} custom-call(bf16[160,2048]{1,0:T(8,128)(2,1)S(1)} %get-tuple-element.38.x_ref, bf16[2048,768]{1,0:T(8,128)(2,1)S(1)} %bitcast.17, bf16[2048,768]{1,0:T(8,128)(2,1)S(1)} %bitcast.29, bf16[2048,768]{1,0:T(8,128)(2,1)S(1)} %bitcast.39, bf16[2048,768]{1,0:T(8,128)(2,1)S(1)} %bitcast.49, ...), custom_call_target="tpu_custom_call" | custom-call | flops 1 | bytes 1 | tf_op jit(solution)/shard_map/pallas_call | solution.py:210
  73.8 1.4 %collective-permute-start.24 = (bf16[160,768]{1,0:T(8,128)(2,1)S(1)}, bf16[160,768]{1,0:T(8,128)(2,1)S(1)}, u32[]{:S(2)}, u32[]{:S(2)}) collective-permute-start(bf16[160,768]{1,0:T(8,128)(2,1)S(1)} %get-tuple-element.40.refs_4_), channel_id=1, source_target_pairs={{0,2},{2,0},{1,3},{3,1},{4,6},{6,4},{5,7},{7,5},{8,10},{10,8},{9,1... | collective-permute-start | bytes 737288 | tf_op jit(solution)/shard_map/ppermute | solution.py:338
  75.1 2.2 %shard_map.78 = (bf16[160,2048]{1,0:T(8,128)(2,1)S(1)}, bf16[160,768]{1,0:T(8,128)(2,1)S(1)}) custom-call(bf16[96,2176]{1,0:T(8,128)(2,1)S(1)} %get-tuple-element.37.refs_0_.refs_2_, bf16[2048,768]{1,0:T(8,128)(2,1)S(1)} %bitcast.18, bf16[2048,768]{1,0:T(8,128)(2,1)S(1)} %bitcast.30, bf16[2048,768]{1,0:T(8,128)(2,1)S(1)} %bitcast.40, ...), custom_call_target="tpu_custom_call" | custom-call | flops 1 | bytes 1 | tf_op jit(solution)/shard_map/pallas_call | solution.py:185
  77.3 0.8 collective-permute-start.18
  78.1 1.2 %shard_map.79.refs_3_ = f32[160,768]{1,0:T(8,128)S(1)} custom-call(bf16[160,2048]{1,0:T(8,128)(2,1)S(1)} %get-tuple-element.41.x_ref, bf16[2048,768]{1,0:T(8,128)(2,1)S(1)} %bitcast.19, bf16[2048,768]{1,0:T(8,128)(2,1)S(1)} %bitcast.31, bf16[2048,768]{1,0:T(8,128)(2,1)S(1)} %bitcast.41, bf16[2048,768]{1,0:T(8,128)(2,1)S(1)} %bitcast.51, ...), custom_call_target="tpu_custom_call" | custom-call | flops 1 | bytes 1 | tf_op jit(solution)/shard_map/pallas_call | solution.py:210
  79.4 2.2 %shard_map.81.refs_2_ = bf16[192,2048]{1,0:T(8,128)(2,1)S(1)} custom-call(bf16[288,384]{1,0:T(8,128)(2,1)S(1)} %fusion.1.refs_6_.refs_0_, bf16[288,384]{1,0:T(8,128)(2,1)S(1)} %collective-permute-done.20.refs_1_, bf16[96,2176]{1,0:T(8,128)(2,1)S(1)} %collective-permute-done.12.refs_0_.refs_4_.refs_2_.refs_6_, ...), custom_call_target="tpu_custom_call" | custom-call | flops 1 | bytes 1 | tf_op jit(solution)/shard_map/pallas_call | solution.py:278
  81.8 0.8 collective-permute-start.21
  82.5 0.7 collective-permute-done.22.refs_1_
  83.4 0.5 collective-permute-done.24
  84.0 0.5 collective-permute-start.25
  84.5 2.8 %collective-permute-done.18 = bf16[160,768]{1,0:T(8,128)(2,1)S(1)} collective-permute-done((bf16[160,768]{1,0:T(8,128)(2,1)S(1)}, bf16[160,768]{1,0:T(8,128)(2,1)S(1)}, u32[]{:S(2)}, u32[]{:S(2)}) %collective-permute-start.18) | collective-permute-done | bytes 245792 | tf_op jit(solution)/shard_map/ppermute | solution.py:338
  87.5 1.5 %collective-permute-done.25.refs_1_ = bf16[160,384]{1,0:T(8,128)(2,1)S(1)} collective-permute-done((bf16[160,384]{1,0:T(8,128)(2,1)S(1)}, bf16[160,384]{1,0:T(8,128)(2,1)S(1)}, u32[]{:S(2)}, u32[]{:S(2)}) %collective-permute-start.25) | collective-permute-done | bytes 122912 | tf_op jit(solution)/shard_map/ppermute | solution.py:338
  89.0 1.8 %shard_map.83.refs_3_ = bf16[96,2048]{1,0:T(8,128)(2,1)S(1)} custom-call(bf16[160,384]{1,0:T(8,128)(2,1)S(1)} %fusion.2.refs_0_.refs_7_, bf16[160,384]{1,0:T(8,128)(2,1)S(1)} %collective-permute-done.25.refs_1_, bf16[96,2176]{1,0:T(8,128)(2,1)S(1)} %collective-permute-done.15.refs_0_.refs_2_, bf16[768,2048]{1,0:T(8,128)(2,1)S(1)} %bitcast.56, ...), custom_call_target="tpu_custom_call" | custom-call | flops 1 | bytes 1 | tf_op jit(solution)/shard_map/pallas_call | solution.py:278
  90.8 1.6 %collective-permute-start.26 = (bf16[96,2048]{1,0:T(8,128)(2,1)S(1)}, bf16[96,2048]{1,0:T(8,128)(2,1)S(1)}, u32[]{:S(2)}, u32[]{:S(2)}) collective-permute-start(bf16[96,2048]{1,0:T(8,128)(2,1)S(1)} %shard_map.83.refs_3_), channel_id=1, source_target_pairs={{0,4},{4,0},{8,12},{12,8},{16,20},{20,16},{24,28},{28,24},{1,5},{5... | collective-permute-start | bytes 1179656 | tf_op jit(solution)/shard_map/ppermute | solution.py:326
  92.4 0.5 collective-permute-done.23.refs_2_
  92.9 0.1 shard_map.84.refs_5_
  93.2 0.7 collective-permute-start.19
  93.9 4.2 %collective-permute-done.19.refs_1_ = bf16[160,384]{1,0:T(8,128)(2,1)S(1)} collective-permute-done((bf16[160,384]{1,0:T(8,128)(2,1)S(1)}, bf16[160,384]{1,0:T(8,128)(2,1)S(1)}, u32[]{:S(2)}, u32[]{:S(2)}) %collective-permute-start.19) | collective-permute-done | bytes 122912 | tf_op jit(solution)/shard_map/ppermute | solution.py:338
  98.1 1.8 %shard_map.85.refs_0_.refs_3_ = bf16[96,2048]{1,0:T(8,128)(2,1)S(1)} custom-call(bf16[160,384]{1,0:T(8,128)(2,1)S(1)} %fusion.3.refs_4_.refs_0_, bf16[160,384]{1,0:T(8,128)(2,1)S(1)} %collective-permute-done.19.refs_1_, bf16[96,2176]{1,0:T(8,128)(2,1)S(1)} %get-tuple-element.37.refs_0_.refs_2_, bf16[768,2048]{1,0:T(8,128)(2,1)S(1)} %bitcast.57, ...), custom_call_target="tpu_custom_call" | custom-call | flops 1 | bytes 1 | tf_op jit(solution)/shard_map/pallas_call | solution.py:278
  99.9 3.7 %collective-permute-done.27.refs_2_ = bf16[96,2048]{1,0:T(8,128)(2,1)S(1)} collective-permute-done((bf16[96,2048]{1,0:T(8,128)(2,1)S(1)}, bf16[96,2048]{1,0:T(8,128)(2,1)S(1)}, u32[]{:S(2)}, u32[]{:S(2)}) %collective-permute-start.27) | collective-permute-done | bytes 393248 | tf_op jit(solution)/shard_map/ppermute | solution.py:329
  103.7 0.1 shard_map.86
  103.9 9.6 %collective-permute-done.28 = bf16[96,2048]{1,0:T(8,128)(2,1)S(1)} collective-permute-done((bf16[96,2048]{1,0:T(8,128)(2,1)S(1)}, bf16[96,2048]{1,0:T(8,128)(2,1)S(1)}, u32[]{:S(2)}, u32[]{:S(2)}) %collective-permute-start.28) | collective-permute-done | bytes 393248 | tf_op jit(solution)/shard_map/ppermute | solution.py:329
  113.4 0.8 add_convert_fusion
  (48 shorter events, 1.5 us)
Async XLA Ops:
  0.0 20.3 %collective-permute-start.5 = (bf16[1,2048,768]{2,1,0:T(8,128)(2,1)}, bf16[1,2048,768]{2,1,0:T(8,128)(2,1)S(1)}, u32[]{:S(2)}, u32[]{:S(2)}) collective-permute-start(bf16[1,2048,768]{2,1,0:T(8,128)(2,1)} %param.9), channel_id=1, source_target_pairs={{0,1},{1,0},{2,3},{3,2},{4,5},{5,4},{6,7},{7,6},{8,9},{9,8},{10,11... | collective-permute-start | bytes 9437192 | tf_op jit(solution)/shard_map/ppermute | solution.py:335
  0.5 19.9 %collective-permute-start.6 = (bf16[1,2048,768]{2,1,0:T(8,128)(2,1)}, bf16[1,2048,768]{2,1,0:T(8,128)(2,1)S(1)}, u32[]{:S(2)}, u32[]{:S(2)}) collective-permute-start(bf16[1,2048,768]{2,1,0:T(8,128)(2,1)} %param.10), channel_id=1, source_target_pairs={{0,1},{1,0},{2,3},{3,2},{4,5},{5,4},{6,7},{7,6},{8,9},{9,8},{10,11... | collective-permute-start | bytes 9437192 | tf_op jit(solution)/shard_map/ppermute | solution.py:335
  0.5 1.0 copy-start.5
  1.5 0.7 copy-start.6
  2.2 0.7 copy-start.7
  3.4 12.8 %collective-permute-start = (bf16[96,2176]{1,0:T(8,128)(2,1)S(1)}, bf16[96,2176]{1,0:T(8,128)(2,1)S(1)}, u32[]{:S(2)}, u32[]{:S(2)}) collective-permute-start(bf16[96,2176]{1,0:T(8,128)(2,1)S(1)} %shard_map.64.refs_0_.refs_2_), channel_id=1, source_target_pairs={{0,4},{4,0},{8,12},{12,8},{16,20},{20,16},{24,28},{28,24},{1,5},{5... | collective-permute-start | bytes 1253384 | tf_op jit(solution)/shard_map/ppermute | solution.py:326
  6.4 13.1 %collective-permute-start.1 = (bf16[96,2176]{1,0:T(8,128)(2,1)S(1)}, bf16[96,2176]{1,0:T(8,128)(2,1)S(1)}, u32[]{:S(2)}, u32[]{:S(2)}) collective-permute-start(bf16[96,2176]{1,0:T(8,128)(2,1)S(1)} %shard_map.64.refs_0_.refs_2_), channel_id=1, source_target_pairs={{0,8},{4,12},{8,16},{12,20},{16,24},{20,28},{24,0},{28,4},{1,9},{5... | collective-permute-start | bytes 1253384 | tf_op jit(solution)/shard_map/ppermute | solution.py:329
  8.0 1.9 %copy-start = (bf16[1,2048,768]{2,1,0:T(8,128)(2,1)S(1)}, bf16[1,2048,768]{2,1,0:T(8,128)(2,1)}, u32[]{:S(2)}) copy-start(bf16[1,2048,768]{2,1,0:T(8,128)(2,1)} %param.9) | copy-start | bytes 9437188
  9.9 1.9 %copy-start.2 = (bf16[1,2048,768]{2,1,0:T(8,128)(2,1)S(1)}, bf16[1,2048,768]{2,1,0:T(8,128)(2,1)}, u32[]{:S(2)}) copy-start(bf16[1,2048,768]{2,1,0:T(8,128)(2,1)} %param.10) | copy-start | bytes 9437188
  11.8 7.8 %copy-start.1 = (bf16[1,2048,768]{2,1,0:T(8,128)(2,1)S(1)}, bf16[1,2048,768]{2,1,0:T(8,128)(2,1)}, u32[]{:S(2)}) copy-start(bf16[1,2048,768]{2,1,0:T(8,128)(2,1)} %param.9) | copy-start | bytes 9437188
  11.8 7.8 %copy-start.3 = (bf16[1,2048,768]{2,1,0:T(8,128)(2,1)S(1)}, bf16[1,2048,768]{2,1,0:T(8,128)(2,1)}, u32[]{:S(2)}) copy-start(bf16[1,2048,768]{2,1,0:T(8,128)(2,1)} %param.10) | copy-start | bytes 9437188
  12.9 7.4 %collective-permute-start.2 = (bf16[80,768]{1,0:T(8,128)(2,1)S(1)}, bf16[80,768]{1,0:T(8,128)(2,1)S(1)}, u32[]{:S(2)}, u32[]{:S(2)}) collective-permute-start(bf16[80,768]{1,0:T(8,128)(2,1)S(1)} %get-tuple-element.25.refs_2_), channel_id=1, source_target_pairs={{0,2},{2,0},{1,3},{3,1},{4,6},{6,4},{5,7},{7,5},{8,10},{10,8},{9,1... | collective-permute-start | bytes 368648 | tf_op jit(solution)/shard_map/ppermute | solution.py:338
  19.5 1.9 %copy-start.4 = (bf16[1,768,2048]{2,1,0:T(8,128)(2,1)S(1)}, bf16[1,768,2048]{2,1,0:T(8,128)(2,1)}, u32[]{:S(2)}) copy-start(bf16[1,768,2048]{2,1,0:T(8,128)(2,1)} %refs_9_.1) | copy-start | bytes 9437188
  24.2 15.1 %collective-permute-start.7 = (bf16[1,768,2048]{2,1,0:T(8,128)(2,1)S(1)}, bf16[1,768,2048]{2,1,0:T(8,128)(2,1)S(1)}, u32[]{:S(2)}, u32[]{:S(2)}) collective-permute-start(bf16[1,768,2048]{2,1,0:T(8,128)(2,1)S(1)} %get-tuple-element.30), channel_id=1, source_target_pairs={{0,1},{1,0},{2,3},{3,2},{4,5},{5,4},{6,7},{7,6},{8,9},{9,8},{10,11... | collective-permute-start | bytes 9437192 | tf_op jit(solution)/shard_map/ppermute | solution.py:335
  24.3 19.8 %collective-permute-start.10 = (bf16[368,768]{1,0:T(8,128)(2,1)S(1)}, bf16[368,768]{1,0:T(8,128)(2,1)S(1)}, u32[]{:S(2)}, u32[]{:S(2)}) collective-permute-start(bf16[368,768]{1,0:T(8,128)(2,1)S(1)} %get-tuple-element.29.refs_4_), channel_id=1, source_target_pairs={{0,2},{2,0},{1,3},{3,1},{4,6},{6,4},{5,7},{7,5},{8,10},{10,8},{9,1... | collective-permute-start | bytes 1695752 | tf_op jit(solution)/shard_map/ppermute | solution.py:338
  25.8 13.5 %collective-permute-start.8 = (bf16[96,2176]{1,0:T(8,128)(2,1)S(1)}, bf16[96,2176]{1,0:T(8,128)(2,1)S(1)}, u32[]{:S(2)}, u32[]{:S(2)}) collective-permute-start(bf16[96,2176]{1,0:T(8,128)(2,1)S(1)} %get-tuple-element.27.refs_2_.refs_4_), channel_id=1, source_target_pairs={{0,8},{4,12},{8,16},{12,20},{16,24},{20,28},{24,0},{28,4},{1,9},{5... | collective-permute-start | bytes 1253384 | tf_op jit(solution)/shard_map/ppermute | solution.py:329
  25.9 15.7 %collective-permute-start.4 = (bf16[96,2176]{1,0:T(8,128)(2,1)S(1)}, bf16[96,2176]{1,0:T(8,128)(2,1)S(1)}, u32[]{:S(2)}, u32[]{:S(2)}) collective-permute-start(bf16[96,2176]{1,0:T(8,128)(2,1)S(1)} %get-tuple-element.27.refs_2_.refs_4_), channel_id=1, source_target_pairs={{0,4},{4,0},{8,12},{12,8},{16,20},{20,16},{24,28},{28,24},{1,5},{5... | collective-permute-start | bytes 1253384 | tf_op jit(solution)/shard_map/ppermute | solution.py:326
  26.4 29.8 %collective-permute-start.3 = (bf16[80,384]{1,0:T(8,128)(2,1)S(1)}, bf16[80,384]{1,0:T(8,128)(2,1)S(1)}, u32[]{:S(2)}, u32[]{:S(2)}) collective-permute-start(bf16[80,384]{1,0:T(8,128)(2,1)S(1)} %fusion.5.refs_8_.refs_0_), channel_id=1, source_target_pairs={{0,2},{2,0},{1,3},{3,1},{4,6},{6,4},{5,7},{7,5},{8,10},{10,8},{9,1... | collective-permute-start | bytes 184328 | tf_op jit(solution)/shard_map/ppermute | solution.py:338
  40.8 12.9 %collective-permute-start.9 = (bf16[96,2176]{1,0:T(8,128)(2,1)S(1)}, bf16[96,2176]{1,0:T(8,128)(2,1)S(1)}, u32[]{:S(2)}, u32[]{:S(2)}) collective-permute-start(bf16[96,2176]{1,0:T(8,128)(2,1)S(1)} %get-tuple-element.34.refs_1_.refs_3_), channel_id=1, source_target_pairs={{0,8},{4,12},{8,16},{12,20},{16,24},{20,28},{24,0},{28,4},{1,9},{5... | collective-permute-start | bytes 1253384 | tf_op jit(solution)/shard_map/ppermute | solution.py:329
  41.0 16.3 %collective-permute-start.12 = (bf16[96,2176]{1,0:T(8,128)(2,1)S(1)}, bf16[96,2176]{1,0:T(8,128)(2,1)S(1)}, u32[]{:S(2)}, u32[]{:S(2)}) collective-permute-start(bf16[96,2176]{1,0:T(8,128)(2,1)S(1)} %get-tuple-element.34.refs_1_.refs_3_), channel_id=1, source_target_pairs={{0,4},{4,0},{8,12},{12,8},{16,20},{20,16},{24,28},{28,24},{1,5},{5... | collective-permute-start | bytes 1253384 | tf_op jit(solution)/shard_map/ppermute | solution.py:326
  43.5 11.4 %collective-permute-start.13 = (bf16[160,768]{1,0:T(8,128)(2,1)S(1)}, bf16[160,768]{1,0:T(8,128)(2,1)S(1)}, u32[]{:S(2)}, u32[]{:S(2)}) collective-permute-start(bf16[160,768]{1,0:T(8,128)(2,1)S(1)} %get-tuple-element.33.refs_4_), channel_id=1, source_target_pairs={{0,2},{2,0},{1,3},{3,1},{4,6},{6,4},{5,7},{7,5},{8,10},{10,8},{9,1... | collective-permute-start | bytes 737288 | tf_op jit(solution)/shard_map/ppermute | solution.py:338
  44.4 16.4 %collective-permute-start.11 = (bf16[368,384]{1,0:T(8,128)(2,1)S(1)}, bf16[368,384]{1,0:T(8,128)(2,1)S(1)}, u32[]{:S(2)}, u32[]{:S(2)}) collective-permute-start(bf16[368,384]{1,0:T(8,128)(2,1)S(1)} %fusion.refs_0_.refs_8_), channel_id=1, source_target_pairs={{0,2},{2,0},{1,3},{3,1},{4,6},{6,4},{5,7},{7,5},{8,10},{10,8},{9,1... | collective-permute-start | bytes 847880 | tf_op jit(solution)/shard_map/ppermute | solution.py:338
  55.1 11.9 %collective-permute-start.15 = (bf16[96,2176]{1,0:T(8,128)(2,1)S(1)}, bf16[96,2176]{1,0:T(8,128)(2,1)S(1)}, u32[]{:S(2)}, u32[]{:S(2)}) collective-permute-start(bf16[96,2176]{1,0:T(8,128)(2,1)S(1)} %get-tuple-element.37.refs_0_.refs_2_), channel_id=1, source_target_pairs={{0,4},{4,0},{8,12},{12,8},{16,20},{20,16},{24,28},{28,24},{1,5},{5... | collective-permute-start | bytes 1253384 | tf_op jit(solution)/shard_map/ppermute | solution.py:326
  55.6 9.5 %collective-permute-start.16 = (bf16[160,384]{1,0:T(8,128)(2,1)S(1)}, bf16[160,384]{1,0:T(8,128)(2,1)S(1)}, u32[]{:S(2)}, u32[]{:S(2)}) collective-permute-start(bf16[160,384]{1,0:T(8,128)(2,1)S(1)} %fusion.4.refs_7_.refs_0_), channel_id=1, source_target_pairs={{0,2},{2,0},{1,3},{3,1},{4,6},{6,4},{5,7},{7,5},{8,10},{10,8},{9,1... | collective-permute-start | bytes 368648 | tf_op jit(solution)/shard_map/ppermute | solution.py:338
  59.3 10.8 %collective-permute-start.17 = (bf16[288,768]{1,0:T(8,128)(2,1)S(1)}, bf16[288,768]{1,0:T(8,128)(2,1)S(1)}, u32[]{:S(2)}, u32[]{:S(2)}) collective-permute-start(bf16[288,768]{1,0:T(8,128)(2,1)S(1)} %get-tuple-element.36.refs_7_), channel_id=1, source_target_pairs={{0,2},{2,0},{1,3},{3,1},{4,6},{6,4},{5,7},{7,5},{8,10},{10,8},{9,1... | collective-permute-start | bytes 1327112 | tf_op jit(solution)/shard_map/ppermute | solution.py:338
  63.5 15.8 %collective-permute-start.14 = (bf16[96,2048]{1,0:T(8,128)(2,1)S(1)}, bf16[96,2048]{1,0:T(8,128)(2,1)S(1)}, u32[]{:S(2)}, u32[]{:S(2)}) collective-permute-start(bf16[96,2048]{1,0:T(8,128)(2,1)S(1)} %get-tuple-element.44), channel_id=1, source_target_pairs={{0,4},{4,0},{8,12},{12,8},{16,20},{20,16},{24,28},{28,24},{1,5},{5... | collective-permute-start | bytes 1179656 | tf_op jit(solution)/shard_map/ppermute | solution.py:326
  70.3 9.2 %collective-permute-start.20 = (bf16[288,384]{1,0:T(8,128)(2,1)S(1)}, bf16[288,384]{1,0:T(8,128)(2,1)S(1)}, u32[]{:S(2)}, u32[]{:S(2)}) collective-permute-start(bf16[288,384]{1,0:T(8,128)(2,1)S(1)} %fusion.1.refs_6_.refs_0_), channel_id=1, source_target_pairs={{0,2},{2,0},{1,3},{3,1},{4,6},{6,4},{5,7},{7,5},{8,10},{10,8},{9,1... | collective-permute-start | bytes 663560 | tf_op jit(solution)/shard_map/ppermute | solution.py:338
  71.0 12.2 %collective-permute-start.22 = (bf16[96,2048]{1,0:T(8,128)(2,1)S(1)}, bf16[96,2048]{1,0:T(8,128)(2,1)S(1)}, u32[]{:S(2)}, u32[]{:S(2)}) collective-permute-start(bf16[96,2048]{1,0:T(8,128)(2,1)S(1)} %shard_map.74.refs_5_), channel_id=1, source_target_pairs={{0,4},{4,0},{8,12},{12,8},{16,20},{20,16},{24,28},{28,24},{1,5},{5... | collective-permute-start | bytes 1179656 | tf_op jit(solution)/shard_map/ppermute | solution.py:326
  73.8 10.1 %collective-permute-start.24 = (bf16[160,768]{1,0:T(8,128)(2,1)S(1)}, bf16[160,768]{1,0:T(8,128)(2,1)S(1)}, u32[]{:S(2)}, u32[]{:S(2)}) collective-permute-start(bf16[160,768]{1,0:T(8,128)(2,1)S(1)} %get-tuple-element.40.refs_4_), channel_id=1, source_target_pairs={{0,2},{2,0},{1,3},{3,1},{4,6},{6,4},{5,7},{7,5},{8,10},{10,8},{9,1... | collective-permute-start | bytes 737288 | tf_op jit(solution)/shard_map/ppermute | solution.py:338
  77.3 10.1 %collective-permute-start.18 = (bf16[160,768]{1,0:T(8,128)(2,1)S(1)}, bf16[160,768]{1,0:T(8,128)(2,1)S(1)}, u32[]{:S(2)}, u32[]{:S(2)}) collective-permute-start(bf16[160,768]{1,0:T(8,128)(2,1)S(1)} %get-tuple-element.42.refs_4_), channel_id=1, source_target_pairs={{0,2},{2,0},{1,3},{3,1},{4,6},{6,4},{5,7},{7,5},{8,10},{10,8},{9,1... | collective-permute-start | bytes 737288 | tf_op jit(solution)/shard_map/ppermute | solution.py:338
  81.8 10.6 %collective-permute-start.21 = (bf16[96,2048]{1,0:T(8,128)(2,1)S(1)}, bf16[96,2048]{1,0:T(8,128)(2,1)S(1)}, u32[]{:S(2)}, u32[]{:S(2)}) collective-permute-start(bf16[96,2048]{1,0:T(8,128)(2,1)S(1)} %get-tuple-element.46), channel_id=1, source_target_pairs={{0,4},{4,0},{8,12},{12,8},{16,20},{20,16},{24,28},{28,24},{1,5},{5... | collective-permute-start | bytes 1179656 | tf_op jit(solution)/shard_map/ppermute | solution.py:326
  83.3 9.6 %collective-permute-start.23 = (bf16[96,2048]{1,0:T(8,128)(2,1)S(1)}, bf16[96,2048]{1,0:T(8,128)(2,1)S(1)}, u32[]{:S(2)}, u32[]{:S(2)}) collective-permute-start(bf16[96,2048]{1,0:T(8,128)(2,1)S(1)} %shard_map.82.refs_5_), channel_id=1, source_target_pairs={{0,8},{4,12},{8,16},{12,20},{16,24},{20,28},{24,0},{28,4},{1,9},{5... | collective-permute-start | bytes 1179656 | tf_op jit(solution)/shard_map/ppermute | solution.py:329
  84.0 4.9 %collective-permute-start.25 = (bf16[160,384]{1,0:T(8,128)(2,1)S(1)}, bf16[160,384]{1,0:T(8,128)(2,1)S(1)}, u32[]{:S(2)}, u32[]{:S(2)}) collective-permute-start(bf16[160,384]{1,0:T(8,128)(2,1)S(1)} %fusion.2.refs_0_.refs_7_), channel_id=1, source_target_pairs={{0,2},{2,0},{1,3},{3,1},{4,6},{6,4},{5,7},{7,5},{8,10},{10,8},{9,1... | collective-permute-start | bytes 368648 | tf_op jit(solution)/shard_map/ppermute | solution.py:338
  90.8 9.1 %collective-permute-start.26 = (bf16[96,2048]{1,0:T(8,128)(2,1)S(1)}, bf16[96,2048]{1,0:T(8,128)(2,1)S(1)}, u32[]{:S(2)}, u32[]{:S(2)}) collective-permute-start(bf16[96,2048]{1,0:T(8,128)(2,1)S(1)} %shard_map.83.refs_3_), channel_id=1, source_target_pairs={{0,4},{4,0},{8,12},{12,8},{16,20},{20,16},{24,28},{28,24},{1,5},{5... | collective-permute-start | bytes 1179656 | tf_op jit(solution)/shard_map/ppermute | solution.py:326
  93.1 10.6 %collective-permute-start.27 = (bf16[96,2048]{1,0:T(8,128)(2,1)S(1)}, bf16[96,2048]{1,0:T(8,128)(2,1)S(1)}, u32[]{:S(2)}, u32[]{:S(2)}) collective-permute-start(bf16[96,2048]{1,0:T(8,128)(2,1)S(1)} %shard_map.84.refs_5_), channel_id=1, source_target_pairs={{0,8},{4,12},{8,16},{12,20},{16,24},{20,28},{24,0},{28,4},{1,9},{5... | collective-permute-start | bytes 1179656 | tf_op jit(solution)/shard_map/ppermute | solution.py:329
  93.2 4.9 %collective-permute-start.19 = (bf16[160,384]{1,0:T(8,128)(2,1)S(1)}, bf16[160,384]{1,0:T(8,128)(2,1)S(1)}, u32[]{:S(2)}, u32[]{:S(2)}) collective-permute-start(bf16[160,384]{1,0:T(8,128)(2,1)S(1)} %fusion.3.refs_4_.refs_0_), channel_id=1, source_target_pairs={{0,2},{2,0},{1,3},{3,1},{4,6},{6,4},{5,7},{7,5},{8,10},{10,8},{9,1... | collective-permute-start | bytes 368648 | tf_op jit(solution)/shard_map/ppermute | solution.py:338
  103.8 9.6 %collective-permute-start.28 = (bf16[96,2048]{1,0:T(8,128)(2,1)S(1)}, bf16[96,2048]{1,0:T(8,128)(2,1)S(1)}, u32[]{:S(2)}, u32[]{:S(2)}) collective-permute-start(bf16[96,2048]{1,0:T(8,128)(2,1)S(1)} %shard_map.86), channel_id=1, source_target_pairs={{0,8},{4,12},{8,16},{12,20},{16,24},{20,28},{24,0},{28,4},{1,9},{5... | collective-permute-start | bytes 1179656 | tf_op jit(solution)/shard_map/ppermute | solution.py:329

commit v8 on v7

--- a/solution.py
+++ b/solution.py
@@ -144,14 +144,9 @@
     return (first + core, first + 1 - core), (rank + 1) % parts * units, rank * units, places
 
 
-def pick_kernel(width, experts, capacity, units, groups, count, kinds, split, copied, *refs):
+def pick_kernel(width, experts, capacity, units, groups, count, kinds, split, *refs):
     blocks, weights = refs[:count], refs[count:]
-    if copied:
-        *_, source_ref, chosen_ref, part_ref, target_ref, sem = refs
-        copy = pltpu.make_async_copy(source_ref, target_ref, sem)
-        copy.start()
-    else:
-        chosen_ref, part_ref = refs[-2:]
+    chosen_ref, part_ref = refs[-2:]
     rows = blocks[0].shape[0]
     mine_and_other, start, _, _ = position(units)
     offsets = layout(groups, capacity)
@@ -169,55 +164,60 @@
     for g in range(len(groups)):
         mine = weights[kinds * g:kinds * (g + 1)]
         multiply(chosen_ref, slice(offsets[g], offsets[g + 1]), mine, start if split else None, units, part_ref)
-    if copied:
-        copy.wait()
-
-
-def pick_rows(groups, blocks, weights, split, copying, after, width, experts, capacity, units):
+
+
+def pick_rows(groups, blocks, weights, split, after, width, experts, capacity, units):
     columns = 2 * units if split else weights[0][0].shape[1]
     taken = layout(groups, capacity)[-1]
     flat = [w for expert, _ in groups for w in weights[expert]]
-    copied = len(copying)
     kernel = functools.partial(
-        pick_kernel, width, experts, capacity, units, groups, len(blocks), len(weights[0]), split, copied
+        pick_kernel, width, experts, capacity, units, groups, len(blocks), len(weights[0]), split
     )
     out = (jax.ShapeDtypeStruct((taken, width), BF16), jax.ShapeDtypeStruct((taken, columns), BF16))
     return pl.pallas_call(
         kernel,
         grid=(1,),
-        out_shape=(*out, *[jax.ShapeDtypeStruct(a.shape, a.dtype) for a in copying]),
-        in_specs=[whole(x) for x in (*blocks, *flat)] + [ANY] * (len(after) + copied),
-        out_specs=(*[whole(o) for o in out], *[ANY] * copied),
-        scratch_shapes=[pltpu.SemaphoreType.DMA] * copied,
+        out_shape=out,
+        in_specs=[whole(x) for x in (*blocks, *flat)] + [ANY] * len(after),
+        out_specs=tuple(whole(o) for o in out),
         compiler_params=params(),
         cost_estimate=cost(),
-    )(*blocks, *flat, *after, *copying)
-
-
-def home_kernel(capacity, units, groups, kinds, split, passed, x_ref, *refs):
+    )(*blocks, *flat, *after)
+
+
+def home_kernel(capacity, units, groups, kinds, split, passed, copied, x_ref, *refs):
+    if copied:
+        source_ref, target_ref, sem = refs[-4 - 2 * passed], refs[-2], refs[-1]
+        copy = pltpu.make_async_copy(source_ref, target_ref, sem)
+        copy.start()
+        refs = refs[:-2]
     _, _, start, _ = position(units)
     out_ref = refs[-1 - passed]
     offsets = layout(groups, capacity)
     for g in range(len(groups)):
         mine = refs[kinds * g:kinds * (g + 1)]
         multiply(x_ref, slice(offsets[g], offsets[g + 1]), mine, start if split else None, units, out_ref)
-
-
-def home_rows(groups, chosen, weights, split, passing, after, capacity, units):
+    if copied:
+        copy.wait()
+
+
+def home_rows(groups, chosen, weights, split, passing, copying, after, capacity, units):
     flat = [w for expert, _ in groups for w in weights[expert]]
     out = jax.ShapeDtypeStruct((chosen.shape[0], 2 * units), F32)
-    args = (chosen, *flat, *after, *passing)
+    args = (chosen, *flat, *after, *copying, *passing)
+    count, copied = len(passing), len(copying)
     result = pl.pallas_call(
-        functools.partial(home_kernel, capacity, units, groups, len(weights[0]), split, len(passing)),
+        functools.partial(home_kernel, capacity, units, groups, len(weights[0]), split, count, copied),
         grid=(1,),
-        out_shape=(out, *[jax.ShapeDtypeStruct(p.shape, p.dtype) for p in passing]),
-        in_specs=[whole(chosen)] + [whole(w) for w in flat] + [ANY] * (len(after) + len(passing)),
-        out_specs=(whole(out), *[ANY] * len(passing)),
-        input_output_aliases={len(args) - len(passing) + i: 1 + i for i in range(len(passing))},
+        out_shape=(out, *[jax.ShapeDtypeStruct(p.shape, p.dtype) for p in (*passing, *copying)]),
+        in_specs=[whole(chosen)] + [whole(w) for w in flat] + [ANY] * (len(after) + copied + count),
+        out_specs=(whole(out), *[ANY] * (count + copied)),
+        input_output_aliases={len(args) - count + i: 1 + i for i in range(count)},
+        scratch_shapes=[pltpu.SemaphoreType.DMA] * copied,
         compiler_params=params(),
         cost_estimate=cost(),
     )(*args)
-    return result[0], result[1:]
+    return result[0], result[1:1 + count], result[1 + count:]
 
 
 def down_kernel(experts, capacity, groups, count, pieces, wide, passed, *refs):
@@ -383,25 +383,27 @@
     def pick(i):
         keys, groups = plan[i]
         mine = [blocks[k] for k in keys]
-        copying = [w_down] if i == 1 else []
-        chosen[i], part, *copies = pick_rows(
-            groups, mine, away, split, copying, order, width, experts, capacity, units
+        chosen[i], part = pick_rows(groups, mine, away, split, order, width, experts, capacity, units)
+        cut = units if i == 1 else 2 * units
+        parts_in[i] = []
+        for step in range(1, parts):
+            columns = range(2 * units * (step - 1), 2 * units * step, cut)
+            parts_in[i].append([over_x(part[:, c:c + cut], step) for c in columns])
+        order[:] = [part]
+
+    def home_product(i, hop=None):
+        copying = [w_down] if i == 0 else []
+        totals[i], passed, copies = home_rows(
+            plan[i][1], chosen[i], home, split, passing(hop), copying, order, capacity, units
         )
         downs.extend(over_core(c)[0] for c in copies)
-        parts_in[i] = [over_x(part[:, 2 * units * (s - 1):2 * units * s], s) for s in range(1, parts)]
-        order[:] = [part]
-
-    def home_product(i, hop=None):
-        totals[i], passed = home_rows(
-            plan[i][1], chosen[i], home, split, passing(hop), order, capacity, units
-        )
         order[:] = [totals[i]]
         take_on(hop, passed)
 
     def activate(i):
         total = totals[i]
-        for piece in parts_in[i]:
-            total = total + piece.astype(F32)
+        for pieces in parts_in[i]:
+            total = total + jnp.concatenate(pieces, axis=1).astype(F32)
         value = (jax.nn.silu(total[:, :units]) * total[:, units:]).astype(BF16)
         hidden[i] = [value] + [over_x(value, s) for s in range(1, parts)]
         order.append(value)
@@ -447,35 +449,37 @@
         pick(0)
         order.append(blocks[0, "b"])
         home_product(0, 1)
+        pick(1)
         activate(0)
-        pick(1)
         order.extend(downs[1:])
         home_product(1, 2)
         pick(2)
+        down_product(0)
         home_product(2, 3)
-        down_product(0)
         activate(2)
+        activate(1)
         pick(3)
-        activate(1)
         down_product(1)
         down_product(2)
         pick(4)
         home_product(3)
+        activate(3)
         home_product(4)
-        activate(3)
         pick(5)
+        order.append(blocks[2, "b"])
+        order.extend(downs[1:])
+        activate(4)
         home_product(5)
-        order.append(blocks[2, "b"])
-        add_hop(0)
-        down_product(3)
         add_hop(1)
         order.append(blocks[2, "b"])
-        activate(4)
+        down_product(3)
         down_product(4)
         activate(5)
         add_hop(2)
+        order.append(blocks[1, "b"])
         down_product(5)
         add_hop(3)
+        add_hop(0)
     else:
         for i in range(count):
             pick(i)

time: 115 us -> 119 us (1.035)
  starting transfers between devices: 24.8 us -> 31.2 us
  waiting for transfers between devices: 48.8 us -> 44.9 us
  local copies, waits for them, and re-layouts: 7.38 us -> 9.19 us
    ppermute x6, waiting for transfers between devices: 37.3 us -> 30.8 us  [over_z(): return lax.ppermute(x, 'expert', [(i, (i + 2) % ring) for i in range(ring)])]
    ppermute x8, waiting for transfers between devices: 2.5 us -> 8.71 us  [over_y(): return lax.ppermute(x, 'expert', [(i, i ^ 1) for i in range(ring)])]
    ppermute x12 -> x13, waiting for transfers between devices: 9.02 us -> 5.31 us  [over_x(): lax.ppermute(x, 'tensor', [(i, (i + step) % parts) for i in range(parts)])]
    ppermute x6, starting transfers between devices: 1.99 us -> 5.26 us  [over_z(): return lax.ppermute(x, 'expert', [(i, (i + 2) % ring) for i in range(ring)])]
    ppermute x8, starting transfers between devices: 10.2 us -> 12.9 us  [over_y(): return lax.ppermute(x, 'expert', [(i, i ^ 1) for i in range(ring)])]
    unnamed x16 -> x18, local copies, waits for them, and re-layouts: 7.24 us -> 9 us
    ppermute x12 -> x13, starting transfers between devices: 12 us -> 12.5 us  [over_x(): lax.ppermute(x, 'tensor', [(i, (i + step) % parts) for i in range(parts)])]
  transfers between devices with their start and end apart: 29 -> 30, of which waited for: 12 -> 12; matrix products, arithmetic and copies ran while one was open for 1% -> 1% of each run, Pallas kernels for 25% -> 26%
where the time goes in v8:
time: 119 us; the launch traced here: 118 us
  waiting for transfers between devices  44.9 us (38%)
  starting transfers between devices  31.2 us (26%)
  Pallas kernels  30.9 us (26%)
  local copies, waits for them, and re-layouts  9.19 us (8%)
  other arithmetic  1.81 us (2%)
    ppermute x6, waiting for transfers between devices, over_z(): return lax.ppermute(x, 'expert', [(i, (i + 2) % ring) for i in range(ring)])  30.8 us
    ppermute x8, starting transfers between devices, over_y(): return lax.ppermute(x, 'expert', [(i, i ^ 1) for i in range(ring)])  12.9 us
    ppermute x13, starting transfers between devices, over_x(): lax.ppermute(x, 'tensor', [(i, (i + step) % parts) for i in range(parts)])  12.5 us
    pallas_call x6, Pallas kernels, pick_rows(): pl.pallas_call(kernel, grid=(1,), out_shape=out, in_specs=[whole(x) for x...  11.7 us
    pallas_call x6, Pallas kernels, down_rows(): pl.pallas_call(functools.partial(down_kernel, experts, capacity, groups,...  11.1 us
    unnamed x18, local copies, waits for them, and re-layouts  9 us
    ppermute x8, waiting for transfers between devices, over_y(): return lax.ppermute(x, 'expert', [(i, i ^ 1) for i in range(ring)])  8.71 us
    pallas_call x6, Pallas kernels, home_rows(): pl.pallas_call(functools.partial(home_kernel, capacity, units, groups, le...  7.16 us
  transfers between devices with their start and end apart: 30, of which 12 were waited for; matrix products, arithmetic and copies ran while one was open for 1% of the time, Pallas kernels for 26%

profile of v8, /device:TPU:0, one launch (start us, length us, event | category | flops | bytes accessed | tf_op | source)
XLA Modules:
  0.0 118.4 jit_solution(15751503700847016452)
XLA Ops:
  0.0 0.5 collective-permute-start.5
  0.5 1.0 copy-done.6
  1.5 0.7 copy-done.7
  2.2 0.7 copy-done.8
  2.9 0.5 shard_map.64.refs_0_.refs_2_
  3.4 3.1 %collective-permute-start.1 = (bf16[96,2176]{1,0:T(8,128)(2,1)S(1)}, bf16[96,2176]{1,0:T(8,128)(2,1)S(1)}, u32[]{:S(2)}, u32[]{:S(2)}) collective-permute-start(bf16[96,2176]{1,0:T(8,128)(2,1)S(1)} %shard_map.64.refs_0_.refs_2_), channel_id=1, source_target_pairs={{0,8},{4,12},{8,16},{12,20},{16,24},{20,28},{24,0},{28,4},{1,9},{5... | collective-permute-start | bytes 1253384 | tf_op jit(solution)/shard_map/ppermute | solution.py:329
  6.5 1.5 %collective-permute-start = (bf16[96,2176]{1,0:T(8,128)(2,1)S(1)}, bf16[96,2176]{1,0:T(8,128)(2,1)S(1)}, u32[]{:S(2)}, u32[]{:S(2)}) collective-permute-start(bf16[96,2176]{1,0:T(8,128)(2,1)S(1)} %shard_map.64.refs_0_.refs_2_), channel_id=1, source_target_pairs={{0,4},{4,0},{8,12},{12,8},{16,20},{20,16},{24,28},{28,24},{1,5},{5... | collective-permute-start | bytes 1253384 | tf_op jit(solution)/shard_map/ppermute | solution.py:326
  8.0 1.9 %copy-done = bf16[1,2048,768]{2,1,0:T(8,128)(2,1)S(1)} copy-done((bf16[1,2048,768]{2,1,0:T(8,128)(2,1)S(1)}, bf16[1,2048,768]{2,1,0:T(8,128)(2,1)}, u32[]{:S(2)}) %copy-start) | copy-done | bytes 3145752
  9.9 1.9 %copy-done.2 = bf16[1,2048,768]{2,1,0:T(8,128)(2,1)S(1)} copy-done((bf16[1,2048,768]{2,1,0:T(8,128)(2,1)S(1)}, bf16[1,2048,768]{2,1,0:T(8,128)(2,1)}, u32[]{:S(2)}) %copy-start.2) | copy-done | bytes 3145752
  11.8 1.1 shard_map.65
  12.8 5.4 %collective-permute-done.1.refs_5_ = bf16[96,2176]{1,0:T(8,128)(2,1)S(1)} collective-permute-done((bf16[96,2176]{1,0:T(8,128)(2,1)S(1)}, bf16[96,2176]{1,0:T(8,128)(2,1)S(1)}, u32[]{:S(2)}, u32[]{:S(2)}) %collective-permute-start.1) | collective-permute-done | bytes 417824 | tf_op jit(solution)/shard_map/ppermute | solution.py:329
  18.3 1.9 %copy-done.4 = bf16[1,768,2048]{2,1,0:T(8,128)(2,1)S(1)} copy-done((bf16[1,768,2048]{2,1,0:T(8,128)(2,1)S(1)}, bf16[1,768,2048]{2,1,0:T(8,128)(2,1)}, u32[]{:S(2)}) %copy-start.4) | copy-done | bytes 3145752
  20.2 0.9 shard_map.66
  21.2 1.6 %collective-permute-start.2 = (bf16[80,768]{1,0:T(8,128)(2,1)S(1)}, bf16[80,768]{1,0:T(8,128)(2,1)S(1)}, u32[]{:S(2)}, u32[]{:S(2)}) collective-permute-start(bf16[80,768]{1,0:T(8,128)(2,1)S(1)} %get-tuple-element.25.refs_2_), channel_id=1, source_target_pairs={{0,2},{2,0},{1,3},{3,1},{4,6},{6,4},{5,7},{7,5},{8,10},{10,8},{9,1... | collective-permute-start | bytes 368648 | tf_op jit(solution)/shard_map/ppermute | solution.py:338
  22.7 1.0 collective-permute-start.8
  23.8 1.5 %collective-permute-start.4 = (bf16[96,2176]{1,0:T(8,128)(2,1)S(1)}, bf16[96,2176]{1,0:T(8,128)(2,1)S(1)}, u32[]{:S(2)}, u32[]{:S(2)}) collective-permute-start(bf16[96,2176]{1,0:T(8,128)(2,1)S(1)} %get-tuple-element.27.refs_2_.refs_4_), channel_id=1, source_target_pairs={{0,4},{4,0},{8,12},{12,8},{16,20},{20,16},{24,28},{28,24},{1,5},{5... | collective-permute-start | bytes 1253384 | tf_op jit(solution)/shard_map/ppermute | solution.py:326
  25.3 2.6 %shard_map.67 = (bf16[368,2048]{1,0:T(8,128)(2,1)S(1)}, bf16[368,768]{1,0:T(8,128)(2,1)S(1)}) custom-call(bf16[96,2176]{1,0:T(8,128)(2,1)S(1)} %shard_map.64.refs_0_.refs_2_, bf16[96,2176]{1,0:T(8,128)(2,1)S(1)} %collective-permute-done.refs_3_.refs_1_, bf16[96,2176]{1,0:T(8,128)(2,1)S(1)} %get-tuple-element.27.refs_2_.refs_4_, ...), custom_call_target="tpu_custom_call" | custom-call | flops 1 | bytes 1 | tf_op jit(solution)/shard_map/pallas_call | solution.py:177
  27.9 0.6 collective-permute-start.9
  28.5 1.5 %collective-permute-start.10 = (bf16[368,384]{1,0:T(8,128)(2,1)S(1)}, bf16[368,384]{1,0:T(8,128)(2,1)S(1)}, u32[]{:S(2)}, u32[]{:S(2)}) collective-permute-start(bf16[368,384]{1,0:T(8,128)(2,1)S(1)} %get-tuple-element.49), channel_id=1, source_target_pairs={{0,2},{2,0},{1,3},{3,1},{4,6},{6,4},{5,7},{7,5},{8,10},{10,8},{9,1... | collective-permute-start | bytes 847880 | tf_op jit(solution)/shard_map/ppermute | solution.py:338
  30.1 6.2 %collective-permute-done.8.refs_7_ = bf16[96,2176]{1,0:T(8,128)(2,1)S(1)} collective-permute-done((bf16[96,2176]{1,0:T(8,128)(2,1)S(1)}, bf16[96,2176]{1,0:T(8,128)(2,1)S(1)}, u32[]{:S(2)}, u32[]{:S(2)}) %collective-permute-start.8) | collective-permute-done | bytes 417824 | tf_op jit(solution)/shard_map/ppermute | solution.py:329
  36.3 0.5 collective-permute-start.3
  36.8 1.4 %shard_map.68 = (f32[368,768]{1,0:T(8,128)S(1)}, bf16[96,2176]{1,0:T(8,128)(2,1)S(1)}) custom-call(bf16[368,2048]{1,0:T(8,128)(2,1)S(1)} %get-tuple-element.28.x_ref, bf16[2048,768]{1,0:T(8,128)(2,1)S(1)} %bitcast.33, bf16[2048,768]{1,0:T(8,128)(2,1)S(1)} %bitcast.43, bf16[2048,768]{1,0:T(8,128)(2,1)S(1)} %bitcast.11, ...), custom_call_target="tpu_custom_call", output_to_operand_aliasing={{1}: (8, {})} | custom-call | flops 1 | bytes 1 | tf_op jit(solution)/shard_map/pallas_call | solution.py:209
  38.2 0.2 collective-permute-start.13
  38.4 1.6 %collective-permute-start.12 = (bf16[96,2176]{1,0:T(8,128)(2,1)S(1)}, bf16[96,2176]{1,0:T(8,128)(2,1)S(1)}, u32[]{:S(2)}, u32[]{:S(2)}) collective-permute-start(bf16[96,2176]{1,0:T(8,128)(2,1)S(1)} %get-tuple-element.33.refs_1_.refs_3_), channel_id=1, source_target_pairs={{0,4},{4,0},{8,12},{12,8},{16,20},{20,16},{24,28},{28,24},{1,5},{5... | collective-permute-start | bytes 1253384 | tf_op jit(solution)/shard_map/ppermute | solution.py:326
  40.0 1.9 %shard_map.69 = (bf16[160,2048]{1,0:T(8,128)(2,1)S(1)}, bf16[160,768]{1,0:T(8,128)(2,1)S(1)}) custom-call(bf16[96,2176]{1,0:T(8,128)(2,1)S(1)} %collective-permute-done.4.refs_0_.refs_2_.refs_6_, bf16[2048,768]{1,0:T(8,128)(2,1)S(1)} %bitcast.12, bf16[2048,768]{1,0:T(8,128)(2,1)S(1)} %bitcast.24, bf16[2048,768]{1,0:T(8,128)(2,1)S(1)} %bitcast.34, ...), custom_call_target="tpu_custom_call" | custom-call | flops 1 | bytes 1 | tf_op jit(solution)/shard_map/pallas_call | solution.py:177
  42.0 1.5 %collective-permute-start.14 = (bf16[160,768]{1,0:T(8,128)(2,1)S(1)}, bf16[160,768]{1,0:T(8,128)(2,1)S(1)}, u32[]{:S(2)}, u32[]{:S(2)}) collective-permute-start(bf16[160,768]{1,0:T(8,128)(2,1)S(1)} %get-tuple-element.32.refs_4_), channel_id=1, source_target_pairs={{0,2},{2,0},{1,3},{3,1},{4,6},{6,4},{5,7},{7,5},{8,10},{10,8},{9,1... | collective-permute-start | bytes 737288 | tf_op jit(solution)/shard_map/ppermute | solution.py:338
  43.8 0.6 collective-permute-start.11
  44.5 1.0 copy-done.5
  45.4 1.1 shard_map.70.refs_4_.refs_0_
  46.5 4.3 %collective-permute-done.13.refs_5_ = bf16[96,2176]{1,0:T(8,128)(2,1)S(1)} collective-permute-done((bf16[96,2176]{1,0:T(8,128)(2,1)S(1)}, bf16[96,2176]{1,0:T(8,128)(2,1)S(1)}, u32[]{:S(2)}, u32[]{:S(2)}) %collective-permute-start.13) | collective-permute-done | bytes 417824 | tf_op jit(solution)/shard_map/ppermute | solution.py:329
  50.8 1.2 %shard_map.71 = (f32[160,768]{1,0:T(8,128)S(1)}, bf16[96,2176]{1,0:T(8,128)(2,1)S(1)}) custom-call(bf16[160,2048]{1,0:T(8,128)(2,1)S(1)} %get-tuple-element.34.x_ref, bf16[2048,768]{1,0:T(8,128)(2,1)S(1)} %bitcast.13, bf16[2048,768]{1,0:T(8,128)(2,1)S(1)} %bitcast.25, bf16[2048,768]{1,0:T(8,128)(2,1)S(1)} %bitcast.35, ...), custom_call_target="tpu_custom_call", output_to_operand_aliasing={{1}: (6, {})} | custom-call | flops 1 | bytes 1 | tf_op jit(solution)/shard_map/pallas_call | solution.py:209
  52.2 1.6 %collective-permute-start.17 = (bf16[160,384]{1,0:T(8,128)(2,1)S(1)}, bf16[160,384]{1,0:T(8,128)(2,1)S(1)}, u32[]{:S(2)}, u32[]{:S(2)}) collective-permute-start(bf16[160,384]{1,0:T(8,128)(2,1)S(1)} %fusion.4.refs_7_.refs_0_), channel_id=1, source_target_pairs={{0,2},{2,0},{1,3},{3,1},{4,6},{6,4},{5,7},{7,5},{8,10},{10,8},{9,1... | collective-permute-start | bytes 368648 | tf_op jit(solution)/shard_map/ppermute | solution.py:338
  53.8 1.5 %collective-permute-start.16 = (bf16[96,2176]{1,0:T(8,128)(2,1)S(1)}, bf16[96,2176]{1,0:T(8,128)(2,1)S(1)}, u32[]{:S(2)}, u32[]{:S(2)}) collective-permute-start(bf16[96,2176]{1,0:T(8,128)(2,1)S(1)} %get-tuple-element.37.refs_0_.refs_2_), channel_id=1, source_target_pairs={{0,4},{4,0},{8,12},{12,8},{16,20},{20,16},{24,28},{28,24},{1,5},{5... | collective-permute-start | bytes 1253384 | tf_op jit(solution)/shard_map/ppermute | solution.py:326
  55.3 2.0 %shard_map.72 = (bf16[288,2048]{1,0:T(8,128)(2,1)S(1)}, bf16[288,768]{1,0:T(8,128)(2,1)S(1)}) custom-call(bf16[96,2176]{1,0:T(8,128)(2,1)S(1)} %collective-permute-done.12.refs_0_.refs_5_.refs_2_.refs_7_, bf16[96,2176]{1,0:T(8,128)(2,1)S(1)} %get-tuple-element.33.refs_1_.refs_3_, bf16[2048,768]{1,0:T(8,128)(2,1)S(1)} %bitcast.14, ...), custom_call_target="tpu_custom_call" | custom-call | flops 1 | bytes 1 | tf_op jit(solution)/shard_map/pallas_call | solution.py:177
  57.3 0.6 collective-permute-start.18
  57.9 2.7 %shard_map.73.refs_5_ = bf16[288,2048]{1,0:T(8,128)(2,1)S(1)} custom-call(bf16[368,384]{1,0:T(8,128)(2,1)S(1)} %fusion.refs_8_.refs_0_, bf16[368,384]{1,0:T(8,128)(2,1)S(1)} %collective-permute-done.11.refs_1_, bf16[96,2176]{1,0:T(8,128)(2,1)S(1)} %shard_map.64.refs_0_.refs_2_, bf16[96,2176]{1,0:T(8,128)(2,1)S(1)} %collective-permute-done.refs_3_.refs_1_, ...), custom_call_target="tpu_custom_call" | custom-call | flops 1 | bytes 1 | tf_op jit(solution)/shard_map/pallas_call | solution.py:278
  60.7 1.7 %shard_map.74.refs_5_ = bf16[96,2048]{1,0:T(8,128)(2,1)S(1)} custom-call(bf16[160,384]{1,0:T(8,128)(2,1)S(1)} %fusion.4.refs_7_.refs_0_, bf16[160,384]{1,0:T(8,128)(2,1)S(1)} %collective-permute-done.17.refs_1_, bf16[96,2176]{1,0:T(8,128)(2,1)S(1)} %collective-permute-done.4.refs_0_.refs_2_.refs_6_, bf16[768,2048]{1,0:T(8,128)(2,1)S(1)} %bitcast.54, ...), custom_call_target="tpu_custom_call" | custom-call | flops 1 | bytes 1 | tf_op jit(solution)/shard_map/pallas_call | solution.py:278
  62.4 0.6 collective-permute-start.23
  62.9 1.1 collective-permute-done.16.refs_0_.refs_2_
  64.0 1.9 %shard_map.75 = (bf16[160,2048]{1,0:T(8,128)(2,1)S(1)}, bf16[160,768]{1,0:T(8,128)(2,1)S(1)}) custom-call(bf16[96,2176]{1,0:T(8,128)(2,1)S(1)} %collective-permute-done.16.refs_0_.refs_2_, bf16[2048,768]{1,0:T(8,128)(2,1)S(1)} %bitcast.15, bf16[2048,768]{1,0:T(8,128)(2,1)S(1)} %bitcast.27, bf16[2048,768]{1,0:T(8,128)(2,1)S(1)} %bitcast.37, ...), custom_call_target="tpu_custom_call" | custom-call | flops 1 | bytes 1 | tf_op jit(solution)/shard_map/pallas_call | solution.py:177
  66.0 0.5 collective-permute-start.19
  66.5 1.1 shard_map.76.refs_4_
  67.6 1.7 %collective-permute-done.18 = bf16[288,768]{1,0:T(8,128)(2,1)S(1)} collective-permute-done((bf16[288,768]{1,0:T(8,128)(2,1)S(1)}, bf16[288,768]{1,0:T(8,128)(2,1)S(1)}, u32[]{:S(2)}, u32[]{:S(2)}) %collective-permute-start.18) | collective-permute-done | bytes 442400 | tf_op jit(solution)/shard_map/ppermute | solution.py:338
  69.5 1.3 %shard_map.77.refs_5_ = f32[160,768]{1,0:T(8,128)S(1)} custom-call(bf16[160,2048]{1,0:T(8,128)(2,1)S(1)} %get-tuple-element.38.x_ref, bf16[2048,768]{1,0:T(8,128)(2,1)S(1)} %bitcast.17, bf16[2048,768]{1,0:T(8,128)(2,1)S(1)} %bitcast.29, bf16[2048,768]{1,0:T(8,128)(2,1)S(1)} %bitcast.39, bf16[2048,768]{1,0:T(8,128)(2,1)S(1)} %bitcast.49, ...), custom_call_target="tpu_custom_call" | custom-call | flops 1 | bytes 1 | tf_op jit(solution)/shard_map/pallas_call | solution.py:209
  70.8 1.3 %collective-permute-start.22 = (bf16[288,384]{1,0:T(8,128)(2,1)S(1)}, bf16[288,384]{1,0:T(8,128)(2,1)S(1)}, u32[]{:S(2)}, u32[]{:S(2)}) collective-permute-start(bf16[288,384]{1,0:T(8,128)(2,1)S(1)} %fusion.1.refs_5_.refs_0_), channel_id=1, source_target_pairs={{0,2},{2,0},{1,3},{3,1},{4,6},{6,4},{5,7},{7,5},{8,10},{10,8},{9,1... | collective-permute-start | bytes 663560 | tf_op jit(solution)/shard_map/ppermute | solution.py:338
  72.1 2.1 %shard_map.78 = (bf16[160,2048]{1,0:T(8,128)(2,1)S(1)}, bf16[160,768]{1,0:T(8,128)(2,1)S(1)}) custom-call(bf16[96,2176]{1,0:T(8,128)(2,1)S(1)} %get-tuple-element.37.refs_0_.refs_2_, bf16[2048,768]{1,0:T(8,128)(2,1)S(1)} %bitcast.18, bf16[2048,768]{1,0:T(8,128)(2,1)S(1)} %bitcast.30, bf16[2048,768]{1,0:T(8,128)(2,1)S(1)} %bitcast.40, ...), custom_call_target="tpu_custom_call" | custom-call | flops 1 | bytes 1 | tf_op jit(solution)/shard_map/pallas_call | solution.py:177
  74.2 0.8 collective-permute-start.20
  75.2 1.3 %collective-permute-start.26 = (bf16[160,384]{1,0:T(8,128)(2,1)S(1)}, bf16[160,384]{1,0:T(8,128)(2,1)S(1)}, u32[]{:S(2)}, u32[]{:S(2)}) collective-permute-start(bf16[160,384]{1,0:T(8,128)(2,1)S(1)} %fusion.3.refs_7_.refs_0_), channel_id=1, source_target_pairs={{0,2},{2,0},{1,3},{3,1},{4,6},{6,4},{5,7},{7,5},{8,10},{10,8},{9,1... | collective-permute-start | bytes 368648 | tf_op jit(solution)/shard_map/ppermute | solution.py:338
  76.5 1.2 %shard_map.79.refs_2_ = f32[160,768]{1,0:T(8,128)S(1)} custom-call(bf16[160,2048]{1,0:T(8,128)(2,1)S(1)} %get-tuple-element.41.x_ref, bf16[2048,768]{1,0:T(8,128)(2,1)S(1)} %bitcast.19, bf16[2048,768]{1,0:T(8,128)(2,1)S(1)} %bitcast.31, bf16[2048,768]{1,0:T(8,128)(2,1)S(1)} %bitcast.41, bf16[2048,768]{1,0:T(8,128)(2,1)S(1)} %bitcast.51, ...), custom_call_target="tpu_custom_call" | custom-call | flops 1 | bytes 1 | tf_op jit(solution)/shard_map/pallas_call | solution.py:209
  77.9 0.8 collective-permute-start.25
  78.7 1.0 collective-permute-done.22.refs_1_
  79.7 2.3 %shard_map.81.refs_5_ = bf16[192,2048]{1,0:T(8,128)(2,1)S(1)} custom-call(bf16[288,384]{1,0:T(8,128)(2,1)S(1)} %fusion.1.refs_5_.refs_0_, bf16[288,384]{1,0:T(8,128)(2,1)S(1)} %collective-permute-done.22.refs_1_, bf16[96,2176]{1,0:T(8,128)(2,1)S(1)} %collective-permute-done.12.refs_0_.refs_5_.refs_2_.refs_7_, ...), custom_call_target="tpu_custom_call" | custom-call | flops 1 | bytes 1 | tf_op jit(solution)/shard_map/pallas_call | solution.py:278
  82.0 2.5 %collective-permute-start.24 = (bf16[96,2048]{1,0:T(8,128)(2,1)S(1)}, bf16[96,2048]{1,0:T(8,128)(2,1)S(1)}, u32[]{:S(2)}, u32[]{:S(2)}) collective-permute-start(bf16[96,2048]{1,0:T(8,128)(2,1)S(1)} %get-tuple-element.46), channel_id=1, source_target_pairs={{0,4},{4,0},{8,12},{12,8},{16,20},{20,16},{24,28},{28,24},{1,5},{5... | collective-permute-start | bytes 1179656 | tf_op jit(solution)/shard_map/ppermute | solution.py:326
  84.7 0.3 collective-permute-done.26.refs_1_
  84.9 1.7 %shard_map.82.refs_3_ = bf16[96,2048]{1,0:T(8,128)(2,1)S(1)} custom-call(bf16[160,384]{1,0:T(8,128)(2,1)S(1)} %fusion.3.refs_7_.refs_0_, bf16[160,384]{1,0:T(8,128)(2,1)S(1)} %collective-permute-done.26.refs_1_, bf16[96,2176]{1,0:T(8,128)(2,1)S(1)} %collective-permute-done.16.refs_0_.refs_2_, bf16[768,2048]{1,0:T(8,128)(2,1)S(1)} %bitcast.56, ...), custom_call_target="tpu_custom_call" | custom-call | flops 1 | bytes 1 | tf_op jit(solution)/shard_map/pallas_call | solution.py:278
  86.6 1.2 collective-permute-start.27
  87.8 6.2 %collective-permute-done.24.refs_1_ = bf16[96,2048]{1,0:T(8,128)(2,1)S(1)} collective-permute-done((bf16[96,2048]{1,0:T(8,128)(2,1)S(1)}, bf16[96,2048]{1,0:T(8,128)(2,1)S(1)}, u32[]{:S(2)}, u32[]{:S(2)}) %collective-permute-start.24) | collective-permute-done | bytes 393248 | tf_op jit(solution)/shard_map/ppermute | solution.py:326
  94.3 2.5 %collective-permute-start.15 = (bf16[96,2048]{1,0:T(8,128)(2,1)S(1)}, bf16[96,2048]{1,0:T(8,128)(2,1)S(1)}, u32[]{:S(2)}, u32[]{:S(2)}) collective-permute-start(bf16[96,2048]{1,0:T(8,128)(2,1)S(1)} %get-tuple-element.44), channel_id=1, source_target_pairs={{0,4},{4,0},{8,12},{12,8},{16,20},{20,16},{24,28},{28,24},{1,5},{5... | collective-permute-start | bytes 1179656 | tf_op jit(solution)/shard_map/ppermute | solution.py:326
  96.9 2.3 %collective-permute-done.21.refs_1_ = bf16[160,384]{1,0:T(8,128)(2,1)S(1)} collective-permute-done((bf16[160,384]{1,0:T(8,128)(2,1)S(1)}, bf16[160,384]{1,0:T(8,128)(2,1)S(1)}, u32[]{:S(2)}, u32[]{:S(2)}) %collective-permute-start.21) | collective-permute-done | bytes 122912 | tf_op jit(solution)/shard_map/ppermute | solution.py:338
  99.2 1.7 %shard_map.84.refs_0_.refs_3_ = bf16[96,2048]{1,0:T(8,128)(2,1)S(1)} custom-call(bf16[160,384]{1,0:T(8,128)(2,1)S(1)} %fusion.2.refs_4_.refs_0_, bf16[160,384]{1,0:T(8,128)(2,1)S(1)} %collective-permute-done.21.refs_1_, bf16[96,2176]{1,0:T(8,128)(2,1)S(1)} %get-tuple-element.37.refs_0_.refs_2_, bf16[768,2048]{1,0:T(8,128)(2,1)S(1)} %bitcast.57, ...), custom_call_target="tpu_custom_call" | custom-call | flops 1 | bytes 1 | tf_op jit(solution)/shard_map/pallas_call | solution.py:278
  100.9 1.4 %collective-permute-done.27.refs_1_ = bf16[96,2048]{1,0:T(8,128)(2,1)S(1)} collective-permute-done((bf16[96,2048]{1,0:T(8,128)(2,1)S(1)}, bf16[96,2048]{1,0:T(8,128)(2,1)S(1)}, u32[]{:S(2)}, u32[]{:S(2)}) %collective-permute-start.27) | collective-permute-done | bytes 393248 | tf_op jit(solution)/shard_map/ppermute | solution.py:326
  102.2 5.5 %collective-permute-done.28.refs_2_ = bf16[96,2048]{1,0:T(8,128)(2,1)S(1)} collective-permute-done((bf16[96,2048]{1,0:T(8,128)(2,1)S(1)}, bf16[96,2048]{1,0:T(8,128)(2,1)S(1)}, u32[]{:S(2)}, u32[]{:S(2)}) %collective-permute-start.28) | collective-permute-done | bytes 393248 | tf_op jit(solution)/shard_map/ppermute | solution.py:329
  108.1 9.4 %collective-permute-done.29 = bf16[96,2048]{1,0:T(8,128)(2,1)S(1)} collective-permute-done((bf16[96,2048]{1,0:T(8,128)(2,1)S(1)}, bf16[96,2048]{1,0:T(8,128)(2,1)S(1)}, u32[]{:S(2)}, u32[]{:S(2)}) %collective-permute-start.29) | collective-permute-done | bytes 393248 | tf_op jit(solution)/shard_map/ppermute | solution.py:329
  117.5 0.8 add_convert_fusion
  (53 shorter events, 2.1 us)
Async XLA Ops:
  0.0 23.8 %collective-permute-start.5 = (bf16[1,2048,768]{2,1,0:T(8,128)(2,1)}, bf16[1,2048,768]{2,1,0:T(8,128)(2,1)S(1)}, u32[]{:S(2)}, u32[]{:S(2)}) collective-permute-start(bf16[1,2048,768]{2,1,0:T(8,128)(2,1)} %param.9), channel_id=1, source_target_pairs={{0,1},{1,0},{2,3},{3,2},{4,5},{5,4},{6,7},{7,6},{8,9},{9,8},{10,11... | collective-permute-start | bytes 9437192 | tf_op jit(solution)/shard_map/ppermute | solution.py:335
  0.5 24.8 %collective-permute-start.6 = (bf16[1,2048,768]{2,1,0:T(8,128)(2,1)}, bf16[1,2048,768]{2,1,0:T(8,128)(2,1)S(1)}, u32[]{:S(2)}, u32[]{:S(2)}) collective-permute-start(bf16[1,2048,768]{2,1,0:T(8,128)(2,1)} %param.10), channel_id=1, source_target_pairs={{0,1},{1,0},{2,3},{3,2},{4,5},{5,4},{6,7},{7,6},{8,9},{9,8},{10,11... | collective-permute-start | bytes 9437192 | tf_op jit(solution)/shard_map/ppermute | solution.py:335
  0.5 1.0 copy-start.6
  1.5 0.7 copy-start.7
  2.2 0.7 copy-start.8
  3.4 14.9 %collective-permute-start.1 = (bf16[96,2176]{1,0:T(8,128)(2,1)S(1)}, bf16[96,2176]{1,0:T(8,128)(2,1)S(1)}, u32[]{:S(2)}, u32[]{:S(2)}) collective-permute-start(bf16[96,2176]{1,0:T(8,128)(2,1)S(1)} %shard_map.64.refs_0_.refs_2_), channel_id=1, source_target_pairs={{0,8},{4,12},{8,16},{12,20},{16,24},{20,28},{24,0},{28,4},{1,9},{5... | collective-permute-start | bytes 1253384 | tf_op jit(solution)/shard_map/ppermute | solution.py:329
  6.5 11.8 %collective-permute-start = (bf16[96,2176]{1,0:T(8,128)(2,1)S(1)}, bf16[96,2176]{1,0:T(8,128)(2,1)S(1)}, u32[]{:S(2)}, u32[]{:S(2)}) collective-permute-start(bf16[96,2176]{1,0:T(8,128)(2,1)S(1)} %shard_map.64.refs_0_.refs_2_), channel_id=1, source_target_pairs={{0,4},{4,0},{8,12},{12,8},{16,20},{20,16},{24,28},{28,24},{1,5},{5... | collective-permute-start | bytes 1253384 | tf_op jit(solution)/shard_map/ppermute | solution.py:326
  8.0 1.9 %copy-start = (bf16[1,2048,768]{2,1,0:T(8,128)(2,1)S(1)}, bf16[1,2048,768]{2,1,0:T(8,128)(2,1)}, u32[]{:S(2)}) copy-start(bf16[1,2048,768]{2,1,0:T(8,128)(2,1)} %param.9) | copy-start | bytes 9437188
  9.9 1.9 %copy-start.2 = (bf16[1,2048,768]{2,1,0:T(8,128)(2,1)S(1)}, bf16[1,2048,768]{2,1,0:T(8,128)(2,1)}, u32[]{:S(2)}) copy-start(bf16[1,2048,768]{2,1,0:T(8,128)(2,1)} %param.10) | copy-start | bytes 9437188
  11.8 6.5 %copy-start.1 = (bf16[1,2048,768]{2,1,0:T(8,128)(2,1)S(1)}, bf16[1,2048,768]{2,1,0:T(8,128)(2,1)}, u32[]{:S(2)}) copy-start(bf16[1,2048,768]{2,1,0:T(8,128)(2,1)} %param.9) | copy-start | bytes 9437188
  11.8 6.5 %copy-start.3 = (bf16[1,2048,768]{2,1,0:T(8,128)(2,1)S(1)}, bf16[1,2048,768]{2,1,0:T(8,128)(2,1)}, u32[]{:S(2)}) copy-start(bf16[1,2048,768]{2,1,0:T(8,128)(2,1)} %param.10) | copy-start | bytes 9437188
  18.3 1.9 %copy-start.4 = (bf16[1,768,2048]{2,1,0:T(8,128)(2,1)S(1)}, bf16[1,768,2048]{2,1,0:T(8,128)(2,1)}, u32[]{:S(2)}) copy-start(bf16[1,768,2048]{2,1,0:T(8,128)(2,1)} %refs_4_.1) | copy-start | bytes 9437188
  21.1 15.7 %collective-permute-start.7 = (bf16[1,768,2048]{2,1,0:T(8,128)(2,1)S(1)}, bf16[1,768,2048]{2,1,0:T(8,128)(2,1)S(1)}, u32[]{:S(2)}, u32[]{:S(2)}) collective-permute-start(bf16[1,768,2048]{2,1,0:T(8,128)(2,1)S(1)} %get-tuple-element.30), channel_id=1, source_target_pairs={{0,1},{1,0},{2,3},{3,2},{4,5},{5,4},{6,7},{7,6},{8,9},{9,8},{10,11... | collective-permute-start | bytes 9437192 | tf_op jit(solution)/shard_map/ppermute | solution.py:335
  21.2 7.3 %collective-permute-start.2 = (bf16[80,768]{1,0:T(8,128)(2,1)S(1)}, bf16[80,768]{1,0:T(8,128)(2,1)S(1)}, u32[]{:S(2)}, u32[]{:S(2)}) collective-permute-start(bf16[80,768]{1,0:T(8,128)(2,1)S(1)} %get-tuple-element.25.refs_2_), channel_id=1, source_target_pairs={{0,2},{2,0},{1,3},{3,1},{4,6},{6,4},{5,7},{7,5},{8,10},{10,8},{9,1... | collective-permute-start | bytes 368648 | tf_op jit(solution)/shard_map/ppermute | solution.py:338
  22.7 13.5 %collective-permute-start.8 = (bf16[96,2176]{1,0:T(8,128)(2,1)S(1)}, bf16[96,2176]{1,0:T(8,128)(2,1)S(1)}, u32[]{:S(2)}, u32[]{:S(2)}) collective-permute-start(bf16[96,2176]{1,0:T(8,128)(2,1)S(1)} %get-tuple-element.27.refs_2_.refs_4_), channel_id=1, source_target_pairs={{0,8},{4,12},{8,16},{12,20},{16,24},{20,28},{24,0},{28,4},{1,9},{5... | collective-permute-start | bytes 1253384 | tf_op jit(solution)/shard_map/ppermute | solution.py:329
  23.8 14.7 %collective-permute-start.4 = (bf16[96,2176]{1,0:T(8,128)(2,1)S(1)}, bf16[96,2176]{1,0:T(8,128)(2,1)S(1)}, u32[]{:S(2)}, u32[]{:S(2)}) collective-permute-start(bf16[96,2176]{1,0:T(8,128)(2,1)S(1)} %get-tuple-element.27.refs_2_.refs_4_), channel_id=1, source_target_pairs={{0,4},{4,0},{8,12},{12,8},{16,20},{20,16},{24,28},{28,24},{1,5},{5... | collective-permute-start | bytes 1253384 | tf_op jit(solution)/shard_map/ppermute | solution.py:326
  27.9 14.1 %collective-permute-start.9 = (bf16[368,384]{1,0:T(8,128)(2,1)S(1)}, bf16[368,384]{1,0:T(8,128)(2,1)S(1)}, u32[]{:S(2)}, u32[]{:S(2)}) collective-permute-start(bf16[368,384]{1,0:T(8,128)(2,1)S(1)} %get-tuple-element.48), channel_id=1, source_target_pairs={{0,2},{2,0},{1,3},{3,1},{4,6},{6,4},{5,7},{7,5},{8,10},{10,8},{9,1... | collective-permute-start | bytes 847880 | tf_op jit(solution)/shard_map/ppermute | solution.py:338
  28.5 15.0 %collective-permute-start.10 = (bf16[368,384]{1,0:T(8,128)(2,1)S(1)}, bf16[368,384]{1,0:T(8,128)(2,1)S(1)}, u32[]{:S(2)}, u32[]{:S(2)}) collective-permute-start(bf16[368,384]{1,0:T(8,128)(2,1)S(1)} %get-tuple-element.49), channel_id=1, source_target_pairs={{0,2},{2,0},{1,3},{3,1},{4,6},{6,4},{5,7},{7,5},{8,10},{10,8},{9,1... | collective-permute-start | bytes 847880 | tf_op jit(solution)/shard_map/ppermute | solution.py:338
  36.3 8.2 %collective-permute-start.3 = (bf16[80,384]{1,0:T(8,128)(2,1)S(1)}, bf16[80,384]{1,0:T(8,128)(2,1)S(1)}, u32[]{:S(2)}, u32[]{:S(2)}) collective-permute-start(bf16[80,384]{1,0:T(8,128)(2,1)S(1)} %fusion.5.refs_5_.refs_0_), channel_id=1, source_target_pairs={{0,2},{2,0},{1,3},{3,1},{4,6},{6,4},{5,7},{7,5},{8,10},{10,8},{9,1... | collective-permute-start | bytes 184328 | tf_op jit(solution)/shard_map/ppermute | solution.py:338
  38.2 12.6 %collective-permute-start.13 = (bf16[96,2176]{1,0:T(8,128)(2,1)S(1)}, bf16[96,2176]{1,0:T(8,128)(2,1)S(1)}, u32[]{:S(2)}, u32[]{:S(2)}) collective-permute-start(bf16[96,2176]{1,0:T(8,128)(2,1)S(1)} %get-tuple-element.33.refs_1_.refs_3_), channel_id=1, source_target_pairs={{0,8},{4,12},{8,16},{12,20},{16,24},{20,28},{24,0},{28,4},{1,9},{5... | collective-permute-start | bytes 1253384 | tf_op jit(solution)/shard_map/ppermute | solution.py:329
  38.4 16.9 %collective-permute-start.12 = (bf16[96,2176]{1,0:T(8,128)(2,1)S(1)}, bf16[96,2176]{1,0:T(8,128)(2,1)S(1)}, u32[]{:S(2)}, u32[]{:S(2)}) collective-permute-start(bf16[96,2176]{1,0:T(8,128)(2,1)S(1)} %get-tuple-element.33.refs_1_.refs_3_), channel_id=1, source_target_pairs={{0,4},{4,0},{8,12},{12,8},{16,20},{20,16},{24,28},{28,24},{1,5},{5... | collective-permute-start | bytes 1253384 | tf_op jit(solution)/shard_map/ppermute | solution.py:326
  42.0 10.1 %collective-permute-start.14 = (bf16[160,768]{1,0:T(8,128)(2,1)S(1)}, bf16[160,768]{1,0:T(8,128)(2,1)S(1)}, u32[]{:S(2)}, u32[]{:S(2)}) collective-permute-start(bf16[160,768]{1,0:T(8,128)(2,1)S(1)} %get-tuple-element.32.refs_4_), channel_id=1, source_target_pairs={{0,2},{2,0},{1,3},{3,1},{4,6},{6,4},{5,7},{7,5},{8,10},{10,8},{9,1... | collective-permute-start | bytes 737288 | tf_op jit(solution)/shard_map/ppermute | solution.py:338
  43.5 1.9 %copy-start.5 = (bf16[1,768,2048]{2,1,0:T(8,128)(2,1)S(1)}, bf16[1,768,2048]{2,1,0:T(8,128)(2,1)}, u32[]{:S(2)}) copy-start(bf16[1,768,2048]{2,1,0:T(8,128)(2,1)} %refs_4_.1) | copy-start | bytes 9437188
  43.8 14.0 %collective-permute-start.11 = (bf16[368,384]{1,0:T(8,128)(2,1)S(1)}, bf16[368,384]{1,0:T(8,128)(2,1)S(1)}, u32[]{:S(2)}, u32[]{:S(2)}) collective-permute-start(bf16[368,384]{1,0:T(8,128)(2,1)S(1)} %fusion.refs_8_.refs_0_), channel_id=1, source_target_pairs={{0,2},{2,0},{1,3},{3,1},{4,6},{6,4},{5,7},{7,5},{8,10},{10,8},{9,1... | collective-permute-start | bytes 847880 | tf_op jit(solution)/shard_map/ppermute | solution.py:338
  52.2 8.4 %collective-permute-start.17 = (bf16[160,384]{1,0:T(8,128)(2,1)S(1)}, bf16[160,384]{1,0:T(8,128)(2,1)S(1)}, u32[]{:S(2)}, u32[]{:S(2)}) collective-permute-start(bf16[160,384]{1,0:T(8,128)(2,1)S(1)} %fusion.4.refs_7_.refs_0_), channel_id=1, source_target_pairs={{0,2},{2,0},{1,3},{3,1},{4,6},{6,4},{5,7},{7,5},{8,10},{10,8},{9,1... | collective-permute-start | bytes 368648 | tf_op jit(solution)/shard_map/ppermute | solution.py:338
  53.8 10.3 %collective-permute-start.16 = (bf16[96,2176]{1,0:T(8,128)(2,1)S(1)}, bf16[96,2176]{1,0:T(8,128)(2,1)S(1)}, u32[]{:S(2)}, u32[]{:S(2)}) collective-permute-start(bf16[96,2176]{1,0:T(8,128)(2,1)S(1)} %get-tuple-element.37.refs_0_.refs_2_), channel_id=1, source_target_pairs={{0,4},{4,0},{8,12},{12,8},{16,20},{20,16},{24,28},{28,24},{1,5},{5... | collective-permute-start | bytes 1253384 | tf_op jit(solution)/shard_map/ppermute | solution.py:326
  57.3 12.0 %collective-permute-start.18 = (bf16[288,768]{1,0:T(8,128)(2,1)S(1)}, bf16[288,768]{1,0:T(8,128)(2,1)S(1)}, u32[]{:S(2)}, u32[]{:S(2)}) collective-permute-start(bf16[288,768]{1,0:T(8,128)(2,1)S(1)} %get-tuple-element.36.refs_7_), channel_id=1, source_target_pairs={{0,2},{2,0},{1,3},{3,1},{4,6},{6,4},{5,7},{7,5},{8,10},{10,8},{9,1... | collective-permute-start | bytes 1327112 | tf_op jit(solution)/shard_map/ppermute | solution.py:338
  62.4 15.4 %collective-permute-start.23 = (bf16[96,2048]{1,0:T(8,128)(2,1)S(1)}, bf16[96,2048]{1,0:T(8,128)(2,1)S(1)}, u32[]{:S(2)}, u32[]{:S(2)}) collective-permute-start(bf16[96,2048]{1,0:T(8,128)(2,1)S(1)} %shard_map.74.refs_5_), channel_id=1, source_target_pairs={{0,4},{4,0},{8,12},{12,8},{16,20},{20,16},{24,28},{28,24},{1,5},{5... | collective-permute-start | bytes 1179656 | tf_op jit(solution)/shard_map/ppermute | solution.py:326
  66.0 9.1 %collective-permute-start.19 = (bf16[160,768]{1,0:T(8,128)(2,1)S(1)}, bf16[160,768]{1,0:T(8,128)(2,1)S(1)}, u32[]{:S(2)}, u32[]{:S(2)}) collective-permute-start(bf16[160,768]{1,0:T(8,128)(2,1)S(1)} %get-tuple-element.40.refs_4_), channel_id=1, source_target_pairs={{0,2},{2,0},{1,3},{3,1},{4,6},{6,4},{5,7},{7,5},{8,10},{10,8},{9,1... | collective-permute-start | bytes 737288 | tf_op jit(solution)/shard_map/ppermute | solution.py:338
  70.8 8.9 %collective-permute-start.22 = (bf16[288,384]{1,0:T(8,128)(2,1)S(1)}, bf16[288,384]{1,0:T(8,128)(2,1)S(1)}, u32[]{:S(2)}, u32[]{:S(2)}) collective-permute-start(bf16[288,384]{1,0:T(8,128)(2,1)S(1)} %fusion.1.refs_5_.refs_0_), channel_id=1, source_target_pairs={{0,2},{2,0},{1,3},{3,1},{4,6},{6,4},{5,7},{7,5},{8,10},{10,8},{9,1... | collective-permute-start | bytes 663560 | tf_op jit(solution)/shard_map/ppermute | solution.py:338
  74.2 10.3 %collective-permute-start.20 = (bf16[160,768]{1,0:T(8,128)(2,1)S(1)}, bf16[160,768]{1,0:T(8,128)(2,1)S(1)}, u32[]{:S(2)}, u32[]{:S(2)}) collective-permute-start(bf16[160,768]{1,0:T(8,128)(2,1)S(1)} %get-tuple-element.42.refs_4_), channel_id=1, source_target_pairs={{0,2},{2,0},{1,3},{3,1},{4,6},{6,4},{5,7},{7,5},{8,10},{10,8},{9,1... | collective-permute-start | bytes 737288 | tf_op jit(solution)/shard_map/ppermute | solution.py:338
  75.2 9.8 %collective-permute-start.26 = (bf16[160,384]{1,0:T(8,128)(2,1)S(1)}, bf16[160,384]{1,0:T(8,128)(2,1)S(1)}, u32[]{:S(2)}, u32[]{:S(2)}) collective-permute-start(bf16[160,384]{1,0:T(8,128)(2,1)S(1)} %fusion.3.refs_7_.refs_0_), channel_id=1, source_target_pairs={{0,2},{2,0},{1,3},{3,1},{4,6},{6,4},{5,7},{7,5},{8,10},{10,8},{9,1... | collective-permute-start | bytes 368648 | tf_op jit(solution)/shard_map/ppermute | solution.py:338
  77.9 10.0 %collective-permute-start.25 = (bf16[96,2048]{1,0:T(8,128)(2,1)S(1)}, bf16[96,2048]{1,0:T(8,128)(2,1)S(1)}, u32[]{:S(2)}, u32[]{:S(2)}) collective-permute-start(bf16[96,2048]{1,0:T(8,128)(2,1)S(1)} %shard_map.80.refs_6_), channel_id=1, source_target_pairs={{0,8},{4,12},{8,16},{12,20},{16,24},{20,28},{24,0},{28,4},{1,9},{5... | collective-permute-start | bytes 1179656 | tf_op jit(solution)/shard_map/ppermute | solution.py:329
  82.0 12.0 %collective-permute-start.24 = (bf16[96,2048]{1,0:T(8,128)(2,1)S(1)}, bf16[96,2048]{1,0:T(8,128)(2,1)S(1)}, u32[]{:S(2)}, u32[]{:S(2)}) collective-permute-start(bf16[96,2048]{1,0:T(8,128)(2,1)S(1)} %get-tuple-element.46), channel_id=1, source_target_pairs={{0,4},{4,0},{8,12},{12,8},{16,20},{20,16},{24,28},{28,24},{1,5},{5... | collective-permute-start | bytes 1179656 | tf_op jit(solution)/shard_map/ppermute | solution.py:326
  86.6 15.6 %collective-permute-start.27 = (bf16[96,2048]{1,0:T(8,128)(2,1)S(1)}, bf16[96,2048]{1,0:T(8,128)(2,1)S(1)}, u32[]{:S(2)}, u32[]{:S(2)}) collective-permute-start(bf16[96,2048]{1,0:T(8,128)(2,1)S(1)} %shard_map.82.refs_3_), channel_id=1, source_target_pairs={{0,4},{4,0},{8,12},{12,8},{16,20},{20,16},{24,28},{28,24},{1,5},{5... | collective-permute-start | bytes 1179656 | tf_op jit(solution)/shard_map/ppermute | solution.py:326
  94.2 13.6 %collective-permute-start.28 = (bf16[96,2048]{1,0:T(8,128)(2,1)S(1)}, bf16[96,2048]{1,0:T(8,128)(2,1)S(1)}, u32[]{:S(2)}, u32[]{:S(2)}) collective-permute-start(bf16[96,2048]{1,0:T(8,128)(2,1)S(1)} %shard_map.83.refs_5_), channel_id=1, source_target_pairs={{0,8},{4,12},{8,16},{12,20},{16,24},{20,28},{24,0},{28,4},{1,9},{5... | collective-permute-start | bytes 1179656 | tf_op jit(solution)/shard_map/ppermute | solution.py:329
  94.2 4.9 %collective-permute-start.21 = (bf16[160,384]{1,0:T(8,128)(2,1)S(1)}, bf16[160,384]{1,0:T(8,128)(2,1)S(1)}, u32[]{:S(2)}, u32[]{:S(2)}) collective-permute-start(bf16[160,384]{1,0:T(8,128)(2,1)S(1)} %fusion.2.refs_4_.refs_0_), channel_id=1, source_target_pairs={{0,2},{2,0},{1,3},{3,1},{4,6},{6,4},{5,7},{7,5},{8,10},{10,8},{9,1... | collective-permute-start | bytes 368648 | tf_op jit(solution)/shard_map/ppermute | solution.py:338
  94.3 13.6 %collective-permute-start.15 = (bf16[96,2048]{1,0:T(8,128)(2,1)S(1)}, bf16[96,2048]{1,0:T(8,128)(2,1)S(1)}, u32[]{:S(2)}, u32[]{:S(2)}) collective-permute-start(bf16[96,2048]{1,0:T(8,128)(2,1)S(1)} %get-tuple-element.44), channel_id=1, source_target_pairs={{0,4},{4,0},{8,12},{12,8},{16,20},{20,16},{24,28},{28,24},{1,5},{5... | collective-permute-start | bytes 1179656 | tf_op jit(solution)/shard_map/ppermute | solution.py:326
  107.9 9.6 %collective-permute-start.29 = (bf16[96,2048]{1,0:T(8,128)(2,1)S(1)}, bf16[96,2048]{1,0:T(8,128)(2,1)S(1)}, u32[]{:S(2)}, u32[]{:S(2)}) collective-permute-start(bf16[96,2048]{1,0:T(8,128)(2,1)S(1)} %shard_map.85.refs_3_), channel_id=1, source_target_pairs={{0,8},{4,12},{8,16},{12,20},{16,24},{20,28},{24,0},{28,4},{1,9},{5... | collective-permute-start | bytes 1179656 | tf_op jit(solution)/shard_map/ppermute | solution.py:329

commit v9 on v7

--- a/solution.py
+++ b/solution.py
@@ -34,47 +34,36 @@
     return pl.CostEstimate(flops=1, bytes_accessed=1, transcendentals=0)
 
 
-def block_kernel(experts, tokens_ref, ids_ref, route_ref, out_ref, ids_buffer, route_buffer, sems):
+def block_kernel(experts, tokens_ref, routes_ref, out_ref, sem):
     rows, width = tokens_ref.shape
-    copies = [
-        pltpu.make_async_copy(ids_ref, ids_buffer, sems.at[0]),
-        pltpu.make_async_copy(route_ref, route_buffer, sems.at[1]),
-        pltpu.make_async_copy(tokens_ref, out_ref.at[:, :width], sems.at[2]),
-    ]
-    for copy in copies:
-        copy.start()
-    copies[0].wait()
-    copies[1].wait()
-    ids = ids_buffer[...].T
-    route = route_buffer[...].T
+    copy = pltpu.make_async_copy(tokens_ref, out_ref.at[:, :width], sem)
+    copy.start()
+    routes = routes_ref[...].T
+    top = routes.shape[1] // 2
     column = lax.broadcasted_iota(jnp.int32, (rows, out_ref.shape[1] - width), 1)
-    expert = jnp.where(column < experts, column, column - experts)
+    expert = jnp.where(column < experts, column, column - experts).astype(F32)
     value = jnp.zeros(column.shape, F32)
-    for k in range(ids.shape[1]):
-        value = value + jnp.where(expert == ids[:, k:k + 1], route[:, k:k + 1], 0.0)
+    for k in range(top):
+        value = value + jnp.where(expert == routes[:, k:k + 1], routes[:, top + k:top + k + 1], 0.0)
     high = value.astype(BF16).astype(F32)
     out_ref[:, width:] = jnp.where(column < experts, high, value - high).astype(BF16)
-    copies[2].wait()
+    copy.wait()
 
 
 def make_block(tokens, expert_ids, route_weights, experts):
     rows, width = tokens.shape
     padded = width + 2 * experts + (-(2 * experts)) % LANES
-    args = (tokens, expert_ids.T, route_weights.T)
+    routes = jnp.concatenate([expert_ids.T.astype(F32), route_weights.T], axis=0)
     return pl.pallas_call(
         functools.partial(block_kernel, experts),
         grid=(1,),
         out_shape=jax.ShapeDtypeStruct((rows, padded), BF16),
-        in_specs=[HBM] * 3,
+        in_specs=[HBM, whole(routes)],
         out_specs=pl.BlockSpec((rows, padded), lambda i: (0, 0)),
-        scratch_shapes=[
-            pltpu.VMEM(args[1].shape, jnp.int32),
-            pltpu.VMEM(args[2].shape, F32),
-            pltpu.SemaphoreType.DMA((3,)),
-        ],
+        scratch_shapes=[pltpu.SemaphoreType.DMA],
         compiler_params=params(),
         cost_estimate=cost(),
-    )(*args)
+    )(tokens, routes)
 
 
 def slot_row(tails, me, experts, rows, capacity):
@@ -452,8 +441,8 @@
         order.extend(downs[1:])
         home_product(1, 2)
         pick(2)
+        down_product(0)
         home_product(2, 3)
-        down_product(0)
         activate(2)
         pick(3)
         activate(1)
@@ -467,8 +456,9 @@
         home_product(5)
         order.append(blocks[2, "b"])
         add_hop(0)
+        add_hop(1)
+        order.append(blocks[0, "b"])
         down_product(3)
-        add_hop(1)
         order.append(blocks[2, "b"])
         activate(4)
         down_product(4)

time: 115 us -> 116 us (level)
  waiting for transfers between devices: 48.8 us -> 50.9 us
  other arithmetic: 1.8 us -> 3.17 us
  local copies, waits for them, and re-layouts: 7.38 us -> 6.02 us
    ppermute x8, waiting for transfers between devices: 2.5 us -> 5.74 us  [over_y(): return lax.ppermute(x, 'expert', [(i, i ^ 1) for i in range(ring)])]
    unnamed x16 -> x12, local copies, waits for them, and re-layouts: 7.24 us -> 5.87 us
    ppermute x6, waiting for transfers between devices: 37.3 us -> 36 us  [over_z(): return lax.ppermute(x, 'expert', [(i, (i + 2) % ring) for i in range(ring)])]
  transfers between devices with their start and end apart: 29 -> 29, of which waited for: 12 -> 12; matrix products, arithmetic and copies ran while one was open for 1% -> 2% of each run, Pallas kernels for 25% -> 24%
where the time goes in v9:
time: 116 us
  waiting for transfers between devices  50.9 us (44%)
  Pallas kernels  31.1 us (27%)
  starting transfers between devices  24.2 us (21%)
  local copies, waits for them, and re-layouts  6.02 us (5%)
  other arithmetic  3.17 us (3%)
    ppermute x6, waiting for transfers between devices, over_z(): return lax.ppermute(x, 'expert', [(i, (i + 2) % ring) for i in range(ring)])  36 us
    pallas_call x6, Pallas kernels, pick_rows(): pl.pallas_call(kernel, grid=(1,), out_shape=(*out, *[jax.ShapeDtypeStruct...  11.9 us
    ppermute x12, starting transfers between devices, over_x(): lax.ppermute(x, 'tensor', [(i, (i + step) % parts) for i in range(parts)])  11.9 us
    pallas_call x6, Pallas kernels, down_rows(): pl.pallas_call(functools.partial(down_kernel, experts, capacity, groups,...  11.4 us
    ppermute x8, starting transfers between devices, over_y(): return lax.ppermute(x, 'expert', [(i, i ^ 1) for i in range(ring)])  9.99 us
    ppermute x12, waiting for transfers between devices, over_x(): lax.ppermute(x, 'tensor', [(i, (i + step) % parts) for i in range(parts)])  9.09 us
    pallas_call x6, Pallas kernels, home_rows(): pl.pallas_call(functools.partial(home_kernel, capacity, units, groups, le...  6.93 us
    unnamed x12, local copies, waits for them, and re-layouts  5.87 us
  transfers between devices with their start and end apart: 29, of which 12 were waited for; matrix products, arithmetic and copies ran while one was open for 2% of the time, Pallas kernels for 24%

profile of v9, /device:TPU:0, one launch (start us, length us, event | category | flops | bytes accessed | tf_op | source)
XLA Modules:
  0.0 115.7 jit_solution(6661679488642594301)
XLA Ops:
  0.0 0.5 collective-permute-start.5
  0.5 0.7 convert_bitcast_fusion
  1.2 0.7 pad_maximum_fusion.routes_ref
  1.9 1.0 copy-done.5
  2.9 0.4 shard_map.64.refs_0_.refs_2_
  3.3 3.0 %collective-permute-start = (bf16[96,2176]{1,0:T(8,128)(2,1)S(1)}, bf16[96,2176]{1,0:T(8,128)(2,1)S(1)}, u32[]{:S(2)}, u32[]{:S(2)}) collective-permute-start(bf16[96,2176]{1,0:T(8,128)(2,1)S(1)} %shard_map.64.refs_0_.refs_2_), channel_id=1, source_target_pairs={{0,4},{4,0},{8,12},{12,8},{16,20},{20,16},{24,28},{28,24},{1,5},{5... | collective-permute-start | bytes 1253384 | tf_op jit(solution)/shard_map/ppermute | solution.py:315
  6.4 1.6 %collective-permute-start.1 = (bf16[96,2176]{1,0:T(8,128)(2,1)S(1)}, bf16[96,2176]{1,0:T(8,128)(2,1)S(1)}, u32[]{:S(2)}, u32[]{:S(2)}) collective-permute-start(bf16[96,2176]{1,0:T(8,128)(2,1)S(1)} %shard_map.64.refs_0_.refs_2_), channel_id=1, source_target_pairs={{0,8},{4,12},{8,16},{12,20},{16,24},{20,28},{24,0},{28,4},{1,9},{5... | collective-permute-start | bytes 1253384 | tf_op jit(solution)/shard_map/ppermute | solution.py:318
  7.9 1.9 %copy-done = bf16[1,2048,768]{2,1,0:T(8,128)(2,1)S(1)} copy-done((bf16[1,2048,768]{2,1,0:T(8,128)(2,1)S(1)}, bf16[1,2048,768]{2,1,0:T(8,128)(2,1)}, u32[]{:S(2)}) %copy-start) | copy-done | bytes 3145752
  9.8 1.9 %copy-done.2 = bf16[1,2048,768]{2,1,0:T(8,128)(2,1)S(1)} copy-done((bf16[1,2048,768]{2,1,0:T(8,128)(2,1)S(1)}, bf16[1,2048,768]{2,1,0:T(8,128)(2,1)}, u32[]{:S(2)}) %copy-start.2) | copy-done | bytes 3145752
  11.7 1.1 shard_map.65
  12.8 1.6 %collective-permute-start.2 = (bf16[80,768]{1,0:T(8,128)(2,1)S(1)}, bf16[80,768]{1,0:T(8,128)(2,1)S(1)}, u32[]{:S(2)}, u32[]{:S(2)}) collective-permute-start(bf16[80,768]{1,0:T(8,128)(2,1)S(1)} %get-tuple-element.25.refs_2_), channel_id=1, source_target_pairs={{0,2},{2,0},{1,3},{3,1},{4,6},{6,4},{5,7},{7,5},{8,10},{10,8},{9,1... | collective-permute-start | bytes 368648 | tf_op jit(solution)/shard_map/ppermute | solution.py:327
  14.4 1.8 %collective-permute-done.refs_3_.refs_1_.refs_7_ = bf16[96,2176]{1,0:T(8,128)(2,1)S(1)} collective-permute-done((bf16[96,2176]{1,0:T(8,128)(2,1)S(1)}, bf16[96,2176]{1,0:T(8,128)(2,1)S(1)}, u32[]{:S(2)}, u32[]{:S(2)}) %collective-permute-start) | collective-permute-done | bytes 417824 | tf_op jit(solution)/shard_map/ppermute | solution.py:315
  16.2 3.3 %collective-permute-done.1.refs_4_ = bf16[96,2176]{1,0:T(8,128)(2,1)S(1)} collective-permute-done((bf16[96,2176]{1,0:T(8,128)(2,1)S(1)}, bf16[96,2176]{1,0:T(8,128)(2,1)S(1)}, u32[]{:S(2)}, u32[]{:S(2)}) %collective-permute-start.1) | collective-permute-done | bytes 417824 | tf_op jit(solution)/shard_map/ppermute | solution.py:318
  19.5 0.7 shard_map.66
  20.3 1.1 copy-done.4
  21.4 2.8 %shard_map.67 = (bf16[368,2048]{1,0:T(8,128)(2,1)S(1)}, bf16[368,768]{1,0:T(8,128)(2,1)S(1)}, bf16[1,768,2048]{2,1,0:T(8,128)(2,1)S(1)}) custom-call(bf16[96,2176]{1,0:T(8,128)(2,1)S(1)} %shard_map.64.refs_0_.refs_2_, bf16[96,2176]{1,0:T(8,128)(2,1)S(1)} %collective-permute-done.refs_3_.refs_1_.refs_7_, ...), custom_call_target="tpu_custom_call" | custom-call | flops 1 | bytes 1 | tf_op jit(solution)/shard_map/pallas_call | solution.py:174
  24.3 1.6 %collective-permute-start.9 = (bf16[368,768]{1,0:T(8,128)(2,1)S(1)}, bf16[368,768]{1,0:T(8,128)(2,1)S(1)}, u32[]{:S(2)}, u32[]{:S(2)}) collective-permute-start(bf16[368,768]{1,0:T(8,128)(2,1)S(1)} %get-tuple-element.29.refs_4_), channel_id=1, source_target_pairs={{0,2},{2,0},{1,3},{3,1},{4,6},{6,4},{5,7},{7,5},{8,10},{10,8},{9,1... | collective-permute-start | bytes 1695752 | tf_op jit(solution)/shard_map/ppermute | solution.py:327
  25.8 0.5 collective-permute-start.4
  26.3 0.5 collective-permute-start.3
  26.9 12.5 %collective-permute-done.8.refs_6_ = bf16[96,2176]{1,0:T(8,128)(2,1)S(1)} collective-permute-done((bf16[96,2176]{1,0:T(8,128)(2,1)S(1)}, bf16[96,2176]{1,0:T(8,128)(2,1)S(1)}, u32[]{:S(2)}, u32[]{:S(2)}) %collective-permute-start.8) | collective-permute-done | bytes 417824 | tf_op jit(solution)/shard_map/ppermute | solution.py:318
  39.3 1.4 %shard_map.68 = (f32[368,768]{1,0:T(8,128)S(1)}, bf16[96,2176]{1,0:T(8,128)(2,1)S(1)}) custom-call(bf16[368,2048]{1,0:T(8,128)(2,1)S(1)} %get-tuple-element.28.x_ref, bf16[2048,768]{1,0:T(8,128)(2,1)S(1)} %bitcast.34, bf16[2048,768]{1,0:T(8,128)(2,1)S(1)} %bitcast.44, bf16[2048,768]{1,0:T(8,128)(2,1)S(1)} %bitcast.12, ...), custom_call_target="tpu_custom_call", output_to_operand_aliasing={{1}: (7, {})} | custom-call | flops 1 | bytes 1 | tf_op jit(solution)/shard_map/pallas_call | solution.py:199
  40.7 0.6 collective-permute-start.11
  41.3 1.9 %shard_map.69 = (bf16[160,2048]{1,0:T(8,128)(2,1)S(1)}, bf16[160,768]{1,0:T(8,128)(2,1)S(1)}) custom-call(bf16[96,2176]{1,0:T(8,128)(2,1)S(1)} %collective-permute-done.4.refs_0_.refs_2_, bf16[2048,768]{1,0:T(8,128)(2,1)S(1)} %bitcast.13, bf16[2048,768]{1,0:T(8,128)(2,1)S(1)} %bitcast.25, bf16[2048,768]{1,0:T(8,128)(2,1)S(1)} %bitcast.35, ...), custom_call_target="tpu_custom_call" | custom-call | flops 1 | bytes 1 | tf_op jit(solution)/shard_map/pallas_call | solution.py:174
  43.2 0.6 collective-permute-start.13
  44.0 0.2 fusion.refs_0_.refs_8_
  44.1 1.6 %collective-permute-start.10 = (bf16[368,384]{1,0:T(8,128)(2,1)S(1)}, bf16[368,384]{1,0:T(8,128)(2,1)S(1)}, u32[]{:S(2)}, u32[]{:S(2)}) collective-permute-start(bf16[368,384]{1,0:T(8,128)(2,1)S(1)} %fusion.refs_0_.refs_8_), channel_id=1, source_target_pairs={{0,2},{2,0},{1,3},{3,1},{4,6},{6,4},{5,7},{7,5},{8,10},{10,8},{9,1... | collective-permute-start | bytes 847880 | tf_op jit(solution)/shard_map/ppermute | solution.py:327
  45.7 1.1 shard_map.70.refs_4_.refs_0_
  46.8 6.9 %collective-permute-done.12.refs_5_ = bf16[96,2176]{1,0:T(8,128)(2,1)S(1)} collective-permute-done((bf16[96,2176]{1,0:T(8,128)(2,1)S(1)}, bf16[96,2176]{1,0:T(8,128)(2,1)S(1)}, u32[]{:S(2)}, u32[]{:S(2)}) %collective-permute-start.12) | collective-permute-done | bytes 417824 | tf_op jit(solution)/shard_map/ppermute | solution.py:318
  53.7 1.2 %shard_map.71 = (f32[160,768]{1,0:T(8,128)S(1)}, bf16[96,2176]{1,0:T(8,128)(2,1)S(1)}) custom-call(bf16[160,2048]{1,0:T(8,128)(2,1)S(1)} %get-tuple-element.34.x_ref, bf16[2048,768]{1,0:T(8,128)(2,1)S(1)} %bitcast.14, bf16[2048,768]{1,0:T(8,128)(2,1)S(1)} %bitcast.26, bf16[2048,768]{1,0:T(8,128)(2,1)S(1)} %bitcast.36, ...), custom_call_target="tpu_custom_call", output_to_operand_aliasing={{1}: (6, {})} | custom-call | flops 1 | bytes 1 | tf_op jit(solution)/shard_map/pallas_call | solution.py:199
  55.0 1.6 %collective-permute-start.15 = (bf16[96,2176]{1,0:T(8,128)(2,1)S(1)}, bf16[96,2176]{1,0:T(8,128)(2,1)S(1)}, u32[]{:S(2)}, u32[]{:S(2)}) collective-permute-start(bf16[96,2176]{1,0:T(8,128)(2,1)S(1)} %get-tuple-element.37.refs_0_.refs_2_), channel_id=1, source_target_pairs={{0,4},{4,0},{8,12},{12,8},{16,20},{20,16},{24,28},{28,24},{1,5},{5... | collective-permute-start | bytes 1253384 | tf_op jit(solution)/shard_map/ppermute | solution.py:315
  56.7 0.6 collective-permute-start.16
  57.3 2.0 %shard_map.72 = (bf16[288,2048]{1,0:T(8,128)(2,1)S(1)}, bf16[288,768]{1,0:T(8,128)(2,1)S(1)}) custom-call(bf16[96,2176]{1,0:T(8,128)(2,1)S(1)} %collective-permute-done.11.refs_0_.refs_4_.refs_2_.refs_6_, bf16[96,2176]{1,0:T(8,128)(2,1)S(1)} %get-tuple-element.33.refs_1_.refs_3_, bf16[2048,768]{1,0:T(8,128)(2,1)S(1)} %bitcast.15, ...), custom_call_target="tpu_custom_call" | custom-call | flops 1 | bytes 1 | tf_op jit(solution)/shard_map/pallas_call | solution.py:174
  59.2 1.6 %collective-permute-start.17 = (bf16[288,768]{1,0:T(8,128)(2,1)S(1)}, bf16[288,768]{1,0:T(8,128)(2,1)S(1)}, u32[]{:S(2)}, u32[]{:S(2)}) collective-permute-start(bf16[288,768]{1,0:T(8,128)(2,1)S(1)} %get-tuple-element.36.refs_7_), channel_id=1, source_target_pairs={{0,2},{2,0},{1,3},{3,1},{4,6},{6,4},{5,7},{7,5},{8,10},{10,8},{9,1... | collective-permute-start | bytes 1327112 | tf_op jit(solution)/shard_map/ppermute | solution.py:327
  60.8 2.6 %shard_map.73.refs_5_ = bf16[288,2048]{1,0:T(8,128)(2,1)S(1)} custom-call(bf16[368,384]{1,0:T(8,128)(2,1)S(1)} %fusion.refs_0_.refs_8_, bf16[368,384]{1,0:T(8,128)(2,1)S(1)} %collective-permute-done.10.refs_1_, bf16[96,2176]{1,0:T(8,128)(2,1)S(1)} %shard_map.64.refs_0_.refs_2_, bf16[96,2176]{1,0:T(8,128)(2,1)S(1)} %collective-permute-done.refs_3_.refs_1_.refs_7_, ...), custom_call_target="tpu_custom_call" | custom-call | flops 1 | bytes 1 | tf_op jit(solution)/shard_map/pallas_call | solution.py:267
  63.5 0.6 collective-permute-start.14
  64.1 1.8 %shard_map.74.refs_5_ = bf16[96,2048]{1,0:T(8,128)(2,1)S(1)} custom-call(bf16[160,384]{1,0:T(8,128)(2,1)S(1)} %fusion.4.refs_7_.refs_0_, bf16[160,384]{1,0:T(8,128)(2,1)S(1)} %collective-permute-done.16.refs_1_, bf16[96,2176]{1,0:T(8,128)(2,1)S(1)} %collective-permute-done.4.refs_0_.refs_2_, bf16[768,2048]{1,0:T(8,128)(2,1)S(1)} %bitcast.55, ...), custom_call_target="tpu_custom_call" | custom-call | flops 1 | bytes 1 | tf_op jit(solution)/shard_map/pallas_call | solution.py:267
  65.9 1.6 %collective-permute-start.21 = (bf16[96,2048]{1,0:T(8,128)(2,1)S(1)}, bf16[96,2048]{1,0:T(8,128)(2,1)S(1)}, u32[]{:S(2)}, u32[]{:S(2)}) collective-permute-start(bf16[96,2048]{1,0:T(8,128)(2,1)S(1)} %shard_map.74.refs_5_), channel_id=1, source_target_pairs={{0,4},{4,0},{8,12},{12,8},{16,20},{20,16},{24,28},{28,24},{1,5},{5... | collective-permute-start | bytes 1179656 | tf_op jit(solution)/shard_map/ppermute | solution.py:315
  67.5 2.0 %shard_map.75 = (bf16[160,2048]{1,0:T(8,128)(2,1)S(1)}, bf16[160,768]{1,0:T(8,128)(2,1)S(1)}) custom-call(bf16[96,2176]{1,0:T(8,128)(2,1)S(1)} %collective-permute-done.15.refs_0_.refs_2_, bf16[2048,768]{1,0:T(8,128)(2,1)S(1)} %bitcast.16, bf16[2048,768]{1,0:T(8,128)(2,1)S(1)} %bitcast.28, bf16[2048,768]{1,0:T(8,128)(2,1)S(1)} %bitcast.38, ...), custom_call_target="tpu_custom_call" | custom-call | flops 1 | bytes 1 | tf_op jit(solution)/shard_map/pallas_call | solution.py:174
  69.4 1.1 shard_map.76.refs_4_
  70.7 0.1 fusion.1.refs_6_.refs_0_
  70.8 1.1 collective-permute-start.20
  71.9 1.2 %shard_map.77.refs_5_ = f32[160,768]{1,0:T(8,128)S(1)} custom-call(bf16[160,2048]{1,0:T(8,128)(2,1)S(1)} %get-tuple-element.38.x_ref, bf16[2048,768]{1,0:T(8,128)(2,1)S(1)} %bitcast.18, bf16[2048,768]{1,0:T(8,128)(2,1)S(1)} %bitcast.30, bf16[2048,768]{1,0:T(8,128)(2,1)S(1)} %bitcast.40, bf16[2048,768]{1,0:T(8,128)(2,1)S(1)} %bitcast.50, ...), custom_call_target="tpu_custom_call" | custom-call | flops 1 | bytes 1 | tf_op jit(solution)/shard_map/pallas_call | solution.py:199
  73.2 1.1 collective-permute-start.24
  74.2 2.2 %shard_map.78 = (bf16[160,2048]{1,0:T(8,128)(2,1)S(1)}, bf16[160,768]{1,0:T(8,128)(2,1)S(1)}) custom-call(bf16[96,2176]{1,0:T(8,128)(2,1)S(1)} %get-tuple-element.37.refs_0_.refs_2_, bf16[2048,768]{1,0:T(8,128)(2,1)S(1)} %bitcast.19, bf16[2048,768]{1,0:T(8,128)(2,1)S(1)} %bitcast.31, bf16[2048,768]{1,0:T(8,128)(2,1)S(1)} %bitcast.41, ...), custom_call_target="tpu_custom_call" | custom-call | flops 1 | bytes 1 | tf_op jit(solution)/shard_map/pallas_call | solution.py:174
  76.4 1.1 collective-permute-start.18
  77.5 1.2 %shard_map.79.refs_3_ = f32[160,768]{1,0:T(8,128)S(1)} custom-call(bf16[160,2048]{1,0:T(8,128)(2,1)S(1)} %get-tuple-element.41.x_ref, bf16[2048,768]{1,0:T(8,128)(2,1)S(1)} %bitcast.20, bf16[2048,768]{1,0:T(8,128)(2,1)S(1)} %bitcast.32, bf16[2048,768]{1,0:T(8,128)(2,1)S(1)} %bitcast.42, bf16[2048,768]{1,0:T(8,128)(2,1)S(1)} %bitcast.52, ...), custom_call_target="tpu_custom_call" | custom-call | flops 1 | bytes 1 | tf_op jit(solution)/shard_map/pallas_call | solution.py:199
  78.7 0.1 shard_map.80.refs_2_
  78.8 2.7 %collective-permute-done.21.refs_1_ = bf16[96,2048]{1,0:T(8,128)(2,1)S(1)} collective-permute-done((bf16[96,2048]{1,0:T(8,128)(2,1)S(1)}, bf16[96,2048]{1,0:T(8,128)(2,1)S(1)}, u32[]{:S(2)}, u32[]{:S(2)}) %collective-permute-start.21) | collective-permute-done | bytes 393248 | tf_op jit(solution)/shard_map/ppermute | solution.py:315
  81.7 2.2 %shard_map.82.refs_5_ = bf16[192,2048]{1,0:T(8,128)(2,1)S(1)} custom-call(bf16[288,384]{1,0:T(8,128)(2,1)S(1)} %fusion.1.refs_6_.refs_0_, bf16[288,384]{1,0:T(8,128)(2,1)S(1)} %collective-permute-done.20.refs_1_, bf16[96,2176]{1,0:T(8,128)(2,1)S(1)} %collective-permute-done.11.refs_0_.refs_4_.refs_2_.refs_6_, ...), custom_call_target="tpu_custom_call" | custom-call | flops 1 | bytes 1 | tf_op jit(solution)/shard_map/pallas_call | solution.py:267
  84.1 1.5 %collective-permute-start.22 = (bf16[96,2048]{1,0:T(8,128)(2,1)S(1)}, bf16[96,2048]{1,0:T(8,128)(2,1)S(1)}, u32[]{:S(2)}, u32[]{:S(2)}) collective-permute-start(bf16[96,2048]{1,0:T(8,128)(2,1)S(1)} %get-tuple-element.46), channel_id=1, source_target_pairs={{0,4},{4,0},{8,12},{12,8},{16,20},{20,16},{24,28},{28,24},{1,5},{5... | collective-permute-start | bytes 1179656 | tf_op jit(solution)/shard_map/ppermute | solution.py:315
  85.8 0.6 collective-permute-start.25
  86.4 0.3 collective-permute-done.18
  86.8 3.9 %collective-permute-done.25.refs_1_ = bf16[160,384]{1,0:T(8,128)(2,1)S(1)} collective-permute-done((bf16[160,384]{1,0:T(8,128)(2,1)S(1)}, bf16[160,384]{1,0:T(8,128)(2,1)S(1)}, u32[]{:S(2)}, u32[]{:S(2)}) %collective-permute-start.25) | collective-permute-done | bytes 122912 | tf_op jit(solution)/shard_map/ppermute | solution.py:327
  90.7 1.8 %shard_map.83.refs_3_ = bf16[96,2048]{1,0:T(8,128)(2,1)S(1)} custom-call(bf16[160,384]{1,0:T(8,128)(2,1)S(1)} %fusion.2.refs_0_.refs_7_, bf16[160,384]{1,0:T(8,128)(2,1)S(1)} %collective-permute-done.25.refs_1_, bf16[96,2176]{1,0:T(8,128)(2,1)S(1)} %collective-permute-done.15.refs_0_.refs_2_, bf16[768,2048]{1,0:T(8,128)(2,1)S(1)} %bitcast.57, ...), custom_call_target="tpu_custom_call" | custom-call | flops 1 | bytes 1 | tf_op jit(solution)/shard_map/pallas_call | solution.py:267
  92.5 0.6 collective-permute-start.26
  93.1 0.9 collective-permute-done.22.refs_1_
  94.1 0.1 shard_map.84.refs_5_
  94.4 4.9 %collective-permute-done.19.refs_1_ = bf16[160,384]{1,0:T(8,128)(2,1)S(1)} collective-permute-done((bf16[160,384]{1,0:T(8,128)(2,1)S(1)}, bf16[160,384]{1,0:T(8,128)(2,1)S(1)}, u32[]{:S(2)}, u32[]{:S(2)}) %collective-permute-start.19) | collective-permute-done | bytes 122912 | tf_op jit(solution)/shard_map/ppermute | solution.py:327
  99.2 1.8 %shard_map.85.refs_0_.refs_3_ = bf16[96,2048]{1,0:T(8,128)(2,1)S(1)} custom-call(bf16[160,384]{1,0:T(8,128)(2,1)S(1)} %fusion.3.refs_4_.refs_0_, bf16[160,384]{1,0:T(8,128)(2,1)S(1)} %collective-permute-done.19.refs_1_, bf16[96,2176]{1,0:T(8,128)(2,1)S(1)} %get-tuple-element.37.refs_0_.refs_2_, bf16[768,2048]{1,0:T(8,128)(2,1)S(1)} %bitcast.58, ...), custom_call_target="tpu_custom_call" | custom-call | flops 1 | bytes 1 | tf_op jit(solution)/shard_map/pallas_call | solution.py:267
  101.0 0.3 collective-permute-done.26.refs_1_
  101.3 3.7 %collective-permute-done.27.refs_2_ = bf16[96,2048]{1,0:T(8,128)(2,1)S(1)} collective-permute-done((bf16[96,2048]{1,0:T(8,128)(2,1)S(1)}, bf16[96,2048]{1,0:T(8,128)(2,1)S(1)}, u32[]{:S(2)}, u32[]{:S(2)}) %collective-permute-start.27) | collective-permute-done | bytes 393248 | tf_op jit(solution)/shard_map/ppermute | solution.py:318
  105.1 0.1 shard_map.86
  105.3 9.6 %collective-permute-done.28 = bf16[96,2048]{1,0:T(8,128)(2,1)S(1)} collective-permute-done((bf16[96,2048]{1,0:T(8,128)(2,1)S(1)}, bf16[96,2048]{1,0:T(8,128)(2,1)S(1)}, u32[]{:S(2)}, u32[]{:S(2)}) %collective-permute-start.28) | collective-permute-done | bytes 393248 | tf_op jit(solution)/shard_map/ppermute | solution.py:318
  114.8 0.8 add_convert_fusion
  (46 shorter events, 1.3 us)
Async XLA Ops:
  0.0 20.3 %collective-permute-start.5 = (bf16[1,2048,768]{2,1,0:T(8,128)(2,1)}, bf16[1,2048,768]{2,1,0:T(8,128)(2,1)S(1)}, u32[]{:S(2)}, u32[]{:S(2)}) collective-permute-start(bf16[1,2048,768]{2,1,0:T(8,128)(2,1)} %param.9), channel_id=1, source_target_pairs={{0,1},{1,0},{2,3},{3,2},{4,5},{5,4},{6,7},{7,6},{8,9},{9,8},{10,11... | collective-permute-start | bytes 9437192 | tf_op jit(solution)/shard_map/ppermute | solution.py:324
  0.5 19.8 %collective-permute-start.6 = (bf16[1,2048,768]{2,1,0:T(8,128)(2,1)}, bf16[1,2048,768]{2,1,0:T(8,128)(2,1)S(1)}, u32[]{:S(2)}, u32[]{:S(2)}) collective-permute-start(bf16[1,2048,768]{2,1,0:T(8,128)(2,1)} %param.10), channel_id=1, source_target_pairs={{0,1},{1,0},{2,3},{3,2},{4,5},{5,4},{6,7},{7,6},{8,9},{9,8},{10,11... | collective-permute-start | bytes 9437192 | tf_op jit(solution)/shard_map/ppermute | solution.py:324
  1.9 1.0 copy-start.5
  3.3 12.8 %collective-permute-start = (bf16[96,2176]{1,0:T(8,128)(2,1)S(1)}, bf16[96,2176]{1,0:T(8,128)(2,1)S(1)}, u32[]{:S(2)}, u32[]{:S(2)}) collective-permute-start(bf16[96,2176]{1,0:T(8,128)(2,1)S(1)} %shard_map.64.refs_0_.refs_2_), channel_id=1, source_target_pairs={{0,4},{4,0},{8,12},{12,8},{16,20},{20,16},{24,28},{28,24},{1,5},{5... | collective-permute-start | bytes 1253384 | tf_op jit(solution)/shard_map/ppermute | solution.py:315
  6.4 13.1 %collective-permute-start.1 = (bf16[96,2176]{1,0:T(8,128)(2,1)S(1)}, bf16[96,2176]{1,0:T(8,128)(2,1)S(1)}, u32[]{:S(2)}, u32[]{:S(2)}) collective-permute-start(bf16[96,2176]{1,0:T(8,128)(2,1)S(1)} %shard_map.64.refs_0_.refs_2_), channel_id=1, source_target_pairs={{0,8},{4,12},{8,16},{12,20},{16,24},{20,28},{24,0},{28,4},{1,9},{5... | collective-permute-start | bytes 1253384 | tf_op jit(solution)/shard_map/ppermute | solution.py:318
  7.9 1.9 %copy-start = (bf16[1,2048,768]{2,1,0:T(8,128)(2,1)S(1)}, bf16[1,2048,768]{2,1,0:T(8,128)(2,1)}, u32[]{:S(2)}) copy-start(bf16[1,2048,768]{2,1,0:T(8,128)(2,1)} %param.9) | copy-start | bytes 9437188
  9.8 1.9 %copy-start.2 = (bf16[1,2048,768]{2,1,0:T(8,128)(2,1)S(1)}, bf16[1,2048,768]{2,1,0:T(8,128)(2,1)}, u32[]{:S(2)}) copy-start(bf16[1,2048,768]{2,1,0:T(8,128)(2,1)} %param.10) | copy-start | bytes 9437188
  11.7 7.8 %copy-start.1 = (bf16[1,2048,768]{2,1,0:T(8,128)(2,1)S(1)}, bf16[1,2048,768]{2,1,0:T(8,128)(2,1)}, u32[]{:S(2)}) copy-start(bf16[1,2048,768]{2,1,0:T(8,128)(2,1)} %param.9) | copy-start | bytes 9437188
  11.7 7.8 %copy-start.3 = (bf16[1,2048,768]{2,1,0:T(8,128)(2,1)S(1)}, bf16[1,2048,768]{2,1,0:T(8,128)(2,1)}, u32[]{:S(2)}) copy-start(bf16[1,2048,768]{2,1,0:T(8,128)(2,1)} %param.10) | copy-start | bytes 9437188
  12.8 7.4 %collective-permute-start.2 = (bf16[80,768]{1,0:T(8,128)(2,1)S(1)}, bf16[80,768]{1,0:T(8,128)(2,1)S(1)}, u32[]{:S(2)}, u32[]{:S(2)}) collective-permute-start(bf16[80,768]{1,0:T(8,128)(2,1)S(1)} %get-tuple-element.25.refs_2_), channel_id=1, source_target_pairs={{0,2},{2,0},{1,3},{3,1},{4,6},{6,4},{5,7},{7,5},{8,10},{10,8},{9,1... | collective-permute-start | bytes 368648 | tf_op jit(solution)/shard_map/ppermute | solution.py:327
  19.5 1.9 %copy-start.4 = (bf16[1,768,2048]{2,1,0:T(8,128)(2,1)S(1)}, bf16[1,768,2048]{2,1,0:T(8,128)(2,1)}, u32[]{:S(2)}) copy-start(bf16[1,768,2048]{2,1,0:T(8,128)(2,1)} %refs_9_.1) | copy-start | bytes 9437188
  24.2 15.1 %collective-permute-start.7 = (bf16[1,768,2048]{2,1,0:T(8,128)(2,1)S(1)}, bf16[1,768,2048]{2,1,0:T(8,128)(2,1)S(1)}, u32[]{:S(2)}, u32[]{:S(2)}) collective-permute-start(bf16[1,768,2048]{2,1,0:T(8,128)(2,1)S(1)} %get-tuple-element.30), channel_id=1, source_target_pairs={{0,1},{1,0},{2,3},{3,2},{4,5},{5,4},{6,7},{7,6},{8,9},{9,8},{10,11... | collective-permute-start | bytes 9437192 | tf_op jit(solution)/shard_map/ppermute | solution.py:324
  24.3 19.6 %collective-permute-start.9 = (bf16[368,768]{1,0:T(8,128)(2,1)S(1)}, bf16[368,768]{1,0:T(8,128)(2,1)S(1)}, u32[]{:S(2)}, u32[]{:S(2)}) collective-permute-start(bf16[368,768]{1,0:T(8,128)(2,1)S(1)} %get-tuple-element.29.refs_4_), channel_id=1, source_target_pairs={{0,2},{2,0},{1,3},{3,1},{4,6},{6,4},{5,7},{7,5},{8,10},{10,8},{9,1... | collective-permute-start | bytes 1695752 | tf_op jit(solution)/shard_map/ppermute | solution.py:327
  25.8 13.5 %collective-permute-start.8 = (bf16[96,2176]{1,0:T(8,128)(2,1)S(1)}, bf16[96,2176]{1,0:T(8,128)(2,1)S(1)}, u32[]{:S(2)}, u32[]{:S(2)}) collective-permute-start(bf16[96,2176]{1,0:T(8,128)(2,1)S(1)} %get-tuple-element.27.refs_2_.refs_4_), channel_id=1, source_target_pairs={{0,8},{4,12},{8,16},{12,20},{16,24},{20,28},{24,0},{28,4},{1,9},{5... | collective-permute-start | bytes 1253384 | tf_op jit(solution)/shard_map/ppermute | solution.py:318
  25.8 15.5 %collective-permute-start.4 = (bf16[96,2176]{1,0:T(8,128)(2,1)S(1)}, bf16[96,2176]{1,0:T(8,128)(2,1)S(1)}, u32[]{:S(2)}, u32[]{:S(2)}) collective-permute-start(bf16[96,2176]{1,0:T(8,128)(2,1)S(1)} %get-tuple-element.27.refs_2_.refs_4_), channel_id=1, source_target_pairs={{0,4},{4,0},{8,12},{12,8},{16,20},{20,16},{24,28},{28,24},{1,5},{5... | collective-permute-start | bytes 1253384 | tf_op jit(solution)/shard_map/ppermute | solution.py:315
  26.3 19.4 %collective-permute-start.3 = (bf16[80,384]{1,0:T(8,128)(2,1)S(1)}, bf16[80,384]{1,0:T(8,128)(2,1)S(1)}, u32[]{:S(2)}, u32[]{:S(2)}) collective-permute-start(bf16[80,384]{1,0:T(8,128)(2,1)S(1)} %fusion.5.refs_8_.refs_0_), channel_id=1, source_target_pairs={{0,2},{2,0},{1,3},{3,1},{4,6},{6,4},{5,7},{7,5},{8,10},{10,8},{9,1... | collective-permute-start | bytes 184328 | tf_op jit(solution)/shard_map/ppermute | solution.py:327
  40.7 16.5 %collective-permute-start.11 = (bf16[96,2176]{1,0:T(8,128)(2,1)S(1)}, bf16[96,2176]{1,0:T(8,128)(2,1)S(1)}, u32[]{:S(2)}, u32[]{:S(2)}) collective-permute-start(bf16[96,2176]{1,0:T(8,128)(2,1)S(1)} %get-tuple-element.33.refs_1_.refs_3_), channel_id=1, source_target_pairs={{0,4},{4,0},{8,12},{12,8},{16,20},{20,16},{24,28},{28,24},{1,5},{5... | collective-permute-start | bytes 1253384 | tf_op jit(solution)/shard_map/ppermute | solution.py:315
  41.3 12.4 %collective-permute-start.12 = (bf16[96,2176]{1,0:T(8,128)(2,1)S(1)}, bf16[96,2176]{1,0:T(8,128)(2,1)S(1)}, u32[]{:S(2)}, u32[]{:S(2)}) collective-permute-start(bf16[96,2176]{1,0:T(8,128)(2,1)S(1)} %get-tuple-element.33.refs_1_.refs_3_), channel_id=1, source_target_pairs={{0,8},{4,12},{8,16},{12,20},{16,24},{20,28},{24,0},{28,4},{1,9},{5... | collective-permute-start | bytes 1253384 | tf_op jit(solution)/shard_map/ppermute | solution.py:318
  43.2 13.3 %collective-permute-start.13 = (bf16[160,768]{1,0:T(8,128)(2,1)S(1)}, bf16[160,768]{1,0:T(8,128)(2,1)S(1)}, u32[]{:S(2)}, u32[]{:S(2)}) collective-permute-start(bf16[160,768]{1,0:T(8,128)(2,1)S(1)} %get-tuple-element.32.refs_4_), channel_id=1, source_target_pairs={{0,2},{2,0},{1,3},{3,1},{4,6},{6,4},{5,7},{7,5},{8,10},{10,8},{9,1... | collective-permute-start | bytes 737288 | tf_op jit(solution)/shard_map/ppermute | solution.py:327
  44.1 16.6 %collective-permute-start.10 = (bf16[368,384]{1,0:T(8,128)(2,1)S(1)}, bf16[368,384]{1,0:T(8,128)(2,1)S(1)}, u32[]{:S(2)}, u32[]{:S(2)}) collective-permute-start(bf16[368,384]{1,0:T(8,128)(2,1)S(1)} %fusion.refs_0_.refs_8_), channel_id=1, source_target_pairs={{0,2},{2,0},{1,3},{3,1},{4,6},{6,4},{5,7},{7,5},{8,10},{10,8},{9,1... | collective-permute-start | bytes 847880 | tf_op jit(solution)/shard_map/ppermute | solution.py:327
  55.0 12.5 %collective-permute-start.15 = (bf16[96,2176]{1,0:T(8,128)(2,1)S(1)}, bf16[96,2176]{1,0:T(8,128)(2,1)S(1)}, u32[]{:S(2)}, u32[]{:S(2)}) collective-permute-start(bf16[96,2176]{1,0:T(8,128)(2,1)S(1)} %get-tuple-element.37.refs_0_.refs_2_), channel_id=1, source_target_pairs={{0,4},{4,0},{8,12},{12,8},{16,20},{20,16},{24,28},{28,24},{1,5},{5... | collective-permute-start | bytes 1253384 | tf_op jit(solution)/shard_map/ppermute | solution.py:315
  56.7 7.5 %collective-permute-start.16 = (bf16[160,384]{1,0:T(8,128)(2,1)S(1)}, bf16[160,384]{1,0:T(8,128)(2,1)S(1)}, u32[]{:S(2)}, u32[]{:S(2)}) collective-permute-start(bf16[160,384]{1,0:T(8,128)(2,1)S(1)} %fusion.4.refs_7_.refs_0_), channel_id=1, source_target_pairs={{0,2},{2,0},{1,3},{3,1},{4,6},{6,4},{5,7},{7,5},{8,10},{10,8},{9,1... | collective-permute-start | bytes 368648 | tf_op jit(solution)/shard_map/ppermute | solution.py:327
  59.2 11.4 %collective-permute-start.17 = (bf16[288,768]{1,0:T(8,128)(2,1)S(1)}, bf16[288,768]{1,0:T(8,128)(2,1)S(1)}, u32[]{:S(2)}, u32[]{:S(2)}) collective-permute-start(bf16[288,768]{1,0:T(8,128)(2,1)S(1)} %get-tuple-element.36.refs_7_), channel_id=1, source_target_pairs={{0,2},{2,0},{1,3},{3,1},{4,6},{6,4},{5,7},{7,5},{8,10},{10,8},{9,1... | collective-permute-start | bytes 1327112 | tf_op jit(solution)/shard_map/ppermute | solution.py:327
  63.5 15.2 %collective-permute-start.14 = (bf16[96,2048]{1,0:T(8,128)(2,1)S(1)}, bf16[96,2048]{1,0:T(8,128)(2,1)S(1)}, u32[]{:S(2)}, u32[]{:S(2)}) collective-permute-start(bf16[96,2048]{1,0:T(8,128)(2,1)S(1)} %get-tuple-element.44), channel_id=1, source_target_pairs={{0,4},{4,0},{8,12},{12,8},{16,20},{20,16},{24,28},{28,24},{1,5},{5... | collective-permute-start | bytes 1179656 | tf_op jit(solution)/shard_map/ppermute | solution.py:315
  65.9 15.6 %collective-permute-start.21 = (bf16[96,2048]{1,0:T(8,128)(2,1)S(1)}, bf16[96,2048]{1,0:T(8,128)(2,1)S(1)}, u32[]{:S(2)}, u32[]{:S(2)}) collective-permute-start(bf16[96,2048]{1,0:T(8,128)(2,1)S(1)} %shard_map.74.refs_5_), channel_id=1, source_target_pairs={{0,4},{4,0},{8,12},{12,8},{16,20},{20,16},{24,28},{28,24},{1,5},{5... | collective-permute-start | bytes 1179656 | tf_op jit(solution)/shard_map/ppermute | solution.py:315
  70.8 10.9 %collective-permute-start.20 = (bf16[288,384]{1,0:T(8,128)(2,1)S(1)}, bf16[288,384]{1,0:T(8,128)(2,1)S(1)}, u32[]{:S(2)}, u32[]{:S(2)}) collective-permute-start(bf16[288,384]{1,0:T(8,128)(2,1)S(1)} %fusion.1.refs_6_.refs_0_), channel_id=1, source_target_pairs={{0,2},{2,0},{1,3},{3,1},{4,6},{6,4},{5,7},{7,5},{8,10},{10,8},{9,1... | collective-permute-start | bytes 663560 | tf_op jit(solution)/shard_map/ppermute | solution.py:327
  73.2 12.5 %collective-permute-start.24 = (bf16[160,768]{1,0:T(8,128)(2,1)S(1)}, bf16[160,768]{1,0:T(8,128)(2,1)S(1)}, u32[]{:S(2)}, u32[]{:S(2)}) collective-permute-start(bf16[160,768]{1,0:T(8,128)(2,1)S(1)} %get-tuple-element.40.refs_4_), channel_id=1, source_target_pairs={{0,2},{2,0},{1,3},{3,1},{4,6},{6,4},{5,7},{7,5},{8,10},{10,8},{9,1... | collective-permute-start | bytes 737288 | tf_op jit(solution)/shard_map/ppermute | solution.py:327
  76.4 10.2 %collective-permute-start.18 = (bf16[160,768]{1,0:T(8,128)(2,1)S(1)}, bf16[160,768]{1,0:T(8,128)(2,1)S(1)}, u32[]{:S(2)}, u32[]{:S(2)}) collective-permute-start(bf16[160,768]{1,0:T(8,128)(2,1)S(1)} %get-tuple-element.42.refs_4_), channel_id=1, source_target_pairs={{0,2},{2,0},{1,3},{3,1},{4,6},{6,4},{5,7},{7,5},{8,10},{10,8},{9,1... | collective-permute-start | bytes 737288 | tf_op jit(solution)/shard_map/ppermute | solution.py:327
  81.7 11.5 %collective-permute-start.23 = (bf16[96,2048]{1,0:T(8,128)(2,1)S(1)}, bf16[96,2048]{1,0:T(8,128)(2,1)S(1)}, u32[]{:S(2)}, u32[]{:S(2)}) collective-permute-start(bf16[96,2048]{1,0:T(8,128)(2,1)S(1)} %shard_map.81.refs_6_), channel_id=1, source_target_pairs={{0,8},{4,12},{8,16},{12,20},{16,24},{20,28},{24,0},{28,4},{1,9},{5... | collective-permute-start | bytes 1179656 | tf_op jit(solution)/shard_map/ppermute | solution.py:318
  84.1 10.0 %collective-permute-start.22 = (bf16[96,2048]{1,0:T(8,128)(2,1)S(1)}, bf16[96,2048]{1,0:T(8,128)(2,1)S(1)}, u32[]{:S(2)}, u32[]{:S(2)}) collective-permute-start(bf16[96,2048]{1,0:T(8,128)(2,1)S(1)} %get-tuple-element.46), channel_id=1, source_target_pairs={{0,4},{4,0},{8,12},{12,8},{16,20},{20,16},{24,28},{28,24},{1,5},{5... | collective-permute-start | bytes 1179656 | tf_op jit(solution)/shard_map/ppermute | solution.py:315
  85.8 4.9 %collective-permute-start.25 = (bf16[160,384]{1,0:T(8,128)(2,1)S(1)}, bf16[160,384]{1,0:T(8,128)(2,1)S(1)}, u32[]{:S(2)}, u32[]{:S(2)}) collective-permute-start(bf16[160,384]{1,0:T(8,128)(2,1)S(1)} %fusion.2.refs_0_.refs_7_), channel_id=1, source_target_pairs={{0,2},{2,0},{1,3},{3,1},{4,6},{6,4},{5,7},{7,5},{8,10},{10,8},{9,1... | collective-permute-start | bytes 368648 | tf_op jit(solution)/shard_map/ppermute | solution.py:327
  92.5 8.8 %collective-permute-start.26 = (bf16[96,2048]{1,0:T(8,128)(2,1)S(1)}, bf16[96,2048]{1,0:T(8,128)(2,1)S(1)}, u32[]{:S(2)}, u32[]{:S(2)}) collective-permute-start(bf16[96,2048]{1,0:T(8,128)(2,1)S(1)} %shard_map.83.refs_3_), channel_id=1, source_target_pairs={{0,4},{4,0},{8,12},{12,8},{16,20},{20,16},{24,28},{28,24},{1,5},{5... | collective-permute-start | bytes 1179656 | tf_op jit(solution)/shard_map/ppermute | solution.py:315
  94.2 10.8 %collective-permute-start.27 = (bf16[96,2048]{1,0:T(8,128)(2,1)S(1)}, bf16[96,2048]{1,0:T(8,128)(2,1)S(1)}, u32[]{:S(2)}, u32[]{:S(2)}) collective-permute-start(bf16[96,2048]{1,0:T(8,128)(2,1)S(1)} %shard_map.84.refs_5_), channel_id=1, source_target_pairs={{0,8},{4,12},{8,16},{12,20},{16,24},{20,28},{24,0},{28,4},{1,9},{5... | collective-permute-start | bytes 1179656 | tf_op jit(solution)/shard_map/ppermute | solution.py:318
  94.3 4.9 %collective-permute-start.19 = (bf16[160,384]{1,0:T(8,128)(2,1)S(1)}, bf16[160,384]{1,0:T(8,128)(2,1)S(1)}, u32[]{:S(2)}, u32[]{:S(2)}) collective-permute-start(bf16[160,384]{1,0:T(8,128)(2,1)S(1)} %fusion.3.refs_4_.refs_0_), channel_id=1, source_target_pairs={{0,2},{2,0},{1,3},{3,1},{4,6},{6,4},{5,7},{7,5},{8,10},{10,8},{9,1... | collective-permute-start | bytes 368648 | tf_op jit(solution)/shard_map/ppermute | solution.py:327
  105.2 9.6 %collective-permute-start.28 = (bf16[96,2048]{1,0:T(8,128)(2,1)S(1)}, bf16[96,2048]{1,0:T(8,128)(2,1)S(1)}, u32[]{:S(2)}, u32[]{:S(2)}) collective-permute-start(bf16[96,2048]{1,0:T(8,128)(2,1)S(1)} %shard_map.86), channel_id=1, source_target_pairs={{0,8},{4,12},{8,16},{12,20},{16,24},{20,28},{24,0},{28,4},{1,9},{5... | collective-permute-start | bytes 1179656 | tf_op jit(solution)/shard_map/ppermute | solution.py:318

commit v10 on v7

--- a/solution.py
+++ b/solution.py
@@ -383,11 +383,12 @@
     def pick(i):
         keys, groups = plan[i]
         mine = [blocks[k] for k in keys]
-        copying = [w_down] if i == 1 else []
-        chosen[i], part, *copies = pick_rows(
-            groups, mine, away, split, copying, order, width, experts, capacity, units
+        chosen[i], part = pick_rows(
+            groups, mine, away, split, [], order, width, experts, capacity, units
         )
-        downs.extend(over_core(c)[0] for c in copies)
+        if i == 1:
+            later, _ = lax.optimization_barrier((w_down, part))
+            downs.append(over_core(later)[0])
         parts_in[i] = [over_x(part[:, 2 * units * (s - 1):2 * units * s], s) for s in range(1, parts)]
         order[:] = [part]
 

time: 115 us -> 114 us (level)
  transfers between devices with their start and end apart: 29 -> 29, of which waited for: 12 -> 12; matrix products, arithmetic and copies ran while one was open for 1% -> 1% of each run, Pallas kernels for 25% -> 24%
where the time goes in v10:
time: 114 us; the launch traced here: 113 us
  waiting for transfers between devices  49.2 us (43%)
  Pallas kernels  30.3 us (27%)
  starting transfers between devices  25.3 us (22%)
  local copies, waits for them, and re-layouts  6.31 us (6%)
  other arithmetic  1.75 us (2%)
    ppermute x6, waiting for transfers between devices, over_z(): return lax.ppermute(x, 'expert', [(i, (i + 2) % ring) for i in range(ring)])  38 us
    ppermute x12, starting transfers between devices, over_x(): lax.ppermute(x, 'tensor', [(i, (i + step) % parts) for i in range(parts)])  12.3 us
    pallas_call x6, Pallas kernels, pick_rows(): pl.pallas_call(kernel, grid=(1,), out_shape=(*out, *[jax.ShapeDtypeStruct...  11.7 us
    pallas_call x6, Pallas kernels, down_rows(): pl.pallas_call(functools.partial(down_kernel, experts, capacity, groups,...  10.7 us
    ppermute x8, starting transfers between devices, over_y(): return lax.ppermute(x, 'expert', [(i, i ^ 1) for i in range(ring)])  10.5 us
    ppermute x12, waiting for transfers between devices, over_x(): lax.ppermute(x, 'tensor', [(i, (i + step) % parts) for i in range(parts)])  8.48 us
    pallas_call x6, Pallas kernels, home_rows(): pl.pallas_call(functools.partial(home_kernel, capacity, units, groups, le...  6.87 us
    unnamed x16, local copies, waits for them, and re-layouts  6.16 us
  transfers between devices with their start and end apart: 29, of which 12 were waited for; matrix products, arithmetic and copies ran while one was open for 1% of the time, Pallas kernels for 24%

profile of v10, /device:TPU:0, one launch (start us, length us, event | category | flops | bytes accessed | tf_op | source)
XLA Modules:
  0.0 113.2 jit_solution(5982584642748418221)
XLA Ops:
  0.0 0.5 collective-permute-start.5
  0.5 1.0 copy-done.5
  1.5 0.7 copy-done.6
  2.2 0.7 copy-done.7
  2.9 0.5 shard_map.64.refs_0_.refs_2_
  3.4 3.0 %collective-permute-start = (bf16[96,2176]{1,0:T(8,128)(2,1)S(1)}, bf16[96,2176]{1,0:T(8,128)(2,1)S(1)}, u32[]{:S(2)}, u32[]{:S(2)}) collective-permute-start(bf16[96,2176]{1,0:T(8,128)(2,1)S(1)} %shard_map.64.refs_0_.refs_2_), channel_id=1, source_target_pairs={{0,4},{4,0},{8,12},{12,8},{16,20},{20,16},{24,28},{28,24},{1,5},{5... | collective-permute-start | bytes 1253384 | tf_op jit(solution)/shard_map/ppermute | solution.py:326
  6.4 1.6 %collective-permute-start.1 = (bf16[96,2176]{1,0:T(8,128)(2,1)S(1)}, bf16[96,2176]{1,0:T(8,128)(2,1)S(1)}, u32[]{:S(2)}, u32[]{:S(2)}) collective-permute-start(bf16[96,2176]{1,0:T(8,128)(2,1)S(1)} %shard_map.64.refs_0_.refs_2_), channel_id=1, source_target_pairs={{0,8},{4,12},{8,16},{12,20},{16,24},{20,28},{24,0},{28,4},{1,9},{5... | collective-permute-start | bytes 1253384 | tf_op jit(solution)/shard_map/ppermute | solution.py:329
  8.0 1.9 %copy-done = bf16[1,2048,768]{2,1,0:T(8,128)(2,1)S(1)} copy-done((bf16[1,2048,768]{2,1,0:T(8,128)(2,1)S(1)}, bf16[1,2048,768]{2,1,0:T(8,128)(2,1)}, u32[]{:S(2)}) %copy-start) | copy-done | bytes 3145752
  9.9 1.9 %copy-done.2 = bf16[1,2048,768]{2,1,0:T(8,128)(2,1)S(1)} copy-done((bf16[1,2048,768]{2,1,0:T(8,128)(2,1)S(1)}, bf16[1,2048,768]{2,1,0:T(8,128)(2,1)}, u32[]{:S(2)}) %copy-start.2) | copy-done | bytes 3145752
  11.8 1.1 shard_map.65
  12.9 1.6 %collective-permute-start.2 = (bf16[80,768]{1,0:T(8,128)(2,1)S(1)}, bf16[80,768]{1,0:T(8,128)(2,1)S(1)}, u32[]{:S(2)}, u32[]{:S(2)}) collective-permute-start(bf16[80,768]{1,0:T(8,128)(2,1)S(1)} %get-tuple-element.25.refs_2_), channel_id=1, source_target_pairs={{0,2},{2,0},{1,3},{3,1},{4,6},{6,4},{5,7},{7,5},{8,10},{10,8},{9,1... | collective-permute-start | bytes 368648 | tf_op jit(solution)/shard_map/ppermute | solution.py:338
  14.4 1.8 %collective-permute-done.refs_3_.refs_1_ = bf16[96,2176]{1,0:T(8,128)(2,1)S(1)} collective-permute-done((bf16[96,2176]{1,0:T(8,128)(2,1)S(1)}, bf16[96,2176]{1,0:T(8,128)(2,1)S(1)}, u32[]{:S(2)}, u32[]{:S(2)}) %collective-permute-start) | collective-permute-done | bytes 417824 | tf_op jit(solution)/shard_map/ppermute | solution.py:326
  16.2 3.3 %collective-permute-done.1.refs_4_ = bf16[96,2176]{1,0:T(8,128)(2,1)S(1)} collective-permute-done((bf16[96,2176]{1,0:T(8,128)(2,1)S(1)}, bf16[96,2176]{1,0:T(8,128)(2,1)S(1)}, u32[]{:S(2)}, u32[]{:S(2)}) %collective-permute-start.1) | collective-permute-done | bytes 417824 | tf_op jit(solution)/shard_map/ppermute | solution.py:329
  19.5 0.7 shard_map.66
  20.3 2.6 %shard_map.67 = (bf16[368,2048]{1,0:T(8,128)(2,1)S(1)}, bf16[368,768]{1,0:T(8,128)(2,1)S(1)}) custom-call(bf16[96,2176]{1,0:T(8,128)(2,1)S(1)} %shard_map.64.refs_0_.refs_2_, bf16[96,2176]{1,0:T(8,128)(2,1)S(1)} %collective-permute-done.refs_3_.refs_1_, bf16[96,2176]{1,0:T(8,128)(2,1)S(1)} %get-tuple-element.27.refs_2_.refs_4_, ...), custom_call_target="tpu_custom_call" | custom-call | flops 1 | bytes 1 | tf_op jit(solution)/shard_map/pallas_call | solution.py:185
  23.0 1.5 %collective-permute-start.10 = (bf16[368,768]{1,0:T(8,128)(2,1)S(1)}, bf16[368,768]{1,0:T(8,128)(2,1)S(1)}, u32[]{:S(2)}, u32[]{:S(2)}) collective-permute-start(bf16[368,768]{1,0:T(8,128)(2,1)S(1)} %get-tuple-element.29.refs_4_), channel_id=1, source_target_pairs={{0,2},{2,0},{1,3},{3,1},{4,6},{6,4},{5,7},{7,5},{8,10},{10,8},{9,1... | collective-permute-start | bytes 1695752 | tf_op jit(solution)/shard_map/ppermute | solution.py:338
  24.5 0.5 collective-permute-start.4
  25.1 0.6 collective-permute-start.3
  25.6 12.4 %collective-permute-done.8.refs_6_ = bf16[96,2176]{1,0:T(8,128)(2,1)S(1)} collective-permute-done((bf16[96,2176]{1,0:T(8,128)(2,1)S(1)}, bf16[96,2176]{1,0:T(8,128)(2,1)S(1)}, u32[]{:S(2)}, u32[]{:S(2)}) %collective-permute-start.8) | collective-permute-done | bytes 417824 | tf_op jit(solution)/shard_map/ppermute | solution.py:329
  38.1 1.4 %shard_map.68 = (f32[368,768]{1,0:T(8,128)S(1)}, bf16[96,2176]{1,0:T(8,128)(2,1)S(1)}) custom-call(bf16[368,2048]{1,0:T(8,128)(2,1)S(1)} %get-tuple-element.28.x_ref, bf16[2048,768]{1,0:T(8,128)(2,1)S(1)} %bitcast.33, bf16[2048,768]{1,0:T(8,128)(2,1)S(1)} %bitcast.43, bf16[2048,768]{1,0:T(8,128)(2,1)S(1)} %bitcast.11, ...), custom_call_target="tpu_custom_call", output_to_operand_aliasing={{1}: (7, {})} | custom-call | flops 1 | bytes 1 | tf_op jit(solution)/shard_map/pallas_call | solution.py:210
  39.4 0.2 collective-permute-start.9
  39.7 0.6 collective-permute-start.12
  40.2 2.0 %shard_map.69 = (bf16[160,2048]{1,0:T(8,128)(2,1)S(1)}, bf16[160,768]{1,0:T(8,128)(2,1)S(1)}) custom-call(bf16[96,2176]{1,0:T(8,128)(2,1)S(1)} %collective-permute-done.4.refs_0_.refs_2_, bf16[2048,768]{1,0:T(8,128)(2,1)S(1)} %bitcast.12, bf16[2048,768]{1,0:T(8,128)(2,1)S(1)} %bitcast.24, bf16[2048,768]{1,0:T(8,128)(2,1)S(1)} %bitcast.34, ...), custom_call_target="tpu_custom_call" | custom-call | flops 1 | bytes 1 | tf_op jit(solution)/shard_map/pallas_call | solution.py:185
  42.2 0.7 collective-permute-start.13
  43.0 0.2 fusion.refs_0_.refs_8_
  43.1 1.5 %collective-permute-start.11 = (bf16[368,384]{1,0:T(8,128)(2,1)S(1)}, bf16[368,384]{1,0:T(8,128)(2,1)S(1)}, u32[]{:S(2)}, u32[]{:S(2)}) collective-permute-start(bf16[368,384]{1,0:T(8,128)(2,1)S(1)} %fusion.refs_0_.refs_8_), channel_id=1, source_target_pairs={{0,2},{2,0},{1,3},{3,1},{4,6},{6,4},{5,7},{7,5},{8,10},{10,8},{9,1... | collective-permute-start | bytes 847880 | tf_op jit(solution)/shard_map/ppermute | solution.py:338
  44.6 7.7 %collective-permute-done.9.refs_5_ = bf16[96,2176]{1,0:T(8,128)(2,1)S(1)} collective-permute-done((bf16[96,2176]{1,0:T(8,128)(2,1)S(1)}, bf16[96,2176]{1,0:T(8,128)(2,1)S(1)}, u32[]{:S(2)}, u32[]{:S(2)}) %collective-permute-start.9) | collective-permute-done | bytes 417824 | tf_op jit(solution)/shard_map/ppermute | solution.py:329
  52.3 1.2 %shard_map.70 = (f32[160,768]{1,0:T(8,128)S(1)}, bf16[96,2176]{1,0:T(8,128)(2,1)S(1)}) custom-call(bf16[160,2048]{1,0:T(8,128)(2,1)S(1)} %get-tuple-element.32.x_ref, bf16[2048,768]{1,0:T(8,128)(2,1)S(1)} %bitcast.13, bf16[2048,768]{1,0:T(8,128)(2,1)S(1)} %bitcast.25, bf16[2048,768]{1,0:T(8,128)(2,1)S(1)} %bitcast.35, ...), custom_call_target="tpu_custom_call", output_to_operand_aliasing={{1}: (6, {})} | custom-call | flops 1 | bytes 1 | tf_op jit(solution)/shard_map/pallas_call | solution.py:210
  53.7 0.6 collective-permute-start.15
  54.3 0.6 collective-permute-start.16
  54.9 1.1 shard_map.71.refs_6_.refs_0_
  56.0 2.0 %shard_map.72 = (bf16[288,2048]{1,0:T(8,128)(2,1)S(1)}, bf16[288,768]{1,0:T(8,128)(2,1)S(1)}) custom-call(bf16[96,2176]{1,0:T(8,128)(2,1)S(1)} %collective-permute-done.12.refs_0_.refs_4_.refs_2_.refs_6_, bf16[96,2176]{1,0:T(8,128)(2,1)S(1)} %get-tuple-element.34.refs_1_.refs_3_, bf16[2048,768]{1,0:T(8,128)(2,1)S(1)} %bitcast.14, ...), custom_call_target="tpu_custom_call" | custom-call | flops 1 | bytes 1 | tf_op jit(solution)/shard_map/pallas_call | solution.py:185
  58.0 1.4 %collective-permute-start.17 = (bf16[288,768]{1,0:T(8,128)(2,1)S(1)}, bf16[288,768]{1,0:T(8,128)(2,1)S(1)}, u32[]{:S(2)}, u32[]{:S(2)}) collective-permute-start(bf16[288,768]{1,0:T(8,128)(2,1)S(1)} %get-tuple-element.36.refs_7_), channel_id=1, source_target_pairs={{0,2},{2,0},{1,3},{3,1},{4,6},{6,4},{5,7},{7,5},{8,10},{10,8},{9,1... | collective-permute-start | bytes 1327112 | tf_op jit(solution)/shard_map/ppermute | solution.py:338
  59.4 2.6 %shard_map.73.refs_5_ = bf16[288,2048]{1,0:T(8,128)(2,1)S(1)} custom-call(bf16[368,384]{1,0:T(8,128)(2,1)S(1)} %fusion.refs_0_.refs_8_, bf16[368,384]{1,0:T(8,128)(2,1)S(1)} %collective-permute-done.11.refs_1_, bf16[96,2176]{1,0:T(8,128)(2,1)S(1)} %shard_map.64.refs_0_.refs_2_, bf16[96,2176]{1,0:T(8,128)(2,1)S(1)} %collective-permute-done.refs_3_.refs_1_, ...), custom_call_target="tpu_custom_call" | custom-call | flops 1 | bytes 1 | tf_op jit(solution)/shard_map/pallas_call | solution.py:278
  62.1 1.6 %collective-permute-start.14 = (bf16[96,2048]{1,0:T(8,128)(2,1)S(1)}, bf16[96,2048]{1,0:T(8,128)(2,1)S(1)}, u32[]{:S(2)}, u32[]{:S(2)}) collective-permute-start(bf16[96,2048]{1,0:T(8,128)(2,1)S(1)} %get-tuple-element.44), channel_id=1, source_target_pairs={{0,4},{4,0},{8,12},{12,8},{16,20},{20,16},{24,28},{28,24},{1,5},{5... | collective-permute-start | bytes 1179656 | tf_op jit(solution)/shard_map/ppermute | solution.py:326
  63.7 1.6 %shard_map.74.refs_5_ = bf16[96,2048]{1,0:T(8,128)(2,1)S(1)} custom-call(bf16[160,384]{1,0:T(8,128)(2,1)S(1)} %fusion.4.refs_7_.refs_0_, bf16[160,384]{1,0:T(8,128)(2,1)S(1)} %collective-permute-done.16.refs_1_, bf16[96,2176]{1,0:T(8,128)(2,1)S(1)} %collective-permute-done.4.refs_0_.refs_2_, bf16[768,2048]{1,0:T(8,128)(2,1)S(1)} %bitcast.54, ...), custom_call_target="tpu_custom_call" | custom-call | flops 1 | bytes 1 | tf_op jit(solution)/shard_map/pallas_call | solution.py:278
  65.4 1.9 %shard_map.75 = (bf16[160,2048]{1,0:T(8,128)(2,1)S(1)}, bf16[160,768]{1,0:T(8,128)(2,1)S(1)}) custom-call(bf16[96,2176]{1,0:T(8,128)(2,1)S(1)} %collective-permute-done.15.refs_0_.refs_2_, bf16[2048,768]{1,0:T(8,128)(2,1)S(1)} %bitcast.15, bf16[2048,768]{1,0:T(8,128)(2,1)S(1)} %bitcast.27, bf16[2048,768]{1,0:T(8,128)(2,1)S(1)} %bitcast.37, ...), custom_call_target="tpu_custom_call" | custom-call | flops 1 | bytes 1 | tf_op jit(solution)/shard_map/pallas_call | solution.py:185
  67.3 1.1 %shard_map.76.refs_4_ = f32[288,768]{1,0:T(8,128)S(1)} custom-call(bf16[288,2048]{1,0:T(8,128)(2,1)S(1)} %get-tuple-element.39.x_ref, bf16[2048,768]{1,0:T(8,128)(2,1)S(1)} %bitcast.16, bf16[2048,768]{1,0:T(8,128)(2,1)S(1)} %bitcast.28, bf16[2048,768]{1,0:T(8,128)(2,1)S(1)} %bitcast.38, bf16[2048,768]{1,0:T(8,128)(2,1)S(1)} %bitcast.48, ...), custom_call_target="tpu_custom_call" | custom-call | flops 1 | bytes 1 | tf_op jit(solution)/shard_map/pallas_call | solution.py:210
  68.5 0.2 collective-permute-done.17
  68.9 0.8 collective-permute-start.20
  69.6 1.5 %collective-permute-start.22 = (bf16[96,2048]{1,0:T(8,128)(2,1)S(1)}, bf16[96,2048]{1,0:T(8,128)(2,1)S(1)}, u32[]{:S(2)}, u32[]{:S(2)}) collective-permute-start(bf16[96,2048]{1,0:T(8,128)(2,1)S(1)} %shard_map.74.refs_5_), channel_id=1, source_target_pairs={{0,4},{4,0},{8,12},{12,8},{16,20},{20,16},{24,28},{28,24},{1,5},{5... | collective-permute-start | bytes 1179656 | tf_op jit(solution)/shard_map/ppermute | solution.py:326
  71.2 1.2 %shard_map.77.refs_5_ = f32[160,768]{1,0:T(8,128)S(1)} custom-call(bf16[160,2048]{1,0:T(8,128)(2,1)S(1)} %get-tuple-element.38.x_ref, bf16[2048,768]{1,0:T(8,128)(2,1)S(1)} %bitcast.17, bf16[2048,768]{1,0:T(8,128)(2,1)S(1)} %bitcast.29, bf16[2048,768]{1,0:T(8,128)(2,1)S(1)} %bitcast.39, bf16[2048,768]{1,0:T(8,128)(2,1)S(1)} %bitcast.49, ...), custom_call_target="tpu_custom_call" | custom-call | flops 1 | bytes 1 | tf_op jit(solution)/shard_map/pallas_call | solution.py:210
  72.4 1.4 %collective-permute-start.24 = (bf16[160,768]{1,0:T(8,128)(2,1)S(1)}, bf16[160,768]{1,0:T(8,128)(2,1)S(1)}, u32[]{:S(2)}, u32[]{:S(2)}) collective-permute-start(bf16[160,768]{1,0:T(8,128)(2,1)S(1)} %get-tuple-element.40.refs_4_), channel_id=1, source_target_pairs={{0,2},{2,0},{1,3},{3,1},{4,6},{6,4},{5,7},{7,5},{8,10},{10,8},{9,1... | collective-permute-start | bytes 737288 | tf_op jit(solution)/shard_map/ppermute | solution.py:338
  73.8 2.2 %shard_map.78 = (bf16[160,2048]{1,0:T(8,128)(2,1)S(1)}, bf16[160,768]{1,0:T(8,128)(2,1)S(1)}) custom-call(bf16[96,2176]{1,0:T(8,128)(2,1)S(1)} %get-tuple-element.37.refs_0_.refs_2_, bf16[2048,768]{1,0:T(8,128)(2,1)S(1)} %bitcast.18, bf16[2048,768]{1,0:T(8,128)(2,1)S(1)} %bitcast.30, bf16[2048,768]{1,0:T(8,128)(2,1)S(1)} %bitcast.40, ...), custom_call_target="tpu_custom_call" | custom-call | flops 1 | bytes 1 | tf_op jit(solution)/shard_map/pallas_call | solution.py:185
  76.0 0.7 collective-permute-start.18
  76.7 1.2 %shard_map.79.refs_3_ = f32[160,768]{1,0:T(8,128)S(1)} custom-call(bf16[160,2048]{1,0:T(8,128)(2,1)S(1)} %get-tuple-element.41.x_ref, bf16[2048,768]{1,0:T(8,128)(2,1)S(1)} %bitcast.19, bf16[2048,768]{1,0:T(8,128)(2,1)S(1)} %bitcast.31, bf16[2048,768]{1,0:T(8,128)(2,1)S(1)} %bitcast.41, bf16[2048,768]{1,0:T(8,128)(2,1)S(1)} %bitcast.51, ...), custom_call_target="tpu_custom_call" | custom-call | flops 1 | bytes 1 | tf_op jit(solution)/shard_map/pallas_call | solution.py:210
  77.9 0.1 shard_map.80.refs_6_
  78.1 2.2 %shard_map.81.refs_2_ = bf16[192,2048]{1,0:T(8,128)(2,1)S(1)} custom-call(bf16[288,384]{1,0:T(8,128)(2,1)S(1)} %fusion.1.refs_6_.refs_0_, bf16[288,384]{1,0:T(8,128)(2,1)S(1)} %collective-permute-done.20.refs_1_, bf16[96,2176]{1,0:T(8,128)(2,1)S(1)} %collective-permute-done.12.refs_0_.refs_4_.refs_2_.refs_6_, ...), custom_call_target="tpu_custom_call" | custom-call | flops 1 | bytes 1 | tf_op jit(solution)/shard_map/pallas_call | solution.py:278
  80.3 0.8 collective-permute-start.21
  81.1 0.9 collective-permute-done.22.refs_1_
  82.4 0.8 collective-permute-start.25
  83.2 2.7 %collective-permute-done.18 = bf16[160,768]{1,0:T(8,128)(2,1)S(1)} collective-permute-done((bf16[160,768]{1,0:T(8,128)(2,1)S(1)}, bf16[160,768]{1,0:T(8,128)(2,1)S(1)}, u32[]{:S(2)}, u32[]{:S(2)}) %collective-permute-start.18) | collective-permute-done | bytes 245792 | tf_op jit(solution)/shard_map/ppermute | solution.py:338
  86.1 1.3 %collective-permute-done.25.refs_1_ = bf16[160,384]{1,0:T(8,128)(2,1)S(1)} collective-permute-done((bf16[160,384]{1,0:T(8,128)(2,1)S(1)}, bf16[160,384]{1,0:T(8,128)(2,1)S(1)}, u32[]{:S(2)}, u32[]{:S(2)}) %collective-permute-start.25) | collective-permute-done | bytes 122912 | tf_op jit(solution)/shard_map/ppermute | solution.py:338
  87.3 1.6 %shard_map.83.refs_3_ = bf16[96,2048]{1,0:T(8,128)(2,1)S(1)} custom-call(bf16[160,384]{1,0:T(8,128)(2,1)S(1)} %fusion.2.refs_0_.refs_7_, bf16[160,384]{1,0:T(8,128)(2,1)S(1)} %collective-permute-done.25.refs_1_, bf16[96,2176]{1,0:T(8,128)(2,1)S(1)} %collective-permute-done.15.refs_0_.refs_2_, bf16[768,2048]{1,0:T(8,128)(2,1)S(1)} %bitcast.56, ...), custom_call_target="tpu_custom_call" | custom-call | flops 1 | bytes 1 | tf_op jit(solution)/shard_map/pallas_call | solution.py:278
  89.0 1.9 %collective-permute-start.26 = (bf16[96,2048]{1,0:T(8,128)(2,1)S(1)}, bf16[96,2048]{1,0:T(8,128)(2,1)S(1)}, u32[]{:S(2)}, u32[]{:S(2)}) collective-permute-start(bf16[96,2048]{1,0:T(8,128)(2,1)S(1)} %shard_map.83.refs_3_), channel_id=1, source_target_pairs={{0,4},{4,0},{8,12},{12,8},{16,20},{20,16},{24,28},{28,24},{1,5},{5... | collective-permute-start | bytes 1179656 | tf_op jit(solution)/shard_map/ppermute | solution.py:326
  90.9 0.9 collective-permute-done.23.refs_2_
  91.8 0.1 shard_map.84.refs_5_
  92.0 0.7 collective-permute-start.19
  92.7 4.3 %collective-permute-done.19.refs_1_ = bf16[160,384]{1,0:T(8,128)(2,1)S(1)} collective-permute-done((bf16[160,384]{1,0:T(8,128)(2,1)S(1)}, bf16[160,384]{1,0:T(8,128)(2,1)S(1)}, u32[]{:S(2)}, u32[]{:S(2)}) %collective-permute-start.19) | collective-permute-done | bytes 122912 | tf_op jit(solution)/shard_map/ppermute | solution.py:338
  97.0 1.6 %shard_map.85.refs_0_.refs_3_ = bf16[96,2048]{1,0:T(8,128)(2,1)S(1)} custom-call(bf16[160,384]{1,0:T(8,128)(2,1)S(1)} %fusion.3.refs_4_.refs_0_, bf16[160,384]{1,0:T(8,128)(2,1)S(1)} %collective-permute-done.19.refs_1_, bf16[96,2176]{1,0:T(8,128)(2,1)S(1)} %get-tuple-element.37.refs_0_.refs_2_, bf16[768,2048]{1,0:T(8,128)(2,1)S(1)} %bitcast.57, ...), custom_call_target="tpu_custom_call" | custom-call | flops 1 | bytes 1 | tf_op jit(solution)/shard_map/pallas_call | solution.py:278
  98.6 4.0 %collective-permute-done.27.refs_2_ = bf16[96,2048]{1,0:T(8,128)(2,1)S(1)} collective-permute-done((bf16[96,2048]{1,0:T(8,128)(2,1)S(1)}, bf16[96,2048]{1,0:T(8,128)(2,1)S(1)}, u32[]{:S(2)}, u32[]{:S(2)}) %collective-permute-start.27) | collective-permute-done | bytes 393248 | tf_op jit(solution)/shard_map/ppermute | solution.py:329
  102.6 0.1 shard_map.86
  102.9 9.6 %collective-permute-done.28 = bf16[96,2048]{1,0:T(8,128)(2,1)S(1)} collective-permute-done((bf16[96,2048]{1,0:T(8,128)(2,1)S(1)}, bf16[96,2048]{1,0:T(8,128)(2,1)S(1)}, u32[]{:S(2)}, u32[]{:S(2)}) %collective-permute-start.28) | collective-permute-done | bytes 393248 | tf_op jit(solution)/shard_map/ppermute | solution.py:329
  112.4 0.8 add_convert_fusion
  (48 shorter events, 1.4 us)
Async XLA Ops:
  0.0 20.3 %collective-permute-start.5 = (bf16[1,2048,768]{2,1,0:T(8,128)(2,1)}, bf16[1,2048,768]{2,1,0:T(8,128)(2,1)S(1)}, u32[]{:S(2)}, u32[]{:S(2)}) collective-permute-start(bf16[1,2048,768]{2,1,0:T(8,128)(2,1)} %param.9), channel_id=1, source_target_pairs={{0,1},{1,0},{2,3},{3,2},{4,5},{5,4},{6,7},{7,6},{8,9},{9,8},{10,11... | collective-permute-start | bytes 9437192 | tf_op jit(solution)/shard_map/ppermute | solution.py:335
  0.5 19.9 %collective-permute-start.6 = (bf16[1,2048,768]{2,1,0:T(8,128)(2,1)}, bf16[1,2048,768]{2,1,0:T(8,128)(2,1)S(1)}, u32[]{:S(2)}, u32[]{:S(2)}) collective-permute-start(bf16[1,2048,768]{2,1,0:T(8,128)(2,1)} %param.10), channel_id=1, source_target_pairs={{0,1},{1,0},{2,3},{3,2},{4,5},{5,4},{6,7},{7,6},{8,9},{9,8},{10,11... | collective-permute-start | bytes 9437192 | tf_op jit(solution)/shard_map/ppermute | solution.py:335
  0.5 1.0 copy-start.5
  1.5 0.7 copy-start.6
  2.2 0.7 copy-start.7
  3.4 12.8 %collective-permute-start = (bf16[96,2176]{1,0:T(8,128)(2,1)S(1)}, bf16[96,2176]{1,0:T(8,128)(2,1)S(1)}, u32[]{:S(2)}, u32[]{:S(2)}) collective-permute-start(bf16[96,2176]{1,0:T(8,128)(2,1)S(1)} %shard_map.64.refs_0_.refs_2_), channel_id=1, source_target_pairs={{0,4},{4,0},{8,12},{12,8},{16,20},{20,16},{24,28},{28,24},{1,5},{5... | collective-permute-start | bytes 1253384 | tf_op jit(solution)/shard_map/ppermute | solution.py:326
  6.4 13.1 %collective-permute-start.1 = (bf16[96,2176]{1,0:T(8,128)(2,1)S(1)}, bf16[96,2176]{1,0:T(8,128)(2,1)S(1)}, u32[]{:S(2)}, u32[]{:S(2)}) collective-permute-start(bf16[96,2176]{1,0:T(8,128)(2,1)S(1)} %shard_map.64.refs_0_.refs_2_), channel_id=1, source_target_pairs={{0,8},{4,12},{8,16},{12,20},{16,24},{20,28},{24,0},{28,4},{1,9},{5... | collective-permute-start | bytes 1253384 | tf_op jit(solution)/shard_map/ppermute | solution.py:329
  8.0 1.9 %copy-start = (bf16[1,2048,768]{2,1,0:T(8,128)(2,1)S(1)}, bf16[1,2048,768]{2,1,0:T(8,128)(2,1)}, u32[]{:S(2)}) copy-start(bf16[1,2048,768]{2,1,0:T(8,128)(2,1)} %param.9) | copy-start | bytes 9437188
  9.9 1.9 %copy-start.2 = (bf16[1,2048,768]{2,1,0:T(8,128)(2,1)S(1)}, bf16[1,2048,768]{2,1,0:T(8,128)(2,1)}, u32[]{:S(2)}) copy-start(bf16[1,2048,768]{2,1,0:T(8,128)(2,1)} %param.10) | copy-start | bytes 9437188
  11.8 7.8 %copy-start.1 = (bf16[1,2048,768]{2,1,0:T(8,128)(2,1)S(1)}, bf16[1,2048,768]{2,1,0:T(8,128)(2,1)}, u32[]{:S(2)}) copy-start(bf16[1,2048,768]{2,1,0:T(8,128)(2,1)} %param.9) | copy-start | bytes 9437188
  11.8 7.8 %copy-start.3 = (bf16[1,2048,768]{2,1,0:T(8,128)(2,1)S(1)}, bf16[1,2048,768]{2,1,0:T(8,128)(2,1)}, u32[]{:S(2)}) copy-start(bf16[1,2048,768]{2,1,0:T(8,128)(2,1)} %param.10) | copy-start | bytes 9437188
  12.9 7.4 %collective-permute-start.2 = (bf16[80,768]{1,0:T(8,128)(2,1)S(1)}, bf16[80,768]{1,0:T(8,128)(2,1)S(1)}, u32[]{:S(2)}, u32[]{:S(2)}) collective-permute-start(bf16[80,768]{1,0:T(8,128)(2,1)S(1)} %get-tuple-element.25.refs_2_), channel_id=1, source_target_pairs={{0,2},{2,0},{1,3},{3,1},{4,6},{6,4},{5,7},{7,5},{8,10},{10,8},{9,1... | collective-permute-start | bytes 368648 | tf_op jit(solution)/shard_map/ppermute | solution.py:338
  20.3 2.6 %copy-start.4 = (bf16[1,768,2048]{2,1,0:T(8,128)(2,1)S(1)}, bf16[1,768,2048]{2,1,0:T(8,128)(2,1)}, u32[]{:S(2)}) copy-start(bf16[1,768,2048]{2,1,0:T(8,128)(2,1)} %param.11) | copy-start | bytes 9437188
  22.9 15.1 %collective-permute-start.7 = (bf16[1,768,2048]{2,1,0:T(8,128)(2,1)S(1)}, bf16[1,768,2048]{2,1,0:T(8,128)(2,1)S(1)}, u32[]{:S(2)}, u32[]{:S(2)}) collective-permute-start(bf16[1,768,2048]{2,1,0:T(8,128)(2,1)S(1)} %copy-done.4), channel_id=1, source_target_pairs={{0,1},{1,0},{2,3},{3,2},{4,5},{5,4},{6,7},{7,6},{8,9},{9,8},{10,11... | collective-permute-start | bytes 9437192 | tf_op jit(solution)/shard_map/ppermute | solution.py:335
  23.0 19.8 %collective-permute-start.10 = (bf16[368,768]{1,0:T(8,128)(2,1)S(1)}, bf16[368,768]{1,0:T(8,128)(2,1)S(1)}, u32[]{:S(2)}, u32[]{:S(2)}) collective-permute-start(bf16[368,768]{1,0:T(8,128)(2,1)S(1)} %get-tuple-element.29.refs_4_), channel_id=1, source_target_pairs={{0,2},{2,0},{1,3},{3,1},{4,6},{6,4},{5,7},{7,5},{8,10},{10,8},{9,1... | collective-permute-start | bytes 1695752 | tf_op jit(solution)/shard_map/ppermute | solution.py:338
  24.5 13.5 %collective-permute-start.8 = (bf16[96,2176]{1,0:T(8,128)(2,1)S(1)}, bf16[96,2176]{1,0:T(8,128)(2,1)S(1)}, u32[]{:S(2)}, u32[]{:S(2)}) collective-permute-start(bf16[96,2176]{1,0:T(8,128)(2,1)S(1)} %get-tuple-element.27.refs_2_.refs_4_), channel_id=1, source_target_pairs={{0,8},{4,12},{8,16},{12,20},{16,24},{20,28},{24,0},{28,4},{1,9},{5... | collective-permute-start | bytes 1253384 | tf_op jit(solution)/shard_map/ppermute | solution.py:329
  24.5 15.7 %collective-permute-start.4 = (bf16[96,2176]{1,0:T(8,128)(2,1)S(1)}, bf16[96,2176]{1,0:T(8,128)(2,1)S(1)}, u32[]{:S(2)}, u32[]{:S(2)}) collective-permute-start(bf16[96,2176]{1,0:T(8,128)(2,1)S(1)} %get-tuple-element.27.refs_2_.refs_4_), channel_id=1, source_target_pairs={{0,4},{4,0},{8,12},{12,8},{16,20},{20,16},{24,28},{28,24},{1,5},{5... | collective-permute-start | bytes 1253384 | tf_op jit(solution)/shard_map/ppermute | solution.py:326
  25.1 29.9 %collective-permute-start.3 = (bf16[80,384]{1,0:T(8,128)(2,1)S(1)}, bf16[80,384]{1,0:T(8,128)(2,1)S(1)}, u32[]{:S(2)}, u32[]{:S(2)}) collective-permute-start(bf16[80,384]{1,0:T(8,128)(2,1)S(1)} %fusion.5.refs_8_.refs_0_), channel_id=1, source_target_pairs={{0,2},{2,0},{1,3},{3,1},{4,6},{6,4},{5,7},{7,5},{8,10},{10,8},{9,1... | collective-permute-start | bytes 184328 | tf_op jit(solution)/shard_map/ppermute | solution.py:338
  39.4 12.9 %collective-permute-start.9 = (bf16[96,2176]{1,0:T(8,128)(2,1)S(1)}, bf16[96,2176]{1,0:T(8,128)(2,1)S(1)}, u32[]{:S(2)}, u32[]{:S(2)}) collective-permute-start(bf16[96,2176]{1,0:T(8,128)(2,1)S(1)} %get-tuple-element.34.refs_1_.refs_3_), channel_id=1, source_target_pairs={{0,8},{4,12},{8,16},{12,20},{16,24},{20,28},{24,0},{28,4},{1,9},{5... | collective-permute-start | bytes 1253384 | tf_op jit(solution)/shard_map/ppermute | solution.py:329
  39.7 16.3 %collective-permute-start.12 = (bf16[96,2176]{1,0:T(8,128)(2,1)S(1)}, bf16[96,2176]{1,0:T(8,128)(2,1)S(1)}, u32[]{:S(2)}, u32[]{:S(2)}) collective-permute-start(bf16[96,2176]{1,0:T(8,128)(2,1)S(1)} %get-tuple-element.34.refs_1_.refs_3_), channel_id=1, source_target_pairs={{0,4},{4,0},{8,12},{12,8},{16,20},{20,16},{24,28},{28,24},{1,5},{5... | collective-permute-start | bytes 1253384 | tf_op jit(solution)/shard_map/ppermute | solution.py:326
  42.2 11.4 %collective-permute-start.13 = (bf16[160,768]{1,0:T(8,128)(2,1)S(1)}, bf16[160,768]{1,0:T(8,128)(2,1)S(1)}, u32[]{:S(2)}, u32[]{:S(2)}) collective-permute-start(bf16[160,768]{1,0:T(8,128)(2,1)S(1)} %get-tuple-element.33.refs_4_), channel_id=1, source_target_pairs={{0,2},{2,0},{1,3},{3,1},{4,6},{6,4},{5,7},{7,5},{8,10},{10,8},{9,1... | collective-permute-start | bytes 737288 | tf_op jit(solution)/shard_map/ppermute | solution.py:338
  43.1 16.3 %collective-permute-start.11 = (bf16[368,384]{1,0:T(8,128)(2,1)S(1)}, bf16[368,384]{1,0:T(8,128)(2,1)S(1)}, u32[]{:S(2)}, u32[]{:S(2)}) collective-permute-start(bf16[368,384]{1,0:T(8,128)(2,1)S(1)} %fusion.refs_0_.refs_8_), channel_id=1, source_target_pairs={{0,2},{2,0},{1,3},{3,1},{4,6},{6,4},{5,7},{7,5},{8,10},{10,8},{9,1... | collective-permute-start | bytes 847880 | tf_op jit(solution)/shard_map/ppermute | solution.py:338
  53.7 11.6 %collective-permute-start.15 = (bf16[96,2176]{1,0:T(8,128)(2,1)S(1)}, bf16[96,2176]{1,0:T(8,128)(2,1)S(1)}, u32[]{:S(2)}, u32[]{:S(2)}) collective-permute-start(bf16[96,2176]{1,0:T(8,128)(2,1)S(1)} %get-tuple-element.37.refs_0_.refs_2_), channel_id=1, source_target_pairs={{0,4},{4,0},{8,12},{12,8},{16,20},{20,16},{24,28},{28,24},{1,5},{5... | collective-permute-start | bytes 1253384 | tf_op jit(solution)/shard_map/ppermute | solution.py:326
  54.3 9.4 %collective-permute-start.16 = (bf16[160,384]{1,0:T(8,128)(2,1)S(1)}, bf16[160,384]{1,0:T(8,128)(2,1)S(1)}, u32[]{:S(2)}, u32[]{:S(2)}) collective-permute-start(bf16[160,384]{1,0:T(8,128)(2,1)S(1)} %fusion.4.refs_7_.refs_0_), channel_id=1, source_target_pairs={{0,2},{2,0},{1,3},{3,1},{4,6},{6,4},{5,7},{7,5},{8,10},{10,8},{9,1... | collective-permute-start | bytes 368648 | tf_op jit(solution)/shard_map/ppermute | solution.py:338
  58.0 10.6 %collective-permute-start.17 = (bf16[288,768]{1,0:T(8,128)(2,1)S(1)}, bf16[288,768]{1,0:T(8,128)(2,1)S(1)}, u32[]{:S(2)}, u32[]{:S(2)}) collective-permute-start(bf16[288,768]{1,0:T(8,128)(2,1)S(1)} %get-tuple-element.36.refs_7_), channel_id=1, source_target_pairs={{0,2},{2,0},{1,3},{3,1},{4,6},{6,4},{5,7},{7,5},{8,10},{10,8},{9,1... | collective-permute-start | bytes 1327112 | tf_op jit(solution)/shard_map/ppermute | solution.py:338
  62.1 15.8 %collective-permute-start.14 = (bf16[96,2048]{1,0:T(8,128)(2,1)S(1)}, bf16[96,2048]{1,0:T(8,128)(2,1)S(1)}, u32[]{:S(2)}, u32[]{:S(2)}) collective-permute-start(bf16[96,2048]{1,0:T(8,128)(2,1)S(1)} %get-tuple-element.44), channel_id=1, source_target_pairs={{0,4},{4,0},{8,12},{12,8},{16,20},{20,16},{24,28},{28,24},{1,5},{5... | collective-permute-start | bytes 1179656 | tf_op jit(solution)/shard_map/ppermute | solution.py:326
  68.9 9.2 %collective-permute-start.20 = (bf16[288,384]{1,0:T(8,128)(2,1)S(1)}, bf16[288,384]{1,0:T(8,128)(2,1)S(1)}, u32[]{:S(2)}, u32[]{:S(2)}) collective-permute-start(bf16[288,384]{1,0:T(8,128)(2,1)S(1)} %fusion.1.refs_6_.refs_0_), channel_id=1, source_target_pairs={{0,2},{2,0},{1,3},{3,1},{4,6},{6,4},{5,7},{7,5},{8,10},{10,8},{9,1... | collective-permute-start | bytes 663560 | tf_op jit(solution)/shard_map/ppermute | solution.py:338
  69.6 12.4 %collective-permute-start.22 = (bf16[96,2048]{1,0:T(8,128)(2,1)S(1)}, bf16[96,2048]{1,0:T(8,128)(2,1)S(1)}, u32[]{:S(2)}, u32[]{:S(2)}) collective-permute-start(bf16[96,2048]{1,0:T(8,128)(2,1)S(1)} %shard_map.74.refs_5_), channel_id=1, source_target_pairs={{0,4},{4,0},{8,12},{12,8},{16,20},{20,16},{24,28},{28,24},{1,5},{5... | collective-permute-start | bytes 1179656 | tf_op jit(solution)/shard_map/ppermute | solution.py:326
  72.4 9.9 %collective-permute-start.24 = (bf16[160,768]{1,0:T(8,128)(2,1)S(1)}, bf16[160,768]{1,0:T(8,128)(2,1)S(1)}, u32[]{:S(2)}, u32[]{:S(2)}) collective-permute-start(bf16[160,768]{1,0:T(8,128)(2,1)S(1)} %get-tuple-element.40.refs_4_), channel_id=1, source_target_pairs={{0,2},{2,0},{1,3},{3,1},{4,6},{6,4},{5,7},{7,5},{8,10},{10,8},{9,1... | collective-permute-start | bytes 737288 | tf_op jit(solution)/shard_map/ppermute | solution.py:338
  76.0 10.0 %collective-permute-start.18 = (bf16[160,768]{1,0:T(8,128)(2,1)S(1)}, bf16[160,768]{1,0:T(8,128)(2,1)S(1)}, u32[]{:S(2)}, u32[]{:S(2)}) collective-permute-start(bf16[160,768]{1,0:T(8,128)(2,1)S(1)} %get-tuple-element.42.refs_4_), channel_id=1, source_target_pairs={{0,2},{2,0},{1,3},{3,1},{4,6},{6,4},{5,7},{7,5},{8,10},{10,8},{9,1... | collective-permute-start | bytes 737288 | tf_op jit(solution)/shard_map/ppermute | solution.py:338
  80.3 10.6 %collective-permute-start.21 = (bf16[96,2048]{1,0:T(8,128)(2,1)S(1)}, bf16[96,2048]{1,0:T(8,128)(2,1)S(1)}, u32[]{:S(2)}, u32[]{:S(2)}) collective-permute-start(bf16[96,2048]{1,0:T(8,128)(2,1)S(1)} %get-tuple-element.46), channel_id=1, source_target_pairs={{0,4},{4,0},{8,12},{12,8},{16,20},{20,16},{24,28},{28,24},{1,5},{5... | collective-permute-start | bytes 1179656 | tf_op jit(solution)/shard_map/ppermute | solution.py:326
  82.2 9.6 %collective-permute-start.23 = (bf16[96,2048]{1,0:T(8,128)(2,1)S(1)}, bf16[96,2048]{1,0:T(8,128)(2,1)S(1)}, u32[]{:S(2)}, u32[]{:S(2)}) collective-permute-start(bf16[96,2048]{1,0:T(8,128)(2,1)S(1)} %shard_map.82.refs_5_), channel_id=1, source_target_pairs={{0,8},{4,12},{8,16},{12,20},{16,24},{20,28},{24,0},{28,4},{1,9},{5... | collective-permute-start | bytes 1179656 | tf_op jit(solution)/shard_map/ppermute | solution.py:329
  82.4 4.9 %collective-permute-start.25 = (bf16[160,384]{1,0:T(8,128)(2,1)S(1)}, bf16[160,384]{1,0:T(8,128)(2,1)S(1)}, u32[]{:S(2)}, u32[]{:S(2)}) collective-permute-start(bf16[160,384]{1,0:T(8,128)(2,1)S(1)} %fusion.2.refs_0_.refs_7_), channel_id=1, source_target_pairs={{0,2},{2,0},{1,3},{3,1},{4,6},{6,4},{5,7},{7,5},{8,10},{10,8},{9,1... | collective-permute-start | bytes 368648 | tf_op jit(solution)/shard_map/ppermute | solution.py:338
  89.0 9.6 %collective-permute-start.26 = (bf16[96,2048]{1,0:T(8,128)(2,1)S(1)}, bf16[96,2048]{1,0:T(8,128)(2,1)S(1)}, u32[]{:S(2)}, u32[]{:S(2)}) collective-permute-start(bf16[96,2048]{1,0:T(8,128)(2,1)S(1)} %shard_map.83.refs_3_), channel_id=1, source_target_pairs={{0,4},{4,0},{8,12},{12,8},{16,20},{20,16},{24,28},{28,24},{1,5},{5... | collective-permute-start | bytes 1179656 | tf_op jit(solution)/shard_map/ppermute | solution.py:326
  91.9 10.7 %collective-permute-start.27 = (bf16[96,2048]{1,0:T(8,128)(2,1)S(1)}, bf16[96,2048]{1,0:T(8,128)(2,1)S(1)}, u32[]{:S(2)}, u32[]{:S(2)}) collective-permute-start(bf16[96,2048]{1,0:T(8,128)(2,1)S(1)} %shard_map.84.refs_5_), channel_id=1, source_target_pairs={{0,8},{4,12},{8,16},{12,20},{16,24},{20,28},{24,0},{28,4},{1,9},{5... | collective-permute-start | bytes 1179656 | tf_op jit(solution)/shard_map/ppermute | solution.py:329
  92.0 4.9 %collective-permute-start.19 = (bf16[160,384]{1,0:T(8,128)(2,1)S(1)}, bf16[160,384]{1,0:T(8,128)(2,1)S(1)}, u32[]{:S(2)}, u32[]{:S(2)}) collective-permute-start(bf16[160,384]{1,0:T(8,128)(2,1)S(1)} %fusion.3.refs_4_.refs_0_), channel_id=1, source_target_pairs={{0,2},{2,0},{1,3},{3,1},{4,6},{6,4},{5,7},{7,5},{8,10},{10,8},{9,1... | collective-permute-start | bytes 368648 | tf_op jit(solution)/shard_map/ppermute | solution.py:338
  102.8 9.6 %collective-permute-start.28 = (bf16[96,2048]{1,0:T(8,128)(2,1)S(1)}, bf16[96,2048]{1,0:T(8,128)(2,1)S(1)}, u32[]{:S(2)}, u32[]{:S(2)}) collective-permute-start(bf16[96,2048]{1,0:T(8,128)(2,1)S(1)} %shard_map.86), channel_id=1, source_target_pairs={{0,8},{4,12},{8,16},{12,20},{16,24},{20,28},{24,0},{28,4},{1,9},{5... | collective-permute-start | bytes 1179656 | tf_op jit(solution)/shard_map/ppermute | solution.py:329

commit v11 on v9

--- a/solution.py
+++ b/solution.py
@@ -372,12 +372,17 @@
     def pick(i):
         keys, groups = plan[i]
         mine = [blocks[k] for k in keys]
-        copying = [w_down] if i == 1 else []
-        chosen[i], part, *copies = pick_rows(
-            groups, mine, away, split, copying, order, width, experts, capacity, units
+        chosen[i], part = pick_rows(
+            groups, mine, away, split, [], order, width, experts, capacity, units
         )
-        downs.extend(over_core(c)[0] for c in copies)
-        parts_in[i] = [over_x(part[:, 2 * units * (s - 1):2 * units * s], s) for s in range(1, parts)]
+        if i == 1:
+            later, _ = lax.optimization_barrier((w_down, part))
+            downs.append(over_core(later)[0])
+        cut = units if i == 1 else 2 * units
+        parts_in[i] = []
+        for step in range(1, parts):
+            columns = range(2 * units * (step - 1), 2 * units * step, cut)
+            parts_in[i].append([over_x(part[:, c:c + cut], step) for c in columns])
         order[:] = [part]
 
     def home_product(i, hop=None):
@@ -389,8 +394,8 @@
 
     def activate(i):
         total = totals[i]
-        for piece in parts_in[i]:
-            total = total + piece.astype(F32)
+        for pieces in parts_in[i]:
+            total = total + jnp.concatenate(pieces, axis=1).astype(F32)
         value = (jax.nn.silu(total[:, :units]) * total[:, units:]).astype(BF16)
         hidden[i] = [value] + [over_x(value, s) for s in range(1, parts)]
         order.append(value)
@@ -439,12 +444,12 @@
         activate(0)
         pick(1)
         order.extend(downs[1:])
+        pick(2)
         home_product(1, 2)
-        pick(2)
+        home_product(2, 3)
         down_product(0)
-        home_product(2, 3)
+        pick(3)
         activate(2)
-        pick(3)
         activate(1)
         down_product(1)
         down_product(2)
@@ -456,9 +461,8 @@
         home_product(5)
         order.append(blocks[2, "b"])
         add_hop(0)
+        down_product(3)
         add_hop(1)
-        order.append(blocks[0, "b"])
-        down_product(3)
         order.append(blocks[2, "b"])
         activate(4)
         down_product(4)

time: 116 us -> 114 us (0.983)
  waiting for transfers between devices: 50.9 us -> 47.8 us
  starting transfers between devices: 24.2 us -> 27.2 us
    ppermute x6, waiting for transfers between devices: 36 us -> 27.6 us  [over_z(): return lax.ppermute(x, 'expert', [(i, (i + 2) % ring) for i in range(ring)])]
    ppermute x8, waiting for transfers between devices: 5.74 us -> 12 us  [over_y(): return lax.ppermute(x, 'expert', [(i, i ^ 1) for i in range(ring)])]
    ppermute x12 -> x13, starting transfers between devices: 11.9 us -> 14.3 us  [over_x(): lax.ppermute(x, 'tensor', [(i, (i + step) % parts) for i in range(parts)])]
    ppermute x12 -> x13, waiting for transfers between devices: 9.09 us -> 8.16 us  [over_x(): lax.ppermute(x, 'tensor', [(i, (i + step) % parts) for i in range(parts)])]
  transfers between devices with their start and end apart: 29 -> 30, of which waited for: 12 -> 12; matrix products, arithmetic and copies ran while one was open for 2% -> 2% of each run, Pallas kernels for 24% -> 24%
where the time goes in v11:
time: 114 us
  waiting for transfers between devices  47.8 us (42%)
  Pallas kernels  30.3 us (27%)
  starting transfers between devices  27.2 us (24%)
  local copies, waits for them, and re-layouts  4.98 us (4%)
  other arithmetic  3.13 us (3%)
    ppermute x6, waiting for transfers between devices, over_z(): return lax.ppermute(x, 'expert', [(i, (i + 2) % ring) for i in range(ring)])  27.6 us
    ppermute x13, starting transfers between devices, over_x(): lax.ppermute(x, 'tensor', [(i, (i + step) % parts) for i in range(parts)])  14.3 us
    ppermute x8, waiting for transfers between devices, over_y(): return lax.ppermute(x, 'expert', [(i, i ^ 1) for i in range(ring)])  12 us
    pallas_call x6, Pallas kernels, pick_rows(): pl.pallas_call(kernel, grid=(1,), out_shape=(*out, *[jax.ShapeDtypeStruct...  11.5 us
    pallas_call x6, Pallas kernels, down_rows(): pl.pallas_call(functools.partial(down_kernel, experts, capacity, groups,...  10.7 us
    ppermute x8, starting transfers between devices, over_y(): return lax.ppermute(x, 'expert', [(i, i ^ 1) for i in range(ring)])  10.3 us
    ppermute x13, waiting for transfers between devices, over_x(): lax.ppermute(x, 'tensor', [(i, (i + step) % parts) for i in range(parts)])  8.16 us
    pallas_call x6, Pallas kernels, home_rows(): pl.pallas_call(functools.partial(home_kernel, capacity, units, groups, le...  7.09 us
  transfers between devices with their start and end apart: 30, of which 12 were waited for; matrix products, arithmetic and copies ran while one was open for 2% of the time, Pallas kernels for 24%

profile of v11, /device:TPU:0, one launch (start us, length us, event | category | flops | bytes accessed | tf_op | source)
XLA Modules:
  0.0 113.7 jit_solution(18285944472029096113)
XLA Ops:
  0.0 0.5 collective-permute-start.5
  0.5 0.7 convert_bitcast_fusion
  1.2 0.7 pad_maximum_fusion.routes_ref
  1.9 1.0 copy-done.5
  2.9 0.4 shard_map.64.refs_0_.refs_2_
  3.3 3.0 %collective-permute-start = (bf16[96,2176]{1,0:T(8,128)(2,1)S(1)}, bf16[96,2176]{1,0:T(8,128)(2,1)S(1)}, u32[]{:S(2)}, u32[]{:S(2)}) collective-permute-start(bf16[96,2176]{1,0:T(8,128)(2,1)S(1)} %shard_map.64.refs_0_.refs_2_), channel_id=1, source_target_pairs={{0,4},{4,0},{8,12},{12,8},{16,20},{20,16},{24,28},{28,24},{1,5},{5... | collective-permute-start | bytes 1253384 | tf_op jit(solution)/shard_map/ppermute | solution.py:315
  6.4 1.6 %collective-permute-start.1 = (bf16[96,2176]{1,0:T(8,128)(2,1)S(1)}, bf16[96,2176]{1,0:T(8,128)(2,1)S(1)}, u32[]{:S(2)}, u32[]{:S(2)}) collective-permute-start(bf16[96,2176]{1,0:T(8,128)(2,1)S(1)} %shard_map.64.refs_0_.refs_2_), channel_id=1, source_target_pairs={{0,8},{4,12},{8,16},{12,20},{16,24},{20,28},{24,0},{28,4},{1,9},{5... | collective-permute-start | bytes 1253384 | tf_op jit(solution)/shard_map/ppermute | solution.py:318
  7.9 1.9 %copy-done = bf16[1,2048,768]{2,1,0:T(8,128)(2,1)S(1)} copy-done((bf16[1,2048,768]{2,1,0:T(8,128)(2,1)S(1)}, bf16[1,2048,768]{2,1,0:T(8,128)(2,1)}, u32[]{:S(2)}) %copy-start) | copy-done | bytes 3145752
  9.8 1.9 %copy-done.2 = bf16[1,2048,768]{2,1,0:T(8,128)(2,1)S(1)} copy-done((bf16[1,2048,768]{2,1,0:T(8,128)(2,1)S(1)}, bf16[1,2048,768]{2,1,0:T(8,128)(2,1)}, u32[]{:S(2)}) %copy-start.2) | copy-done | bytes 3145752
  11.7 1.1 shard_map.65
  12.8 1.6 %collective-permute-start.2 = (bf16[80,768]{1,0:T(8,128)(2,1)S(1)}, bf16[80,768]{1,0:T(8,128)(2,1)S(1)}, u32[]{:S(2)}, u32[]{:S(2)}) collective-permute-start(bf16[80,768]{1,0:T(8,128)(2,1)S(1)} %get-tuple-element.25.refs_2_), channel_id=1, source_target_pairs={{0,2},{2,0},{1,3},{3,1},{4,6},{6,4},{5,7},{7,5},{8,10},{10,8},{9,1... | collective-permute-start | bytes 368648 | tf_op jit(solution)/shard_map/ppermute | solution.py:327
  14.4 1.8 %collective-permute-done.refs_3_.refs_1_ = bf16[96,2176]{1,0:T(8,128)(2,1)S(1)} collective-permute-done((bf16[96,2176]{1,0:T(8,128)(2,1)S(1)}, bf16[96,2176]{1,0:T(8,128)(2,1)S(1)}, u32[]{:S(2)}, u32[]{:S(2)}) %collective-permute-start) | collective-permute-done | bytes 417824 | tf_op jit(solution)/shard_map/ppermute | solution.py:315
  16.2 3.3 %collective-permute-done.1.refs_4_ = bf16[96,2176]{1,0:T(8,128)(2,1)S(1)} collective-permute-done((bf16[96,2176]{1,0:T(8,128)(2,1)S(1)}, bf16[96,2176]{1,0:T(8,128)(2,1)S(1)}, u32[]{:S(2)}, u32[]{:S(2)}) %collective-permute-start.1) | collective-permute-done | bytes 417824 | tf_op jit(solution)/shard_map/ppermute | solution.py:318
  19.5 0.7 shard_map.66
  20.3 2.6 %shard_map.67 = (bf16[368,2048]{1,0:T(8,128)(2,1)S(1)}, bf16[368,768]{1,0:T(8,128)(2,1)S(1)}) custom-call(bf16[96,2176]{1,0:T(8,128)(2,1)S(1)} %shard_map.64.refs_0_.refs_2_, bf16[96,2176]{1,0:T(8,128)(2,1)S(1)} %collective-permute-done.refs_3_.refs_1_, bf16[96,2176]{1,0:T(8,128)(2,1)S(1)} %get-tuple-element.27.refs_2_.refs_4_, ...), custom_call_target="tpu_custom_call" | custom-call | flops 1 | bytes 1 | tf_op jit(solution)/shard_map/pallas_call | solution.py:174
  23.0 0.6 collective-permute-start.4
  23.6 1.5 %collective-permute-start.11 = (bf16[368,384]{1,0:T(8,128)(2,1)S(1)}, bf16[368,384]{1,0:T(8,128)(2,1)S(1)}, u32[]{:S(2)}, u32[]{:S(2)}) collective-permute-start(bf16[368,384]{1,0:T(8,128)(2,1)S(1)} %get-tuple-element.49), channel_id=1, source_target_pairs={{0,2},{2,0},{1,3},{3,1},{4,6},{6,4},{5,7},{7,5},{8,10},{10,8},{9,1... | collective-permute-start | bytes 847880 | tf_op jit(solution)/shard_map/ppermute | solution.py:327
  25.1 0.5 collective-permute-start.10
  25.7 9.3 %collective-permute-done.4.refs_0_.refs_2_ = bf16[96,2176]{1,0:T(8,128)(2,1)S(1)} collective-permute-done((bf16[96,2176]{1,0:T(8,128)(2,1)S(1)}, bf16[96,2176]{1,0:T(8,128)(2,1)S(1)}, u32[]{:S(2)}, u32[]{:S(2)}) %collective-permute-start.4) | collective-permute-done | bytes 417824 | tf_op jit(solution)/shard_map/ppermute | solution.py:315
  35.0 1.5 %collective-permute-start.3 = (bf16[80,384]{1,0:T(8,128)(2,1)S(1)}, bf16[80,384]{1,0:T(8,128)(2,1)S(1)}, u32[]{:S(2)}, u32[]{:S(2)}) collective-permute-start(bf16[80,384]{1,0:T(8,128)(2,1)S(1)} %fusion.5.refs_8_.refs_0_), channel_id=1, source_target_pairs={{0,2},{2,0},{1,3},{3,1},{4,6},{6,4},{5,7},{7,5},{8,10},{10,8},{9,1... | collective-permute-start | bytes 184328 | tf_op jit(solution)/shard_map/ppermute | solution.py:327
  36.5 2.0 %shard_map.68 = (bf16[160,2048]{1,0:T(8,128)(2,1)S(1)}, bf16[160,768]{1,0:T(8,128)(2,1)S(1)}) custom-call(bf16[96,2176]{1,0:T(8,128)(2,1)S(1)} %collective-permute-done.4.refs_0_.refs_2_, bf16[2048,768]{1,0:T(8,128)(2,1)S(1)} %bitcast.12, bf16[2048,768]{1,0:T(8,128)(2,1)S(1)} %bitcast.24, bf16[2048,768]{1,0:T(8,128)(2,1)S(1)} %bitcast.34, ...), custom_call_target="tpu_custom_call" | custom-call | flops 1 | bytes 1 | tf_op jit(solution)/shard_map/pallas_call | solution.py:174
  38.5 1.4 %shard_map.69 = (f32[368,768]{1,0:T(8,128)S(1)}, bf16[96,2176]{1,0:T(8,128)(2,1)S(1)}) custom-call(bf16[368,2048]{1,0:T(8,128)(2,1)S(1)} %get-tuple-element.31.x_ref, bf16[2048,768]{1,0:T(8,128)(2,1)S(1)} %bitcast.35, bf16[2048,768]{1,0:T(8,128)(2,1)S(1)} %bitcast.45, bf16[2048,768]{1,0:T(8,128)(2,1)S(1)} %bitcast.13, ...), custom_call_target="tpu_custom_call", output_to_operand_aliasing={{1}: (6, {})} | custom-call | flops 1 | bytes 1 | tf_op jit(solution)/shard_map/pallas_call | solution.py:199
  39.9 0.2 collective-permute-start.9
  40.1 0.6 collective-permute-start.13
  40.7 1.1 collective-permute-start.14
  41.9 0.2 fusion.refs_0_.refs_9_
  42.1 1.0 collective-permute-start.12
  43.1 9.8 %collective-permute-done.9.refs_5_ = bf16[96,2176]{1,0:T(8,128)(2,1)S(1)} collective-permute-done((bf16[96,2176]{1,0:T(8,128)(2,1)S(1)}, bf16[96,2176]{1,0:T(8,128)(2,1)S(1)}, u32[]{:S(2)}, u32[]{:S(2)}) %collective-permute-start.9) | collective-permute-done | bytes 417824 | tf_op jit(solution)/shard_map/ppermute | solution.py:318
  52.8 1.2 %shard_map.70 = (f32[160,768]{1,0:T(8,128)S(1)}, bf16[96,2176]{1,0:T(8,128)(2,1)S(1)}) custom-call(bf16[160,2048]{1,0:T(8,128)(2,1)S(1)} %get-tuple-element.30.x_ref, bf16[2048,768]{1,0:T(8,128)(2,1)S(1)} %bitcast.14, bf16[2048,768]{1,0:T(8,128)(2,1)S(1)} %bitcast.26, bf16[2048,768]{1,0:T(8,128)(2,1)S(1)} %bitcast.36, ...), custom_call_target="tpu_custom_call", output_to_operand_aliasing={{1}: (6, {})} | custom-call | flops 1 | bytes 1 | tf_op jit(solution)/shard_map/pallas_call | solution.py:199
  54.2 0.6 collective-permute-start.16
  54.8 1.1 collective-permute-start.17
  55.8 1.1 shard_map.71.refs_6_.refs_0_
  56.9 2.0 %shard_map.72 = (bf16[288,2048]{1,0:T(8,128)(2,1)S(1)}, bf16[288,768]{1,0:T(8,128)(2,1)S(1)}) custom-call(bf16[96,2176]{1,0:T(8,128)(2,1)S(1)} %collective-permute-done.13.refs_0_.refs_4_.refs_2_.refs_6_, bf16[96,2176]{1,0:T(8,128)(2,1)S(1)} %get-tuple-element.34.refs_1_.refs_3_, bf16[2048,768]{1,0:T(8,128)(2,1)S(1)} %bitcast.15, ...), custom_call_target="tpu_custom_call" | custom-call | flops 1 | bytes 1 | tf_op jit(solution)/shard_map/pallas_call | solution.py:174
  58.9 1.0 collective-permute-start.18
  59.9 2.6 %shard_map.73.refs_5_ = bf16[288,2048]{1,0:T(8,128)(2,1)S(1)} custom-call(bf16[368,384]{1,0:T(8,128)(2,1)S(1)} %fusion.refs_0_.refs_9_, bf16[368,384]{1,0:T(8,128)(2,1)S(1)} %collective-permute-done.12.refs_1_, bf16[96,2176]{1,0:T(8,128)(2,1)S(1)} %shard_map.64.refs_0_.refs_2_, bf16[96,2176]{1,0:T(8,128)(2,1)S(1)} %collective-permute-done.refs_3_.refs_1_, ...), custom_call_target="tpu_custom_call" | custom-call | flops 1 | bytes 1 | tf_op jit(solution)/shard_map/pallas_call | solution.py:267
  62.6 1.6 %collective-permute-start.15 = (bf16[96,2048]{1,0:T(8,128)(2,1)S(1)}, bf16[96,2048]{1,0:T(8,128)(2,1)S(1)}, u32[]{:S(2)}, u32[]{:S(2)}) collective-permute-start(bf16[96,2048]{1,0:T(8,128)(2,1)S(1)} %get-tuple-element.44), channel_id=1, source_target_pairs={{0,4},{4,0},{8,12},{12,8},{16,20},{20,16},{24,28},{28,24},{1,5},{5... | collective-permute-start | bytes 1179656 | tf_op jit(solution)/shard_map/ppermute | solution.py:315
  64.2 1.6 %shard_map.74.refs_5_ = bf16[96,2048]{1,0:T(8,128)(2,1)S(1)} custom-call(bf16[160,384]{1,0:T(8,128)(2,1)S(1)} %fusion.4.refs_8_.refs_0_, bf16[160,384]{1,0:T(8,128)(2,1)S(1)} %collective-permute-done.17.refs_1_, bf16[96,2176]{1,0:T(8,128)(2,1)S(1)} %collective-permute-done.4.refs_0_.refs_2_, bf16[768,2048]{1,0:T(8,128)(2,1)S(1)} %bitcast.55, ...), custom_call_target="tpu_custom_call" | custom-call | flops 1 | bytes 1 | tf_op jit(solution)/shard_map/pallas_call | solution.py:267
  65.8 1.9 %shard_map.75 = (bf16[160,2048]{1,0:T(8,128)(2,1)S(1)}, bf16[160,768]{1,0:T(8,128)(2,1)S(1)}) custom-call(bf16[96,2176]{1,0:T(8,128)(2,1)S(1)} %collective-permute-done.16.refs_0_.refs_2_, bf16[2048,768]{1,0:T(8,128)(2,1)S(1)} %bitcast.16, bf16[2048,768]{1,0:T(8,128)(2,1)S(1)} %bitcast.28, bf16[2048,768]{1,0:T(8,128)(2,1)S(1)} %bitcast.38, ...), custom_call_target="tpu_custom_call" | custom-call | flops 1 | bytes 1 | tf_op jit(solution)/shard_map/pallas_call | solution.py:174
  67.8 1.1 %shard_map.76.refs_4_ = f32[288,768]{1,0:T(8,128)S(1)} custom-call(bf16[288,2048]{1,0:T(8,128)(2,1)S(1)} %get-tuple-element.39.x_ref, bf16[2048,768]{1,0:T(8,128)(2,1)S(1)} %bitcast.17, bf16[2048,768]{1,0:T(8,128)(2,1)S(1)} %bitcast.29, bf16[2048,768]{1,0:T(8,128)(2,1)S(1)} %bitcast.39, bf16[2048,768]{1,0:T(8,128)(2,1)S(1)} %bitcast.49, ...), custom_call_target="tpu_custom_call" | custom-call | flops 1 | bytes 1 | tf_op jit(solution)/shard_map/pallas_call | solution.py:199
  68.9 0.2 collective-permute-done.18
  69.3 1.1 collective-permute-start.21
  70.5 1.2 %collective-permute-start.23 = (bf16[96,2048]{1,0:T(8,128)(2,1)S(1)}, bf16[96,2048]{1,0:T(8,128)(2,1)S(1)}, u32[]{:S(2)}, u32[]{:S(2)}) collective-permute-start(bf16[96,2048]{1,0:T(8,128)(2,1)S(1)} %shard_map.74.refs_5_), channel_id=1, source_target_pairs={{0,4},{4,0},{8,12},{12,8},{16,20},{20,16},{24,28},{28,24},{1,5},{5... | collective-permute-start | bytes 1179656 | tf_op jit(solution)/shard_map/ppermute | solution.py:315
  71.7 1.2 %shard_map.77.refs_5_ = f32[160,768]{1,0:T(8,128)S(1)} custom-call(bf16[160,2048]{1,0:T(8,128)(2,1)S(1)} %get-tuple-element.38.x_ref, bf16[2048,768]{1,0:T(8,128)(2,1)S(1)} %bitcast.18, bf16[2048,768]{1,0:T(8,128)(2,1)S(1)} %bitcast.30, bf16[2048,768]{1,0:T(8,128)(2,1)S(1)} %bitcast.40, bf16[2048,768]{1,0:T(8,128)(2,1)S(1)} %bitcast.50, ...), custom_call_target="tpu_custom_call" | custom-call | flops 1 | bytes 1 | tf_op jit(solution)/shard_map/pallas_call | solution.py:199
  72.9 1.4 %collective-permute-start.25 = (bf16[160,768]{1,0:T(8,128)(2,1)S(1)}, bf16[160,768]{1,0:T(8,128)(2,1)S(1)}, u32[]{:S(2)}, u32[]{:S(2)}) collective-permute-start(bf16[160,768]{1,0:T(8,128)(2,1)S(1)} %get-tuple-element.40.refs_4_), channel_id=1, source_target_pairs={{0,2},{2,0},{1,3},{3,1},{4,6},{6,4},{5,7},{7,5},{8,10},{10,8},{9,1... | collective-permute-start | bytes 737288 | tf_op jit(solution)/shard_map/ppermute | solution.py:327
  74.3 2.0 %shard_map.78 = (bf16[160,2048]{1,0:T(8,128)(2,1)S(1)}, bf16[160,768]{1,0:T(8,128)(2,1)S(1)}) custom-call(bf16[96,2176]{1,0:T(8,128)(2,1)S(1)} %get-tuple-element.37.refs_0_.refs_2_, bf16[2048,768]{1,0:T(8,128)(2,1)S(1)} %bitcast.19, bf16[2048,768]{1,0:T(8,128)(2,1)S(1)} %bitcast.31, bf16[2048,768]{1,0:T(8,128)(2,1)S(1)} %bitcast.41, ...), custom_call_target="tpu_custom_call" | custom-call | flops 1 | bytes 1 | tf_op jit(solution)/shard_map/pallas_call | solution.py:174
  76.2 0.8 collective-permute-start.19
  77.0 1.4 %shard_map.79.refs_3_ = f32[160,768]{1,0:T(8,128)S(1)} custom-call(bf16[160,2048]{1,0:T(8,128)(2,1)S(1)} %get-tuple-element.41.x_ref, bf16[2048,768]{1,0:T(8,128)(2,1)S(1)} %bitcast.20, bf16[2048,768]{1,0:T(8,128)(2,1)S(1)} %bitcast.32, bf16[2048,768]{1,0:T(8,128)(2,1)S(1)} %bitcast.42, bf16[2048,768]{1,0:T(8,128)(2,1)S(1)} %bitcast.52, ...), custom_call_target="tpu_custom_call" | custom-call | flops 1 | bytes 1 | tf_op jit(solution)/shard_map/pallas_call | solution.py:199
  78.6 2.2 %shard_map.81.refs_2_ = bf16[192,2048]{1,0:T(8,128)(2,1)S(1)} custom-call(bf16[288,384]{1,0:T(8,128)(2,1)S(1)} %fusion.1.refs_6_.refs_0_, bf16[288,384]{1,0:T(8,128)(2,1)S(1)} %collective-permute-done.21.refs_1_, bf16[96,2176]{1,0:T(8,128)(2,1)S(1)} %collective-permute-done.13.refs_0_.refs_4_.refs_2_.refs_6_, ...), custom_call_target="tpu_custom_call" | custom-call | flops 1 | bytes 1 | tf_op jit(solution)/shard_map/pallas_call | solution.py:267
  80.8 0.9 collective-permute-start.22
  81.7 0.9 collective-permute-done.23.refs_1_
  82.9 1.3 %collective-permute-start.26 = (bf16[160,384]{1,0:T(8,128)(2,1)S(1)}, bf16[160,384]{1,0:T(8,128)(2,1)S(1)}, u32[]{:S(2)}, u32[]{:S(2)}) collective-permute-start(bf16[160,384]{1,0:T(8,128)(2,1)S(1)} %fusion.2.refs_0_.refs_7_), channel_id=1, source_target_pairs={{0,2},{2,0},{1,3},{3,1},{4,6},{6,4},{5,7},{7,5},{8,10},{10,8},{9,1... | collective-permute-start | bytes 368648 | tf_op jit(solution)/shard_map/ppermute | solution.py:327
  84.3 2.2 %collective-permute-done.19 = bf16[160,768]{1,0:T(8,128)(2,1)S(1)} collective-permute-done((bf16[160,768]{1,0:T(8,128)(2,1)S(1)}, bf16[160,768]{1,0:T(8,128)(2,1)S(1)}, u32[]{:S(2)}, u32[]{:S(2)}) %collective-permute-start.19) | collective-permute-done | bytes 245792 | tf_op jit(solution)/shard_map/ppermute | solution.py:327
  86.6 1.3 %collective-permute-done.26.refs_1_ = bf16[160,384]{1,0:T(8,128)(2,1)S(1)} collective-permute-done((bf16[160,384]{1,0:T(8,128)(2,1)S(1)}, bf16[160,384]{1,0:T(8,128)(2,1)S(1)}, u32[]{:S(2)}, u32[]{:S(2)}) %collective-permute-start.26) | collective-permute-done | bytes 122912 | tf_op jit(solution)/shard_map/ppermute | solution.py:327
  87.9 1.6 %shard_map.83.refs_3_ = bf16[96,2048]{1,0:T(8,128)(2,1)S(1)} custom-call(bf16[160,384]{1,0:T(8,128)(2,1)S(1)} %fusion.2.refs_0_.refs_7_, bf16[160,384]{1,0:T(8,128)(2,1)S(1)} %collective-permute-done.26.refs_1_, bf16[96,2176]{1,0:T(8,128)(2,1)S(1)} %collective-permute-done.16.refs_0_.refs_2_, bf16[768,2048]{1,0:T(8,128)(2,1)S(1)} %bitcast.57, ...), custom_call_target="tpu_custom_call" | custom-call | flops 1 | bytes 1 | tf_op jit(solution)/shard_map/pallas_call | solution.py:267
  89.5 1.9 %collective-permute-start.27 = (bf16[96,2048]{1,0:T(8,128)(2,1)S(1)}, bf16[96,2048]{1,0:T(8,128)(2,1)S(1)}, u32[]{:S(2)}, u32[]{:S(2)}) collective-permute-start(bf16[96,2048]{1,0:T(8,128)(2,1)S(1)} %shard_map.83.refs_3_), channel_id=1, source_target_pairs={{0,4},{4,0},{8,12},{12,8},{16,20},{20,16},{24,28},{28,24},{1,5},{5... | collective-permute-start | bytes 1179656 | tf_op jit(solution)/shard_map/ppermute | solution.py:315
  91.4 1.0 collective-permute-done.24.refs_2_
  92.3 0.1 shard_map.84.refs_5_
  92.5 0.5 collective-permute-start.20
  93.0 4.5 %collective-permute-done.20.refs_1_ = bf16[160,384]{1,0:T(8,128)(2,1)S(1)} collective-permute-done((bf16[160,384]{1,0:T(8,128)(2,1)S(1)}, bf16[160,384]{1,0:T(8,128)(2,1)S(1)}, u32[]{:S(2)}, u32[]{:S(2)}) %collective-permute-start.20) | collective-permute-done | bytes 122912 | tf_op jit(solution)/shard_map/ppermute | solution.py:327
  97.5 1.6 %shard_map.85.refs_0_.refs_3_ = bf16[96,2048]{1,0:T(8,128)(2,1)S(1)} custom-call(bf16[160,384]{1,0:T(8,128)(2,1)S(1)} %fusion.3.refs_4_.refs_0_, bf16[160,384]{1,0:T(8,128)(2,1)S(1)} %collective-permute-done.20.refs_1_, bf16[96,2176]{1,0:T(8,128)(2,1)S(1)} %get-tuple-element.37.refs_0_.refs_2_, bf16[768,2048]{1,0:T(8,128)(2,1)S(1)} %bitcast.58, ...), custom_call_target="tpu_custom_call" | custom-call | flops 1 | bytes 1 | tf_op jit(solution)/shard_map/pallas_call | solution.py:267
  99.1 4.0 %collective-permute-done.28.refs_2_ = bf16[96,2048]{1,0:T(8,128)(2,1)S(1)} collective-permute-done((bf16[96,2048]{1,0:T(8,128)(2,1)S(1)}, bf16[96,2048]{1,0:T(8,128)(2,1)S(1)}, u32[]{:S(2)}, u32[]{:S(2)}) %collective-permute-start.28) | collective-permute-done | bytes 393248 | tf_op jit(solution)/shard_map/ppermute | solution.py:318
  103.1 0.1 shard_map.86
  103.3 9.6 %collective-permute-done.29 = bf16[96,2048]{1,0:T(8,128)(2,1)S(1)} collective-permute-done((bf16[96,2048]{1,0:T(8,128)(2,1)S(1)}, bf16[96,2048]{1,0:T(8,128)(2,1)S(1)}, u32[]{:S(2)}, u32[]{:S(2)}) %collective-permute-start.29) | collective-permute-done | bytes 393248 | tf_op jit(solution)/shard_map/ppermute | solution.py:318
  112.9 0.8 add_convert_fusion
  (49 shorter events, 1.5 us)
Async XLA Ops:
  0.0 20.3 %collective-permute-start.5 = (bf16[1,2048,768]{2,1,0:T(8,128)(2,1)}, bf16[1,2048,768]{2,1,0:T(8,128)(2,1)S(1)}, u32[]{:S(2)}, u32[]{:S(2)}) collective-permute-start(bf16[1,2048,768]{2,1,0:T(8,128)(2,1)} %param.9), channel_id=1, source_target_pairs={{0,1},{1,0},{2,3},{3,2},{4,5},{5,4},{6,7},{7,6},{8,9},{9,8},{10,11... | collective-permute-start | bytes 9437192 | tf_op jit(solution)/shard_map/ppermute | solution.py:324
  0.5 19.8 %collective-permute-start.6 = (bf16[1,2048,768]{2,1,0:T(8,128)(2,1)}, bf16[1,2048,768]{2,1,0:T(8,128)(2,1)S(1)}, u32[]{:S(2)}, u32[]{:S(2)}) collective-permute-start(bf16[1,2048,768]{2,1,0:T(8,128)(2,1)} %param.10), channel_id=1, source_target_pairs={{0,1},{1,0},{2,3},{3,2},{4,5},{5,4},{6,7},{7,6},{8,9},{9,8},{10,11... | collective-permute-start | bytes 9437192 | tf_op jit(solution)/shard_map/ppermute | solution.py:324
  1.9 1.0 copy-start.5
  3.3 12.8 %collective-permute-start = (bf16[96,2176]{1,0:T(8,128)(2,1)S(1)}, bf16[96,2176]{1,0:T(8,128)(2,1)S(1)}, u32[]{:S(2)}, u32[]{:S(2)}) collective-permute-start(bf16[96,2176]{1,0:T(8,128)(2,1)S(1)} %shard_map.64.refs_0_.refs_2_), channel_id=1, source_target_pairs={{0,4},{4,0},{8,12},{12,8},{16,20},{20,16},{24,28},{28,24},{1,5},{5... | collective-permute-start | bytes 1253384 | tf_op jit(solution)/shard_map/ppermute | solution.py:315
  6.4 13.1 %collective-permute-start.1 = (bf16[96,2176]{1,0:T(8,128)(2,1)S(1)}, bf16[96,2176]{1,0:T(8,128)(2,1)S(1)}, u32[]{:S(2)}, u32[]{:S(2)}) collective-permute-start(bf16[96,2176]{1,0:T(8,128)(2,1)S(1)} %shard_map.64.refs_0_.refs_2_), channel_id=1, source_target_pairs={{0,8},{4,12},{8,16},{12,20},{16,24},{20,28},{24,0},{28,4},{1,9},{5... | collective-permute-start | bytes 1253384 | tf_op jit(solution)/shard_map/ppermute | solution.py:318
  7.9 1.9 %copy-start = (bf16[1,2048,768]{2,1,0:T(8,128)(2,1)S(1)}, bf16[1,2048,768]{2,1,0:T(8,128)(2,1)}, u32[]{:S(2)}) copy-start(bf16[1,2048,768]{2,1,0:T(8,128)(2,1)} %param.9) | copy-start | bytes 9437188
  9.8 1.9 %copy-start.2 = (bf16[1,2048,768]{2,1,0:T(8,128)(2,1)S(1)}, bf16[1,2048,768]{2,1,0:T(8,128)(2,1)}, u32[]{:S(2)}) copy-start(bf16[1,2048,768]{2,1,0:T(8,128)(2,1)} %param.10) | copy-start | bytes 9437188
  11.7 7.8 %copy-start.1 = (bf16[1,2048,768]{2,1,0:T(8,128)(2,1)S(1)}, bf16[1,2048,768]{2,1,0:T(8,128)(2,1)}, u32[]{:S(2)}) copy-start(bf16[1,2048,768]{2,1,0:T(8,128)(2,1)} %param.9) | copy-start | bytes 9437188
  11.7 7.8 %copy-start.3 = (bf16[1,2048,768]{2,1,0:T(8,128)(2,1)S(1)}, bf16[1,2048,768]{2,1,0:T(8,128)(2,1)}, u32[]{:S(2)}) copy-start(bf16[1,2048,768]{2,1,0:T(8,128)(2,1)} %param.10) | copy-start | bytes 9437188
  12.8 7.4 %collective-permute-start.2 = (bf16[80,768]{1,0:T(8,128)(2,1)S(1)}, bf16[80,768]{1,0:T(8,128)(2,1)S(1)}, u32[]{:S(2)}, u32[]{:S(2)}) collective-permute-start(bf16[80,768]{1,0:T(8,128)(2,1)S(1)} %get-tuple-element.25.refs_2_), channel_id=1, source_target_pairs={{0,2},{2,0},{1,3},{3,1},{4,6},{6,4},{5,7},{7,5},{8,10},{10,8},{9,1... | collective-permute-start | bytes 368648 | tf_op jit(solution)/shard_map/ppermute | solution.py:327
  20.3 2.6 %copy-start.4 = (bf16[1,768,2048]{2,1,0:T(8,128)(2,1)S(1)}, bf16[1,768,2048]{2,1,0:T(8,128)(2,1)}, u32[]{:S(2)}) copy-start(bf16[1,768,2048]{2,1,0:T(8,128)(2,1)} %param.11) | copy-start | bytes 9437188
  22.9 13.6 %collective-permute-start.7 = (bf16[1,768,2048]{2,1,0:T(8,128)(2,1)S(1)}, bf16[1,768,2048]{2,1,0:T(8,128)(2,1)S(1)}, u32[]{:S(2)}, u32[]{:S(2)}) collective-permute-start(bf16[1,768,2048]{2,1,0:T(8,128)(2,1)S(1)} %copy-done.4), channel_id=1, source_target_pairs={{0,1},{1,0},{2,3},{3,2},{4,5},{5,4},{6,7},{7,6},{8,9},{9,8},{10,11... | collective-permute-start | bytes 9437192 | tf_op jit(solution)/shard_map/ppermute | solution.py:324
  23.0 12.1 %collective-permute-start.4 = (bf16[96,2176]{1,0:T(8,128)(2,1)S(1)}, bf16[96,2176]{1,0:T(8,128)(2,1)S(1)}, u32[]{:S(2)}, u32[]{:S(2)}) collective-permute-start(bf16[96,2176]{1,0:T(8,128)(2,1)S(1)} %get-tuple-element.27.refs_2_.refs_4_), channel_id=1, source_target_pairs={{0,4},{4,0},{8,12},{12,8},{16,20},{20,16},{24,28},{28,24},{1,5},{5... | collective-permute-start | bytes 1253384 | tf_op jit(solution)/shard_map/ppermute | solution.py:315
  23.5 14.9 %collective-permute-start.8 = (bf16[96,2176]{1,0:T(8,128)(2,1)S(1)}, bf16[96,2176]{1,0:T(8,128)(2,1)S(1)}, u32[]{:S(2)}, u32[]{:S(2)}) collective-permute-start(bf16[96,2176]{1,0:T(8,128)(2,1)S(1)} %get-tuple-element.27.refs_2_.refs_4_), channel_id=1, source_target_pairs={{0,8},{4,12},{8,16},{12,20},{16,24},{20,28},{24,0},{28,4},{1,9},{5... | collective-permute-start | bytes 1253384 | tf_op jit(solution)/shard_map/ppermute | solution.py:318
  23.6 17.1 %collective-permute-start.11 = (bf16[368,384]{1,0:T(8,128)(2,1)S(1)}, bf16[368,384]{1,0:T(8,128)(2,1)S(1)}, u32[]{:S(2)}, u32[]{:S(2)}) collective-permute-start(bf16[368,384]{1,0:T(8,128)(2,1)S(1)} %get-tuple-element.49), channel_id=1, source_target_pairs={{0,2},{2,0},{1,3},{3,1},{4,6},{6,4},{5,7},{7,5},{8,10},{10,8},{9,1... | collective-permute-start | bytes 847880 | tf_op jit(solution)/shard_map/ppermute | solution.py:327
  25.1 16.6 %collective-permute-start.10 = (bf16[368,384]{1,0:T(8,128)(2,1)S(1)}, bf16[368,384]{1,0:T(8,128)(2,1)S(1)}, u32[]{:S(2)}, u32[]{:S(2)}) collective-permute-start(bf16[368,384]{1,0:T(8,128)(2,1)S(1)} %get-tuple-element.48), channel_id=1, source_target_pairs={{0,2},{2,0},{1,3},{3,1},{4,6},{6,4},{5,7},{7,5},{8,10},{10,8},{9,1... | collective-permute-start | bytes 847880 | tf_op jit(solution)/shard_map/ppermute | solution.py:327
  35.0 20.8 %collective-permute-start.3 = (bf16[80,384]{1,0:T(8,128)(2,1)S(1)}, bf16[80,384]{1,0:T(8,128)(2,1)S(1)}, u32[]{:S(2)}, u32[]{:S(2)}) collective-permute-start(bf16[80,384]{1,0:T(8,128)(2,1)S(1)} %fusion.5.refs_8_.refs_0_), channel_id=1, source_target_pairs={{0,2},{2,0},{1,3},{3,1},{4,6},{6,4},{5,7},{7,5},{8,10},{10,8},{9,1... | collective-permute-start | bytes 184328 | tf_op jit(solution)/shard_map/ppermute | solution.py:327
  39.9 13.0 %collective-permute-start.9 = (bf16[96,2176]{1,0:T(8,128)(2,1)S(1)}, bf16[96,2176]{1,0:T(8,128)(2,1)S(1)}, u32[]{:S(2)}, u32[]{:S(2)}) collective-permute-start(bf16[96,2176]{1,0:T(8,128)(2,1)S(1)} %get-tuple-element.34.refs_1_.refs_3_), channel_id=1, source_target_pairs={{0,8},{4,12},{8,16},{12,20},{16,24},{20,28},{24,0},{28,4},{1,9},{5... | collective-permute-start | bytes 1253384 | tf_op jit(solution)/shard_map/ppermute | solution.py:318
  40.1 16.8 %collective-permute-start.13 = (bf16[96,2176]{1,0:T(8,128)(2,1)S(1)}, bf16[96,2176]{1,0:T(8,128)(2,1)S(1)}, u32[]{:S(2)}, u32[]{:S(2)}) collective-permute-start(bf16[96,2176]{1,0:T(8,128)(2,1)S(1)} %get-tuple-element.34.refs_1_.refs_3_), channel_id=1, source_target_pairs={{0,4},{4,0},{8,12},{12,8},{16,20},{20,16},{24,28},{28,24},{1,5},{5... | collective-permute-start | bytes 1253384 | tf_op jit(solution)/shard_map/ppermute | solution.py:315
  40.7 13.4 %collective-permute-start.14 = (bf16[160,768]{1,0:T(8,128)(2,1)S(1)}, bf16[160,768]{1,0:T(8,128)(2,1)S(1)}, u32[]{:S(2)}, u32[]{:S(2)}) collective-permute-start(bf16[160,768]{1,0:T(8,128)(2,1)S(1)} %get-tuple-element.32.refs_4_), channel_id=1, source_target_pairs={{0,2},{2,0},{1,3},{3,1},{4,6},{6,4},{5,7},{7,5},{8,10},{10,8},{9,1... | collective-permute-start | bytes 737288 | tf_op jit(solution)/shard_map/ppermute | solution.py:327
  42.1 17.9 %collective-permute-start.12 = (bf16[368,384]{1,0:T(8,128)(2,1)S(1)}, bf16[368,384]{1,0:T(8,128)(2,1)S(1)}, u32[]{:S(2)}, u32[]{:S(2)}) collective-permute-start(bf16[368,384]{1,0:T(8,128)(2,1)S(1)} %fusion.refs_0_.refs_9_), channel_id=1, source_target_pairs={{0,2},{2,0},{1,3},{3,1},{4,6},{6,4},{5,7},{7,5},{8,10},{10,8},{9,1... | collective-permute-start | bytes 847880 | tf_op jit(solution)/shard_map/ppermute | solution.py:327
  54.2 11.6 %collective-permute-start.16 = (bf16[96,2176]{1,0:T(8,128)(2,1)S(1)}, bf16[96,2176]{1,0:T(8,128)(2,1)S(1)}, u32[]{:S(2)}, u32[]{:S(2)}) collective-permute-start(bf16[96,2176]{1,0:T(8,128)(2,1)S(1)} %get-tuple-element.37.refs_0_.refs_2_), channel_id=1, source_target_pairs={{0,4},{4,0},{8,12},{12,8},{16,20},{20,16},{24,28},{28,24},{1,5},{5... | collective-permute-start | bytes 1253384 | tf_op jit(solution)/shard_map/ppermute | solution.py:315
  54.8 9.4 %collective-permute-start.17 = (bf16[160,384]{1,0:T(8,128)(2,1)S(1)}, bf16[160,384]{1,0:T(8,128)(2,1)S(1)}, u32[]{:S(2)}, u32[]{:S(2)}) collective-permute-start(bf16[160,384]{1,0:T(8,128)(2,1)S(1)} %fusion.4.refs_8_.refs_0_), channel_id=1, source_target_pairs={{0,2},{2,0},{1,3},{3,1},{4,6},{6,4},{5,7},{7,5},{8,10},{10,8},{9,1... | collective-permute-start | bytes 368648 | tf_op jit(solution)/shard_map/ppermute | solution.py:327
  58.9 10.2 %collective-permute-start.18 = (bf16[288,768]{1,0:T(8,128)(2,1)S(1)}, bf16[288,768]{1,0:T(8,128)(2,1)S(1)}, u32[]{:S(2)}, u32[]{:S(2)}) collective-permute-start(bf16[288,768]{1,0:T(8,128)(2,1)S(1)} %get-tuple-element.36.refs_7_), channel_id=1, source_target_pairs={{0,2},{2,0},{1,3},{3,1},{4,6},{6,4},{5,7},{7,5},{8,10},{10,8},{9,1... | collective-permute-start | bytes 1327112 | tf_op jit(solution)/shard_map/ppermute | solution.py:327
  62.6 15.8 %collective-permute-start.15 = (bf16[96,2048]{1,0:T(8,128)(2,1)S(1)}, bf16[96,2048]{1,0:T(8,128)(2,1)S(1)}, u32[]{:S(2)}, u32[]{:S(2)}) collective-permute-start(bf16[96,2048]{1,0:T(8,128)(2,1)S(1)} %get-tuple-element.44), channel_id=1, source_target_pairs={{0,4},{4,0},{8,12},{12,8},{16,20},{20,16},{24,28},{28,24},{1,5},{5... | collective-permute-start | bytes 1179656 | tf_op jit(solution)/shard_map/ppermute | solution.py:315
  69.3 9.2 %collective-permute-start.21 = (bf16[288,384]{1,0:T(8,128)(2,1)S(1)}, bf16[288,384]{1,0:T(8,128)(2,1)S(1)}, u32[]{:S(2)}, u32[]{:S(2)}) collective-permute-start(bf16[288,384]{1,0:T(8,128)(2,1)S(1)} %fusion.1.refs_6_.refs_0_), channel_id=1, source_target_pairs={{0,2},{2,0},{1,3},{3,1},{4,6},{6,4},{5,7},{7,5},{8,10},{10,8},{9,1... | collective-permute-start | bytes 663560 | tf_op jit(solution)/shard_map/ppermute | solution.py:327
  70.5 12.1 %collective-permute-start.23 = (bf16[96,2048]{1,0:T(8,128)(2,1)S(1)}, bf16[96,2048]{1,0:T(8,128)(2,1)S(1)}, u32[]{:S(2)}, u32[]{:S(2)}) collective-permute-start(bf16[96,2048]{1,0:T(8,128)(2,1)S(1)} %shard_map.74.refs_5_), channel_id=1, source_target_pairs={{0,4},{4,0},{8,12},{12,8},{16,20},{20,16},{24,28},{28,24},{1,5},{5... | collective-permute-start | bytes 1179656 | tf_op jit(solution)/shard_map/ppermute | solution.py:315
  72.9 9.8 %collective-permute-start.25 = (bf16[160,768]{1,0:T(8,128)(2,1)S(1)}, bf16[160,768]{1,0:T(8,128)(2,1)S(1)}, u32[]{:S(2)}, u32[]{:S(2)}) collective-permute-start(bf16[160,768]{1,0:T(8,128)(2,1)S(1)} %get-tuple-element.40.refs_4_), channel_id=1, source_target_pairs={{0,2},{2,0},{1,3},{3,1},{4,6},{6,4},{5,7},{7,5},{8,10},{10,8},{9,1... | collective-permute-start | bytes 737288 | tf_op jit(solution)/shard_map/ppermute | solution.py:327
  76.2 10.2 %collective-permute-start.19 = (bf16[160,768]{1,0:T(8,128)(2,1)S(1)}, bf16[160,768]{1,0:T(8,128)(2,1)S(1)}, u32[]{:S(2)}, u32[]{:S(2)}) collective-permute-start(bf16[160,768]{1,0:T(8,128)(2,1)S(1)} %get-tuple-element.42.refs_4_), channel_id=1, source_target_pairs={{0,2},{2,0},{1,3},{3,1},{4,6},{6,4},{5,7},{7,5},{8,10},{10,8},{9,1... | collective-permute-start | bytes 737288 | tf_op jit(solution)/shard_map/ppermute | solution.py:327
  80.8 10.5 %collective-permute-start.22 = (bf16[96,2048]{1,0:T(8,128)(2,1)S(1)}, bf16[96,2048]{1,0:T(8,128)(2,1)S(1)}, u32[]{:S(2)}, u32[]{:S(2)}) collective-permute-start(bf16[96,2048]{1,0:T(8,128)(2,1)S(1)} %get-tuple-element.46), channel_id=1, source_target_pairs={{0,4},{4,0},{8,12},{12,8},{16,20},{20,16},{24,28},{28,24},{1,5},{5... | collective-permute-start | bytes 1179656 | tf_op jit(solution)/shard_map/ppermute | solution.py:315
  82.7 9.6 %collective-permute-start.24 = (bf16[96,2048]{1,0:T(8,128)(2,1)S(1)}, bf16[96,2048]{1,0:T(8,128)(2,1)S(1)}, u32[]{:S(2)}, u32[]{:S(2)}) collective-permute-start(bf16[96,2048]{1,0:T(8,128)(2,1)S(1)} %shard_map.82.refs_5_), channel_id=1, source_target_pairs={{0,8},{4,12},{8,16},{12,20},{16,24},{20,28},{24,0},{28,4},{1,9},{5... | collective-permute-start | bytes 1179656 | tf_op jit(solution)/shard_map/ppermute | solution.py:318
  82.9 4.9 %collective-permute-start.26 = (bf16[160,384]{1,0:T(8,128)(2,1)S(1)}, bf16[160,384]{1,0:T(8,128)(2,1)S(1)}, u32[]{:S(2)}, u32[]{:S(2)}) collective-permute-start(bf16[160,384]{1,0:T(8,128)(2,1)S(1)} %fusion.2.refs_0_.refs_7_), channel_id=1, source_target_pairs={{0,2},{2,0},{1,3},{3,1},{4,6},{6,4},{5,7},{7,5},{8,10},{10,8},{9,1... | collective-permute-start | bytes 368648 | tf_op jit(solution)/shard_map/ppermute | solution.py:327
  89.5 9.6 %collective-permute-start.27 = (bf16[96,2048]{1,0:T(8,128)(2,1)S(1)}, bf16[96,2048]{1,0:T(8,128)(2,1)S(1)}, u32[]{:S(2)}, u32[]{:S(2)}) collective-permute-start(bf16[96,2048]{1,0:T(8,128)(2,1)S(1)} %shard_map.83.refs_3_), channel_id=1, source_target_pairs={{0,4},{4,0},{8,12},{12,8},{16,20},{20,16},{24,28},{28,24},{1,5},{5... | collective-permute-start | bytes 1179656 | tf_op jit(solution)/shard_map/ppermute | solution.py:315
  92.5 10.6 %collective-permute-start.28 = (bf16[96,2048]{1,0:T(8,128)(2,1)S(1)}, bf16[96,2048]{1,0:T(8,128)(2,1)S(1)}, u32[]{:S(2)}, u32[]{:S(2)}) collective-permute-start(bf16[96,2048]{1,0:T(8,128)(2,1)S(1)} %shard_map.84.refs_5_), channel_id=1, source_target_pairs={{0,8},{4,12},{8,16},{12,20},{16,24},{20,28},{24,0},{28,4},{1,9},{5... | collective-permute-start | bytes 1179656 | tf_op jit(solution)/shard_map/ppermute | solution.py:318
  92.5 4.9 %collective-permute-start.20 = (bf16[160,384]{1,0:T(8,128)(2,1)S(1)}, bf16[160,384]{1,0:T(8,128)(2,1)S(1)}, u32[]{:S(2)}, u32[]{:S(2)}) collective-permute-start(bf16[160,384]{1,0:T(8,128)(2,1)S(1)} %fusion.3.refs_4_.refs_0_), channel_id=1, source_target_pairs={{0,2},{2,0},{1,3},{3,1},{4,6},{6,4},{5,7},{7,5},{8,10},{10,8},{9,1... | collective-permute-start | bytes 368648 | tf_op jit(solution)/shard_map/ppermute | solution.py:327
  103.2 9.6 %collective-permute-start.29 = (bf16[96,2048]{1,0:T(8,128)(2,1)S(1)}, bf16[96,2048]{1,0:T(8,128)(2,1)S(1)}, u32[]{:S(2)}, u32[]{:S(2)}) collective-permute-start(bf16[96,2048]{1,0:T(8,128)(2,1)S(1)} %shard_map.86), channel_id=1, source_target_pairs={{0,8},{4,12},{8,16},{12,20},{16,24},{20,28},{24,0},{28,4},{1,9},{5... | collective-permute-start | bytes 1179656 | tf_op jit(solution)/shard_map/ppermute | solution.py:318

commit v12 on v11

--- a/solution.py
+++ b/solution.py
@@ -95,12 +95,17 @@
     return jnp.where(live, before.astype(jnp.int32) + number * capacity, -1), weight
 
 
+def tight(groups, capacity):
+    return len(groups) == 2 and capacity % 8 == 0 and all(len(members) == 1 for _, members in groups)
+
+
 def layout(groups, capacity):
-    offsets, total = [], 0
+    if tight(groups, capacity):
+        return [0, capacity, -(-2 * capacity // 16) * 16]
+    offsets = [0]
     for _, members in groups:
-        offsets.append(total)
-        total += -(-len(members) * capacity // 16) * 16
-    return offsets + [total]
+        offsets.append(offsets[-1] + -(-len(members) * capacity // 16) * 16)
+    return offsets
 
 
 def multiply(x_ref, rows, weights, start, units, out_ref):
@@ -126,6 +131,29 @@
         out_ref[rows, units + full:] = y[:, units - full:]
 
 
+def multiply_both(x_ref, bound, first, second, start, units, out_ref):
+    x = x_ref[...]
+    for (column, count, v), (_, _, w) in zip(tiles(first, start, units), tiles(second, start, units)):
+        upper = lax.broadcasted_iota(jnp.int32, (x.shape[0], count), 0) < bound
+        a = jnp.dot(x, v(), preferred_element_type=F32)
+        b = jnp.dot(x, w(), preferred_element_type=F32)
+        out_ref[:, column:column + count] = jnp.where(upper, a, b).astype(out_ref.dtype)
+
+
+def tiles(weights, start, units):
+    if start is None:
+        ref = weights[0]
+        step = tile(ref.shape[1], (256, 384))
+        return [(c, step, lambda c=c: ref[:, c:c + step]) for c in range(0, ref.shape[1], step)]
+    parts = []
+    step = tile(units, (384, 256, LANES))
+    for i, ref in enumerate(weights):
+        for c in range(0, units, step):
+            span = pl.ds(pl.multiple_of(start + c, LANES), step)
+            parts.append((i * units + c, step, lambda ref=ref, span=span: ref[:, span]))
+    return parts
+
+
 def position(units):
     core, rank, parts = lax.axis_index("dp"), lax.axis_index("tensor"), lax.axis_size("tensor")
     first = lax.axis_index("expert") * 2
@@ -145,6 +173,20 @@
     mine_and_other, start, _, _ = position(units)
     offsets = layout(groups, capacity)
     step = tile(width, (512, 256))
+    if tight(groups, capacity):
+        taken = offsets[-1]
+        place = lax.broadcasted_iota(jnp.int32, (taken, rows), 0)
+        pick = jnp.zeros((taken, rows), F32)
+        for g, (expert, _) in enumerate(groups):
+            slot = slot_row(blocks[0][:, width:], mine_and_other[expert], experts, rows, capacity)
+            pick = pick + jnp.where((place == slot + offsets[g]) & (slot >= 0), 1.0, 0.0)
+        pick = pick.astype(BF16)
+        for column in range(0, width, step):
+            value = jnp.dot(pick, blocks[0][:, column:column + step], preferred_element_type=F32)
+            chosen_ref[:, column:column + step] = value.astype(BF16)
+        first, second = weights[:kinds], weights[kinds:2 * kinds]
+        multiply_both(chosen_ref, offsets[1], first, second, start if split else None, units, part_ref)
+        return
     for g, (expert, members) in enumerate(groups):
         tails = jnp.concatenate([blocks[m][:, width:] for m in members], axis=0)
         slot = slot_row(tails, mine_and_other[expert], experts, rows, capacity)
@@ -187,6 +229,10 @@
     _, _, start, _ = position(units)
     out_ref = refs[-1 - passed]
     offsets = layout(groups, capacity)
+    if tight(groups, capacity):
+        first, second = refs[:kinds], refs[kinds:2 * kinds]
+        multiply_both(x_ref, offsets[1], first, second, start if split else None, units, out_ref)
+        return
     for g in range(len(groups)):
         mine = refs[kinds * g:kinds * (g + 1)]
         multiply(x_ref, slice(offsets[g], offsets[g + 1]), mine, start if split else None, units, out_ref)
@@ -225,10 +271,11 @@
         tails = jnp.concatenate([tail_refs[m][...] for m in members], axis=0)
         slot, weight = slot_column(tails, mine_and_other[expert], experts, rows, capacity)
         shares.append(jnp.broadcast_to(weight, (len(members) * rows, step)))
-        place = lax.broadcasted_iota(jnp.int32, (len(members) * rows, offsets[g + 1] - offsets[g]), 1)
-        spread = jnp.where(place == slot, 1.0, 0.0).astype(BF16)
+        low, high = (0, offsets[-1]) if tight(groups, capacity) else (offsets[g], offsets[g + 1])
+        place = lax.broadcasted_iota(jnp.int32, (len(members) * rows, high - low), 1) - (offsets[g] - low)
+        spread = jnp.where((place == slot) & (slot >= 0), 1.0, 0.0).astype(BF16)
         for s, ref in enumerate(hiddens):
-            value = jnp.dot(spread, ref[offsets[g]:offsets[g + 1], :], preferred_element_type=F32).astype(BF16)
+            value = jnp.dot(spread, ref[low:high, :], preferred_element_type=F32).astype(BF16)
             if wide:
                 scratch[g][:, pl.ds(pl.multiple_of(starts[s], LANES), units)] = value
             else:
@@ -449,8 +496,8 @@
         home_product(2, 3)
         down_product(0)
         pick(3)
+        activate(1)
         activate(2)
-        activate(1)
         down_product(1)
         down_product(2)
         pick(4)
@@ -458,16 +505,15 @@
         home_product(4)
         activate(3)
         pick(5)
+        add_hop(0)
+        order.append(blocks[2, "b"])
         home_product(5)
-        order.append(blocks[2, "b"])
-        add_hop(0)
         down_product(3)
+        activate(4)
         add_hop(1)
-        order.append(blocks[2, "b"])
-        activate(4)
         down_product(4)
+        add_hop(2)
         activate(5)
-        add_hop(2)
         down_product(5)
         add_hop(3)
     else:

time: 114 us -> 114 us (level)
  Pallas kernels: 30.3 us -> 31.6 us
    ppermute x13, waiting for transfers between devices: 8.16 us -> 10.3 us  [over_x(): lax.ppermute(x, 'tensor', [(i, (i + step) % parts) for i in range(parts)])]
    ppermute x6, waiting for transfers between devices: 27.6 us -> 25.6 us  [over_z(): return lax.ppermute(x, 'expert', [(i, (i + 2) % ring) for i in range(ring)])]
    ppermute x8, starting transfers between devices: 10.3 us -> 9.06 us  [over_y(): return lax.ppermute(x, 'expert', [(i, i ^ 1) for i in range(ring)])]
  transfers between devices with their start and end apart: 30 -> 30, of which waited for: 12 -> 9; matrix products, arithmetic and copies ran while one was open for 2% -> 2% of each run, Pallas kernels for 24% -> 25%
where the time goes in v12:
time: 114 us
  waiting for transfers between devices  47.1 us (41%)
  Pallas kernels  31.6 us (28%)
  starting transfers between devices  26.6 us (23%)
  local copies, waits for them, and re-layouts  5.01 us (4%)
  other arithmetic  3.41 us (3%)
    ppermute x6, waiting for transfers between devices, over_z(): return lax.ppermute(x, 'expert', [(i, (i + 2) % ring) for i in range(ring)])  25.6 us
    ppermute x13, starting transfers between devices, over_x(): lax.ppermute(x, 'tensor', [(i, (i + step) % parts) for i in range(parts)])  14.9 us
    pallas_call x6, Pallas kernels, down_rows(): pl.pallas_call(functools.partial(down_kernel, experts, capacity, groups,...  11.6 us
    pallas_call x6, Pallas kernels, pick_rows(): pl.pallas_call(kernel, grid=(1,), out_shape=(*out, *[jax.ShapeDtypeStruct...  11.4 us
    ppermute x8, waiting for transfers between devices, over_y(): return lax.ppermute(x, 'expert', [(i, i ^ 1) for i in range(ring)])  11.1 us
    ppermute x13, waiting for transfers between devices, over_x(): lax.ppermute(x, 'tensor', [(i, (i + step) % parts) for i in range(parts)])  10.3 us
    ppermute x8, starting transfers between devices, over_y(): return lax.ppermute(x, 'expert', [(i, i ^ 1) for i in range(ring)])  9.06 us
    pallas_call x6, Pallas kernels, home_rows(): pl.pallas_call(functools.partial(home_kernel, capacity, units, groups, le...  7.61 us
  transfers between devices with their start and end apart: 30, of which 9 were waited for; matrix products, arithmetic and copies ran while one was open for 2% of the time, Pallas kernels for 25%

profile of v12, /device:TPU:0, one launch (start us, length us, event | category | flops | bytes accessed | tf_op | source)
XLA Modules:
  0.0 114.1 jit_solution(3179998824473931318)
XLA Ops:
  0.0 0.5 collective-permute-start.5
  0.5 0.7 convert_bitcast_fusion
  1.2 0.7 pad_maximum_fusion.routes_ref
  1.9 1.0 copy-done.5
  2.9 0.4 shard_map.64.refs_0_.refs_2_
  3.3 3.0 %collective-permute-start = (bf16[96,2176]{1,0:T(8,128)(2,1)S(1)}, bf16[96,2176]{1,0:T(8,128)(2,1)S(1)}, u32[]{:S(2)}, u32[]{:S(2)}) collective-permute-start(bf16[96,2176]{1,0:T(8,128)(2,1)S(1)} %shard_map.64.refs_0_.refs_2_), channel_id=1, source_target_pairs={{0,4},{4,0},{8,12},{12,8},{16,20},{20,16},{24,28},{28,24},{1,5},{5... | collective-permute-start | bytes 1253384 | tf_op jit(solution)/shard_map/ppermute | solution.py:362
  6.4 1.6 %collective-permute-start.1 = (bf16[96,2176]{1,0:T(8,128)(2,1)S(1)}, bf16[96,2176]{1,0:T(8,128)(2,1)S(1)}, u32[]{:S(2)}, u32[]{:S(2)}) collective-permute-start(bf16[96,2176]{1,0:T(8,128)(2,1)S(1)} %shard_map.64.refs_0_.refs_2_), channel_id=1, source_target_pairs={{0,8},{4,12},{8,16},{12,20},{16,24},{20,28},{24,0},{28,4},{1,9},{5... | collective-permute-start | bytes 1253384 | tf_op jit(solution)/shard_map/ppermute | solution.py:365
  7.9 1.9 %copy-done = bf16[1,2048,768]{2,1,0:T(8,128)(2,1)S(1)} copy-done((bf16[1,2048,768]{2,1,0:T(8,128)(2,1)S(1)}, bf16[1,2048,768]{2,1,0:T(8,128)(2,1)}, u32[]{:S(2)}) %copy-start) | copy-done | bytes 3145752
  9.8 1.9 %copy-done.2 = bf16[1,2048,768]{2,1,0:T(8,128)(2,1)S(1)} copy-done((bf16[1,2048,768]{2,1,0:T(8,128)(2,1)S(1)}, bf16[1,2048,768]{2,1,0:T(8,128)(2,1)}, u32[]{:S(2)}) %copy-start.2) | copy-done | bytes 3145752
  11.7 1.1 shard_map.65
  12.8 1.6 %collective-permute-start.2 = (bf16[80,768]{1,0:T(8,128)(2,1)S(1)}, bf16[80,768]{1,0:T(8,128)(2,1)S(1)}, u32[]{:S(2)}, u32[]{:S(2)}) collective-permute-start(bf16[80,768]{1,0:T(8,128)(2,1)S(1)} %get-tuple-element.25.refs_2_), channel_id=1, source_target_pairs={{0,2},{2,0},{1,3},{3,1},{4,6},{6,4},{5,7},{7,5},{8,10},{10,8},{9,1... | collective-permute-start | bytes 368648 | tf_op jit(solution)/shard_map/ppermute | solution.py:374
  14.4 1.8 %collective-permute-done.refs_3_.refs_1_ = bf16[96,2176]{1,0:T(8,128)(2,1)S(1)} collective-permute-done((bf16[96,2176]{1,0:T(8,128)(2,1)S(1)}, bf16[96,2176]{1,0:T(8,128)(2,1)S(1)}, u32[]{:S(2)}, u32[]{:S(2)}) %collective-permute-start) | collective-permute-done | bytes 417824 | tf_op jit(solution)/shard_map/ppermute | solution.py:362
  16.2 3.3 %collective-permute-done.1.refs_4_ = bf16[96,2176]{1,0:T(8,128)(2,1)S(1)} collective-permute-done((bf16[96,2176]{1,0:T(8,128)(2,1)S(1)}, bf16[96,2176]{1,0:T(8,128)(2,1)S(1)}, u32[]{:S(2)}, u32[]{:S(2)}) %collective-permute-start.1) | collective-permute-done | bytes 417824 | tf_op jit(solution)/shard_map/ppermute | solution.py:365
  19.5 0.7 shard_map.66
  20.3 2.6 %shard_map.67 = (bf16[368,2048]{1,0:T(8,128)(2,1)S(1)}, bf16[368,768]{1,0:T(8,128)(2,1)S(1)}) custom-call(bf16[96,2176]{1,0:T(8,128)(2,1)S(1)} %shard_map.64.refs_0_.refs_2_, bf16[96,2176]{1,0:T(8,128)(2,1)S(1)} %collective-permute-done.refs_3_.refs_1_, bf16[96,2176]{1,0:T(8,128)(2,1)S(1)} %get-tuple-element.27.refs_2_.refs_4_, ...), custom_call_target="tpu_custom_call" | custom-call | flops 1 | bytes 1 | tf_op jit(solution)/shard_map/pallas_call | solution.py:216
  23.0 0.6 collective-permute-start.4
  23.6 1.6 %collective-permute-start.11 = (bf16[368,384]{1,0:T(8,128)(2,1)S(1)}, bf16[368,384]{1,0:T(8,128)(2,1)S(1)}, u32[]{:S(2)}, u32[]{:S(2)}) collective-permute-start(bf16[368,384]{1,0:T(8,128)(2,1)S(1)} %get-tuple-element.49), channel_id=1, source_target_pairs={{0,2},{2,0},{1,3},{3,1},{4,6},{6,4},{5,7},{7,5},{8,10},{10,8},{9,1... | collective-permute-start | bytes 847880 | tf_op jit(solution)/shard_map/ppermute | solution.py:374
  25.2 0.5 collective-permute-start.10
  25.7 9.3 %collective-permute-done.4.refs_0_.refs_2_ = bf16[96,2176]{1,0:T(8,128)(2,1)S(1)} collective-permute-done((bf16[96,2176]{1,0:T(8,128)(2,1)S(1)}, bf16[96,2176]{1,0:T(8,128)(2,1)S(1)}, u32[]{:S(2)}, u32[]{:S(2)}) %collective-permute-start.4) | collective-permute-done | bytes 417824 | tf_op jit(solution)/shard_map/ppermute | solution.py:362
  35.0 1.5 %collective-permute-start.3 = (bf16[80,384]{1,0:T(8,128)(2,1)S(1)}, bf16[80,384]{1,0:T(8,128)(2,1)S(1)}, u32[]{:S(2)}, u32[]{:S(2)}) collective-permute-start(bf16[80,384]{1,0:T(8,128)(2,1)S(1)} %fusion.5.refs_8_.refs_0_), channel_id=1, source_target_pairs={{0,2},{2,0},{1,3},{3,1},{4,6},{6,4},{5,7},{7,5},{8,10},{10,8},{9,1... | collective-permute-start | bytes 184328 | tf_op jit(solution)/shard_map/ppermute | solution.py:374
  36.5 1.9 %shard_map.68 = (bf16[144,2048]{1,0:T(8,128)(2,1)S(1)}, bf16[144,768]{1,0:T(8,128)(2,1)S(1)}) custom-call(bf16[96,2176]{1,0:T(8,128)(2,1)S(1)} %collective-permute-done.4.refs_0_.refs_2_, bf16[2048,768]{1,0:T(8,128)(2,1)S(1)} %bitcast.12, bf16[2048,768]{1,0:T(8,128)(2,1)S(1)} %bitcast.24, bf16[2048,768]{1,0:T(8,128)(2,1)S(1)} %bitcast.34, ...), custom_call_target="tpu_custom_call" | custom-call | flops 1 | bytes 1 | tf_op jit(solution)/shard_map/pallas_call | solution.py:216
  38.5 1.4 %shard_map.69 = (f32[368,768]{1,0:T(8,128)S(1)}, bf16[96,2176]{1,0:T(8,128)(2,1)S(1)}) custom-call(bf16[368,2048]{1,0:T(8,128)(2,1)S(1)} %get-tuple-element.31.x_ref, bf16[2048,768]{1,0:T(8,128)(2,1)S(1)} %bitcast.35, bf16[2048,768]{1,0:T(8,128)(2,1)S(1)} %bitcast.45, bf16[2048,768]{1,0:T(8,128)(2,1)S(1)} %bitcast.13, ...), custom_call_target="tpu_custom_call", output_to_operand_aliasing={{1}: (6, {})} | custom-call | flops 1 | bytes 1 | tf_op jit(solution)/shard_map/pallas_call | solution.py:245
  39.9 0.2 collective-permute-start.9
  40.2 0.6 collective-permute-start.13
  40.7 1.0 collective-permute-start.14
  41.9 0.2 fusion.refs_0_.refs_8_
  42.1 1.0 collective-permute-start.12
  43.1 9.7 %collective-permute-done.9.refs_5_ = bf16[96,2176]{1,0:T(8,128)(2,1)S(1)} collective-permute-done((bf16[96,2176]{1,0:T(8,128)(2,1)S(1)}, bf16[96,2176]{1,0:T(8,128)(2,1)S(1)}, u32[]{:S(2)}, u32[]{:S(2)}) %collective-permute-start.9) | collective-permute-done | bytes 417824 | tf_op jit(solution)/shard_map/ppermute | solution.py:365
  52.9 1.4 %shard_map.70 = (f32[144,768]{1,0:T(8,128)S(1)}, bf16[96,2176]{1,0:T(8,128)(2,1)S(1)}) custom-call(bf16[144,2048]{1,0:T(8,128)(2,1)S(1)} %get-tuple-element.30.x_ref, bf16[2048,768]{1,0:T(8,128)(2,1)S(1)} %bitcast.14, bf16[2048,768]{1,0:T(8,128)(2,1)S(1)} %bitcast.26, bf16[2048,768]{1,0:T(8,128)(2,1)S(1)} %bitcast.36, ...), custom_call_target="tpu_custom_call", output_to_operand_aliasing={{1}: (6, {})} | custom-call | flops 1 | bytes 1 | tf_op jit(solution)/shard_map/pallas_call | solution.py:245
  54.4 0.6 collective-permute-start.16
  55.0 1.0 collective-permute-start.17
  56.0 1.1 shard_map.71.refs_6_.refs_0_
  57.1 2.0 %shard_map.72 = (bf16[288,2048]{1,0:T(8,128)(2,1)S(1)}, bf16[288,768]{1,0:T(8,128)(2,1)S(1)}) custom-call(bf16[96,2176]{1,0:T(8,128)(2,1)S(1)} %collective-permute-done.13.refs_0_.refs_5_.refs_2_, bf16[96,2176]{1,0:T(8,128)(2,1)S(1)} %get-tuple-element.34.refs_1_.refs_3_, bf16[2048,768]{1,0:T(8,128)(2,1)S(1)} %bitcast.15, bf16[2048,768]{1,0:T(8,128)(2,1)S(1)} %bitcast.27, ...), custom_call_target="tpu_custom_call" | custom-call | flops 1 | bytes 1 | tf_op jit(solution)/shard_map/pallas_call | solution.py:216
  59.1 1.2 %collective-permute-start.18 = (bf16[288,768]{1,0:T(8,128)(2,1)S(1)}, bf16[288,768]{1,0:T(8,128)(2,1)S(1)}, u32[]{:S(2)}, u32[]{:S(2)}) collective-permute-start(bf16[288,768]{1,0:T(8,128)(2,1)S(1)} %get-tuple-element.36.refs_7_), channel_id=1, source_target_pairs={{0,2},{2,0},{1,3},{3,1},{4,6},{6,4},{5,7},{7,5},{8,10},{10,8},{9,1... | collective-permute-start | bytes 1327112 | tf_op jit(solution)/shard_map/ppermute | solution.py:374
  60.2 2.8 %shard_map.73.refs_5_ = bf16[288,2048]{1,0:T(8,128)(2,1)S(1)} custom-call(bf16[368,384]{1,0:T(8,128)(2,1)S(1)} %fusion.refs_0_.refs_8_, bf16[368,384]{1,0:T(8,128)(2,1)S(1)} %collective-permute-done.12.refs_1_, bf16[96,2176]{1,0:T(8,128)(2,1)S(1)} %shard_map.64.refs_0_.refs_2_, bf16[96,2176]{1,0:T(8,128)(2,1)S(1)} %collective-permute-done.refs_3_.refs_1_, ...), custom_call_target="tpu_custom_call" | custom-call | flops 1 | bytes 1 | tf_op jit(solution)/shard_map/pallas_call | solution.py:314
  63.1 1.6 %collective-permute-start.15 = (bf16[96,2048]{1,0:T(8,128)(2,1)S(1)}, bf16[96,2048]{1,0:T(8,128)(2,1)S(1)}, u32[]{:S(2)}, u32[]{:S(2)}) collective-permute-start(bf16[96,2048]{1,0:T(8,128)(2,1)S(1)} %get-tuple-element.44), channel_id=1, source_target_pairs={{0,4},{4,0},{8,12},{12,8},{16,20},{20,16},{24,28},{28,24},{1,5},{5... | collective-permute-start | bytes 1179656 | tf_op jit(solution)/shard_map/ppermute | solution.py:362
  64.7 1.8 %shard_map.74.refs_5_ = bf16[96,2048]{1,0:T(8,128)(2,1)S(1)} custom-call(bf16[144,384]{1,0:T(8,128)(2,1)S(1)} %fusion.4.refs_9_.refs_0_, bf16[144,384]{1,0:T(8,128)(2,1)S(1)} %collective-permute-done.17.refs_1_, bf16[96,2176]{1,0:T(8,128)(2,1)S(1)} %collective-permute-done.4.refs_0_.refs_2_, bf16[768,2048]{1,0:T(8,128)(2,1)S(1)} %bitcast.55, ...), custom_call_target="tpu_custom_call" | custom-call | flops 1 | bytes 1 | tf_op jit(solution)/shard_map/pallas_call | solution.py:314
  66.5 0.6 collective-permute-start.23
  67.1 1.9 %shard_map.75 = (bf16[144,2048]{1,0:T(8,128)(2,1)S(1)}, bf16[144,768]{1,0:T(8,128)(2,1)S(1)}) custom-call(bf16[96,2176]{1,0:T(8,128)(2,1)S(1)} %collective-permute-done.16.refs_0_.refs_2_, bf16[2048,768]{1,0:T(8,128)(2,1)S(1)} %bitcast.16, bf16[2048,768]{1,0:T(8,128)(2,1)S(1)} %bitcast.28, bf16[2048,768]{1,0:T(8,128)(2,1)S(1)} %bitcast.38, ...), custom_call_target="tpu_custom_call" | custom-call | flops 1 | bytes 1 | tf_op jit(solution)/shard_map/pallas_call | solution.py:216
  69.0 1.1 collective-permute-start.24
  70.1 1.2 %shard_map.76.refs_4_ = f32[288,768]{1,0:T(8,128)S(1)} custom-call(bf16[288,2048]{1,0:T(8,128)(2,1)S(1)} %get-tuple-element.39.x_ref, bf16[2048,768]{1,0:T(8,128)(2,1)S(1)} %bitcast.17, bf16[2048,768]{1,0:T(8,128)(2,1)S(1)} %bitcast.29, bf16[2048,768]{1,0:T(8,128)(2,1)S(1)} %bitcast.39, bf16[2048,768]{1,0:T(8,128)(2,1)S(1)} %bitcast.49, ...), custom_call_target="tpu_custom_call" | custom-call | flops 1 | bytes 1 | tf_op jit(solution)/shard_map/pallas_call | solution.py:245
  71.2 1.5 %shard_map.77.refs_5_ = f32[144,768]{1,0:T(8,128)S(1)} custom-call(bf16[144,2048]{1,0:T(8,128)(2,1)S(1)} %get-tuple-element.38.x_ref, bf16[2048,768]{1,0:T(8,128)(2,1)S(1)} %bitcast.18, bf16[2048,768]{1,0:T(8,128)(2,1)S(1)} %bitcast.30, bf16[2048,768]{1,0:T(8,128)(2,1)S(1)} %bitcast.40, bf16[2048,768]{1,0:T(8,128)(2,1)S(1)} %bitcast.50, ...), custom_call_target="tpu_custom_call" | custom-call | flops 1 | bytes 1 | tf_op jit(solution)/shard_map/pallas_call | solution.py:245
  72.7 0.3 convert_add_fusion.1
  73.0 0.1 fusion.1.refs_6_.refs_0_
  73.2 1.0 collective-permute-start.21
  74.2 1.9 %shard_map.78 = (bf16[144,2048]{1,0:T(8,128)(2,1)S(1)}, bf16[144,768]{1,0:T(8,128)(2,1)S(1)}) custom-call(bf16[96,2176]{1,0:T(8,128)(2,1)S(1)} %get-tuple-element.37.refs_0_.refs_2_, bf16[2048,768]{1,0:T(8,128)(2,1)S(1)} %bitcast.19, bf16[2048,768]{1,0:T(8,128)(2,1)S(1)} %bitcast.31, bf16[2048,768]{1,0:T(8,128)(2,1)S(1)} %bitcast.41, ...), custom_call_target="tpu_custom_call" | custom-call | flops 1 | bytes 1 | tf_op jit(solution)/shard_map/pallas_call | solution.py:216
  76.2 0.2 shard_map.79.refs_4_
  76.3 1.4 %shard_map.80.refs_6_ = f32[144,768]{1,0:T(8,128)S(1)} custom-call(bf16[144,2048]{1,0:T(8,128)(2,1)S(1)} %get-tuple-element.42.x_ref, bf16[2048,768]{1,0:T(8,128)(2,1)S(1)} %bitcast.20, bf16[2048,768]{1,0:T(8,128)(2,1)S(1)} %bitcast.32, bf16[2048,768]{1,0:T(8,128)(2,1)S(1)} %bitcast.42, bf16[2048,768]{1,0:T(8,128)(2,1)S(1)} %bitcast.52, ...), custom_call_target="tpu_custom_call" | custom-call | flops 1 | bytes 1 | tf_op jit(solution)/shard_map/pallas_call | solution.py:245
  77.9 1.8 %collective-permute-done.21.refs_1_ = bf16[288,384]{1,0:T(8,128)(2,1)S(1)} collective-permute-done((bf16[288,384]{1,0:T(8,128)(2,1)S(1)}, bf16[288,384]{1,0:T(8,128)(2,1)S(1)}, u32[]{:S(2)}, u32[]{:S(2)}) %collective-permute-start.21) | collective-permute-done | bytes 221216 | tf_op jit(solution)/shard_map/ppermute | solution.py:374
  79.7 2.4 %shard_map.81.refs_2_ = bf16[192,2048]{1,0:T(8,128)(2,1)S(1)} custom-call(bf16[288,384]{1,0:T(8,128)(2,1)S(1)} %fusion.1.refs_6_.refs_0_, bf16[288,384]{1,0:T(8,128)(2,1)S(1)} %collective-permute-done.21.refs_1_, bf16[96,2176]{1,0:T(8,128)(2,1)S(1)} %collective-permute-done.13.refs_0_.refs_5_.refs_2_, ...), custom_call_target="tpu_custom_call" | custom-call | flops 1 | bytes 1 | tf_op jit(solution)/shard_map/pallas_call | solution.py:314
  82.1 1.2 %collective-permute-start.22 = (bf16[96,2048]{1,0:T(8,128)(2,1)S(1)}, bf16[96,2048]{1,0:T(8,128)(2,1)S(1)}, u32[]{:S(2)}, u32[]{:S(2)}) collective-permute-start(bf16[96,2048]{1,0:T(8,128)(2,1)S(1)} %get-tuple-element.46), channel_id=1, source_target_pairs={{0,4},{4,0},{8,12},{12,8},{16,20},{20,16},{24,28},{28,24},{1,5},{5... | collective-permute-start | bytes 1179656 | tf_op jit(solution)/shard_map/ppermute | solution.py:362
  83.4 1.1 collective-permute-start.19
  84.5 1.0 collective-permute-start.26
  85.5 5.1 %collective-permute-done.26.refs_1_ = bf16[144,384]{1,0:T(8,128)(2,1)S(1)} collective-permute-done((bf16[144,384]{1,0:T(8,128)(2,1)S(1)}, bf16[144,384]{1,0:T(8,128)(2,1)S(1)}, u32[]{:S(2)}, u32[]{:S(2)}) %collective-permute-start.26) | collective-permute-done | bytes 110624 | tf_op jit(solution)/shard_map/ppermute | solution.py:374
  90.6 1.8 %shard_map.83.refs_3_ = bf16[96,2048]{1,0:T(8,128)(2,1)S(1)} custom-call(bf16[144,384]{1,0:T(8,128)(2,1)S(1)} %fusion.2.refs_3_.refs_0_, bf16[144,384]{1,0:T(8,128)(2,1)S(1)} %collective-permute-done.26.refs_1_, bf16[96,2176]{1,0:T(8,128)(2,1)S(1)} %collective-permute-done.16.refs_0_.refs_2_, bf16[768,2048]{1,0:T(8,128)(2,1)S(1)} %bitcast.57, ...), custom_call_target="tpu_custom_call" | custom-call | flops 1 | bytes 1 | tf_op jit(solution)/shard_map/pallas_call | solution.py:314
  92.4 1.0 collective-permute-start.27
  93.4 0.1 shard_map.84.refs_5_
  93.8 1.4 %collective-permute-start.20 = (bf16[144,384]{1,0:T(8,128)(2,1)S(1)}, bf16[144,384]{1,0:T(8,128)(2,1)S(1)}, u32[]{:S(2)}, u32[]{:S(2)}) collective-permute-start(bf16[144,384]{1,0:T(8,128)(2,1)S(1)} %fusion.3.refs_0_.refs_6_), channel_id=1, source_target_pairs={{0,2},{2,0},{1,3},{3,1},{4,6},{6,4},{5,7},{7,5},{8,10},{10,8},{9,1... | collective-permute-start | bytes 331784 | tf_op jit(solution)/shard_map/ppermute | solution.py:374
  95.2 3.4 %collective-permute-done.20.refs_1_ = bf16[144,384]{1,0:T(8,128)(2,1)S(1)} collective-permute-done((bf16[144,384]{1,0:T(8,128)(2,1)S(1)}, bf16[144,384]{1,0:T(8,128)(2,1)S(1)}, u32[]{:S(2)}, u32[]{:S(2)}) %collective-permute-start.20) | collective-permute-done | bytes 110624 | tf_op jit(solution)/shard_map/ppermute | solution.py:374
  98.6 1.8 %shard_map.85.refs_0_.refs_3_ = bf16[96,2048]{1,0:T(8,128)(2,1)S(1)} custom-call(bf16[144,384]{1,0:T(8,128)(2,1)S(1)} %fusion.3.refs_0_.refs_6_, bf16[144,384]{1,0:T(8,128)(2,1)S(1)} %collective-permute-done.20.refs_1_, bf16[96,2176]{1,0:T(8,128)(2,1)S(1)} %get-tuple-element.37.refs_0_.refs_2_, bf16[768,2048]{1,0:T(8,128)(2,1)S(1)} %bitcast.58, ...), custom_call_target="tpu_custom_call" | custom-call | flops 1 | bytes 1 | tf_op jit(solution)/shard_map/pallas_call | solution.py:314
  100.4 3.0 %collective-permute-done.28.refs_2_ = bf16[96,2048]{1,0:T(8,128)(2,1)S(1)} collective-permute-done((bf16[96,2048]{1,0:T(8,128)(2,1)S(1)}, bf16[96,2048]{1,0:T(8,128)(2,1)S(1)}, u32[]{:S(2)}, u32[]{:S(2)}) %collective-permute-start.28) | collective-permute-done | bytes 393248 | tf_op jit(solution)/shard_map/ppermute | solution.py:365
  103.4 0.1 shard_map.86
  103.7 9.6 %collective-permute-done.29 = bf16[96,2048]{1,0:T(8,128)(2,1)S(1)} collective-permute-done((bf16[96,2048]{1,0:T(8,128)(2,1)S(1)}, bf16[96,2048]{1,0:T(8,128)(2,1)S(1)}, u32[]{:S(2)}, u32[]{:S(2)}) %collective-permute-start.29) | collective-permute-done | bytes 393248 | tf_op jit(solution)/shard_map/ppermute | solution.py:365
  113.2 0.8 add_convert_fusion
  (49 shorter events, 1.3 us)
Async XLA Ops:
  0.0 20.3 %collective-permute-start.5 = (bf16[1,2048,768]{2,1,0:T(8,128)(2,1)}, bf16[1,2048,768]{2,1,0:T(8,128)(2,1)S(1)}, u32[]{:S(2)}, u32[]{:S(2)}) collective-permute-start(bf16[1,2048,768]{2,1,0:T(8,128)(2,1)} %param.9), channel_id=1, source_target_pairs={{0,1},{1,0},{2,3},{3,2},{4,5},{5,4},{6,7},{7,6},{8,9},{9,8},{10,11... | collective-permute-start | bytes 9437192 | tf_op jit(solution)/shard_map/ppermute | solution.py:371
  0.5 19.8 %collective-permute-start.6 = (bf16[1,2048,768]{2,1,0:T(8,128)(2,1)}, bf16[1,2048,768]{2,1,0:T(8,128)(2,1)S(1)}, u32[]{:S(2)}, u32[]{:S(2)}) collective-permute-start(bf16[1,2048,768]{2,1,0:T(8,128)(2,1)} %param.10), channel_id=1, source_target_pairs={{0,1},{1,0},{2,3},{3,2},{4,5},{5,4},{6,7},{7,6},{8,9},{9,8},{10,11... | collective-permute-start | bytes 9437192 | tf_op jit(solution)/shard_map/ppermute | solution.py:371
  1.9 1.0 copy-start.5
  3.3 12.8 %collective-permute-start = (bf16[96,2176]{1,0:T(8,128)(2,1)S(1)}, bf16[96,2176]{1,0:T(8,128)(2,1)S(1)}, u32[]{:S(2)}, u32[]{:S(2)}) collective-permute-start(bf16[96,2176]{1,0:T(8,128)(2,1)S(1)} %shard_map.64.refs_0_.refs_2_), channel_id=1, source_target_pairs={{0,4},{4,0},{8,12},{12,8},{16,20},{20,16},{24,28},{28,24},{1,5},{5... | collective-permute-start | bytes 1253384 | tf_op jit(solution)/shard_map/ppermute | solution.py:362
  6.4 13.1 %collective-permute-start.1 = (bf16[96,2176]{1,0:T(8,128)(2,1)S(1)}, bf16[96,2176]{1,0:T(8,128)(2,1)S(1)}, u32[]{:S(2)}, u32[]{:S(2)}) collective-permute-start(bf16[96,2176]{1,0:T(8,128)(2,1)S(1)} %shard_map.64.refs_0_.refs_2_), channel_id=1, source_target_pairs={{0,8},{4,12},{8,16},{12,20},{16,24},{20,28},{24,0},{28,4},{1,9},{5... | collective-permute-start | bytes 1253384 | tf_op jit(solution)/shard_map/ppermute | solution.py:365
  7.9 1.9 %copy-start = (bf16[1,2048,768]{2,1,0:T(8,128)(2,1)S(1)}, bf16[1,2048,768]{2,1,0:T(8,128)(2,1)}, u32[]{:S(2)}) copy-start(bf16[1,2048,768]{2,1,0:T(8,128)(2,1)} %param.9) | copy-start | bytes 9437188
  9.8 1.9 %copy-start.2 = (bf16[1,2048,768]{2,1,0:T(8,128)(2,1)S(1)}, bf16[1,2048,768]{2,1,0:T(8,128)(2,1)}, u32[]{:S(2)}) copy-start(bf16[1,2048,768]{2,1,0:T(8,128)(2,1)} %param.10) | copy-start | bytes 9437188
  11.7 7.8 %copy-start.1 = (bf16[1,2048,768]{2,1,0:T(8,128)(2,1)S(1)}, bf16[1,2048,768]{2,1,0:T(8,128)(2,1)}, u32[]{:S(2)}) copy-start(bf16[1,2048,768]{2,1,0:T(8,128)(2,1)} %param.9) | copy-start | bytes 9437188
  11.7 7.8 %copy-start.3 = (bf16[1,2048,768]{2,1,0:T(8,128)(2,1)S(1)}, bf16[1,2048,768]{2,1,0:T(8,128)(2,1)}, u32[]{:S(2)}) copy-start(bf16[1,2048,768]{2,1,0:T(8,128)(2,1)} %param.10) | copy-start | bytes 9437188
  12.8 7.4 %collective-permute-start.2 = (bf16[80,768]{1,0:T(8,128)(2,1)S(1)}, bf16[80,768]{1,0:T(8,128)(2,1)S(1)}, u32[]{:S(2)}, u32[]{:S(2)}) collective-permute-start(bf16[80,768]{1,0:T(8,128)(2,1)S(1)} %get-tuple-element.25.refs_2_), channel_id=1, source_target_pairs={{0,2},{2,0},{1,3},{3,1},{4,6},{6,4},{5,7},{7,5},{8,10},{10,8},{9,1... | collective-permute-start | bytes 368648 | tf_op jit(solution)/shard_map/ppermute | solution.py:374
  20.3 2.6 %copy-start.4 = (bf16[1,768,2048]{2,1,0:T(8,128)(2,1)S(1)}, bf16[1,768,2048]{2,1,0:T(8,128)(2,1)}, u32[]{:S(2)}) copy-start(bf16[1,768,2048]{2,1,0:T(8,128)(2,1)} %param.11) | copy-start | bytes 9437188
  22.9 13.6 %collective-permute-start.7 = (bf16[1,768,2048]{2,1,0:T(8,128)(2,1)S(1)}, bf16[1,768,2048]{2,1,0:T(8,128)(2,1)S(1)}, u32[]{:S(2)}, u32[]{:S(2)}) collective-permute-start(bf16[1,768,2048]{2,1,0:T(8,128)(2,1)S(1)} %copy-done.4), channel_id=1, source_target_pairs={{0,1},{1,0},{2,3},{3,2},{4,5},{5,4},{6,7},{7,6},{8,9},{9,8},{10,11... | collective-permute-start | bytes 9437192 | tf_op jit(solution)/shard_map/ppermute | solution.py:371
  23.0 12.1 %collective-permute-start.4 = (bf16[96,2176]{1,0:T(8,128)(2,1)S(1)}, bf16[96,2176]{1,0:T(8,128)(2,1)S(1)}, u32[]{:S(2)}, u32[]{:S(2)}) collective-permute-start(bf16[96,2176]{1,0:T(8,128)(2,1)S(1)} %get-tuple-element.27.refs_2_.refs_4_), channel_id=1, source_target_pairs={{0,4},{4,0},{8,12},{12,8},{16,20},{20,16},{24,28},{28,24},{1,5},{5... | collective-permute-start | bytes 1253384 | tf_op jit(solution)/shard_map/ppermute | solution.py:362
  23.5 14.9 %collective-permute-start.8 = (bf16[96,2176]{1,0:T(8,128)(2,1)S(1)}, bf16[96,2176]{1,0:T(8,128)(2,1)S(1)}, u32[]{:S(2)}, u32[]{:S(2)}) collective-permute-start(bf16[96,2176]{1,0:T(8,128)(2,1)S(1)} %get-tuple-element.27.refs_2_.refs_4_), channel_id=1, source_target_pairs={{0,8},{4,12},{8,16},{12,20},{16,24},{20,28},{24,0},{28,4},{1,9},{5... | collective-permute-start | bytes 1253384 | tf_op jit(solution)/shard_map/ppermute | solution.py:365
  23.6 17.1 %collective-permute-start.11 = (bf16[368,384]{1,0:T(8,128)(2,1)S(1)}, bf16[368,384]{1,0:T(8,128)(2,1)S(1)}, u32[]{:S(2)}, u32[]{:S(2)}) collective-permute-start(bf16[368,384]{1,0:T(8,128)(2,1)S(1)} %get-tuple-element.49), channel_id=1, source_target_pairs={{0,2},{2,0},{1,3},{3,1},{4,6},{6,4},{5,7},{7,5},{8,10},{10,8},{9,1... | collective-permute-start | bytes 847880 | tf_op jit(solution)/shard_map/ppermute | solution.py:374
  25.2 16.6 %collective-permute-start.10 = (bf16[368,384]{1,0:T(8,128)(2,1)S(1)}, bf16[368,384]{1,0:T(8,128)(2,1)S(1)}, u32[]{:S(2)}, u32[]{:S(2)}) collective-permute-start(bf16[368,384]{1,0:T(8,128)(2,1)S(1)} %get-tuple-element.48), channel_id=1, source_target_pairs={{0,2},{2,0},{1,3},{3,1},{4,6},{6,4},{5,7},{7,5},{8,10},{10,8},{9,1... | collective-permute-start | bytes 847880 | tf_op jit(solution)/shard_map/ppermute | solution.py:374
  35.0 21.0 %collective-permute-start.3 = (bf16[80,384]{1,0:T(8,128)(2,1)S(1)}, bf16[80,384]{1,0:T(8,128)(2,1)S(1)}, u32[]{:S(2)}, u32[]{:S(2)}) collective-permute-start(bf16[80,384]{1,0:T(8,128)(2,1)S(1)} %fusion.5.refs_8_.refs_0_), channel_id=1, source_target_pairs={{0,2},{2,0},{1,3},{3,1},{4,6},{6,4},{5,7},{7,5},{8,10},{10,8},{9,1... | collective-permute-start | bytes 184328 | tf_op jit(solution)/shard_map/ppermute | solution.py:374
  39.9 13.0 %collective-permute-start.9 = (bf16[96,2176]{1,0:T(8,128)(2,1)S(1)}, bf16[96,2176]{1,0:T(8,128)(2,1)S(1)}, u32[]{:S(2)}, u32[]{:S(2)}) collective-permute-start(bf16[96,2176]{1,0:T(8,128)(2,1)S(1)} %get-tuple-element.34.refs_1_.refs_3_), channel_id=1, source_target_pairs={{0,8},{4,12},{8,16},{12,20},{16,24},{20,28},{24,0},{28,4},{1,9},{5... | collective-permute-start | bytes 1253384 | tf_op jit(solution)/shard_map/ppermute | solution.py:365
  40.2 16.9 %collective-permute-start.13 = (bf16[96,2176]{1,0:T(8,128)(2,1)S(1)}, bf16[96,2176]{1,0:T(8,128)(2,1)S(1)}, u32[]{:S(2)}, u32[]{:S(2)}) collective-permute-start(bf16[96,2176]{1,0:T(8,128)(2,1)S(1)} %get-tuple-element.34.refs_1_.refs_3_), channel_id=1, source_target_pairs={{0,4},{4,0},{8,12},{12,8},{16,20},{20,16},{24,28},{28,24},{1,5},{5... | collective-permute-start | bytes 1253384 | tf_op jit(solution)/shard_map/ppermute | solution.py:362
  40.7 13.6 %collective-permute-start.14 = (bf16[144,768]{1,0:T(8,128)(2,1)S(1)}, bf16[144,768]{1,0:T(8,128)(2,1)S(1)}, u32[]{:S(2)}, u32[]{:S(2)}) collective-permute-start(bf16[144,768]{1,0:T(8,128)(2,1)S(1)} %get-tuple-element.32.refs_4_), channel_id=1, source_target_pairs={{0,2},{2,0},{1,3},{3,1},{4,6},{6,4},{5,7},{7,5},{8,10},{10,8},{9,1... | collective-permute-start | bytes 663560 | tf_op jit(solution)/shard_map/ppermute | solution.py:374
  42.1 18.1 %collective-permute-start.12 = (bf16[368,384]{1,0:T(8,128)(2,1)S(1)}, bf16[368,384]{1,0:T(8,128)(2,1)S(1)}, u32[]{:S(2)}, u32[]{:S(2)}) collective-permute-start(bf16[368,384]{1,0:T(8,128)(2,1)S(1)} %fusion.refs_0_.refs_8_), channel_id=1, source_target_pairs={{0,2},{2,0},{1,3},{3,1},{4,6},{6,4},{5,7},{7,5},{8,10},{10,8},{9,1... | collective-permute-start | bytes 847880 | tf_op jit(solution)/shard_map/ppermute | solution.py:374
  54.4 12.6 %collective-permute-start.16 = (bf16[96,2176]{1,0:T(8,128)(2,1)S(1)}, bf16[96,2176]{1,0:T(8,128)(2,1)S(1)}, u32[]{:S(2)}, u32[]{:S(2)}) collective-permute-start(bf16[96,2176]{1,0:T(8,128)(2,1)S(1)} %get-tuple-element.37.refs_0_.refs_2_), channel_id=1, source_target_pairs={{0,4},{4,0},{8,12},{12,8},{16,20},{20,16},{24,28},{28,24},{1,5},{5... | collective-permute-start | bytes 1253384 | tf_op jit(solution)/shard_map/ppermute | solution.py:362
  55.0 9.7 %collective-permute-start.17 = (bf16[144,384]{1,0:T(8,128)(2,1)S(1)}, bf16[144,384]{1,0:T(8,128)(2,1)S(1)}, u32[]{:S(2)}, u32[]{:S(2)}) collective-permute-start(bf16[144,384]{1,0:T(8,128)(2,1)S(1)} %fusion.4.refs_9_.refs_0_), channel_id=1, source_target_pairs={{0,2},{2,0},{1,3},{3,1},{4,6},{6,4},{5,7},{7,5},{8,10},{10,8},{9,1... | collective-permute-start | bytes 331784 | tf_op jit(solution)/shard_map/ppermute | solution.py:374
  59.1 13.6 %collective-permute-start.18 = (bf16[288,768]{1,0:T(8,128)(2,1)S(1)}, bf16[288,768]{1,0:T(8,128)(2,1)S(1)}, u32[]{:S(2)}, u32[]{:S(2)}) collective-permute-start(bf16[288,768]{1,0:T(8,128)(2,1)S(1)} %get-tuple-element.36.refs_7_), channel_id=1, source_target_pairs={{0,2},{2,0},{1,3},{3,1},{4,6},{6,4},{5,7},{7,5},{8,10},{10,8},{9,1... | collective-permute-start | bytes 1327112 | tf_op jit(solution)/shard_map/ppermute | solution.py:374
  63.1 13.0 %collective-permute-start.15 = (bf16[96,2048]{1,0:T(8,128)(2,1)S(1)}, bf16[96,2048]{1,0:T(8,128)(2,1)S(1)}, u32[]{:S(2)}, u32[]{:S(2)}) collective-permute-start(bf16[96,2048]{1,0:T(8,128)(2,1)S(1)} %get-tuple-element.44), channel_id=1, source_target_pairs={{0,4},{4,0},{8,12},{12,8},{16,20},{20,16},{24,28},{28,24},{1,5},{5... | collective-permute-start | bytes 1179656 | tf_op jit(solution)/shard_map/ppermute | solution.py:362
  66.5 16.7 %collective-permute-start.23 = (bf16[96,2048]{1,0:T(8,128)(2,1)S(1)}, bf16[96,2048]{1,0:T(8,128)(2,1)S(1)}, u32[]{:S(2)}, u32[]{:S(2)}) collective-permute-start(bf16[96,2048]{1,0:T(8,128)(2,1)S(1)} %shard_map.74.refs_5_), channel_id=1, source_target_pairs={{0,4},{4,0},{8,12},{12,8},{16,20},{20,16},{24,28},{28,24},{1,5},{5... | collective-permute-start | bytes 1179656 | tf_op jit(solution)/shard_map/ppermute | solution.py:362
  69.0 8.8 %collective-permute-start.24 = (bf16[144,768]{1,0:T(8,128)(2,1)S(1)}, bf16[144,768]{1,0:T(8,128)(2,1)S(1)}, u32[]{:S(2)}, u32[]{:S(2)}) collective-permute-start(bf16[144,768]{1,0:T(8,128)(2,1)S(1)} %get-tuple-element.40.refs_4_), channel_id=1, source_target_pairs={{0,2},{2,0},{1,3},{3,1},{4,6},{6,4},{5,7},{7,5},{8,10},{10,8},{9,1... | collective-permute-start | bytes 663560 | tf_op jit(solution)/shard_map/ppermute | solution.py:374
  73.2 6.5 %collective-permute-start.21 = (bf16[288,384]{1,0:T(8,128)(2,1)S(1)}, bf16[288,384]{1,0:T(8,128)(2,1)S(1)}, u32[]{:S(2)}, u32[]{:S(2)}) collective-permute-start(bf16[288,384]{1,0:T(8,128)(2,1)S(1)} %fusion.1.refs_6_.refs_0_), channel_id=1, source_target_pairs={{0,2},{2,0},{1,3},{3,1},{4,6},{6,4},{5,7},{7,5},{8,10},{10,8},{9,1... | collective-permute-start | bytes 663560 | tf_op jit(solution)/shard_map/ppermute | solution.py:374
  82.1 11.3 %collective-permute-start.22 = (bf16[96,2048]{1,0:T(8,128)(2,1)S(1)}, bf16[96,2048]{1,0:T(8,128)(2,1)S(1)}, u32[]{:S(2)}, u32[]{:S(2)}) collective-permute-start(bf16[96,2048]{1,0:T(8,128)(2,1)S(1)} %get-tuple-element.46), channel_id=1, source_target_pairs={{0,4},{4,0},{8,12},{12,8},{16,20},{20,16},{24,28},{28,24},{1,5},{5... | collective-permute-start | bytes 1179656 | tf_op jit(solution)/shard_map/ppermute | solution.py:362
  83.4 10.1 %collective-permute-start.25 = (bf16[96,2048]{1,0:T(8,128)(2,1)S(1)}, bf16[96,2048]{1,0:T(8,128)(2,1)S(1)}, u32[]{:S(2)}, u32[]{:S(2)}) collective-permute-start(bf16[96,2048]{1,0:T(8,128)(2,1)S(1)} %shard_map.82.refs_5_), channel_id=1, source_target_pairs={{0,8},{4,12},{8,16},{12,20},{16,24},{20,28},{24,0},{28,4},{1,9},{5... | collective-permute-start | bytes 1179656 | tf_op jit(solution)/shard_map/ppermute | solution.py:365
  83.4 10.2 %collective-permute-start.19 = (bf16[144,768]{1,0:T(8,128)(2,1)S(1)}, bf16[144,768]{1,0:T(8,128)(2,1)S(1)}, u32[]{:S(2)}, u32[]{:S(2)}) collective-permute-start(bf16[144,768]{1,0:T(8,128)(2,1)S(1)} %get-tuple-element.41.refs_3_), channel_id=1, source_target_pairs={{0,2},{2,0},{1,3},{3,1},{4,6},{6,4},{5,7},{7,5},{8,10},{10,8},{9,1... | collective-permute-start | bytes 663560 | tf_op jit(solution)/shard_map/ppermute | solution.py:374
  84.5 6.1 %collective-permute-start.26 = (bf16[144,384]{1,0:T(8,128)(2,1)S(1)}, bf16[144,384]{1,0:T(8,128)(2,1)S(1)}, u32[]{:S(2)}, u32[]{:S(2)}) collective-permute-start(bf16[144,384]{1,0:T(8,128)(2,1)S(1)} %fusion.2.refs_3_.refs_0_), channel_id=1, source_target_pairs={{0,2},{2,0},{1,3},{3,1},{4,6},{6,4},{5,7},{7,5},{8,10},{10,8},{9,1... | collective-permute-start | bytes 331784 | tf_op jit(solution)/shard_map/ppermute | solution.py:374
  92.4 8.0 %collective-permute-start.27 = (bf16[96,2048]{1,0:T(8,128)(2,1)S(1)}, bf16[96,2048]{1,0:T(8,128)(2,1)S(1)}, u32[]{:S(2)}, u32[]{:S(2)}) collective-permute-start(bf16[96,2048]{1,0:T(8,128)(2,1)S(1)} %shard_map.83.refs_3_), channel_id=1, source_target_pairs={{0,4},{4,0},{8,12},{12,8},{16,20},{20,16},{24,28},{28,24},{1,5},{5... | collective-permute-start | bytes 1179656 | tf_op jit(solution)/shard_map/ppermute | solution.py:362
  93.6 9.9 %collective-permute-start.28 = (bf16[96,2048]{1,0:T(8,128)(2,1)S(1)}, bf16[96,2048]{1,0:T(8,128)(2,1)S(1)}, u32[]{:S(2)}, u32[]{:S(2)}) collective-permute-start(bf16[96,2048]{1,0:T(8,128)(2,1)S(1)} %shard_map.84.refs_5_), channel_id=1, source_target_pairs={{0,8},{4,12},{8,16},{12,20},{16,24},{20,28},{24,0},{28,4},{1,9},{5... | collective-permute-start | bytes 1179656 | tf_op jit(solution)/shard_map/ppermute | solution.py:365
  93.8 4.8 %collective-permute-start.20 = (bf16[144,384]{1,0:T(8,128)(2,1)S(1)}, bf16[144,384]{1,0:T(8,128)(2,1)S(1)}, u32[]{:S(2)}, u32[]{:S(2)}) collective-permute-start(bf16[144,384]{1,0:T(8,128)(2,1)S(1)} %fusion.3.refs_0_.refs_6_), channel_id=1, source_target_pairs={{0,2},{2,0},{1,3},{3,1},{4,6},{6,4},{5,7},{7,5},{8,10},{10,8},{9,1... | collective-permute-start | bytes 331784 | tf_op jit(solution)/shard_map/ppermute | solution.py:374
  103.6 9.6 %collective-permute-start.29 = (bf16[96,2048]{1,0:T(8,128)(2,1)S(1)}, bf16[96,2048]{1,0:T(8,128)(2,1)S(1)}, u32[]{:S(2)}, u32[]{:S(2)}) collective-permute-start(bf16[96,2048]{1,0:T(8,128)(2,1)S(1)} %shard_map.86), channel_id=1, source_target_pairs={{0,8},{4,12},{8,16},{12,20},{16,24},{20,28},{24,0},{28,4},{1,9},{5... | collective-permute-start | bytes 1179656 | tf_op jit(solution)/shard_map/ppermute | solution.py:365

commit v13 on v12

--- a/solution.py
+++ b/solution.py
@@ -425,7 +425,7 @@
         if i == 1:
             later, _ = lax.optimization_barrier((w_down, part))
             downs.append(over_core(later)[0])
-        cut = units if i == 1 else 2 * units
+        cut = 2 * units
         parts_in[i] = []
         for step in range(1, parts):
             columns = range(2 * units * (step - 1), 2 * units * step, cut)
@@ -491,28 +491,30 @@
         activate(0)
         pick(1)
         order.extend(downs[1:])
+        down_product(0)
+        home_product(1, 2)
         pick(2)
-        home_product(1, 2)
         home_product(2, 3)
-        down_product(0)
+        activate(2)
         pick(3)
         activate(1)
-        activate(2)
         down_product(1)
         down_product(2)
+        order.append(blocks[2, "b"])
         pick(4)
         home_product(3)
+        order.extend(downs[1:])
         home_product(4)
+        pick(5)
         activate(3)
-        pick(5)
+        home_product(5)
         add_hop(0)
+        down_product(3)
+        add_hop(1)
+        add_hop(2)
         order.append(blocks[2, "b"])
-        home_product(5)
-        down_product(3)
         activate(4)
-        add_hop(1)
         down_product(4)
-        add_hop(2)
         activate(5)
         down_product(5)
         add_hop(3)

time: 114 us -> 117 us (1.026)
  waiting for transfers between devices: 47.1 us -> 51.9 us
  starting transfers between devices: 26.6 us -> 25.2 us
    ppermute x13 -> x12, waiting for transfers between devices: 10.3 us -> 20.1 us  [over_x(): lax.ppermute(x, 'tensor', [(i, (i + step) % parts) for i in range(parts)])]
    ppermute x8, waiting for transfers between devices: 11.1 us -> 7.93 us  [over_y(): return lax.ppermute(x, 'expert', [(i, i ^ 1) for i in range(ring)])]
    ppermute x13 -> x12, starting transfers between devices: 14.9 us -> 12.5 us  [over_x(): lax.ppermute(x, 'tensor', [(i, (i + step) % parts) for i in range(parts)])]
    ppermute x6, waiting for transfers between devices: 25.6 us -> 23.9 us  [over_z(): return lax.ppermute(x, 'expert', [(i, (i + 2) % ring) for i in range(ring)])]
    ppermute x8, starting transfers between devices: 9.06 us -> 10.3 us  [over_y(): return lax.ppermute(x, 'expert', [(i, i ^ 1) for i in range(ring)])]
  transfers between devices with their start and end apart: 30 -> 29, of which waited for: 9 -> 11; matrix products, arithmetic and copies ran while one was open for 2% -> 2% of each run, Pallas kernels for 25% -> 24%
where the time goes in v13:
time: 117 us
  waiting for transfers between devices  51.9 us (44%)
  Pallas kernels  31.1 us (27%)
  starting transfers between devices  25.2 us (22%)
  local copies, waits for them, and re-layouts  4.94 us (4%)
  other arithmetic  3.09 us (3%)
    ppermute x6, waiting for transfers between devices, over_z(): return lax.ppermute(x, 'expert', [(i, (i + 2) % ring) for i in range(ring)])  23.9 us
    ppermute x12, waiting for transfers between devices, over_x(): lax.ppermute(x, 'tensor', [(i, (i + step) % parts) for i in range(parts)])  20.1 us
    ppermute x12, starting transfers between devices, over_x(): lax.ppermute(x, 'tensor', [(i, (i + step) % parts) for i in range(parts)])  12.5 us
    pallas_call x6, Pallas kernels, pick_rows(): pl.pallas_call(kernel, grid=(1,), out_shape=(*out, *[jax.ShapeDtypeStruct...  11.4 us
    pallas_call x6, Pallas kernels, down_rows(): pl.pallas_call(functools.partial(down_kernel, experts, capacity, groups,...  11 us
    ppermute x8, starting transfers between devices, over_y(): return lax.ppermute(x, 'expert', [(i, i ^ 1) for i in range(ring)])  10.3 us
    ppermute x8, waiting for transfers between devices, over_y(): return lax.ppermute(x, 'expert', [(i, i ^ 1) for i in range(ring)])  7.93 us
    pallas_call x6, Pallas kernels, home_rows(): pl.pallas_call(functools.partial(home_kernel, capacity, units, groups, le...  7.71 us
  transfers between devices with their start and end apart: 29, of which 11 were waited for; matrix products, arithmetic and copies ran while one was open for 2% of the time, Pallas kernels for 24%

profile of v13, /device:TPU:0, one launch (start us, length us, event | category | flops | bytes accessed | tf_op | source)
XLA Modules:
  0.0 116.6 jit_solution(15067140467528781224)
XLA Ops:
  0.0 0.5 collective-permute-start.4
  0.5 0.7 convert_bitcast_fusion
  1.2 0.7 pad_maximum_fusion.routes_ref
  1.9 1.0 copy-done.5
  2.9 0.4 shard_map.64.refs_0_.refs_2_
  3.3 3.0 %collective-permute-start = (bf16[96,2176]{1,0:T(8,128)(2,1)S(1)}, bf16[96,2176]{1,0:T(8,128)(2,1)S(1)}, u32[]{:S(2)}, u32[]{:S(2)}) collective-permute-start(bf16[96,2176]{1,0:T(8,128)(2,1)S(1)} %shard_map.64.refs_0_.refs_2_), channel_id=1, source_target_pairs={{0,4},{4,0},{8,12},{12,8},{16,20},{20,16},{24,28},{28,24},{1,5},{5... | collective-permute-start | bytes 1253384 | tf_op jit(solution)/shard_map/ppermute | solution.py:362
  6.4 1.6 %collective-permute-start.1 = (bf16[96,2176]{1,0:T(8,128)(2,1)S(1)}, bf16[96,2176]{1,0:T(8,128)(2,1)S(1)}, u32[]{:S(2)}, u32[]{:S(2)}) collective-permute-start(bf16[96,2176]{1,0:T(8,128)(2,1)S(1)} %shard_map.64.refs_0_.refs_2_), channel_id=1, source_target_pairs={{0,8},{4,12},{8,16},{12,20},{16,24},{20,28},{24,0},{28,4},{1,9},{5... | collective-permute-start | bytes 1253384 | tf_op jit(solution)/shard_map/ppermute | solution.py:365
  7.9 1.9 %copy-done = bf16[1,2048,768]{2,1,0:T(8,128)(2,1)S(1)} copy-done((bf16[1,2048,768]{2,1,0:T(8,128)(2,1)S(1)}, bf16[1,2048,768]{2,1,0:T(8,128)(2,1)}, u32[]{:S(2)}) %copy-start) | copy-done | bytes 3145752
  9.8 1.9 %copy-done.2 = bf16[1,2048,768]{2,1,0:T(8,128)(2,1)S(1)} copy-done((bf16[1,2048,768]{2,1,0:T(8,128)(2,1)S(1)}, bf16[1,2048,768]{2,1,0:T(8,128)(2,1)}, u32[]{:S(2)}) %copy-start.2) | copy-done | bytes 3145752
  11.7 1.1 shard_map.65
  12.8 1.6 %collective-permute-start.2 = (bf16[80,768]{1,0:T(8,128)(2,1)S(1)}, bf16[80,768]{1,0:T(8,128)(2,1)S(1)}, u32[]{:S(2)}, u32[]{:S(2)}) collective-permute-start(bf16[80,768]{1,0:T(8,128)(2,1)S(1)} %get-tuple-element.25.refs_2_), channel_id=1, source_target_pairs={{0,2},{2,0},{1,3},{3,1},{4,6},{6,4},{5,7},{7,5},{8,10},{10,8},{9,1... | collective-permute-start | bytes 368648 | tf_op jit(solution)/shard_map/ppermute | solution.py:374
  14.4 1.8 %collective-permute-done.refs_3_.refs_1_ = bf16[96,2176]{1,0:T(8,128)(2,1)S(1)} collective-permute-done((bf16[96,2176]{1,0:T(8,128)(2,1)S(1)}, bf16[96,2176]{1,0:T(8,128)(2,1)S(1)}, u32[]{:S(2)}, u32[]{:S(2)}) %collective-permute-start) | collective-permute-done | bytes 417824 | tf_op jit(solution)/shard_map/ppermute | solution.py:362
  16.2 3.3 %collective-permute-done.1.refs_4_ = bf16[96,2176]{1,0:T(8,128)(2,1)S(1)} collective-permute-done((bf16[96,2176]{1,0:T(8,128)(2,1)S(1)}, bf16[96,2176]{1,0:T(8,128)(2,1)S(1)}, u32[]{:S(2)}, u32[]{:S(2)}) %collective-permute-start.1) | collective-permute-done | bytes 417824 | tf_op jit(solution)/shard_map/ppermute | solution.py:365
  19.5 0.7 shard_map.66
  20.3 2.6 %shard_map.67 = (bf16[368,2048]{1,0:T(8,128)(2,1)S(1)}, bf16[368,768]{1,0:T(8,128)(2,1)S(1)}) custom-call(bf16[96,2176]{1,0:T(8,128)(2,1)S(1)} %shard_map.64.refs_0_.refs_2_, bf16[96,2176]{1,0:T(8,128)(2,1)S(1)} %collective-permute-done.refs_3_.refs_1_, bf16[96,2176]{1,0:T(8,128)(2,1)S(1)} %get-tuple-element.27.refs_2_.refs_4_, ...), custom_call_target="tpu_custom_call" | custom-call | flops 1 | bytes 1 | tf_op jit(solution)/shard_map/pallas_call | solution.py:216
  23.0 1.6 %collective-permute-start.8 = (bf16[368,768]{1,0:T(8,128)(2,1)S(1)}, bf16[368,768]{1,0:T(8,128)(2,1)S(1)}, u32[]{:S(2)}, u32[]{:S(2)}) collective-permute-start(bf16[368,768]{1,0:T(8,128)(2,1)S(1)} %get-tuple-element.28.refs_4_), channel_id=1, source_target_pairs={{0,2},{2,0},{1,3},{3,1},{4,6},{6,4},{5,7},{7,5},{8,10},{10,8},{9,1... | collective-permute-start | bytes 1695752 | tf_op jit(solution)/shard_map/ppermute | solution.py:374
  24.5 0.5 collective-permute-start.11
  25.0 0.5 collective-permute-start.3
  25.6 13.9 %collective-permute-done.3.refs_1_ = bf16[80,384]{1,0:T(8,128)(2,1)S(1)} collective-permute-done((bf16[80,384]{1,0:T(8,128)(2,1)S(1)}, bf16[80,384]{1,0:T(8,128)(2,1)S(1)}, u32[]{:S(2)}, u32[]{:S(2)}) %collective-permute-start.3) | collective-permute-done | bytes 61472 | tf_op jit(solution)/shard_map/ppermute | solution.py:374
  39.5 1.1 shard_map.68.refs_4_.refs_0_
  40.6 1.4 %shard_map.69 = (f32[368,768]{1,0:T(8,128)S(1)}, bf16[96,2176]{1,0:T(8,128)(2,1)S(1)}) custom-call(bf16[368,2048]{1,0:T(8,128)(2,1)S(1)} %get-tuple-element.30.x_ref, bf16[2048,768]{1,0:T(8,128)(2,1)S(1)} %bitcast.34, bf16[2048,768]{1,0:T(8,128)(2,1)S(1)} %bitcast.44, bf16[2048,768]{1,0:T(8,128)(2,1)S(1)} %bitcast.12, ...), custom_call_target="tpu_custom_call", output_to_operand_aliasing={{1}: (6, {})} | custom-call | flops 1 | bytes 1 | tf_op jit(solution)/shard_map/pallas_call | solution.py:245
  42.0 0.6 collective-permute-start.10
  42.6 1.9 %shard_map.70 = (bf16[144,2048]{1,0:T(8,128)(2,1)S(1)}, bf16[144,768]{1,0:T(8,128)(2,1)S(1)}) custom-call(bf16[96,2176]{1,0:T(8,128)(2,1)S(1)} %collective-permute-done.11.refs_0_.refs_2_, bf16[2048,768]{1,0:T(8,128)(2,1)S(1)} %bitcast.13, bf16[2048,768]{1,0:T(8,128)(2,1)S(1)} %bitcast.25, bf16[2048,768]{1,0:T(8,128)(2,1)S(1)} %bitcast.35, ...), custom_call_target="tpu_custom_call" | custom-call | flops 1 | bytes 1 | tf_op jit(solution)/shard_map/pallas_call | solution.py:216
  44.5 1.6 %collective-permute-start.13 = (bf16[144,768]{1,0:T(8,128)(2,1)S(1)}, bf16[144,768]{1,0:T(8,128)(2,1)S(1)}, u32[]{:S(2)}, u32[]{:S(2)}) collective-permute-start(bf16[144,768]{1,0:T(8,128)(2,1)S(1)} %get-tuple-element.34.refs_4_), channel_id=1, source_target_pairs={{0,2},{2,0},{1,3},{3,1},{4,6},{6,4},{5,7},{7,5},{8,10},{10,8},{9,1... | collective-permute-start | bytes 663560 | tf_op jit(solution)/shard_map/ppermute | solution.py:374
  46.1 0.1 convert_add_fusion
  46.2 0.2 fusion.refs_0_.refs_8_
  46.4 0.6 collective-permute-start.9
  47.0 8.3 %collective-permute-done.12.refs_5_ = bf16[96,2176]{1,0:T(8,128)(2,1)S(1)} collective-permute-done((bf16[96,2176]{1,0:T(8,128)(2,1)S(1)}, bf16[96,2176]{1,0:T(8,128)(2,1)S(1)}, u32[]{:S(2)}, u32[]{:S(2)}) %collective-permute-start.12) | collective-permute-done | bytes 417824 | tf_op jit(solution)/shard_map/ppermute | solution.py:365
  55.3 1.4 %shard_map.71 = (f32[144,768]{1,0:T(8,128)S(1)}, bf16[96,2176]{1,0:T(8,128)(2,1)S(1)}) custom-call(bf16[144,2048]{1,0:T(8,128)(2,1)S(1)} %get-tuple-element.33.x_ref, bf16[2048,768]{1,0:T(8,128)(2,1)S(1)} %bitcast.14, bf16[2048,768]{1,0:T(8,128)(2,1)S(1)} %bitcast.26, bf16[2048,768]{1,0:T(8,128)(2,1)S(1)} %bitcast.36, ...), custom_call_target="tpu_custom_call", output_to_operand_aliasing={{1}: (6, {})} | custom-call | flops 1 | bytes 1 | tf_op jit(solution)/shard_map/pallas_call | solution.py:245
  56.7 1.6 %collective-permute-start.15 = (bf16[96,2176]{1,0:T(8,128)(2,1)S(1)}, bf16[96,2176]{1,0:T(8,128)(2,1)S(1)}, u32[]{:S(2)}, u32[]{:S(2)}) collective-permute-start(bf16[96,2176]{1,0:T(8,128)(2,1)S(1)} %get-tuple-element.37.refs_0_.refs_2_), channel_id=1, source_target_pairs={{0,4},{4,0},{8,12},{12,8},{16,20},{20,16},{24,28},{28,24},{1,5},{5... | collective-permute-start | bytes 1253384 | tf_op jit(solution)/shard_map/ppermute | solution.py:362
  58.4 1.6 %collective-permute-start.16 = (bf16[144,384]{1,0:T(8,128)(2,1)S(1)}, bf16[144,384]{1,0:T(8,128)(2,1)S(1)}, u32[]{:S(2)}, u32[]{:S(2)}) collective-permute-start(bf16[144,384]{1,0:T(8,128)(2,1)S(1)} %fusion.4.refs_7_.refs_0_), channel_id=1, source_target_pairs={{0,2},{2,0},{1,3},{3,1},{4,6},{6,4},{5,7},{7,5},{8,10},{10,8},{9,1... | collective-permute-start | bytes 331784 | tf_op jit(solution)/shard_map/ppermute | solution.py:374
  60.0 2.0 %shard_map.72 = (bf16[288,2048]{1,0:T(8,128)(2,1)S(1)}, bf16[288,768]{1,0:T(8,128)(2,1)S(1)}) custom-call(bf16[96,2176]{1,0:T(8,128)(2,1)S(1)} %collective-permute-done.10.refs_0_.refs_6_.refs_2_, bf16[96,2176]{1,0:T(8,128)(2,1)S(1)} %get-tuple-element.32.refs_1_.refs_3_, bf16[2048,768]{1,0:T(8,128)(2,1)S(1)} %bitcast.15, bf16[2048,768]{1,0:T(8,128)(2,1)S(1)} %bitcast.27, ...), custom_call_target="tpu_custom_call" | custom-call | flops 1 | bytes 1 | tf_op jit(solution)/shard_map/pallas_call | solution.py:216
  62.0 0.6 collective-permute-start.17
  62.6 2.6 %shard_map.73.refs_5_ = bf16[288,2048]{1,0:T(8,128)(2,1)S(1)} custom-call(bf16[368,384]{1,0:T(8,128)(2,1)S(1)} %fusion.refs_0_.refs_8_, bf16[368,384]{1,0:T(8,128)(2,1)S(1)} %collective-permute-done.9.refs_1_, bf16[96,2176]{1,0:T(8,128)(2,1)S(1)} %shard_map.64.refs_0_.refs_2_, bf16[96,2176]{1,0:T(8,128)(2,1)S(1)} %collective-permute-done.refs_3_.refs_1_, ...), custom_call_target="tpu_custom_call" | custom-call | flops 1 | bytes 1 | tf_op jit(solution)/shard_map/pallas_call | solution.py:314
  65.3 0.6 collective-permute-start.14
  65.9 1.7 %shard_map.74.refs_5_ = bf16[96,2048]{1,0:T(8,128)(2,1)S(1)} custom-call(bf16[144,384]{1,0:T(8,128)(2,1)S(1)} %fusion.4.refs_7_.refs_0_, bf16[144,384]{1,0:T(8,128)(2,1)S(1)} %collective-permute-done.16.refs_1_, bf16[96,2176]{1,0:T(8,128)(2,1)S(1)} %collective-permute-done.11.refs_0_.refs_2_, bf16[768,2048]{1,0:T(8,128)(2,1)S(1)} %bitcast.62, ...), custom_call_target="tpu_custom_call" | custom-call | flops 1 | bytes 1 | tf_op jit(solution)/shard_map/pallas_call | solution.py:314
  67.6 0.5 collective-permute-done.15.refs_0_.refs_2_
  68.0 1.9 %shard_map.75 = (bf16[144,2048]{1,0:T(8,128)(2,1)S(1)}, bf16[144,768]{1,0:T(8,128)(2,1)S(1)}) custom-call(bf16[96,2176]{1,0:T(8,128)(2,1)S(1)} %collective-permute-done.15.refs_0_.refs_2_, bf16[2048,768]{1,0:T(8,128)(2,1)S(1)} %bitcast.16, bf16[2048,768]{1,0:T(8,128)(2,1)S(1)} %bitcast.28, bf16[2048,768]{1,0:T(8,128)(2,1)S(1)} %bitcast.38, ...), custom_call_target="tpu_custom_call" | custom-call | flops 1 | bytes 1 | tf_op jit(solution)/shard_map/pallas_call | solution.py:216
  70.0 1.2 shard_map.76.refs_4_
  71.1 1.6 %collective-permute-done.17 = bf16[288,768]{1,0:T(8,128)(2,1)S(1)} collective-permute-done((bf16[288,768]{1,0:T(8,128)(2,1)S(1)}, bf16[288,768]{1,0:T(8,128)(2,1)S(1)}, u32[]{:S(2)}, u32[]{:S(2)}) %collective-permute-start.17) | collective-permute-done | bytes 442400 | tf_op jit(solution)/shard_map/ppermute | solution.py:374
  72.8 0.1 fusion.1.refs_5_.refs_0_
  72.9 1.1 collective-permute-start.22
  74.0 1.4 %collective-permute-start.24 = (bf16[96,2048]{1,0:T(8,128)(2,1)S(1)}, bf16[96,2048]{1,0:T(8,128)(2,1)S(1)}, u32[]{:S(2)}, u32[]{:S(2)}) collective-permute-start(bf16[96,2048]{1,0:T(8,128)(2,1)S(1)} %shard_map.74.refs_5_), channel_id=1, source_target_pairs={{0,4},{4,0},{8,12},{12,8},{16,20},{20,16},{24,28},{28,24},{1,5},{5... | collective-permute-start | bytes 1179656 | tf_op jit(solution)/shard_map/ppermute | solution.py:362
  75.4 1.6 %shard_map.77.refs_5_ = f32[144,768]{1,0:T(8,128)S(1)} custom-call(bf16[144,2048]{1,0:T(8,128)(2,1)S(1)} %get-tuple-element.38.x_ref, bf16[2048,768]{1,0:T(8,128)(2,1)S(1)} %bitcast.18, bf16[2048,768]{1,0:T(8,128)(2,1)S(1)} %bitcast.30, bf16[2048,768]{1,0:T(8,128)(2,1)S(1)} %bitcast.40, bf16[2048,768]{1,0:T(8,128)(2,1)S(1)} %bitcast.50, ...), custom_call_target="tpu_custom_call" | custom-call | flops 1 | bytes 1 | tf_op jit(solution)/shard_map/pallas_call | solution.py:245
  77.0 0.6 collective-permute-start.20
  77.6 1.9 %shard_map.78 = (bf16[144,2048]{1,0:T(8,128)(2,1)S(1)}, bf16[144,768]{1,0:T(8,128)(2,1)S(1)}) custom-call(bf16[96,2176]{1,0:T(8,128)(2,1)S(1)} %get-tuple-element.37.refs_0_.refs_2_, bf16[2048,768]{1,0:T(8,128)(2,1)S(1)} %bitcast.19, bf16[2048,768]{1,0:T(8,128)(2,1)S(1)} %bitcast.31, bf16[2048,768]{1,0:T(8,128)(2,1)S(1)} %bitcast.41, ...), custom_call_target="tpu_custom_call" | custom-call | flops 1 | bytes 1 | tf_op jit(solution)/shard_map/pallas_call | solution.py:216
  79.6 1.5 %collective-permute-start.18 = (bf16[144,768]{1,0:T(8,128)(2,1)S(1)}, bf16[144,768]{1,0:T(8,128)(2,1)S(1)}, u32[]{:S(2)}, u32[]{:S(2)}) collective-permute-start(bf16[144,768]{1,0:T(8,128)(2,1)S(1)} %get-tuple-element.42.refs_4_), channel_id=1, source_target_pairs={{0,2},{2,0},{1,3},{3,1},{4,6},{6,4},{5,7},{7,5},{8,10},{10,8},{9,1... | collective-permute-start | bytes 663560 | tf_op jit(solution)/shard_map/ppermute | solution.py:374
  81.1 1.4 %shard_map.79.refs_3_ = f32[144,768]{1,0:T(8,128)S(1)} custom-call(bf16[144,2048]{1,0:T(8,128)(2,1)S(1)} %get-tuple-element.41.x_ref, bf16[2048,768]{1,0:T(8,128)(2,1)S(1)} %bitcast.20, bf16[2048,768]{1,0:T(8,128)(2,1)S(1)} %bitcast.32, bf16[2048,768]{1,0:T(8,128)(2,1)S(1)} %bitcast.42, bf16[2048,768]{1,0:T(8,128)(2,1)S(1)} %bitcast.52, ...), custom_call_target="tpu_custom_call" | custom-call | flops 1 | bytes 1 | tf_op jit(solution)/shard_map/pallas_call | solution.py:245
  82.5 0.2 shard_map.80.refs_6_
  82.7 2.2 %shard_map.81.refs_2_ = bf16[192,2048]{1,0:T(8,128)(2,1)S(1)} custom-call(bf16[288,384]{1,0:T(8,128)(2,1)S(1)} %fusion.1.refs_5_.refs_0_, bf16[288,384]{1,0:T(8,128)(2,1)S(1)} %collective-permute-done.22.refs_1_, bf16[96,2176]{1,0:T(8,128)(2,1)S(1)} %collective-permute-done.10.refs_0_.refs_6_.refs_2_, ...), custom_call_target="tpu_custom_call" | custom-call | flops 1 | bytes 1 | tf_op jit(solution)/shard_map/pallas_call | solution.py:314
  85.0 0.7 collective-permute-start.23
  85.9 0.1 collective-permute-done.20
  86.2 1.0 collective-permute-start.21
  87.2 5.7 %collective-permute-done.23.refs_1_ = bf16[96,2048]{1,0:T(8,128)(2,1)S(1)} collective-permute-done((bf16[96,2048]{1,0:T(8,128)(2,1)S(1)}, bf16[96,2048]{1,0:T(8,128)(2,1)S(1)}, u32[]{:S(2)}, u32[]{:S(2)}) %collective-permute-start.23) | collective-permute-done | bytes 393248 | tf_op jit(solution)/shard_map/ppermute | solution.py:362
  92.8 2.6 %collective-permute-done.25.refs_2_ = bf16[96,2048]{1,0:T(8,128)(2,1)S(1)} collective-permute-done((bf16[96,2048]{1,0:T(8,128)(2,1)S(1)}, bf16[96,2048]{1,0:T(8,128)(2,1)S(1)}, u32[]{:S(2)}, u32[]{:S(2)}) %collective-permute-start.25) | collective-permute-done | bytes 393248 | tf_op jit(solution)/shard_map/ppermute | solution.py:365
  95.5 0.1 shard_map.83.refs_5_
  95.7 1.7 %shard_map.84.refs_5_ = bf16[96,2048]{1,0:T(8,128)(2,1)S(1)} custom-call(bf16[144,384]{1,0:T(8,128)(2,1)S(1)} %fusion.2.refs_0_.refs_7_, bf16[144,384]{1,0:T(8,128)(2,1)S(1)} %collective-permute-done.21.refs_1_, bf16[96,2176]{1,0:T(8,128)(2,1)S(1)} %collective-permute-done.15.refs_0_.refs_2_, bf16[768,2048]{1,0:T(8,128)(2,1)S(1)} %bitcast.64, ...), custom_call_target="tpu_custom_call" | custom-call | flops 1 | bytes 1 | tf_op jit(solution)/shard_map/pallas_call | solution.py:314
  97.4 2.0 %collective-permute-start.26 = (bf16[96,2048]{1,0:T(8,128)(2,1)S(1)}, bf16[96,2048]{1,0:T(8,128)(2,1)S(1)}, u32[]{:S(2)}, u32[]{:S(2)}) collective-permute-start(bf16[96,2048]{1,0:T(8,128)(2,1)S(1)} %shard_map.84.refs_5_), channel_id=1, source_target_pairs={{0,4},{4,0},{8,12},{12,8},{16,20},{20,16},{24,28},{28,24},{1,5},{5... | collective-permute-start | bytes 1179656 | tf_op jit(solution)/shard_map/ppermute | solution.py:362
  99.5 0.3 collective-permute-start.19
  99.8 4.5 %collective-permute-done.19.refs_1_ = bf16[144,384]{1,0:T(8,128)(2,1)S(1)} collective-permute-done((bf16[144,384]{1,0:T(8,128)(2,1)S(1)}, bf16[144,384]{1,0:T(8,128)(2,1)S(1)}, u32[]{:S(2)}, u32[]{:S(2)}) %collective-permute-start.19) | collective-permute-done | bytes 110624 | tf_op jit(solution)/shard_map/ppermute | solution.py:374
  104.3 1.7 %shard_map.85.refs_0_.refs_3_ = bf16[96,2048]{1,0:T(8,128)(2,1)S(1)} custom-call(bf16[144,384]{1,0:T(8,128)(2,1)S(1)} %fusion.3.refs_0_.refs_6_, bf16[144,384]{1,0:T(8,128)(2,1)S(1)} %collective-permute-done.19.refs_1_, bf16[96,2176]{1,0:T(8,128)(2,1)S(1)} %get-tuple-element.37.refs_0_.refs_2_, bf16[768,2048]{1,0:T(8,128)(2,1)S(1)} %bitcast.65, ...), custom_call_target="tpu_custom_call" | custom-call | flops 1 | bytes 1 | tf_op jit(solution)/shard_map/pallas_call | solution.py:314
  106.0 0.2 shard_map.86
  106.2 9.6 %collective-permute-done.28 = bf16[96,2048]{1,0:T(8,128)(2,1)S(1)} collective-permute-done((bf16[96,2048]{1,0:T(8,128)(2,1)S(1)}, bf16[96,2048]{1,0:T(8,128)(2,1)S(1)}, u32[]{:S(2)}, u32[]{:S(2)}) %collective-permute-start.28) | collective-permute-done | bytes 393248 | tf_op jit(solution)/shard_map/ppermute | solution.py:365
  115.8 0.8 add_convert_fusion
  (46 shorter events, 1.1 us)
Async XLA Ops:
  0.0 20.3 %collective-permute-start.4 = (bf16[1,2048,768]{2,1,0:T(8,128)(2,1)}, bf16[1,2048,768]{2,1,0:T(8,128)(2,1)S(1)}, u32[]{:S(2)}, u32[]{:S(2)}) collective-permute-start(bf16[1,2048,768]{2,1,0:T(8,128)(2,1)} %param.9), channel_id=1, source_target_pairs={{0,1},{1,0},{2,3},{3,2},{4,5},{5,4},{6,7},{7,6},{8,9},{9,8},{10,11... | collective-permute-start | bytes 9437192 | tf_op jit(solution)/shard_map/ppermute | solution.py:371
  0.5 19.8 %collective-permute-start.5 = (bf16[1,2048,768]{2,1,0:T(8,128)(2,1)}, bf16[1,2048,768]{2,1,0:T(8,128)(2,1)S(1)}, u32[]{:S(2)}, u32[]{:S(2)}) collective-permute-start(bf16[1,2048,768]{2,1,0:T(8,128)(2,1)} %param.10), channel_id=1, source_target_pairs={{0,1},{1,0},{2,3},{3,2},{4,5},{5,4},{6,7},{7,6},{8,9},{9,8},{10,11... | collective-permute-start | bytes 9437192 | tf_op jit(solution)/shard_map/ppermute | solution.py:371
  1.9 1.0 copy-start.5
  3.3 12.8 %collective-permute-start = (bf16[96,2176]{1,0:T(8,128)(2,1)S(1)}, bf16[96,2176]{1,0:T(8,128)(2,1)S(1)}, u32[]{:S(2)}, u32[]{:S(2)}) collective-permute-start(bf16[96,2176]{1,0:T(8,128)(2,1)S(1)} %shard_map.64.refs_0_.refs_2_), channel_id=1, source_target_pairs={{0,4},{4,0},{8,12},{12,8},{16,20},{20,16},{24,28},{28,24},{1,5},{5... | collective-permute-start | bytes 1253384 | tf_op jit(solution)/shard_map/ppermute | solution.py:362
  6.4 13.1 %collective-permute-start.1 = (bf16[96,2176]{1,0:T(8,128)(2,1)S(1)}, bf16[96,2176]{1,0:T(8,128)(2,1)S(1)}, u32[]{:S(2)}, u32[]{:S(2)}) collective-permute-start(bf16[96,2176]{1,0:T(8,128)(2,1)S(1)} %shard_map.64.refs_0_.refs_2_), channel_id=1, source_target_pairs={{0,8},{4,12},{8,16},{12,20},{16,24},{20,28},{24,0},{28,4},{1,9},{5... | collective-permute-start | bytes 1253384 | tf_op jit(solution)/shard_map/ppermute | solution.py:365
  7.9 1.9 %copy-start = (bf16[1,2048,768]{2,1,0:T(8,128)(2,1)S(1)}, bf16[1,2048,768]{2,1,0:T(8,128)(2,1)}, u32[]{:S(2)}) copy-start(bf16[1,2048,768]{2,1,0:T(8,128)(2,1)} %param.9) | copy-start | bytes 9437188
  9.8 1.9 %copy-start.2 = (bf16[1,2048,768]{2,1,0:T(8,128)(2,1)S(1)}, bf16[1,2048,768]{2,1,0:T(8,128)(2,1)}, u32[]{:S(2)}) copy-start(bf16[1,2048,768]{2,1,0:T(8,128)(2,1)} %param.10) | copy-start | bytes 9437188
  11.7 7.8 %copy-start.1 = (bf16[1,2048,768]{2,1,0:T(8,128)(2,1)S(1)}, bf16[1,2048,768]{2,1,0:T(8,128)(2,1)}, u32[]{:S(2)}) copy-start(bf16[1,2048,768]{2,1,0:T(8,128)(2,1)} %param.9) | copy-start | bytes 9437188
  11.7 7.8 %copy-start.3 = (bf16[1,2048,768]{2,1,0:T(8,128)(2,1)S(1)}, bf16[1,2048,768]{2,1,0:T(8,128)(2,1)}, u32[]{:S(2)}) copy-start(bf16[1,2048,768]{2,1,0:T(8,128)(2,1)} %param.10) | copy-start | bytes 9437188
  12.8 7.4 %collective-permute-start.2 = (bf16[80,768]{1,0:T(8,128)(2,1)S(1)}, bf16[80,768]{1,0:T(8,128)(2,1)S(1)}, u32[]{:S(2)}, u32[]{:S(2)}) collective-permute-start(bf16[80,768]{1,0:T(8,128)(2,1)S(1)} %get-tuple-element.25.refs_2_), channel_id=1, source_target_pairs={{0,2},{2,0},{1,3},{3,1},{4,6},{6,4},{5,7},{7,5},{8,10},{10,8},{9,1... | collective-permute-start | bytes 368648 | tf_op jit(solution)/shard_map/ppermute | solution.py:374
  20.3 2.6 %copy-start.4 = (bf16[1,768,2048]{2,1,0:T(8,128)(2,1)S(1)}, bf16[1,768,2048]{2,1,0:T(8,128)(2,1)}, u32[]{:S(2)}) copy-start(bf16[1,768,2048]{2,1,0:T(8,128)(2,1)} %param.11) | copy-start | bytes 9437188
  22.9 16.6 %collective-permute-start.6 = (bf16[1,768,2048]{2,1,0:T(8,128)(2,1)S(1)}, bf16[1,768,2048]{2,1,0:T(8,128)(2,1)S(1)}, u32[]{:S(2)}, u32[]{:S(2)}) collective-permute-start(bf16[1,768,2048]{2,1,0:T(8,128)(2,1)S(1)} %copy-done.4), channel_id=1, source_target_pairs={{0,1},{1,0},{2,3},{3,2},{4,5},{5,4},{6,7},{7,6},{8,9},{9,8},{10,11... | collective-permute-start | bytes 9437192 | tf_op jit(solution)/shard_map/ppermute | solution.py:371
  23.0 23.1 %collective-permute-start.8 = (bf16[368,768]{1,0:T(8,128)(2,1)S(1)}, bf16[368,768]{1,0:T(8,128)(2,1)S(1)}, u32[]{:S(2)}, u32[]{:S(2)}) collective-permute-start(bf16[368,768]{1,0:T(8,128)(2,1)S(1)} %get-tuple-element.28.refs_4_), channel_id=1, source_target_pairs={{0,2},{2,0},{1,3},{3,1},{4,6},{6,4},{5,7},{7,5},{8,10},{10,8},{9,1... | collective-permute-start | bytes 1695752 | tf_op jit(solution)/shard_map/ppermute | solution.py:374
  24.5 16.0 %collective-permute-start.7 = (bf16[96,2176]{1,0:T(8,128)(2,1)S(1)}, bf16[96,2176]{1,0:T(8,128)(2,1)S(1)}, u32[]{:S(2)}, u32[]{:S(2)}) collective-permute-start(bf16[96,2176]{1,0:T(8,128)(2,1)S(1)} %get-tuple-element.27.refs_2_.refs_4_), channel_id=1, source_target_pairs={{0,8},{4,12},{8,16},{12,20},{16,24},{20,28},{24,0},{28,4},{1,9},{5... | collective-permute-start | bytes 1253384 | tf_op jit(solution)/shard_map/ppermute | solution.py:365
  24.5 18.0 %collective-permute-start.11 = (bf16[96,2176]{1,0:T(8,128)(2,1)S(1)}, bf16[96,2176]{1,0:T(8,128)(2,1)S(1)}, u32[]{:S(2)}, u32[]{:S(2)}) collective-permute-start(bf16[96,2176]{1,0:T(8,128)(2,1)S(1)} %get-tuple-element.27.refs_2_.refs_4_), channel_id=1, source_target_pairs={{0,4},{4,0},{8,12},{12,8},{16,20},{20,16},{24,28},{28,24},{1,5},{5... | collective-permute-start | bytes 1253384 | tf_op jit(solution)/shard_map/ppermute | solution.py:362
  25.0 14.4 %collective-permute-start.3 = (bf16[80,384]{1,0:T(8,128)(2,1)S(1)}, bf16[80,384]{1,0:T(8,128)(2,1)S(1)}, u32[]{:S(2)}, u32[]{:S(2)}) collective-permute-start(bf16[80,384]{1,0:T(8,128)(2,1)S(1)} %fusion.5.refs_8_.refs_0_), channel_id=1, source_target_pairs={{0,2},{2,0},{1,3},{3,1},{4,6},{6,4},{5,7},{7,5},{8,10},{10,8},{9,1... | collective-permute-start | bytes 184328 | tf_op jit(solution)/shard_map/ppermute | solution.py:374
  42.0 18.0 %collective-permute-start.10 = (bf16[96,2176]{1,0:T(8,128)(2,1)S(1)}, bf16[96,2176]{1,0:T(8,128)(2,1)S(1)}, u32[]{:S(2)}, u32[]{:S(2)}) collective-permute-start(bf16[96,2176]{1,0:T(8,128)(2,1)S(1)} %get-tuple-element.32.refs_1_.refs_3_), channel_id=1, source_target_pairs={{0,4},{4,0},{8,12},{12,8},{16,20},{20,16},{24,28},{28,24},{1,5},{5... | collective-permute-start | bytes 1253384 | tf_op jit(solution)/shard_map/ppermute | solution.py:362
  42.6 12.7 %collective-permute-start.12 = (bf16[96,2176]{1,0:T(8,128)(2,1)S(1)}, bf16[96,2176]{1,0:T(8,128)(2,1)S(1)}, u32[]{:S(2)}, u32[]{:S(2)}) collective-permute-start(bf16[96,2176]{1,0:T(8,128)(2,1)S(1)} %get-tuple-element.32.refs_1_.refs_3_), channel_id=1, source_target_pairs={{0,8},{4,12},{8,16},{12,20},{16,24},{20,28},{24,0},{28,4},{1,9},{5... | collective-permute-start | bytes 1253384 | tf_op jit(solution)/shard_map/ppermute | solution.py:365
  44.5 13.8 %collective-permute-start.13 = (bf16[144,768]{1,0:T(8,128)(2,1)S(1)}, bf16[144,768]{1,0:T(8,128)(2,1)S(1)}, u32[]{:S(2)}, u32[]{:S(2)}) collective-permute-start(bf16[144,768]{1,0:T(8,128)(2,1)S(1)} %get-tuple-element.34.refs_4_), channel_id=1, source_target_pairs={{0,2},{2,0},{1,3},{3,1},{4,6},{6,4},{5,7},{7,5},{8,10},{10,8},{9,1... | collective-permute-start | bytes 663560 | tf_op jit(solution)/shard_map/ppermute | solution.py:374
  46.4 16.2 %collective-permute-start.9 = (bf16[368,384]{1,0:T(8,128)(2,1)S(1)}, bf16[368,384]{1,0:T(8,128)(2,1)S(1)}, u32[]{:S(2)}, u32[]{:S(2)}) collective-permute-start(bf16[368,384]{1,0:T(8,128)(2,1)S(1)} %fusion.refs_0_.refs_8_), channel_id=1, source_target_pairs={{0,2},{2,0},{1,3},{3,1},{4,6},{6,4},{5,7},{7,5},{8,10},{10,8},{9,1... | collective-permute-start | bytes 847880 | tf_op jit(solution)/shard_map/ppermute | solution.py:374
  56.7 11.3 %collective-permute-start.15 = (bf16[96,2176]{1,0:T(8,128)(2,1)S(1)}, bf16[96,2176]{1,0:T(8,128)(2,1)S(1)}, u32[]{:S(2)}, u32[]{:S(2)}) collective-permute-start(bf16[96,2176]{1,0:T(8,128)(2,1)S(1)} %get-tuple-element.37.refs_0_.refs_2_), channel_id=1, source_target_pairs={{0,4},{4,0},{8,12},{12,8},{16,20},{20,16},{24,28},{28,24},{1,5},{5... | collective-permute-start | bytes 1253384 | tf_op jit(solution)/shard_map/ppermute | solution.py:362
  58.4 7.4 %collective-permute-start.16 = (bf16[144,384]{1,0:T(8,128)(2,1)S(1)}, bf16[144,384]{1,0:T(8,128)(2,1)S(1)}, u32[]{:S(2)}, u32[]{:S(2)}) collective-permute-start(bf16[144,384]{1,0:T(8,128)(2,1)S(1)} %fusion.4.refs_7_.refs_0_), channel_id=1, source_target_pairs={{0,2},{2,0},{1,3},{3,1},{4,6},{6,4},{5,7},{7,5},{8,10},{10,8},{9,1... | collective-permute-start | bytes 331784 | tf_op jit(solution)/shard_map/ppermute | solution.py:374
  62.0 10.7 %collective-permute-start.17 = (bf16[288,768]{1,0:T(8,128)(2,1)S(1)}, bf16[288,768]{1,0:T(8,128)(2,1)S(1)}, u32[]{:S(2)}, u32[]{:S(2)}) collective-permute-start(bf16[288,768]{1,0:T(8,128)(2,1)S(1)} %get-tuple-element.36.refs_7_), channel_id=1, source_target_pairs={{0,2},{2,0},{1,3},{3,1},{4,6},{6,4},{5,7},{7,5},{8,10},{10,8},{9,1... | collective-permute-start | bytes 1327112 | tf_op jit(solution)/shard_map/ppermute | solution.py:374
  65.3 17.3 %collective-permute-start.14 = (bf16[96,2048]{1,0:T(8,128)(2,1)S(1)}, bf16[96,2048]{1,0:T(8,128)(2,1)S(1)}, u32[]{:S(2)}, u32[]{:S(2)}) collective-permute-start(bf16[96,2048]{1,0:T(8,128)(2,1)S(1)} %get-tuple-element.44), channel_id=1, source_target_pairs={{0,4},{4,0},{8,12},{12,8},{16,20},{20,16},{24,28},{28,24},{1,5},{5... | collective-permute-start | bytes 1179656 | tf_op jit(solution)/shard_map/ppermute | solution.py:362
  72.9 9.8 %collective-permute-start.22 = (bf16[288,384]{1,0:T(8,128)(2,1)S(1)}, bf16[288,384]{1,0:T(8,128)(2,1)S(1)}, u32[]{:S(2)}, u32[]{:S(2)}) collective-permute-start(bf16[288,384]{1,0:T(8,128)(2,1)S(1)} %fusion.1.refs_5_.refs_0_), channel_id=1, source_target_pairs={{0,2},{2,0},{1,3},{3,1},{4,6},{6,4},{5,7},{7,5},{8,10},{10,8},{9,1... | collective-permute-start | bytes 663560 | tf_op jit(solution)/shard_map/ppermute | solution.py:374
  74.0 11.7 %collective-permute-start.24 = (bf16[96,2048]{1,0:T(8,128)(2,1)S(1)}, bf16[96,2048]{1,0:T(8,128)(2,1)S(1)}, u32[]{:S(2)}, u32[]{:S(2)}) collective-permute-start(bf16[96,2048]{1,0:T(8,128)(2,1)S(1)} %shard_map.74.refs_5_), channel_id=1, source_target_pairs={{0,4},{4,0},{8,12},{12,8},{16,20},{20,16},{24,28},{28,24},{1,5},{5... | collective-permute-start | bytes 1179656 | tf_op jit(solution)/shard_map/ppermute | solution.py:362
  77.0 9.0 %collective-permute-start.20 = (bf16[144,768]{1,0:T(8,128)(2,1)S(1)}, bf16[144,768]{1,0:T(8,128)(2,1)S(1)}, u32[]{:S(2)}, u32[]{:S(2)}) collective-permute-start(bf16[144,768]{1,0:T(8,128)(2,1)S(1)} %get-tuple-element.40.refs_4_), channel_id=1, source_target_pairs={{0,2},{2,0},{1,3},{3,1},{4,6},{6,4},{5,7},{7,5},{8,10},{10,8},{9,1... | collective-permute-start | bytes 663560 | tf_op jit(solution)/shard_map/ppermute | solution.py:374
  79.6 19.8 %collective-permute-start.18 = (bf16[144,768]{1,0:T(8,128)(2,1)S(1)}, bf16[144,768]{1,0:T(8,128)(2,1)S(1)}, u32[]{:S(2)}, u32[]{:S(2)}) collective-permute-start(bf16[144,768]{1,0:T(8,128)(2,1)S(1)} %get-tuple-element.42.refs_4_), channel_id=1, source_target_pairs={{0,2},{2,0},{1,3},{3,1},{4,6},{6,4},{5,7},{7,5},{8,10},{10,8},{9,1... | collective-permute-start | bytes 663560 | tf_op jit(solution)/shard_map/ppermute | solution.py:374
  85.0 7.8 %collective-permute-start.23 = (bf16[96,2048]{1,0:T(8,128)(2,1)S(1)}, bf16[96,2048]{1,0:T(8,128)(2,1)S(1)}, u32[]{:S(2)}, u32[]{:S(2)}) collective-permute-start(bf16[96,2048]{1,0:T(8,128)(2,1)S(1)} %get-tuple-element.46), channel_id=1, source_target_pairs={{0,4},{4,0},{8,12},{12,8},{16,20},{20,16},{24,28},{28,24},{1,5},{5... | collective-permute-start | bytes 1179656 | tf_op jit(solution)/shard_map/ppermute | solution.py:362
  85.8 9.6 %collective-permute-start.25 = (bf16[96,2048]{1,0:T(8,128)(2,1)S(1)}, bf16[96,2048]{1,0:T(8,128)(2,1)S(1)}, u32[]{:S(2)}, u32[]{:S(2)}) collective-permute-start(bf16[96,2048]{1,0:T(8,128)(2,1)S(1)} %shard_map.82.refs_3_), channel_id=1, source_target_pairs={{0,8},{4,12},{8,16},{12,20},{16,24},{20,28},{24,0},{28,4},{1,9},{5... | collective-permute-start | bytes 1179656 | tf_op jit(solution)/shard_map/ppermute | solution.py:365
  86.2 9.5 %collective-permute-start.21 = (bf16[144,384]{1,0:T(8,128)(2,1)S(1)}, bf16[144,384]{1,0:T(8,128)(2,1)S(1)}, u32[]{:S(2)}, u32[]{:S(2)}) collective-permute-start(bf16[144,384]{1,0:T(8,128)(2,1)S(1)} %fusion.2.refs_0_.refs_7_), channel_id=1, source_target_pairs={{0,2},{2,0},{1,3},{3,1},{4,6},{6,4},{5,7},{7,5},{8,10},{10,8},{9,1... | collective-permute-start | bytes 331784 | tf_op jit(solution)/shard_map/ppermute | solution.py:374
  95.6 10.4 %collective-permute-start.27 = (bf16[96,2048]{1,0:T(8,128)(2,1)S(1)}, bf16[96,2048]{1,0:T(8,128)(2,1)S(1)}, u32[]{:S(2)}, u32[]{:S(2)}) collective-permute-start(bf16[96,2048]{1,0:T(8,128)(2,1)S(1)} %shard_map.83.refs_5_), channel_id=1, source_target_pairs={{0,8},{4,12},{8,16},{12,20},{16,24},{20,28},{24,0},{28,4},{1,9},{5... | collective-permute-start | bytes 1179656 | tf_op jit(solution)/shard_map/ppermute | solution.py:365
  97.4 8.6 %collective-permute-start.26 = (bf16[96,2048]{1,0:T(8,128)(2,1)S(1)}, bf16[96,2048]{1,0:T(8,128)(2,1)S(1)}, u32[]{:S(2)}, u32[]{:S(2)}) collective-permute-start(bf16[96,2048]{1,0:T(8,128)(2,1)S(1)} %shard_map.84.refs_5_), channel_id=1, source_target_pairs={{0,4},{4,0},{8,12},{12,8},{16,20},{20,16},{24,28},{28,24},{1,5},{5... | collective-permute-start | bytes 1179656 | tf_op jit(solution)/shard_map/ppermute | solution.py:362
  99.5 4.8 %collective-permute-start.19 = (bf16[144,384]{1,0:T(8,128)(2,1)S(1)}, bf16[144,384]{1,0:T(8,128)(2,1)S(1)}, u32[]{:S(2)}, u32[]{:S(2)}) collective-permute-start(bf16[144,384]{1,0:T(8,128)(2,1)S(1)} %fusion.3.refs_0_.refs_6_), channel_id=1, source_target_pairs={{0,2},{2,0},{1,3},{3,1},{4,6},{6,4},{5,7},{7,5},{8,10},{10,8},{9,1... | collective-permute-start | bytes 331784 | tf_op jit(solution)/shard_map/ppermute | solution.py:374
  106.2 9.6 %collective-permute-start.28 = (bf16[96,2048]{1,0:T(8,128)(2,1)S(1)}, bf16[96,2048]{1,0:T(8,128)(2,1)S(1)}, u32[]{:S(2)}, u32[]{:S(2)}) collective-permute-start(bf16[96,2048]{1,0:T(8,128)(2,1)S(1)} %shard_map.86), channel_id=1, source_target_pairs={{0,8},{4,12},{8,16},{12,20},{16,24},{20,28},{24,0},{28,4},{1,9},{5... | collective-permute-start | bytes 1179656 | tf_op jit(solution)/shard_map/ppermute | solution.py:365
